TPU v7x, 32 devices: a whole 2x2x4 slice. The times are simulated.
32 devices in a mesh: fsdp: 2 (over x), ctx: 4 (over y, core), tp: 4 (over z).
Axes of the slice: x: 2, y: 2, z: 4, core: 2. Of those that a mesh axis runs over, the one named last changes fastest.
Arguments:
- tokens: bfloat16 [2, 1024, 2048], P('fsdp', 'ctx'), may hold values from -6 to 6
- gain_attn: bfloat16 [2048], P(('fsdp', 'ctx')), may hold values from 0.5 to 1.5
- gain_mlp: bfloat16 [2048], P(('fsdp', 'ctx')), may hold values from 0.5 to 1.5
- w_kv: bfloat16 [2048, 2, 2048], P(('fsdp', 'ctx'), None, 'tp'), may hold values from -0.125 to 0.125
- w_query: bfloat16 [2048, 4, 2048], P(('fsdp', 'ctx'), None, 'tp'), may hold values from -0.125 to 0.125
- w_out_attn: bfloat16 [2048, 4, 2048], P(('fsdp', 'ctx'), None, 'tp'), may hold values from -1 to 1
- w_in: bfloat16 [2048, 4, 2, 5632], P(('fsdp', 'ctx'), None, None, 'tp'), may hold values from -0.125 to 0.125
- w_down: bfloat16 [2048, 4, 5632], P(('fsdp', 'ctx'), None, 'tp'), may hold values from -0.15625 to 0.15625
- segments: int32 [2, 1024], P('fsdp'), may hold values from 0 to 255, as said below
- attn_routes: int32 [2, 1024, 2], P('fsdp', 'ctx'), may hold values from 0 to 3, all different within a row; in each aligned block of 256 rows (0 to 255, 256 to 511, ..., all dimensions but the last counted through in order) at most 144 rows name the same one
- attn_gates: float32 [2, 1024, 2], P('fsdp', 'ctx'), may hold values from 0.2 to 0.8
- mlp_routes: int32 [2, 1024, 2], P('fsdp', 'ctx'), may hold values from 0 to 3, all different within a row; in each aligned block of 256 rows (0 to 255, 256 to 511, ..., all dimensions but the last counted through in order) at most 144 rows name the same one
- mlp_gates: float32 [2, 1024, 2], P('fsdp', 'ctx'), may hold values from 0.2 to 0.8
- cotangent: bfloat16 [2, 1024, 2048], P('fsdp', 'ctx'), may hold values from -6 to 6
Outputs:
- output: bfloat16 [2, 1024, 2048], P('fsdp', 'ctx')
- grad_tokens: bfloat16 [2, 1024, 2048], P('fsdp', 'ctx')
- grad_gain_attn: float32 [2048], P(('fsdp', 'ctx'))
- grad_gain_mlp: float32 [2048], P(('fsdp', 'ctx'))
- grad_w_kv: float32 [2048, 2, 2048], P(('fsdp', 'ctx'), None, 'tp')
- grad_w_query: float32 [2048, 4, 2048], P(('fsdp', 'ctx'), None, 'tp')
- grad_w_out_attn: float32 [2048, 4, 2048], P(('fsdp', 'ctx'), None, 'tp')
- grad_w_in: float32 [2048, 4, 2, 5632], P(('fsdp', 'ctx'), None, None, 'tp')
- grad_w_down: float32 [2048, 4, 5632], P(('fsdp', 'ctx'), None, 'tp')
Inputs may be any that keep to these rules, and one draw needn't show every extreme that they name: `segments`: along each sequence the segment numbers start at 0, never fall and end at 255; positions 255 to 768 of every sequence lie in one segment. `attn_routes`: among the 256 tokens of one context index of a sequence, no attention expert is named by more than 144 tokens, a bound that some block reaches in some such block. `mlp_routes`: among the 256 tokens of one context index of a sequence, no feed-forward expert is named by more than 144 tokens, a bound that some block reaches in some such block.
All inputs are finite; a program needn't handle non-finite values.
Results may differ from a plain program's by a relative error of at most 0.024.
Values may be sent and summed in bfloat16 or wider, within the bound.
A program may use at most 576 MiB of HBM per device.

v0:
```python
import jax
import jax.numpy as jnp
from jax import lax
from jax.sharding import PartitionSpec as P

HD = 128


EPSILON = 1e-06
ROPE_BASE = 10000.0
MASKED = -1e30


def positions(seg_row):
    place_idx = jnp.arange(seg_row.shape[0], dtype=jnp.int32)
    before = jnp.concatenate([seg_row[:1] - 1, seg_row[:-1]])
    doc_start = lax.cummax(jnp.where(seg_row != before, place_idx, 0), axis=0)
    return (place_idx - doc_start).astype(jnp.float32)


def rotary(pos_rows, size):
    frequency = ROPE_BASE ** (-(jnp.arange(size // 2, dtype=jnp.float32) * 2.0) / size)
    angles = pos_rows[:, None] * frequency[None, :]
    return (jnp.cos(angles), jnp.sin(angles))


def rotate(tensor, cos_table, sin_table, size):
    dims_all = tensor.shape
    per_head = tensor.reshape(dims_all[:-1] + (dims_all[-1] // size, size))
    ones_pad = (1,) * (per_head.ndim - 2)
    cos_wide = cos_table.reshape((cos_table.shape[0],) + ones_pad + (size // 2,))
    sin_wide = sin_table.reshape((sin_table.shape[0],) + ones_pad + (size // 2,))
    front_half = per_head[..., : size // 2]
    back_half = per_head[..., size // 2 :]
    turned = jnp.concatenate(
        [
            front_half * cos_wide - back_half * sin_wide,
            back_half * cos_wide + front_half * sin_wide,
        ],
        axis=-1,
    )
    return turned.reshape(dims_all)


def normalize(tensor, gain_vec):
    inverse = lax.rsqrt(jnp.mean(tensor * tensor, axis=-1, keepdims=True) + EPSILON)
    normed = tensor * inverse
    return (normed, inverse, normed * gain_vec)


def norm_back(grad_in, normed, inverse, gain_vec):
    scaled = grad_in * gain_vec
    inner_mean = jnp.mean(scaled * normed, axis=-1, keepdims=True)
    return (inverse * (scaled - normed * inner_mean), jnp.sum(grad_in * normed, axis=0))


def to_heads(tensor, head_count):
    row_count, slot_count = (tensor.shape[0], tensor.shape[1])
    return (
        tensor.reshape(row_count, slot_count, head_count, HD)
        .transpose(2, 0, 1, 3)
        .reshape(head_count, row_count * slot_count, HD)
    )


def from_heads(tensor, row_count):
    head_count = tensor.shape[0]
    slot_count = tensor.shape[1] // row_count
    return (
        tensor.reshape(head_count, row_count, slot_count, HD)
        .transpose(1, 2, 0, 3)
        .reshape(row_count, slot_count, head_count * HD)
    )


def dispatch(routes, expert_count, capacity):
    flat_routes = routes.reshape(-1)
    pair_count = flat_routes.shape[0]
    onehot = (flat_routes[:, None] == jnp.arange(expert_count, dtype=jnp.int32)[None, :]).astype(
        jnp.int32
    )
    before_count = jnp.cumsum(onehot, axis=0) - onehot
    slot_num = jnp.sum(before_count * onehot, axis=1)
    place = flat_routes * capacity + slot_num
    token_of = jnp.arange(pair_count, dtype=jnp.int32) // routes.shape[1]
    source = jnp.zeros((expert_count * capacity,), jnp.int32).at[place].set(token_of)
    return (place, source)


def combine_rows(slot_rows, source, row_count):
    flat_rows = slot_rows.reshape(-1, slot_rows.shape[-1])
    return jnp.zeros((row_count, flat_rows.shape[1]), jnp.float32).at[source].add(flat_rows)


def local(
    tokens,
    gain_attn,
    gain_mlp,
    w_kv,
    w_query,
    w_out_attn,
    w_in,
    w_down,
    segments,
    attn_routes,
    attn_gates,
    mlp_routes,
    mlp_gates,
    cotangent,
):
    gathered = (
        lax.all_gather(gain_attn, ("fsdp", "ctx"), axis=0, tiled=True),
        lax.all_gather(gain_mlp, ("fsdp", "ctx"), axis=0, tiled=True),
        lax.all_gather(w_kv, ("fsdp", "ctx"), axis=0, tiled=True),
        lax.all_gather(w_query, ("fsdp", "ctx"), axis=0, tiled=True),
        lax.all_gather(w_out_attn, ("fsdp", "ctx"), axis=0, tiled=True),
    )
    gain_one = gathered[0].astype(jnp.float32)
    gain_two = gathered[1].astype(jnp.float32)
    kv_full = gathered[2]
    query_full = gathered[3]
    outw_full = gathered[4]
    inputs = tokens[0].astype(jnp.float32)
    row_count = inputs.shape[0]
    width = inputs.shape[1]
    capacity = 9 * row_count // 16
    seg_row = segments[0]
    seq_total = seg_row.shape[0]
    slot_count = attn_routes.shape[2]
    attn_experts = query_full.shape[1]
    my_first = lax.axis_index("ctx") * row_count
    pos_mine = lax.dynamic_slice_in_dim(positions(seg_row), my_first, row_count)
    cos_table, sin_table = rotary(pos_mine, HD)
    score_scale = HD ** (-0.5)
    normed_one, inverse_one, pre_one = normalize(inputs, gain_one)
    hidden_one = pre_one.astype(jnp.bfloat16)
    kv_raw = jnp.einsum("td,dck->tck", hidden_one, kv_full, preferred_element_type=jnp.float32)
    head_count = kv_raw.shape[2] // HD
    head_width = head_count * HD
    key_rows = rotate(kv_raw[:, 0], cos_table, sin_table, HD).astype(jnp.bfloat16)
    value_rows = kv_raw[:, 1].astype(jnp.bfloat16)
    key_h = key_rows.reshape(row_count, head_count, HD).transpose(1, 0, 2)
    value_h = value_rows.reshape(row_count, head_count, HD).transpose(1, 0, 2)
    place_attn, source_attn = dispatch(attn_routes[0], attn_experts, capacity)
    gates_attn = attn_gates[0]
    one_slots = hidden_one[source_attn].reshape(attn_experts, capacity, width)
    query_exp = jnp.einsum(
        "ecd,deq->ecq", one_slots, query_full, preferred_element_type=jnp.float32
    )
    query_sel = query_exp.reshape(attn_experts * capacity, head_width)[place_attn].reshape(
        row_count, slot_count, head_width
    )
    query_h = to_heads(rotate(query_sel, cos_table, sin_table, HD).astype(jnp.bfloat16), head_count)
    query_seg = jnp.repeat(lax.dynamic_slice_in_dim(seg_row, my_first, row_count), slot_count)
    query_idx = jnp.repeat(my_first + jnp.arange(row_count, dtype=jnp.int32), slot_count)

    def pair_mask(key_first, key_count):
        key_seg = lax.dynamic_slice_in_dim(seg_row, key_first, key_count)
        key_idx = key_first + jnp.arange(key_count, dtype=jnp.int32)
        return (query_seg[:, None] == key_seg[None, :]) & (key_idx[None, :] <= query_idx[:, None])

    def attend_block(carried, key_block, value_block, key_first):
        allowed = pair_mask(key_first, key_block.shape[1])

        def attend_update(running):
            top_score, total, weighted = running
            scores = (
                jnp.einsum("hqd,hkd->hqk", query_h, key_block, preferred_element_type=jnp.float32)
                * score_scale
            )
            scores = jnp.where(allowed[None], scores, MASKED)
            new_max = jnp.maximum(top_score, jnp.max(scores, axis=-1))
            exp_scores = jnp.where(allowed[None], jnp.exp(scores - new_max[..., None]), 0.0)
            rescale = jnp.exp(top_score - new_max)
            new_total = total * rescale + jnp.sum(exp_scores, axis=-1)
            new_weighted = weighted * rescale[..., None] + jnp.einsum(
                "hqk,hkd->hqd",
                exp_scores.astype(jnp.bfloat16),
                value_block,
                preferred_element_type=jnp.float32,
            )
            return (new_max, new_total, new_weighted)

        return lax.cond(jnp.any(allowed), attend_update, lambda running: running, carried)

    start_fwd = (
        jnp.full((head_count, row_count * slot_count), MASKED, jnp.float32),
        jnp.zeros((head_count, row_count * slot_count), jnp.float32),
        jnp.zeros((head_count, row_count * slot_count, HD), jnp.float32),
    )
    key_part = lax.all_gather(key_h, "ctx", axis=1, tiled=True)
    value_part = lax.all_gather(value_h, "ctx", axis=1, tiled=True)

    def step(block_num, running):
        key_block = lax.dynamic_slice_in_dim(key_part, block_num * row_count, row_count, 1)
        value_block = lax.dynamic_slice_in_dim(value_part, block_num * row_count, row_count, 1)
        return attend_block(running, key_block, value_block, block_num * row_count)

    top_score, total, weighted = lax.fori_loop(0, key_part.shape[1] // row_count, step, start_fwd)
    attn_h = weighted / total[..., None]
    log_total = top_score + jnp.log(total)
    attn_rows = from_heads(attn_h, row_count)
    gated_rows = (attn_rows * gates_attn[:, :, None]).reshape(row_count * slot_count, head_width)
    mixed_slots = (
        jnp.zeros((attn_experts * capacity, head_width), jnp.float32)
        .at[place_attn]
        .set(gated_rows)
        .astype(jnp.bfloat16)
        .reshape(attn_experts, capacity, head_width)
    )
    attn_slots = jnp.einsum(
        "ecq,deq->ecd", mixed_slots, outw_full, preferred_element_type=jnp.float32
    )
    attn_part = combine_rows(attn_slots, source_attn, row_count)
    attn_total = lax.psum(attn_part.astype(jnp.bfloat16), "tp").astype(jnp.float32)
    resid = inputs + attn_total
    normed_two, inverse_two, pre_two = normalize(resid, gain_two)
    hidden_two = pre_two.astype(jnp.bfloat16)
    inw_full, down_full = (
        lax.all_gather(w_in, ("fsdp", "ctx"), axis=0, tiled=True),
        lax.all_gather(w_down, ("fsdp", "ctx"), axis=0, tiled=True),
    )
    mlp_experts = inw_full.shape[1]
    place_mlp, source_mlp = dispatch(mlp_routes[0], mlp_experts, capacity)
    slot_weight = (
        jnp.zeros((mlp_experts * capacity,), jnp.float32)
        .at[place_mlp]
        .set(mlp_gates[0].reshape(-1))
        .reshape(mlp_experts, capacity)
    )
    two_slots = hidden_two[source_mlp].reshape(mlp_experts, capacity, width)
    gate_up = jnp.einsum("ecd,deaf->ecaf", two_slots, inw_full, preferred_element_type=jnp.float32)
    gate_part = gate_up[:, :, 0]
    up_part = gate_up[:, :, 1]
    sigmoid_gate = jax.nn.sigmoid(gate_part)
    silu_gate = gate_part * sigmoid_gate
    active = (silu_gate * up_part * slot_weight[:, :, None]).astype(jnp.bfloat16)
    mlp_slots = jnp.einsum("ecf,def->ecd", active, down_full, preferred_element_type=jnp.float32)
    mlp_total = lax.psum(
        combine_rows(mlp_slots, source_mlp, row_count).astype(jnp.bfloat16), "tp"
    ).astype(jnp.float32)
    output = (resid + mlp_total).astype(jnp.bfloat16)
    grad_out = cotangent[0]
    grad_outf = grad_out.astype(jnp.float32)
    grad_slots = grad_out[source_mlp].reshape(mlp_experts, capacity, width)
    grad_active = jnp.einsum(
        "ecd,def->ecf", grad_slots, down_full, preferred_element_type=jnp.float32
    )
    down_half = lax.psum_scatter(
        jnp.einsum("ecd,ecf->def", grad_slots, active, preferred_element_type=jnp.float32).astype(
            jnp.bfloat16
        ),
        "fsdp",
        scatter_dimension=0,
        tiled=True,
    )
    share = grad_active * slot_weight[:, :, None]
    grad_gate = share * up_part * sigmoid_gate * (1.0 + gate_part * (1.0 - sigmoid_gate))
    grad_up = share * silu_gate
    grad_gu = jnp.stack([grad_gate, grad_up], axis=2).astype(jnp.bfloat16)
    in_half = lax.psum_scatter(
        jnp.einsum("ecd,ecaf->deaf", two_slots, grad_gu, preferred_element_type=jnp.float32).astype(
            jnp.bfloat16
        ),
        "fsdp",
        scatter_dimension=0,
        tiled=True,
    )
    back_two_slots = jnp.einsum(
        "ecaf,deaf->ecd", grad_gu, inw_full, preferred_element_type=jnp.float32
    )
    back_two = lax.psum(
        combine_rows(back_two_slots, source_mlp, row_count).astype(jnp.bfloat16), "tp"
    ).astype(jnp.float32)
    grad_resid_norm, gain_two_grad = norm_back(back_two, normed_two, inverse_two, gain_two)
    grad_resid = grad_outf + grad_resid_norm
    grad_branch = grad_resid.astype(jnp.bfloat16)
    branch_slots = grad_branch[source_attn].reshape(attn_experts, capacity, width)
    grad_mixed = jnp.einsum(
        "ecd,deq->ecq", branch_slots, outw_full, preferred_element_type=jnp.float32
    )
    grad_outw = jnp.einsum(
        "ecd,ecq->deq", branch_slots, mixed_slots, preferred_element_type=jnp.float32
    )
    grad_mixed_sel = grad_mixed.reshape(attn_experts * capacity, head_width)[place_attn].reshape(
        row_count, slot_count, head_width
    )
    grad_attn_rows = (grad_mixed_sel * gates_attn[:, :, None]).astype(jnp.bfloat16)
    grad_attn_h = to_heads(grad_attn_rows, head_count)
    delta = jnp.sum(grad_attn_h.astype(jnp.float32) * attn_h, axis=-1)

    def grad_block(carried, key_block, value_block, key_first):
        allowed = pair_mask(key_first, key_block.shape[1])

        def grad_update(running):
            grad_query, grad_key_all, grad_value_all = running
            scores = (
                jnp.einsum("hqd,hkd->hqk", query_h, key_block, preferred_element_type=jnp.float32)
                * score_scale
            )
            probs_all = jnp.where(allowed[None], jnp.exp(scores - log_total[..., None]), 0.0)
            value_grad = jnp.einsum(
                "hqk,hqd->hkd",
                probs_all.astype(jnp.bfloat16),
                grad_attn_h,
                preferred_element_type=jnp.float32,
            )
            grad_probs = jnp.einsum(
                "hqd,hkd->hqk", grad_attn_h, value_block, preferred_element_type=jnp.float32
            )
            grad_scores = (probs_all * (grad_probs - delta[..., None])).astype(jnp.bfloat16)
            grad_query = (
                grad_query
                + jnp.einsum(
                    "hqk,hkd->hqd", grad_scores, key_block, preferred_element_type=jnp.float32
                )
                * score_scale
            )
            key_grad = (
                jnp.einsum("hqk,hqd->hkd", grad_scores, query_h, preferred_element_type=jnp.float32)
                * score_scale
            )
            key_count = key_block.shape[1]
            grad_key_all = lax.dynamic_update_slice_in_dim(
                grad_key_all,
                lax.dynamic_slice_in_dim(grad_key_all, key_first, key_count, 1) + key_grad,
                key_first,
                1,
            )
            grad_value_all = lax.dynamic_update_slice_in_dim(
                grad_value_all,
                lax.dynamic_slice_in_dim(grad_value_all, key_first, key_count, 1) + value_grad,
                key_first,
                1,
            )
            return (grad_query, grad_key_all, grad_value_all)

        return lax.cond(jnp.any(allowed), grad_update, lambda running: running, carried)

    start_back = (
        jnp.zeros((head_count, row_count * slot_count, HD), jnp.float32),
        jnp.zeros((head_count, seq_total, HD), jnp.float32),
        jnp.zeros((head_count, seq_total, HD), jnp.float32),
    )
    fold_key_part = lax.all_gather(key_h, "ctx", axis=1, tiled=True)
    fold_value_part = lax.all_gather(value_h, "ctx", axis=1, tiled=True)

    def step(block_num, running):
        key_block = lax.dynamic_slice_in_dim(fold_key_part, block_num * row_count, row_count, 1)
        value_block = lax.dynamic_slice_in_dim(fold_value_part, block_num * row_count, row_count, 1)
        return grad_block(running, key_block, value_block, block_num * row_count)

    grad_query, grad_key_all, grad_value_all = lax.fori_loop(
        0, fold_key_part.shape[1] // row_count, step, start_back
    )
    grad_key_mine, grad_value_mine = (
        lax.psum_scatter(
            grad_key_all.astype(jnp.bfloat16), "ctx", scatter_dimension=1, tiled=True
        ).astype(jnp.float32),
        lax.psum_scatter(
            grad_value_all.astype(jnp.bfloat16), "ctx", scatter_dimension=1, tiled=True
        ).astype(jnp.float32),
    )
    grad_keys = rotate(
        grad_key_mine.transpose(1, 0, 2).reshape(row_count, head_width), cos_table, -sin_table, HD
    )
    grad_values = grad_value_mine.transpose(1, 0, 2).reshape(row_count, head_width)
    grad_kv = jnp.stack([grad_keys, grad_values], axis=1).astype(jnp.bfloat16)
    grad_query_sel = rotate(from_heads(grad_query, row_count), cos_table, -sin_table, HD)
    grad_query_slots = (
        jnp.zeros((attn_experts * capacity, head_width), jnp.float32)
        .at[place_attn]
        .set(grad_query_sel.reshape(row_count * slot_count, head_width))
        .astype(jnp.bfloat16)
        .reshape(attn_experts, capacity, head_width)
    )
    query_back = jnp.einsum(
        "ecq,deq->ecd", grad_query_slots, query_full, preferred_element_type=jnp.float32
    )
    back_one_part = combine_rows(query_back, source_attn, row_count) + jnp.einsum(
        "tck,dck->td", grad_kv, kv_full, preferred_element_type=jnp.float32
    )
    back_one = lax.psum(back_one_part.astype(jnp.bfloat16), "tp").astype(jnp.float32)
    grad_input_norm, gain_one_grad = norm_back(back_one, normed_one, inverse_one, gain_one)
    grad_tokens = (grad_resid + grad_input_norm).astype(jnp.bfloat16)
    grad_query_w = jnp.einsum(
        "ecd,ecq->deq", one_slots, grad_query_slots, preferred_element_type=jnp.float32
    )
    grad_kv_w = jnp.einsum("td,tck->dck", hidden_one, grad_kv, preferred_element_type=jnp.float32)
    halves = (
        lax.psum_scatter(
            gain_one_grad.astype(jnp.bfloat16), "fsdp", scatter_dimension=0, tiled=True
        ).astype(jnp.float32),
        lax.psum_scatter(
            gain_two_grad.astype(jnp.bfloat16), "fsdp", scatter_dimension=0, tiled=True
        ).astype(jnp.float32),
        lax.psum_scatter(
            grad_kv_w.astype(jnp.bfloat16), "fsdp", scatter_dimension=0, tiled=True
        ).astype(jnp.float32),
        lax.psum_scatter(
            grad_query_w.astype(jnp.bfloat16), "fsdp", scatter_dimension=0, tiled=True
        ).astype(jnp.float32),
        lax.psum_scatter(
            grad_outw.astype(jnp.bfloat16), "fsdp", scatter_dimension=0, tiled=True
        ).astype(jnp.float32),
    )
    summed = (
        lax.psum_scatter(
            halves[0].astype(jnp.bfloat16), "ctx", scatter_dimension=0, tiled=True
        ).astype(jnp.float32),
        lax.psum_scatter(
            halves[1].astype(jnp.bfloat16), "ctx", scatter_dimension=0, tiled=True
        ).astype(jnp.float32),
        lax.psum_scatter(
            halves[2].astype(jnp.bfloat16), "ctx", scatter_dimension=0, tiled=True
        ).astype(jnp.float32),
        lax.psum_scatter(
            halves[3].astype(jnp.bfloat16), "ctx", scatter_dimension=0, tiled=True
        ).astype(jnp.float32),
        lax.psum_scatter(
            halves[4].astype(jnp.bfloat16), "ctx", scatter_dimension=0, tiled=True
        ).astype(jnp.float32),
        lax.psum_scatter(in_half, "ctx", scatter_dimension=0, tiled=True).astype(jnp.float32),
        lax.psum_scatter(down_half, "ctx", scatter_dimension=0, tiled=True).astype(jnp.float32),
    )
    return (
        output[None],
        grad_tokens[None],
        summed[0],
        summed[1],
        summed[2],
        summed[3],
        summed[4],
        summed[5],
        summed[6],
    )


def solution(mesh):
    return jax.shard_map(
        local,
        mesh=mesh,
        in_specs=(
            P("fsdp", "ctx", None),
            P(("fsdp", "ctx")),
            P(("fsdp", "ctx")),
            P(("fsdp", "ctx"), None, "tp"),
            P(("fsdp", "ctx"), None, "tp"),
            P(("fsdp", "ctx"), None, "tp"),
            P(("fsdp", "ctx"), None, None, "tp"),
            P(("fsdp", "ctx"), None, "tp"),
            P("fsdp", None),
            P("fsdp", "ctx", None),
            P("fsdp", "ctx", None),
            P("fsdp", "ctx", None),
            P("fsdp", "ctx", None),
            P("fsdp", "ctx", None),
        ),
        out_specs=(
            P("fsdp", "ctx", None),
            P("fsdp", "ctx", None),
            P(("fsdp", "ctx")),
            P(("fsdp", "ctx")),
            P(("fsdp", "ctx"), None, "tp"),
            P(("fsdp", "ctx"), None, "tp"),
            P(("fsdp", "ctx"), None, "tp"),
            P(("fsdp", "ctx"), None, None, "tp"),
            P(("fsdp", "ctx"), None, "tp"),
        ),
        check_vma=False,
    )
```

profile of v0, /device:TPU:0, one launch (start us, length us, event | category | flops | bytes accessed | tf_op | source)
XLA Modules:
  0.0 2387.3 jit_solution(15182008233574992518)
XLA Ops:
  10.6 10.3 all-gather
  24.7 25.3 %all-gather.10.cloned.1.call-done = bf16[2048,2,512]{2,0,1:T(8,128)(2,1)} async-done(((bf16[256,2,512]{2,0,1:T(8,128)(2,1)}), bf16[2048,2,512]{2,0,1:T(8,128)(2,1)}) %all-gather.10.cloned.1.call-update) | async-done | bytes 4194320 | tf_op jit(solution)/shard_map/all_gather | solution.py:114
  71.4 35.5 %all-gather.14.cloned.1.call-done = bf16[2048,4,512]{2,0,1:T(8,128)(2,1)} async-done(((bf16[256,4,512]{2,0,1:T(8,128)(2,1)}), bf16[2048,4,512]{2,0,1:T(8,128)(2,1)}) %all-gather.14.cloned.1.call-update) | async-done | bytes 8388624 | tf_op jit(solution)/shard_map/all_gather | solution.py:115
  106.9 5.5 fusion.107
  117.2 8.5 all-gather.12.cloned.1.call-done
  125.8 18.8 all-gather.16.cloned.1.call-done
  144.6 12.8 while.36
  163.4 37.9 %all-gather.18.cloned.1.call-done = bf16[2048,4,512]{2,0,1:T(8,128)(2,1)} async-done(((bf16[256,4,512]{2,0,1:T(8,128)(2,1)}), bf16[2048,4,512]{2,0,1:T(8,128)(2,1)}) %all-gather.18.cloned.1.call-update) | async-done | bytes 8388624 | tf_op jit(solution)/shard_map/all_gather | solution.py:116
  201.3 8.4 fusion.108
  209.7 15.2 scatter_custom_fusion.2
  226.1 5.9 copy.97
  241.6 9.0 all-gather.1
  257.6 20.5 all-reduce.11.cloned.1.call-done
  284.3 210.1 %all-gather.20.cloned.1.call-done = bf16[2048,4,2,1408]{3,0,2,1:T(8,128)(2,1)} async-done(((bf16[256,4,2,1408]{3,0,2,1:T(8,128)(2,1)}), bf16[2048,4,2,1408]{3,0,2,1:T(8,128)(2,1)}) %all-gather.20.cloned.1.call-update) | async-done | bytes 46137360 | tf_op jit(solution)/shard_map/all_gather | solution.py:220
  494.4 23.8 fusion.109
  518.2 94.8 %all-gather.22.cloned.1.call-done = bf16[2048,4,1408]{2,0,1:T(8,128)(2,1)} async-done(((bf16[256,4,1408]{2,0,1:T(8,128)(2,1)}), bf16[2048,4,1408]{2,0,1:T(8,128)(2,1)}) %all-gather.22.cloned.1.call-update) | async-done | bytes 23068688 | tf_op jit(solution)/shard_map/all_gather | solution.py:221
  612.9 17.0 fusion.62
  629.9 23.1 fusion.37
  653.0 16.1 scatter_custom_fusion.6
  672.7 51.2 %all-reduce.13.cloned.1.call-done = bf16[256,2048]{1,0:T(8,128)(2,1)} async-done(((bf16[256,2048]{1,0:T(8,128)(2,1)}), bf16[256,2048]{1,0:T(8,128)(2,1)}) %all-reduce.13.cloned.1.call-update) | async-done | bytes 1048592 | tf_op jit(solution)/shard_map/psum | solution.py:272
  732.3 5.5 fusion.111
  745.6 22.0 while.37
  748.4 10.9 conditional.7
  773.2 53.7 %reduce-scatter.13.cloned.1.call-done = bf16[4,256,128]{2,1,0:T(8,128)(2,1)} async-done(((bf16[4,1024,128]{2,1,0:T(8,128)(2,1)}), bf16[4,256,128]{2,1,0:T(8,128)(2,1)}) %reduce-scatter.13.cloned.1.call-update) | async-done | bytes 262160 | tf_op jit(solution)/shard_map/reduce_scatter | solution.py:357
  828.7 26.4 %reduce-scatter.15.cloned.1.call-done = bf16[4,256,128]{2,1,0:T(8,128)(2,1)} async-done(((bf16[4,1024,128]{2,1,0:T(8,128)(2,1)}), bf16[4,256,128]{2,1,0:T(8,128)(2,1)}) %reduce-scatter.15.cloned.1.call-update) | async-done | bytes 262160 | tf_op jit(solution)/shard_map/reduce_scatter | solution.py:360
  868.2 5.8 convert_bitcast_fusion.2
  876.1 5.8 convert_bitcast_fusion.1
  883.5 12.7 fusion.39
  897.9 20.6 convert_bitcast_fusion
  919.9 14.1 fusion.110
  934.0 15.6 scatter_custom_fusion.5
  950.7 8.6 fusion.112
  960.6 15.5 scatter_fusion
  977.9 38.6 %reduce-scatter.21.cloned.1.call-done = bf16[1024,4,512]{0,2,1:T(8,128)(2,1)} async-done(((bf16[2048,4,512]{0,2,1:T(8,128)(2,1)}), bf16[1024,4,512]{0,2,1:T(8,128)(2,1)}) %reduce-scatter.21.cloned.1.call-update) | async-done | bytes 4194320 | tf_op jit(solution)/shard_map/reduce_scatter | solution.py:400
  1016.6 101.4 %reduce-scatter.25.cloned.1.call-done = bf16[1024,4,512]{0,2,1:T(8,128)(2,1)} async-done(((bf16[2048,4,512]{0,2,1:T(8,128)(2,1)}), bf16[1024,4,512]{0,2,1:T(8,128)(2,1)}) %reduce-scatter.25.cloned.1.call-update) | async-done | bytes 4194320 | tf_op jit(solution)/shard_map/reduce_scatter | solution.py:403
  1118.0 259.0 %reduce-scatter.33.cloned.1.call-done = bf16[1024,4,1408]{0,2,1:T(8,128)(2,1)} async-done(((bf16[2048,4,1408]{0,2,1:T(8,128)(2,1)}), bf16[1024,4,1408]{0,2,1:T(8,128)(2,1)}) %reduce-scatter.33.cloned.1.call-update) | async-done | bytes 11534352 | tf_op jit(solution)/shard_map/reduce_scatter | solution.py:249
  1377.0 506.2 %reduce-scatter.29.cloned.1.call-done = bf16[1024,4,2,1408]{0,3,2,1:T(8,128)(2,1)} async-done(((bf16[2048,4,2,1408]{0,3,2,1:T(8,128)(2,1)}), bf16[1024,4,2,1408]{0,3,2,1:T(8,128)(2,1)}) %reduce-scatter.29.cloned.1.call-update) | async-done | bytes 23068688 | tf_op jit(solution)/shard_map/reduce_scatter | solution.py:261
  1886.3 86.9 %all-reduce.15.cloned.1.call-done = (bf16[256,2048]{1,0:T(8,128)(2,1)}, bf16[256,2048]{1,0:T(8,128)(2,1)}) async-done(((bf16[256,2048]{1,0:T(8,128)(2,1)}, bf16[256,2048]{1,0:T(8,128)(2,1)}), (bf16[256,2048]{1,0:T(8,128)(2,1)}, bf16[256,2048]{1,0:T(8,128)(2,1)})) %all-reduce.15.cloned.1.call-update) | async-done | bytes 2097168 | tf_op jit(solution)/shard_map/psum | solution.py:239
  1975.3 5.0 all-reduce.6
  1980.4 5.8 all-reduce.5
  1986.9 4.9 fusion.64
  1991.8 14.3 reduce-scatter.19.cloned.1.call-done
  2008.6 44.7 %reduce-scatter.23.cloned.1.call-done = bf16[256,4,512]{0,2,1:T(8,128)(2,1)} async-done(((bf16[1024,4,512]{0,2,1:T(8,128)(2,1)}), bf16[256,4,512]{0,2,1:T(8,128)(2,1)}) %reduce-scatter.23.cloned.1.call-update) | async-done | bytes 1048592 | tf_op jit(solution)/shard_map/reduce_scatter | solution.py:417
  2056.0 44.2 %reduce-scatter.27.cloned.1.call-done = bf16[256,4,512]{0,2,1:T(8,128)(2,1)} async-done(((bf16[1024,4,512]{0,2,1:T(8,128)(2,1)}), bf16[256,4,512]{0,2,1:T(8,128)(2,1)}) %reduce-scatter.27.cloned.1.call-update) | async-done | bytes 1048592 | tf_op jit(solution)/shard_map/reduce_scatter | solution.py:420
  2102.9 92.3 %reduce-scatter.35.cloned.1.call-done = bf16[256,4,1408]{0,2,1:T(8,128)(2,1)} async-done(((bf16[1024,4,1408]{0,2,1:T(8,128)(2,1)}), bf16[256,4,1408]{0,2,1:T(8,128)(2,1)}) %reduce-scatter.35.cloned.1.call-update) | async-done | bytes 2883600 | tf_op jit(solution)/shard_map/reduce_scatter | solution.py:424
  2195.2 6.4 copy.112
  2201.6 163.2 %reduce-scatter.31.cloned.1.call-done = bf16[256,4,2,1408]{0,3,2,1:T(8,128)(2,1)} async-done(((bf16[1024,4,2,1408]{0,3,2,1:T(8,128)(2,1)}), bf16[256,4,2,1408]{0,3,2,1:T(8,128)(2,1)}) %reduce-scatter.31.cloned.1.call-update) | async-done | bytes 5767184 | tf_op jit(solution)/shard_map/reduce_scatter | solution.py:423
  2364.8 15.5 copy.111
  (375 shorter events, 159.1 us)
Async XLA Ops:
  7.2 42.8 %all-gather.10.cloned.1.call-start = ((), (), s32[]{:S(2)}) async-start(), calls=%async_computation.12 | async-start | bytes 4718592 | tf_op jit(solution)/shard_map/all_gather | solution.py:114
  9.2 11.7 copy-start.32
  9.2 13.7 copy-start.7
  9.2 97.6 %all-gather.14.cloned.1.call-start = ((), (), s32[]{:S(2)}) async-start(), calls=%async_computation.14 | async-start | bytes 9437184 | tf_op jit(solution)/shard_map/all_gather | solution.py:115
  10.5 115.3 %all-gather.12.cloned.1.call-start = ((), (), s32[]{:S(2)}) async-start(), calls=%async_computation.13 | async-start | bytes 1310720 | tf_op jit(solution)/shard_map/all_gather | solution.py:191
  20.9 32.5 %copy-start.30 = (f32[8,1,256]{2,1,0:T(1,128)}, f32[8,1,256]{2,1,0:T(1,128)S(1)}, u32[]{:S(2)}) copy-start(f32[8,1,256]{2,1,0:T(1,128)S(1)} %convert_element_type.249) | copy-start | bytes 24580
  23.2 30.2 %copy-start.42 = (f32[256]{0:T(256)}, f32[256]{0:T(256)S(1)}, u32[]{:S(2)}) copy-start(f32[256]{0:T(256)S(1)} %add_rsqrt_fusion.1) | copy-start | bytes 3076
  24.7 41.2 %copy-start.2 = (bf16[256,2048]{1,0:T(8,128)(2,1)}, bf16[256,2048]{1,0:T(8,128)(2,1)S(1)}, u32[]{:S(2)}) copy-start(bf16[256,2048]{1,0:T(8,128)(2,1)S(1)} %fusion.56) | copy-start | bytes 3145732
  56.0 88.6 %all-gather.16.cloned.1.call-start = ((), (), s32[]{:S(2)}) async-start(), calls=%async_computation.15 | async-start | bytes 1310720 | tf_op jit(solution)/shard_map/all_gather | solution.py:192
  57.9 143.3 %all-gather.18.cloned.1.call-start = ((), (), s32[]{:S(2)}) async-start(), calls=%async_computation.16 | async-start | bytes 9437184 | tf_op jit(solution)/shard_map/all_gather | solution.py:116
  60.5 217.5 %all-reduce.11.cloned.1.call-start = ((), (), s32[]{:S(2)}) async-start(), calls=%async_computation.17 | async-start | bytes 2097152 | tf_op jit(solution)/shard_map/psum | solution.py:215
  65.8 143.9 %copy-start.35 = (s32[576]{0:T(1024)}, s32[576]{0:T(1024)S(1)}, u32[]{:S(2)}) copy-start(s32[576]{0:T(1024)S(1)} %compare_select_fusion.3) | copy-start | bytes 6916
  163.4 46.3 %copy-start.20 = (bf16[576,512]{1,0:T(8,128)(2,1)}, bf16[576,512]{1,0:T(8,128)(2,1)S(1)}, u32[]{:S(2)}) copy-start(bf16[576,512]{1,0:T(8,128)(2,1)S(1)} %convert_element_type.207) | copy-start | bytes 1769476
  226.1 268.3 %all-gather.20.cloned.1.call-start = ((), (), s32[]{:S(2)}) async-start(), calls=%async_computation.18 | async-start | bytes 51904512 | tf_op jit(solution)/shard_map/all_gather | solution.py:220
  232.0 380.9 %all-gather.22.cloned.1.call-start = ((), (), s32[]{:S(2)}) async-start(), calls=%async_computation.19 | async-start | bytes 25952256 | tf_op jit(solution)/shard_map/all_gather | solution.py:221
  235.8 14.8 copy-start.53
  235.8 17.7 copy-start
  235.8 488.1 %all-reduce.13.cloned.1.call-start = ((), (), s32[]{:S(2)}) async-start(), calls=%async_computation.20 | async-start | bytes 2097152 | tf_op jit(solution)/shard_map/psum | solution.py:272
  250.6 476.2 %copy-start.28 = (f32[8,1,256]{2,1,0:T(1,128)}, f32[8,1,256]{2,1,0:T(1,128)S(1)}, u32[]{:S(2)}) copy-start(f32[8,1,256]{2,1,0:T(1,128)S(1)} %convert_element_type.250) | copy-start | bytes 24580
  253.5 399.5 %copy-start.41 = (s32[576]{0:T(1024)}, s32[576]{0:T(1024)S(1)}, u32[]{:S(2)}) copy-start(s32[576]{0:T(1024)S(1)} %compare_select_fusion.2) | copy-start | bytes 6916
  279.8 447.0 %copy-start.37 = (f32[256]{0:T(256)}, f32[256]{0:T(256)S(1)}, u32[]{:S(2)}) copy-start(f32[256]{0:T(256)S(1)} %add_rsqrt_fusion) | copy-start | bytes 3076
  669.1 54.8 %copy-start.12 = (bf16[256,2048]{1,0:T(8,128)(2,1)S(1)}, bf16[256,2048]{1,0:T(8,128)(2,1)}, u32[]{:S(2)}) copy-start(bf16[256,2048]{1,0:T(8,128)(2,1)} %all-reduce.11.cloned.1.call-done) | copy-start | bytes 3145732
  671.9 155.0 %reduce-scatter.13.cloned.1.call-start = ((), (), s32[]{:S(2)}) async-start(), calls=%async_computation.21 | async-start | bytes 1310720 | tf_op jit(solution)/shard_map/reduce_scatter | solution.py:357
  770.4 84.8 %reduce-scatter.15.cloned.1.call-start = ((), (), s32[]{:S(2)}) async-start(), calls=%async_computation.22 | async-start | bytes 1310720 | tf_op jit(solution)/shard_map/reduce_scatter | solution.py:360
  770.4 57.5 %copy-start.23 = (f32[256,64]{1,0:T(8,128)S(1)}, f32[256,64]{1,0:T(8,128)}, u32[]{:S(2)}) copy-start(f32[256,64]{1,0:T(8,128)} %get-tuple-element.758) | copy-start | bytes 196612
  773.2 204.1 %reduce-scatter.17.cloned.1.call-start = ((), (), s32[]{:S(2)}) async-start(), calls=%async_computation.23 | async-start | bytes 6291456 | tf_op jit(solution)/shard_map/reduce_scatter | solution.py:397
  828.2 28.2 %copy-start.3 = (bf16[256,2048]{1,0:T(8,128)(2,1)S(1)}, bf16[256,2048]{1,0:T(8,128)(2,1)}, u32[]{:S(2)}) copy-start(bf16[256,2048]{1,0:T(8,128)(2,1)} %copy-done.2) | copy-start | bytes 3145732
  859.8 156.7 %reduce-scatter.21.cloned.1.call-start = ((), (), s32[]{:S(2)}) async-start(), calls=%async_computation.25 | async-start | bytes 12582912 | tf_op jit(solution)/shard_map/reduce_scatter | solution.py:400
  874.1 243.8 %reduce-scatter.25.cloned.1.call-start = ((), (), s32[]{:S(2)}) async-start(), calls=%async_computation.27 | async-start | bytes 12582912 | tf_op jit(solution)/shard_map/reduce_scatter | solution.py:403
  881.9 495.1 %reduce-scatter.33.cloned.1.call-start = ((), (), s32[]{:S(2)}) async-start(), calls=%async_computation.31 | async-start | bytes 34603008 | tf_op jit(solution)/shard_map/reduce_scatter | solution.py:249
  896.2 987.0 %reduce-scatter.29.cloned.1.call-start = ((), (), s32[]{:S(2)}) async-start(), calls=%async_computation.29 | async-start | bytes 69206016 | tf_op jit(solution)/shard_map/reduce_scatter | solution.py:261
  918.5 1054.7 %all-reduce.15.cloned.1.call-start = ((), (), s32[]{:S(2)}) async-start(), calls=%async_computation.33 | async-start | bytes 4194304 | tf_op jit(solution)/shard_map/psum | solution.py:239
  950.7 8.6 copy-start.25
  950.7 8.6 copy-start.55
  977.3 1028.8 %reduce-scatter.19.cloned.1.call-start = ((), (), s32[]{:S(2)}) async-start(), calls=%async_computation.24 | async-start | bytes 2621440 | tf_op jit(solution)/shard_map/reduce_scatter | solution.py:414
  977.8 1075.5 %reduce-scatter.23.cloned.1.call-start = ((), (), s32[]{:S(2)}) async-start(), calls=%async_computation.26 | async-start | bytes 5242880 | tf_op jit(solution)/shard_map/reduce_scatter | solution.py:417
  1016.5 1083.7 %reduce-scatter.27.cloned.1.call-start = ((), (), s32[]{:S(2)}) async-start(), calls=%async_computation.28 | async-start | bytes 5242880 | tf_op jit(solution)/shard_map/reduce_scatter | solution.py:420
  1117.9 1077.3 %reduce-scatter.35.cloned.1.call-start = ((), (), s32[]{:S(2)}) async-start(), calls=%async_computation.32 | async-start | bytes 14417920 | tf_op jit(solution)/shard_map/reduce_scatter | solution.py:424
  1377.0 987.8 %reduce-scatter.31.cloned.1.call-start = ((), (), s32[]{:S(2)}) async-start(), calls=%async_computation.30 | async-start | bytes 28835840 | tf_op jit(solution)/shard_map/reduce_scatter | solution.py:423
  1883.2 90.1 %copy-start.8 = (bf16[1,256,2048]{2,1,0:T(8,128)(2,1)S(1)}, bf16[1,256,2048]{2,1,0:T(8,128)(2,1)}, u32[]{:S(2)}) copy-start(bf16[1,256,2048]{2,1,0:T(8,128)(2,1)} %param.22) | copy-start | bytes 3145732
  1883.2 90.1 %copy-start.31 = (f32[8,1,256]{2,1,0:T(1,128)S(1)}, f32[8,1,256]{2,1,0:T(1,128)}, u32[]{:S(2)}) copy-start(f32[8,1,256]{2,1,0:T(1,128)} %copy-done.30) | copy-start | bytes 24580
  1883.2 90.1 %copy-start.43 = (f32[256]{0:T(256)S(1)}, f32[256]{0:T(256)}, u32[]{:S(2)}) copy-start(f32[256]{0:T(256)} %copy-done.42) | copy-start | bytes 3076
  1883.2 92.1 %copy-start.39 = (bf16[2048]{0:T(1024)(128)(2,1)S(1)}, bf16[2048]{0:T(1024)(128)(2,1)}, u32[]{:S(2)}) copy-start(bf16[2048]{0:T(1024)(128)(2,1)} %get-tuple-element.679) | copy-start | bytes 12292
  1883.2 103.6 %copy-start.1 = (bf16[1,256,2048]{2,1,0:T(8,128)(2,1)S(1)}, bf16[1,256,2048]{2,1,0:T(8,128)(2,1)}, u32[]{:S(2)}) copy-start(bf16[1,256,2048]{2,1,0:T(8,128)(2,1)} %param.35) | copy-start | bytes 3145732
  1883.2 103.6 %copy-start.14 = (bf16[256,2048]{1,0:T(8,128)(2,1)S(1)}, bf16[256,2048]{1,0:T(8,128)(2,1)}, u32[]{:S(2)}) copy-start(bf16[256,2048]{1,0:T(8,128)(2,1)} %all-reduce.11.cloned.1.call-done) | copy-start | bytes 3145732
  1883.3 103.6 %copy-start.29 = (f32[8,1,256]{2,1,0:T(1,128)S(1)}, f32[8,1,256]{2,1,0:T(1,128)}, u32[]{:S(2)}) copy-start(f32[8,1,256]{2,1,0:T(1,128)} %copy-done.28) | copy-start | bytes 24580
  1883.3 103.6 %copy-start.38 = (f32[256]{0:T(256)S(1)}, f32[256]{0:T(256)}, u32[]{:S(2)}) copy-start(f32[256]{0:T(256)} %copy-done.37) | copy-start | bytes 3076
  1883.3 103.6 %copy-start.45 = (f32[256]{0:T(256)S(1)}, f32[256]{0:T(256)}, u32[]{:S(2)}) copy-start(f32[256]{0:T(256)} %copy-done.44) | copy-start | bytes 3076
  (34 other events, 91.2 us)
Sparse Core Ops, SparseCore 0:
  10.5 39.4 all-gather.9
  52.4 54.3 all-gather.13
  109.0 16.7 all-gather.11
  127.8 16.7 all-gather.15
  146.8 54.3 all-gather.17
  226.2 51.8 all-reduce.10
  280.7 213.6 all-gather.19
  496.4 116.4 all-gather.21
  672.1 51.8 all-reduce.12
  770.5 56.4 reduce-scatter.12
  830.2 24.8 reduce-scatter.14
  859.9 54.2 reduce-scatter.16
  917.2 99.2 reduce-scatter.20
  1018.6 99.2 reduce-scatter.24
  1120.2 256.7 reduce-scatter.32
  1379.2 503.9 reduce-scatter.28
  1886.1 87.0 all-reduce.14
  1975.6 30.4 reduce-scatter.18
  2008.7 44.5 reduce-scatter.22
  2055.7 44.4 reduce-scatter.26
  2103.0 92.1 reduce-scatter.34
  2198.0 166.7 reduce-scatter.30
where the time goes:
time: 2390 us
  waiting for transfers between devices  1930 us (81%)
  matrix products  173 us (7%)
  other arithmetic  114 us (5%)
  local copies, waits for them, and re-layouts  111 us (5%)
  blocking collectives  30.2 us (1%)
    reduce_scatter x1, waiting for transfers between devices, local(): lax.psum_scatter(jnp.einsum('ecd,ecaf->deaf', two_slots, grad_gu, preferr...  506 us
    reduce_scatter x1, waiting for transfers between devices, local(): lax.psum_scatter(jnp.einsum('ecd,ecf->def', grad_slots, active, preferred...  259 us
    all_gather x1, waiting for transfers between devices, local(): lax.all_gather(w_in, ('fsdp', 'ctx'), axis=0, tiled=True)  210 us
    reduce_scatter x1, waiting for transfers between devices, local(): lax.psum_scatter(in_half, 'ctx', scatter_dimension=0, tiled=True)  163 us
    reduce_scatter x1, waiting for transfers between devices, local(): lax.psum_scatter(grad_outw.astype(jnp.bfloat16), 'fsdp', scatter_dimensio...  101 us
    all_gather x1, waiting for transfers between devices, local(): lax.all_gather(w_down, ('fsdp', 'ctx'), axis=0, tiled=True)  94.8 us
    reduce_scatter x1, waiting for transfers between devices, local(): lax.psum_scatter(down_half, 'ctx', scatter_dimension=0, tiled=True)  92.3 us
    psum x1, waiting for transfers between devices, local(): lax.psum(combine_rows(mlp_slots, source_mlp, row_count).astype(jnp.bfloat...  86.9 us
  transfers between devices with their start and end apart: 22, of which 21 were waited for; matrix products, arithmetic and copies ran while one was open for 10% of the time, Pallas kernels for 0%

commit v1 on v0

v1 whole, which is shorter than its diff:
```python
import functools

import jax
import jax.numpy as jnp
from jax import lax
from jax.experimental import pallas as pl
from jax.experimental.pallas import tpu as pltpu
from jax.sharding import PartitionSpec as P

HD = 128
EPSILON = 1e-06
ROPE_BASE = 10000.0
MASKED = -1e30
GROUP = ("fsdp", "ctx")
BF = jnp.bfloat16
F32 = jnp.float32
VMEM_LIMIT = 56 * 1024 * 1024


def normalize(tensor, gain_vec):
    inverse = lax.rsqrt(jnp.mean(tensor * tensor, axis=-1, keepdims=True) + EPSILON)
    normed = tensor * inverse
    return (normed, inverse, normed * gain_vec)


def norm_back(grad_in, normed, inverse, gain_vec):
    scaled = grad_in * gain_vec
    inner_mean = jnp.mean(scaled * normed, axis=-1, keepdims=True)
    return (inverse * (scaled - normed * inner_mean), jnp.sum(grad_in * normed, axis=0))


def dot(a, b, ca, cb):
    return lax.dot_general(a, b, (((ca,), (cb,)), ((), ())), preferred_element_type=F32)


def turn(x, cos, sin):
    return x * cos + pltpu.roll(x, HD // 2, 1) * sin


def swap(x, mask, axes, count):
    return lax.ppermute(x, axes, [(i, i ^ mask) for i in range(count)])


def bits_of(count):
    return count.bit_length() - 1


def project_kernel(h_ref, w_ref, cos_ref, sin_ref, out_ref):
    y = jnp.dot(h_ref[...], w_ref[0], preferred_element_type=F32)
    for head in range(y.shape[1] // HD):
        cols = slice(head * HD, (head + 1) * HD)
        out_ref[:, cols] = turn(y[:, cols], cos_ref[0], sin_ref[0]).astype(BF)


def project(hidden, planes, cos, sin, plain):
    rows, width = hidden.shape
    count, _, cols = planes.shape
    tables = [
        jnp.stack([cos, jnp.ones_like(cos)]),
        jnp.stack([sin, jnp.zeros_like(sin)]),
    ]
    table_spec = pl.BlockSpec((1, rows, HD), lambda p: (p // plain, 0, 0))
    return pl.pallas_call(
        project_kernel,
        out_shape=jax.ShapeDtypeStruct((rows, count * cols), BF),
        grid=(count,),
        in_specs=[
            pl.BlockSpec((rows, width), lambda p: (0, 0)),
            pl.BlockSpec((1, width, cols), lambda p: (p, 0, 0)),
            table_spec,
            table_spec,
        ],
        out_specs=pl.BlockSpec((rows, cols), lambda p: (0, p)),
        compiler_params=pltpu.CompilerParams(vmem_limit_bytes=VMEM_LIMIT),
        name="project",
    )(hidden, planes, *tables)


def scores_of(d_ref, q_ref, k_ref, segq_ref, idxq_ref, segk_ref, idxk_ref):
    slots = dot(d_ref[0], q_ref[...], 1, 0).astype(BF)
    scores = dot(slots, k_ref[...], 1, 1) * (HD**-0.5)
    allowed = (segq_ref[0] == segk_ref[...]) & (idxk_ref[...] <= idxq_ref[0])
    scores = jnp.where(allowed, scores, MASKED)
    top = jnp.max(scores, axis=-1, keepdims=True)
    exps = jnp.exp(scores - top)
    total = jnp.sum(exps, axis=-1, keepdims=True)
    return slots, exps, 1.0 / total


def attend_kernel(
    q_ref, k_ref, v_ref, d_ref, segq_ref, idxq_ref, gate_ref, segk_ref, idxk_ref, out_ref
):
    _, exps, inv = scores_of(d_ref, q_ref, k_ref, segq_ref, idxq_ref, segk_ref, idxk_ref)
    attn = dot(exps.astype(BF), v_ref[...], 1, 0) * inv
    mixed = (attn * gate_ref[0]).astype(BF)
    out_ref[...] = dot(d_ref[0], mixed, 0, 0).astype(BF)


def attend_back_kernel(
    heads,
    experts,
    q_ref,
    k_ref,
    v_ref,
    d_ref,
    segq_ref,
    idxq_ref,
    segk_ref,
    idxk_ref,
    da_ref,
    cosq_ref,
    sinq_ref,
    cosk_ref,
    sink_ref,
    dq_ref,
    dk_ref,
    dv_ref,
    dk_acc,
    dv_acc,
):
    expert = pl.program_id(1)

    @pl.when(expert == 0)
    def _():
        dk_acc[...] = jnp.zeros_like(dk_acc)
        dv_acc[...] = jnp.zeros_like(dv_acc)

    slots, exps, inv = scores_of(d_ref, q_ref, k_ref, segq_ref, idxq_ref, segk_ref, idxk_ref)
    attn = dot(exps.astype(BF), v_ref[...], 1, 0) * inv
    probs = exps * inv
    grad = dot(d_ref[0], da_ref[...], 1, 0)
    delta = jnp.sum(grad * attn, axis=-1, keepdims=True)
    grad = grad.astype(BF)
    dv_acc[...] += dot(probs.astype(BF), grad, 0, 0)
    grad_probs = dot(grad, v_ref[...], 1, 1)
    grad_scores = (probs * (grad_probs - delta)).astype(BF)
    dq = dot(grad_scores, k_ref[...], 1, 0) * (HD**-0.5)
    dk_acc[...] += dot(grad_scores, slots, 0, 0) * (HD**-0.5)
    high = dq.astype(BF)
    low = (dq - high.astype(F32)).astype(BF)
    rows = dot(d_ref[0], high, 0, 0) + dot(d_ref[0], low, 0, 0)
    dq_ref[...] = turn(rows, cosq_ref[...], -sinq_ref[...]).astype(BF)

    @pl.when(expert == experts - 1)
    def _():
        dk_ref[...] = turn(dk_acc[...], cosk_ref[...], -sink_ref[...]).astype(BF)
        dv_ref[...] = dv_acc[...].astype(BF)


def attend_specs(rows, keys, heads, experts, cap):
    q_spec = pl.BlockSpec((rows, HD), lambda h, e: (0, e * heads + h))
    k_spec = pl.BlockSpec((keys, HD), lambda h, e: (0, h))
    v_spec = pl.BlockSpec((keys, HD), lambda h, e: (0, heads + h))
    d_spec = pl.BlockSpec((1, cap, rows), lambda h, e: (e, 0, 0))
    s_spec = pl.BlockSpec((1, cap, 1), lambda h, e: (e, 0, 0))
    t_spec = pl.BlockSpec((1, keys), lambda h, e: (0, 0))
    return q_spec, k_spec, v_spec, d_spec, s_spec, t_spec


def attend(qkv, kv, place, slot_seg, slot_idx, slot_gate, key_seg, key_idx):
    experts, cap, rows = place.shape
    keys = kv.shape[0]
    heads = kv.shape[1] // (2 * HD)
    q_spec, k_spec, v_spec, d_spec, s_spec, t_spec = attend_specs(rows, keys, heads, experts, cap)
    return pl.pallas_call(
        attend_kernel,
        out_shape=jax.ShapeDtypeStruct((rows, experts * heads * HD), BF),
        grid=(heads, experts),
        in_specs=[q_spec, k_spec, v_spec, d_spec, s_spec, s_spec, s_spec, t_spec, t_spec],
        out_specs=q_spec,
        compiler_params=pltpu.CompilerParams(vmem_limit_bytes=VMEM_LIMIT),
        name="attend",
    )(qkv, kv, kv, place, slot_seg, slot_idx, slot_gate, key_seg, key_idx)


def attend_back(qkv, kv, place, slot_seg, slot_idx, key_seg, key_idx, grad, tables):
    experts, cap, rows = place.shape
    keys = kv.shape[0]
    heads = kv.shape[1] // (2 * HD)
    q_spec, k_spec, v_spec, d_spec, s_spec, t_spec = attend_specs(rows, keys, heads, experts, cap)
    cos, sin = tables
    cq_spec = pl.BlockSpec((rows, HD), lambda h, e: (0, 0))
    ck_spec = pl.BlockSpec((keys, HD), lambda h, e: (0, 0))
    return pl.pallas_call(
        functools.partial(attend_back_kernel, heads, experts),
        out_shape=(
            jax.ShapeDtypeStruct((rows, experts * heads * HD), BF),
            jax.ShapeDtypeStruct((keys, heads * HD), BF),
            jax.ShapeDtypeStruct((keys, heads * HD), BF),
        ),
        grid=(heads, experts),
        in_specs=[q_spec, k_spec, v_spec, d_spec, s_spec, s_spec, t_spec, t_spec]
        + [q_spec, cq_spec, cq_spec, ck_spec, ck_spec],
        out_specs=(q_spec, k_spec, k_spec),
        scratch_shapes=[pltpu.VMEM((keys, HD), F32)] * 2,
        compiler_params=pltpu.CompilerParams(vmem_limit_bytes=VMEM_LIMIT),
        name="attend_back",
    )(qkv, kv, kv, place, slot_seg, slot_idx, key_seg, key_idx, grad, cos, sin, cos, sin)


def places(routes, gates, experts, cap, room):
    rows = routes.shape[0]
    named = routes[:, :, None] == jnp.arange(experts, dtype=jnp.int32)[None, None, :]
    member = jnp.any(named, axis=1)
    gate = jnp.sum(jnp.where(named, gates[:, :, None], 0.0), axis=1)
    token = jnp.arange(rows, dtype=jnp.int32)
    earlier = (token[None, :] < token[:, None]).astype(BF)
    rank = dot(earlier, member.astype(BF), 1, 0).astype(jnp.int32)
    slot = jnp.where(member, rank, -1).T
    taken = slot[:, None, :] == jnp.arange(room, dtype=jnp.int32)[None, :, None]
    return taken, gate


def slot_sum(taken, values):
    return jnp.sum(jnp.where(taken, values, 0), axis=-1, keepdims=True)


def layer(
    counts,
    tokens,
    gain_attn,
    gain_mlp,
    w_kv,
    w_query,
    w_out_attn,
    w_in,
    w_down,
    segments,
    attn_routes,
    attn_gates,
    mlp_routes,
    mlp_gates,
    cotangent,
):
    fsdp_count, ctx_count = counts
    group = fsdp_count * ctx_count
    me = lax.axis_index(GROUP)
    ctx_me = lax.axis_index("ctx")
    inputs = tokens[0].astype(F32)
    rows, width = inputs.shape
    cap = 9 * rows // 16
    room = -(-cap // 16) * 16
    part = width // group
    attn_experts = w_query.shape[1]
    experts = w_in.shape[1]
    share = group // experts
    expert_me = me // share
    hidden_units = w_down.shape[2]
    head_width = w_kv.shape[2]

    def piece(x, index, size=part, axis=1):
        return lax.dynamic_slice_in_dim(x, index * size, size, axis)

    def relative(x, order):
        return jnp.concatenate([piece(x, me ^ j) for j in order], axis=1)

    def exchange(x, mask):
        return swap(x, mask, GROUP, group)

    qkv_own = jnp.concatenate([w_query, w_kv], axis=1).transpose(1, 0, 2)
    qkv_full = lax.all_gather(qkv_own, GROUP, axis=1, tiled=True)
    outw_full = lax.all_gather(w_out_attn.transpose(1, 0, 2), GROUP, axis=1, tiled=True)
    gains = lax.all_gather(jnp.stack([gain_attn, gain_mlp]), GROUP, axis=1, tiled=True).astype(F32)
    gain_one, gain_two = gains[0], gains[1]

    seg_row = segments[0]
    seq_total = seg_row.shape[0]
    ctx_bits = list(range(bits_of(ctx_count)))[::-1]
    key_order = [0]
    for bit in ctx_bits:
        key_order = key_order + [j | (1 << bit) for j in key_order]
    key_seg = jnp.concatenate([piece(seg_row, ctx_me ^ j, rows, 0) for j in key_order])
    key_idx = jnp.concatenate(
        [(ctx_me ^ j) * rows + jnp.arange(rows, dtype=jnp.int32) for j in key_order]
    )
    place_idx = jnp.arange(seq_total, dtype=jnp.int32)
    pos = jnp.sum(
        (seg_row[None, :] == key_seg[:, None]) & (place_idx[None, :] < key_idx[:, None]),
        axis=1,
        dtype=jnp.int32,
    ).astype(F32)
    frequency = ROPE_BASE ** (-(jnp.arange(HD // 2, dtype=F32) * 2.0) / HD)
    angles = pos[:, None] * frequency[None, :]
    cos_half, sin_half = jnp.cos(angles), jnp.sin(angles)
    cos = jnp.concatenate([cos_half, cos_half], axis=1)
    sin = jnp.concatenate([-sin_half, sin_half], axis=1)
    taken_attn, gate_attn = places(attn_routes[0], attn_gates[0], attn_experts, cap, room)
    place_attn = taken_attn.astype(BF)
    own_seg, own_idx = key_seg[:rows], key_idx[:rows]
    filled = jnp.any(taken_attn, axis=-1, keepdims=True)
    slot_seg = jnp.where(filled, slot_sum(taken_attn, own_seg), own_seg[0])
    slot_idx = jnp.where(filled, slot_sum(taken_attn, own_idx), own_idx[0])
    slot_gate = slot_sum(taken_attn, gate_attn.T[:, None, :])
    taken_mlp, gate_mlp = places(mlp_routes[0], mlp_gates[0], experts, cap, room)
    mine_first = [expert_me ^ k for k in range(experts)]
    place_mlp = jnp.concatenate([piece(taken_mlp, e, 1, 0) for e in mine_first]).astype(BF)
    weight_slots = slot_sum(taken_mlp, gate_mlp.T[:, None, :])

    normed_one, inverse_one, pre_one = normalize(inputs, gain_one)
    hidden_one = pre_one.astype(BF)
    qkv = project(hidden_one, qkv_full, cos[:rows], sin[:rows], attn_experts + 1)
    kv = qkv[:, attn_experts * head_width :]
    for bit in ctx_bits:
        kv = jnp.concatenate([kv, swap(kv, 1 << bit, "ctx", ctx_count)], axis=0)
    key_row = (key_seg[None, :], key_idx[None, :])
    mixed = attend(qkv, kv, place_attn, slot_seg, slot_idx, slot_gate, *key_row)

    def planes(x):
        return x.reshape(rows, x.shape[1] // head_width, head_width)

    branch = jnp.einsum("tpc,pdc->td", planes(mixed), outw_full, preferred_element_type=F32)
    resid = inputs + lax.psum(branch.astype(BF), "tp").astype(F32)
    normed_two, inverse_two, pre_two = normalize(resid, gain_two)
    hidden_two = pre_two.astype(BF)

    w_in_late, w_down_late, _ = lax.optimization_barrier((w_in, w_down, outw_full))

    def expert_rows(k):
        in_rows = piece(w_in_late, expert_me ^ k, 1, 1).reshape(part, 2 * hidden_units)
        down_rows = piece(w_down_late, expert_me ^ k, 1, 1).reshape(part, hidden_units)
        return jnp.concatenate([in_rows, down_rows], axis=1)

    by_source = [expert_rows(0)] + [
        exchange(expert_rows(k), k * share) for k in range(1, experts)
    ]
    blocks = []
    for block in by_source:
        blocks += [block] + [exchange(block, t) for t in range(1, share)]
    in_full = jnp.concatenate([b[:, : 2 * hidden_units] for b in blocks], axis=0)
    down_full = jnp.concatenate([b[:, 2 * hidden_units :] for b in blocks], axis=0)

    def turned(x, k):
        wide = share * part
        return jnp.concatenate(
            [x[:, (i ^ k) * wide : ((i ^ k) + 1) * wide] for i in range(experts)], axis=1
        )

    def send_out(x):
        slots = jnp.einsum("kct,td->kcd", place_mlp, x, preferred_element_type=F32).astype(BF)
        got = [slots[0]]
        for k in range(1, experts):
            got.append(exchange(turned(slots[k], k), k * share))
        return jnp.concatenate(got, axis=0)

    def send_back(x):
        slots = x.reshape(experts, room, width)
        got = [slots[0]]
        for k in range(1, experts):
            got.append(turned(exchange(slots[k], k * share), k))
        rows_rel = jnp.einsum(
            "kct,kcd->td", place_mlp, jnp.stack(got), preferred_element_type=F32
        ).astype(BF)
        return relative(rows_rel, range(group))

    every = range(group)
    weight_own = [piece(weight_slots, expert_me ^ k, 1, 0)[0] for k in range(experts)]
    slot_weight = jnp.concatenate(
        [weight_own[0]] + [exchange(weight_own[k], k * share) for k in range(1, experts)]
    )
    grad_out = cotangent[0]
    grad_slots = send_out(relative(grad_out, every))
    two_slots = send_out(relative(hidden_two, every))
    gate_up = dot(two_slots, in_full, 1, 0)
    gate_part, up_part = gate_up[:, :hidden_units], gate_up[:, hidden_units:]
    sigmoid_gate = jax.nn.sigmoid(gate_part)
    silu_gate = gate_part * sigmoid_gate
    active = (silu_gate * up_part * slot_weight).astype(BF)
    mlp_slots = dot(active, down_full, 1, 1).astype(BF)
    grad_active = dot(grad_slots, down_full, 1, 0)
    scaled = grad_active * slot_weight
    grad_gate = scaled * up_part * sigmoid_gate * (1.0 + gate_part * (1.0 - sigmoid_gate))
    grad_up = scaled * silu_gate
    grad_gu = jnp.concatenate([grad_gate, grad_up], axis=1).astype(BF)
    back_two_slots = dot(grad_gu, in_full, 1, 1).astype(BF)
    back_two = lax.psum(send_back(back_two_slots), "tp").astype(F32)
    mlp_total = lax.psum(send_back(mlp_slots), "tp").astype(F32)
    output = (resid + mlp_total).astype(BF)

    def for_share(x, t):
        return jnp.concatenate(
            [x[:, (k * share + t) * part : (k * share + t + 1) * part] for k in range(experts)],
            axis=1,
        )

    def every_share(x, cut):
        got = [for_share(x, 0) if cut else x]
        for t in range(1, share):
            got.append(exchange(for_share(x, t) if cut else x, t))
        return jnp.concatenate(got, axis=0)

    grad_in_w = dot(every_share(two_slots, True), every_share(grad_gu, False), 0, 0).astype(BF)
    grad_down_w = dot(every_share(grad_slots, True), every_share(active, False), 0, 0).astype(BF)
    expert_grads = []
    for k in range(experts):
        cut = slice(k * part, (k + 1) * part)
        block = jnp.concatenate([grad_in_w[cut], grad_down_w[cut]], axis=1)
        expert_grads.append(exchange(block, k * share) if k else block)
    expert_grads = jnp.stack(expert_grads)
    expert_grads = jnp.stack(
        [piece(expert_grads, expert_me ^ e, 1, 0)[0] for e in range(experts)], axis=1
    ).astype(F32)
    grad_in_out = expert_grads[:, :, : 2 * hidden_units].reshape(w_in.shape)
    grad_down_out = expert_grads[:, :, 2 * hidden_units :]

    grad_resid_norm, gain_two_grad = norm_back(back_two, normed_two, inverse_two, gain_two)
    grad_resid = grad_out.astype(F32) + grad_resid_norm
    grad_branch = grad_resid.astype(BF)
    grad_mixed = jnp.einsum("td,pdc->tpc", grad_branch, outw_full, preferred_element_type=F32)
    grad_attn = (grad_mixed * gate_attn[:, :, None]).astype(BF).reshape(mixed.shape)
    grad_query, grad_key, grad_value = attend_back(
        qkv, kv, place_attn, slot_seg, slot_idx, *key_row, grad_attn, (cos, sin)
    )
    grad_kv = jnp.concatenate([grad_key, grad_value], axis=1)
    for bit in ctx_bits[::-1]:
        half = grad_kv.shape[0] // 2
        got = swap(grad_kv[half:], 1 << bit, "ctx", ctx_count)
        grad_kv = (grad_kv[:half].astype(F32) + got.astype(F32)).astype(BF)
    grad_qkv = jnp.concatenate([grad_query, grad_kv], axis=1)
    back_one_part = jnp.einsum(
        "tpc,pdc->td", planes(grad_qkv), qkv_full, preferred_element_type=F32
    )
    back_one = lax.psum(back_one_part.astype(BF), "tp").astype(F32)
    grad_input_norm, gain_one_grad = norm_back(back_one, normed_one, inverse_one, gain_one)
    grad_tokens = (grad_resid + grad_input_norm).astype(BF)

    ours = [j for j in every if j % 2 == 0]
    theirs = [j for j in every if j % 2 == 1]

    def both(x):
        return jnp.concatenate([x, exchange(x, 1)], axis=0)

    def both_cut(x):
        return jnp.concatenate([relative(x, ours), exchange(relative(x, theirs), 1)], axis=0)

    def reduced(x, bits):
        x = x.astype(BF).reshape((2,) * (bits_of(group) - 1) + (part, x.shape[1]))
        axes = list(range(1, bits_of(group)))[::-1]
        for bit in bits:
            at = axes.index(bit)
            keep = lax.index_in_dim(x, 0, at, False).astype(F32)
            got = exchange(lax.index_in_dim(x, 1, at, False), 1 << bit).astype(F32)
            axes.remove(bit)
            x = keep + got
            if axes:
                x = x.astype(BF)
        return x

    def reduced_both(x):
        bits = list(range(1, bits_of(group)))
        half = x.shape[1] // 2
        return jnp.concatenate([reduced(x[:, :half], bits), reduced(x[:, half:], bits[::-1])], axis=1)

    grad_outw = reduced_both(dot(both_cut(grad_branch), both(mixed), 0, 0))
    grad_qkvw = reduced_both(dot(both_cut(hidden_one), both(grad_qkv), 0, 0))
    grad_outw = grad_outw.reshape(w_out_attn.shape)
    grad_qkvw = grad_qkvw.reshape(part, attn_experts + 2, head_width)
    gain_grads = lax.psum(jnp.stack([gain_one_grad, gain_two_grad]), GROUP)
    gain_grads = piece(gain_grads, me)
    return (
        output[None],
        grad_tokens[None],
        gain_grads[0],
        gain_grads[1],
        grad_qkvw[:, attn_experts:],
        grad_qkvw[:, :attn_experts],
        grad_outw,
        grad_in_out,
        grad_down_out,
    )


def solution(mesh):
    rows = P("fsdp", "ctx", None)
    weight = P(GROUP, None, "tp")
    weight_in = P(GROUP, None, None, "tp")
    return jax.shard_map(
        functools.partial(layer, (mesh.shape["fsdp"], mesh.shape["ctx"])),
        mesh=mesh,
        in_specs=(
            rows,
            P(GROUP),
            P(GROUP),
            weight,
            weight,
            weight,
            weight_in,
            weight,
            P("fsdp", None),
            rows,
            rows,
            rows,
            rows,
            rows,
        ),
        out_specs=(rows, rows, P(GROUP), P(GROUP), weight, weight, weight, weight_in, weight),
        check_vma=False,
    )
```

time: 2390 us -> 921 us (0.39)
  waiting for transfers between devices: 1930 us -> 363 us
  blocking collectives: 30.2 us -> 123 us
  matrix products: 173 us -> 95.3 us
  Pallas kernels: 0 us -> 57.2 us
  other arithmetic: 114 us -> 66.6 us
  starting transfers between devices: 1.28 us -> 41.8 us
  local copies, waits for them, and re-layouts: 111 us -> 150 us
    reduce_scatter x12 -> x0, waiting for transfers between devices: 1340 us -> none  [the longest x1 506 us: local(): lax.psum_scatter(jnp.einsum('ecd,ecaf->deaf', two_slots, grad_gu, preferr...]
    all_gather x7 -> x2, waiting for transfers between devices: 431 us -> 14.3 us  [the longest x1 14.3 us: layer(): lax.all_gather(w_out_attn.transpose(1, 0, 2), GROUP, axis=1, tiled=True)]
    ppermute x0 -> x45, waiting for transfers between devices: none -> 273 us  [swap(): return lax.ppermute(x, axes, [(i, i ^ mask) for i in range(count)])]
    psum x0 -> x1, blocking collectives: none -> 92.7 us  [layer(): gain_grads = lax.psum(jnp.stack([gain_one_grad, gain_two_grad]), GROUP)]
    psum x3, waiting for transfers between devices: 159 us -> 75.8 us  [the longest x1 47.5 us: layer(): resid = inputs + lax.psum(branch.astype(BF), 'tp').astype(F32)]
    dot_general x22 -> x17, matrix products: 173 us -> 95.3 us  [the longest x10 69.4 us: dot(): lax.dot_general(a, b, (((ca,), (cb,)), ((), ())), preferred_element_type=...]
    scatter-add x4 -> x0, other arithmetic: 62.4 us -> none  [combine_rows(): jnp.zeros((row_count, flat_rows.shape[1]), jnp.float32).at[source]]
    pallas_call x0 -> x3, Pallas kernels: none -> 57.2 us  [the longest x1 29.6 us: attend_back(): pl.pallas_call(functools.partial(attend_back_kernel, heads, experts), out...]
  transfers between devices with their start and end apart: 22 -> 50, of which waited for: 21 -> 17; matrix products, arithmetic and copies ran while one was open for 10% -> 33% of each run, Pallas kernels for 0% -> 6%
where the time goes in v1:
time: 921 us; the launch traced here: 913 us
  waiting for transfers between devices  363 us (39%)
  local copies, waits for them, and re-layouts  150 us (16%)
  blocking collectives  123 us (13%)
  matrix products  95.3 us (10%)
  other arithmetic  66.6 us (7%)
  Pallas kernels  57.2 us (6%)
  starting transfers between devices  41.8 us (5%)
  between operations  15.9 us (2%)
    ppermute x45, waiting for transfers between devices, swap(): return lax.ppermute(x, axes, [(i, i ^ mask) for i in range(count)])  273 us
    psum x1, blocking collectives, layer(): gain_grads = lax.psum(jnp.stack([gain_one_grad, gain_two_grad]), GROUP)  92.7 us
    dot_general x10, matrix products, dot(): lax.dot_general(a, b, (((ca,), (cb,)), ((), ())), preferred_element_type=...  69.4 us
    unnamed x204, local copies, waits for them, and re-layouts  66.9 us
    psum x1, waiting for transfers between devices, layer(): resid = inputs + lax.psum(branch.astype(BF), 'tp').astype(F32)  47.5 us
    ppermute x45, starting transfers between devices, swap(): return lax.ppermute(x, axes, [(i, i ^ mask) for i in range(count)])  41 us
    all_gather x1, blocking collectives, layer(): lax.all_gather(jnp.stack([gain_attn, gain_mlp]), GROUP, axis=1, tiled=True)  29.9 us
    pallas_call x1, Pallas kernels, attend_back(): pl.pallas_call(functools.partial(attend_back_kernel, heads, experts), out...  29.6 us
  transfers between devices with their start and end apart: 50, of which 17 were waited for; matrix products, arithmetic and copies ran while one was open for 33% of the time, Pallas kernels for 6%

profile of v1, /device:TPU:0, one launch (start us, length us, event | category | flops | bytes accessed | tf_op | source)
XLA Modules:
  0.0 912.8 jit_solution(2460606653612586565)
XLA Ops:
  12.6 3.9 collective-permute-start.14
  21.0 2.9 collective-permute-start.20
  38.3 29.9 %all_gather.9 = bf16[2,2048]{1,0:T(2,128)(2,1)S(1)} all-gather(bf16[2,256]{1,0:T(2,128)(2,1)S(1)} %pad_maximum_fusion.29), channel_id=1, replica_groups=mesh['fsdp'=2,'ctx'=4,'tp'=4] {'fsdp','ctx'}, dimensions={1}, use_global_device_ids=true | all-gather | bytes 9216 | tf_op jit(solution)/shard_map/all_gather | solution.py:263
  70.1 14.3 %all-gather.5.cloned.1.call-done = bf16[4,2048,512]{2,1,0:T(8,128)(2,1)} async-done(((bf16[4,256,512]{2,1,0:T(8,128)(2,1)}), bf16[4,2048,512]{2,1,0:T(8,128)(2,1)}) %all-gather.5.cloned.1.call-update) | async-done | bytes 8388624 | tf_op jit(solution)/shard_map/all_gather | solution.py:262
  84.4 5.8 constant_dynamic-slice_fusion.21
  102.8 149.9 %collective-permute-done.18 = bf16[144,2048]{1,0:T(8,128)(2,1)S(1)} collective-permute-done((bf16[144,2048]{1,0:T(8,128)(2,1)S(1)}, bf16[144,2048]{1,0:T(8,128)(2,1)S(1)}, u32[]{:S(2)}, u32[]{:S(2)}) %collective-permute-start.18) | collective-permute-done | bytes 589856 | tf_op jit(solution)/shard_map/ppermute | solution.py:41
  252.7 2.9 pad_maximum_fusion.4
  263.3 4.8 collective-permute-done.7
  273.2 9.9 %project.1.q_ref = bf16[256,3072]{1,0:T(8,128)(2,1)} custom-call(bf16[256,2048]{1,0:T(8,128)(2,1)} %copy-done.10, bf16[6,2048,512]{2,1,0:T(8,128)(2,1)} %all-gather.3.cloned.1.call-done.w_ref, f32[2,256,128]{2,1,0:T(8,128)} %stack.76.cos_ref, f32[2,256,128]{2,1,0:T(8,128)} %stack.78.sin_ref), custom_call_target="tpu_custom_call" | custom-call | tf_op jit(solution)/shard_map/project/pallas_call | solution.py:63
  290.1 8.1 collective-permute-done
  304.4 17.7 %attend.1 = bf16[256,2048]{1,0:T(8,128)(2,1)} custom-call(bf16[256,3072]{1,0:T(8,128)(2,1)} %project.1.q_ref, bf16[1024,1024]{1,0:T(8,128)(2,1)} %pad_maximum_fusion.12.k_ref.v_ref, bf16[1024,1024]{1,0:T(8,128)(2,1)} %pad_maximum_fusion.12.k_ref.v_ref, bf16[4,144,256]{2,1,0:T(8,128)(2,1)} %get-tuple-element.190.d_ref, s32[4,144,1]{2,1,0:T(8,128)} %copy.99.segq_ref, ...), custom_call_target="tpu_custom_call" | custom-call | tf_op jit(solution)/shard_map/attend/pallas_call | solution.py:165
  322.1 7.0 fusion.26
  334.2 47.5 %all-reduce.7.cloned.1.call-done = bf16[256,2048]{1,0:T(8,128)(2,1)} async-done(((bf16[256,2048]{1,0:T(8,128)(2,1)}), bf16[256,2048]{1,0:T(8,128)(2,1)}) %all-reduce.7.cloned.1.call-update) | async-done | bytes 1048592 | tf_op jit(solution)/shard_map/psum | solution.py:312
  391.8 10.9 %collective-permute-done.4 = bf16[144,2048]{1,0:T(8,128)(2,1)S(1)} collective-permute-done((bf16[144,2048]{1,0:T(8,128)(2,1)S(1)}, bf16[144,2048]{1,0:T(8,128)(2,1)S(1)}, u32[]{:S(2)}, u32[]{:S(2)}) %collective-permute-start.4) | collective-permute-done | bytes 589856 | tf_op jit(solution)/shard_map/ppermute | solution.py:41
  402.7 11.7 %collective-permute-done.3 = bf16[144,2048]{1,0:T(8,128)(2,1)S(1)} collective-permute-done((bf16[144,2048]{1,0:T(8,128)(2,1)S(1)}, bf16[144,2048]{1,0:T(8,128)(2,1)S(1)}, u32[]{:S(2)}, u32[]{:S(2)}) %collective-permute-start.3) | collective-permute-done | bytes 589856 | tf_op jit(solution)/shard_map/ppermute | solution.py:41
  414.4 12.2 %fusion.128 = f32[576,2816]{1,0:T(8,128)} fusion(bf16[2048,2816]{1,0:T(8,128)(2,1)} %slice_dynamic-update-slice_fusion, bf16[144,2048]{1,0:T(8,128)(2,1)S(1)} %collective-permute-done.4, bf16[144,2048]{1,0:T(8,128)(2,1)S(1)} %collective-permute-done.3, bf16[144,2048]{1,0:T(8,128)(2,1)S(1)} %collective-permute-done.2, ...), kind=kOutput, calls=%fused_computation.351 | convolution fusion | flops 6653214720 | bytes 20381696 | tf_op jit(solution)/shard_map/dot_general | solution.py:33
  426.6 7.9 multiply_convert_fusion.1
  434.5 4.1 convolution_convert_fusion.4
  440.1 9.8 %convolution_convert_fusion.3 = bf16[576,2048]{1,0:T(8,128)(2,1)S(1)} fusion(bf16[2048,2816]{1,0:T(8,128)(2,1)} %slice_dynamic-update-slice_fusion, bf16[576,1408]{1,0:T(8,128)(2,1)S(1)} %get-tuple-element.57, bf16[576,1408]{1,0:T(8,128)(2,1)S(1)} %get-tuple-element.56), kind=kOutput, calls=%fused_computation.41 | convolution fusion | flops 6651445248 | bytes 17137664 | tf_op jit(solution)/shard_map/dot_general | solution.py:33
  457.8 21.2 %collective-permute-done.22 = bf16[144,2048]{1,0:T(8,128)(2,1)S(1)} collective-permute-done((bf16[144,2048]{1,0:T(8,128)(2,1)S(1)}, bf16[144,2048]{1,0:T(8,128)(2,1)S(1)}, u32[]{:S(2)}, u32[]{:S(2)}) %collective-permute-start.22) | collective-permute-done | bytes 589856 | tf_op jit(solution)/shard_map/ppermute | solution.py:41
  482.2 23.9 %collective-permute-done.21 = bf16[144,2048]{1,0:T(8,128)(2,1)S(1)} collective-permute-done((bf16[144,2048]{1,0:T(8,128)(2,1)S(1)}, bf16[144,2048]{1,0:T(8,128)(2,1)S(1)}, u32[]{:S(2)}, u32[]{:S(2)}) %collective-permute-start.21) | collective-permute-done | bytes 589856 | tf_op jit(solution)/shard_map/ppermute | solution.py:41
  514.3 5.8 collective-permute-done.16
  522.8 10.3 %collective-permute-done.15 = bf16[144,2048]{1,0:T(8,128)(2,1)S(1)} collective-permute-done((bf16[144,2048]{1,0:T(8,128)(2,1)}, bf16[144,2048]{1,0:T(8,128)(2,1)S(1)}, u32[]{:S(2)}, u32[]{:S(2)}) %collective-permute-start.15) | collective-permute-done | bytes 589856 | tf_op jit(solution)/shard_map/ppermute | solution.py:41
  539.7 7.1 convolution_convert_fusion.1
  546.9 16.7 %all-reduce.9.cloned.1.call-done = bf16[256,2048]{1,0:T(8,128)(2,1)} async-done(((bf16[256,2048]{1,0:T(8,128)(2,1)}), bf16[256,2048]{1,0:T(8,128)(2,1)}) %all-reduce.9.cloned.1.call-update) | async-done | bytes 1048592 | tf_op jit(solution)/shard_map/psum | solution.py:375
  566.9 5.7 fusion.80
  573.7 29.6 %attend_back.1 = (bf16[256,2048]{1,0:T(8,128)(2,1)}, bf16[1024,512]{1,0:T(8,128)(2,1)}, bf16[1024,512]{1,0:T(8,128)(2,1)}) custom-call(bf16[256,3072]{1,0:T(8,128)(2,1)} %project.1.q_ref, bf16[1024,1024]{1,0:T(8,128)(2,1)} %pad_maximum_fusion.12.k_ref.v_ref, bf16[1024,1024]{1,0:T(8,128)(2,1)} %pad_maximum_fusion.12.k_ref.v_ref, ...), custom_call_target="tpu_custom_call" | custom-call | tf_op jit(solution)/shard_map/attend_back/pallas_call | solution.py:184
  608.6 3.9 convolution_convert_fusion.2
  618.9 8.7 collective-permute-done.25
  633.9 9.5 %fusion.27 = bf16[256,2048]{1,0:T(8,128)(2,1)} fusion(bf16[256,6,512]{0,2,1:T(8,128)(2,1)} %bitcast.275, bf16[6,2048,512]{2,1,0:T(8,128)(2,1)} %all-gather.3.cloned.1.call-done.w_ref), kind=kOutput, calls=%fused_computation.56 | convolution fusion | flops 3221749760 | bytes 15204352 | tf_op jit(solution)/shard_map/tpc,pdc->td/dot_general | solution.py:419
  645.7 7.0 collective-permute-done.34
  657.5 18.3 %fusion.6 = bf16[1024,2816]{1,0:T(8,128)(2,1)S(1)} fusion(bf16[576,2816]{1,0:T(8,128)(2,1)} %collective-permute-done.39, bf16[576,1408]{1,0:T(8,128)(2,1)S(1)} %copy-done.28, bf16[576,1408]{1,0:T(8,128)(2,1)S(1)} %copy-done.26, bf16[576,1024]{1,0:T(8,128)(2,1)} %collective-permute-done.38, bf16[576,256]{1,0:T(8,128)(2,1)S(1)} %copy-done.45, ...), kind=kOutput, calls=%fused_computation.9 | convolution fusion | flops 6677921792 | bytes 14614528 | tf_op jit(solution)/shard_map/dot_general | solution.py:33
  688.3 3.7 reshape.221
  692.0 5.7 convolution_convert_fusion
  701.6 3.1 copy.116
  707.9 3.8 fusion.132
  711.7 2.7 copy.125
  717.5 11.6 %all-reduce.11.cloned.1.call-done = (bf16[256,2048]{1,0:T(8,128)(2,1)}, bf16[256,2048]{1,0:T(8,128)(2,1)}) async-done(((bf16[256,2048]{1,0:T(8,128)(2,1)}, bf16[256,2048]{1,0:T(8,128)(2,1)}), (bf16[256,2048]{1,0:T(8,128)(2,1)}, bf16[256,2048]{1,0:T(8,128)(2,1)})) %all-reduce.11.cloned.1.call-update) | async-done | bytes 2097168 | tf_op jit(solution)/shard_map/psum | solution.py:376
  731.2 92.7 %psum.39 = f32[2,2048]{1,0:T(2,128)S(1)} all-reduce(f32[2,2048]{1,0:T(2,128)S(1)} %pad_maximum_fusion.28), channel_id=1, replica_groups=mesh['fsdp'=2,'ctx'=4,'tp'=4] {'fsdp','ctx'}, use_global_device_ids=true, to_apply=%region_20.21 | all-reduce | flops 4096 | bytes 32768 | tf_op jit(solution)/shard_map/psum | solution.py:457
  824.6 5.0 fusion.84
  829.6 4.0 pad_maximum_fusion
  835.6 7.7 maximum_convert_fusion
  843.3 9.9 %slice.696 = f32[256,4,2816]{2,0,1:T(8,128)} slice(f32[256,4,4224]{2,0,1:T(8,128)} %maximum_convert_fusion), slice={[0:256], [0:4], [0:2816]} | slice | bytes 23068672 | tf_op jit(solution)/shard_map/slice | solution.py:402
  853.2 14.4 %reshape.222 = f32[256,4,2,1408]{3,2,0,1:T(2,128)} reshape(f32[256,4,2816]{2,0,1:T(8,128)} %slice.696) | data formatting | bytes 23068672 | tf_op jit(solution)/shard_map/reshape | solution.py:402
  867.6 11.2 %copy.121 = f32[256,4,2,1408]{3,2,1,0:T(2,128)} copy(f32[256,4,2,1408]{3,2,0,1:T(2,128)} %reshape.222) | data formatting | bytes 23068672
  885.0 6.2 copy.122
  891.2 7.4 collective-permute-done.31
  898.7 3.2 collective-permute-done.29
  (436 shorter events, 175.6 us)
Async XLA Ops:
  7.2 77.2 %all-gather.5.cloned.1.call-start = ((), (), s32[]{:S(2)}) async-start(), calls=%async_computation.1 | async-start | bytes 9437184 | tf_op jit(solution)/shard_map/all_gather | solution.py:262
  9.8 263.4 %all-gather.3.cloned.1.call-start = ((), (), s32[]{:S(2)}) async-start(), calls=%async_computation | async-start | bytes 14155776 | tf_op jit(solution)/shard_map/all_gather | solution.py:261
  11.4 370.2 %all-reduce.7.cloned.1.call-start = ((), (), s32[]{:S(2)}) async-start(), calls=%async_computation.2 | async-start | bytes 2097152 | tf_op jit(solution)/shard_map/psum | solution.py:312
  12.6 81.3 %collective-permute-start.14 = (f32[144,1]{0,1:T(1,128)}, f32[144,1]{0,1:T(1,128)}, u32[]{:S(2)}, u32[]{:S(2)}) collective-permute-start(f32[144,1]{0,1:T(1,128)} %get-tuple-element.186), channel_id=1, source_target_pairs={{0,24},{4,28},{8,16},{12,20},{16,8},{20,12},{24,0},{28,4},{1,25},{... | collective-permute-start | bytes 1736 | tf_op jit(solution)/shard_map/ppermute | solution.py:41
  16.5 77.7 %collective-permute-start.13 = (f32[144,1]{0,1:T(1,128)}, f32[144,1]{0,1:T(1,128)}, u32[]{:S(2)}, u32[]{:S(2)}) collective-permute-start(f32[144,1]{0,1:T(1,128)} %get-tuple-element.187), channel_id=1, source_target_pairs={{0,16},{4,20},{8,24},{12,28},{16,0},{20,4},{24,8},{28,12},{1,17},{... | collective-permute-start | bytes 1736 | tf_op jit(solution)/shard_map/ppermute | solution.py:41
  17.0 78.0 %collective-permute-start.12 = (f32[144,1]{0,1:T(1,128)}, f32[144,1]{0,1:T(1,128)}, u32[]{:S(2)}, u32[]{:S(2)}) collective-permute-start(f32[144,1]{0,1:T(1,128)} %get-tuple-element.188), channel_id=1, source_target_pairs={{0,8},{4,12},{8,0},{12,4},{16,24},{20,28},{24,16},{28,20},{1,9},{5... | collective-permute-start | bytes 1736 | tf_op jit(solution)/shard_map/ppermute | solution.py:41
  21.0 75.2 %collective-permute-start.20 = (bf16[144,2048]{1,0:T(8,128)(2,1)}, bf16[144,2048]{1,0:T(8,128)(2,1)}, u32[]{:S(2)}, u32[]{:S(2)}) collective-permute-start(bf16[144,2048]{1,0:T(8,128)(2,1)} %pad_maximum_fusion.23), channel_id=1, source_target_pairs={{0,24},{4,28},{8,16},{12,20},{16,8},{20,12},{24,0},{28,4},{1,25},{... | collective-permute-start | bytes 1769480 | tf_op jit(solution)/shard_map/ppermute | solution.py:41
  24.8 73.9 %collective-permute-start.19 = (bf16[144,2048]{1,0:T(8,128)(2,1)}, bf16[144,2048]{1,0:T(8,128)(2,1)}, u32[]{:S(2)}, u32[]{:S(2)}) collective-permute-start(bf16[144,2048]{1,0:T(8,128)(2,1)} %pad_maximum_fusion.22), channel_id=1, source_target_pairs={{0,16},{4,20},{8,24},{12,28},{16,0},{20,4},{24,8},{28,12},{1,17},{... | collective-permute-start | bytes 1769480 | tf_op jit(solution)/shard_map/ppermute | solution.py:41
  93.9 165.2 %collective-permute-start.5 = (bf16[256,4224]{1,0:T(8,128)(2,1)S(1)}, bf16[256,4224]{1,0:T(8,128)(2,1)S(1)}, u32[]{:S(2)}, u32[]{:S(2)}) collective-permute-start(bf16[256,4224]{1,0:T(8,128)(2,1)S(1)} %pad_maximum_fusion.5), channel_id=1, source_target_pairs={{0,4},{4,0},{8,12},{12,8},{16,20},{20,16},{24,28},{28,24},{1,5},{5... | collective-permute-start | bytes 6488072 | tf_op jit(solution)/shard_map/ppermute | solution.py:41
  94.2 165.3 %collective-permute-start.6 = (bf16[256,4224]{1,0:T(8,128)(2,1)S(1)}, bf16[256,4224]{1,0:T(8,128)(2,1)S(1)}, u32[]{:S(2)}, u32[]{:S(2)}) collective-permute-start(bf16[256,4224]{1,0:T(8,128)(2,1)S(1)} %pad_maximum_fusion.6), channel_id=1, source_target_pairs={{0,8},{4,12},{8,0},{12,4},{16,24},{20,28},{24,16},{28,20},{1,9},{5... | collective-permute-start | bytes 6488072 | tf_op jit(solution)/shard_map/ppermute | solution.py:41
  95.0 164.6 %collective-permute-start.8 = (bf16[256,4224]{1,0:T(8,128)(2,1)S(1)}, bf16[256,4224]{1,0:T(8,128)(2,1)}, u32[]{:S(2)}, u32[]{:S(2)}) collective-permute-start(bf16[256,4224]{1,0:T(8,128)(2,1)S(1)} %pad_maximum_fusion.7), channel_id=1, source_target_pairs={{0,16},{4,20},{8,24},{12,28},{16,0},{20,4},{24,8},{28,12},{1,17},{... | collective-permute-start | bytes 6488072 | tf_op jit(solution)/shard_map/ppermute | solution.py:41
  96.2 163.8 %collective-permute-start.10 = (bf16[256,4224]{1,0:T(8,128)(2,1)S(1)}, bf16[256,4224]{1,0:T(8,128)(2,1)}, u32[]{:S(2)}, u32[]{:S(2)}) collective-permute-start(bf16[256,4224]{1,0:T(8,128)(2,1)S(1)} %pad_maximum_fusion.8), channel_id=1, source_target_pairs={{0,24},{4,28},{8,16},{12,20},{16,8},{20,12},{24,0},{28,4},{1,25},{... | collective-permute-start | bytes 6488072 | tf_op jit(solution)/shard_map/ppermute | solution.py:41
  98.8 153.9 %collective-permute-start.18 = (bf16[144,2048]{1,0:T(8,128)(2,1)S(1)}, bf16[144,2048]{1,0:T(8,128)(2,1)S(1)}, u32[]{:S(2)}, u32[]{:S(2)}) collective-permute-start(bf16[144,2048]{1,0:T(8,128)(2,1)S(1)} %pad_maximum_fusion.21), channel_id=1, source_target_pairs={{0,8},{4,12},{8,0},{12,4},{16,24},{20,28},{24,16},{28,20},{1,9},{5... | collective-permute-start | bytes 1769480 | tf_op jit(solution)/shard_map/ppermute | solution.py:41
  252.7 439.4 %collective-permute-start.26 = (bf16[256,1024]{1,0:T(8,128)(2,1)}, bf16[256,1024]{1,0:T(8,128)(2,1)}, u32[]{:S(2)}, u32[]{:S(2)}) collective-permute-start(bf16[256,1024]{1,0:T(8,128)(2,1)} %pad_maximum_fusion.24), channel_id=1, source_target_pairs={{0,4},{4,0},{8,12},{12,8},{16,20},{20,16},{24,28},{28,24},{1,5},{5... | collective-permute-start | bytes 1572872 | tf_op jit(solution)/shard_map/ppermute | solution.py:41
  259.1 280.6 %collective-permute-start.40 = (bf16[576,1024]{1,0:T(8,128)(2,1)}, bf16[576,1024]{1,0:T(8,128)(2,1)}, u32[]{:S(2)}, u32[]{:S(2)}) collective-permute-start(bf16[576,1024]{1,0:T(8,128)(2,1)} %pad_maximum_fusion.16), channel_id=1, source_target_pairs={{0,4},{4,0},{8,12},{12,8},{16,20},{20,16},{24,28},{28,24},{1,5},{5... | collective-permute-start | bytes 3538952 | tf_op jit(solution)/shard_map/ppermute | solution.py:41
  259.5 8.6 collective-permute-start.7
  259.6 25.9 %collective-permute-start.9 = (bf16[256,4224]{1,0:T(8,128)(2,1)}, bf16[256,4224]{1,0:T(8,128)(2,1)}, u32[]{:S(2)}, u32[]{:S(2)}) collective-permute-start(bf16[256,4224]{1,0:T(8,128)(2,1)} %collective-permute-done.8), channel_id=1, source_target_pairs={{0,4},{4,0},{8,12},{12,8},{16,20},{20,16},{24,28},{28,24},{1,5},{5... | collective-permute-start | bytes 6488072 | tf_op jit(solution)/shard_map/ppermute | solution.py:41
  260.1 71.6 %collective-permute-start.11 = (bf16[256,4224]{1,0:T(8,128)(2,1)}, bf16[256,4224]{1,0:T(8,128)(2,1)}, u32[]{:S(2)}, u32[]{:S(2)}) collective-permute-start(bf16[256,4224]{1,0:T(8,128)(2,1)} %collective-permute-done.10), channel_id=1, source_target_pairs={{0,4},{4,0},{8,12},{12,8},{16,20},{20,16},{24,28},{28,24},{1,5},{5... | collective-permute-start | bytes 6488072 | tf_op jit(solution)/shard_map/ppermute | solution.py:41
  284.2 14.0 %collective-permute-start = (bf16[256,1024]{1,0:T(8,128)(2,1)S(1)}, bf16[256,1024]{1,0:T(8,128)(2,1)S(1)}, u32[]{:S(2)}, u32[]{:S(2)}) collective-permute-start(bf16[256,1024]{1,0:T(8,128)(2,1)S(1)} %slice.574), channel_id=1, source_target_pairs={{0,8},{4,12},{8,0},{12,4},{1,9},{5,13},{9,1},{13,5},{2,10},{6,14},... | collective-permute-start | bytes 1572872 | tf_op jit(solution)/shard_map/ppermute | solution.py:41
  329.2 234.4 %all-reduce.9.cloned.1.call-start = ((), (), s32[]{:S(2)}) async-start(), calls=%async_computation.3 | async-start | bytes 2097152 | tf_op jit(solution)/shard_map/psum | solution.py:375
  385.5 17.2 %collective-permute-start.4 = (bf16[144,2048]{1,0:T(8,128)(2,1)S(1)}, bf16[144,2048]{1,0:T(8,128)(2,1)S(1)}, u32[]{:S(2)}, u32[]{:S(2)}) collective-permute-start(bf16[144,2048]{1,0:T(8,128)(2,1)S(1)} %pad_maximum_fusion.20), channel_id=1, source_target_pairs={{0,24},{4,28},{8,16},{12,20},{16,8},{20,12},{24,0},{28,4},{1,25},{... | collective-permute-start | bytes 1769480 | tf_op jit(solution)/shard_map/ppermute | solution.py:41
  388.0 26.4 %collective-permute-start.3 = (bf16[144,2048]{1,0:T(8,128)(2,1)S(1)}, bf16[144,2048]{1,0:T(8,128)(2,1)S(1)}, u32[]{:S(2)}, u32[]{:S(2)}) collective-permute-start(bf16[144,2048]{1,0:T(8,128)(2,1)S(1)} %pad_maximum_fusion.19), channel_id=1, source_target_pairs={{0,16},{4,20},{8,24},{12,28},{16,0},{20,4},{24,8},{28,12},{1,17},{... | collective-permute-start | bytes 1769480 | tf_op jit(solution)/shard_map/ppermute | solution.py:41
  388.7 25.7 %collective-permute-start.2 = (bf16[144,2048]{1,0:T(8,128)(2,1)S(1)}, bf16[144,2048]{1,0:T(8,128)(2,1)S(1)}, u32[]{:S(2)}, u32[]{:S(2)}) collective-permute-start(bf16[144,2048]{1,0:T(8,128)(2,1)S(1)} %pad_maximum_fusion.18), channel_id=1, source_target_pairs={{0,8},{4,12},{8,0},{12,4},{16,24},{20,28},{24,16},{28,20},{1,9},{5... | collective-permute-start | bytes 1769480 | tf_op jit(solution)/shard_map/ppermute | solution.py:41
  402.7 205.9 %collective-permute-start.33 = (bf16[256,2048]{1,0:T(8,128)(2,1)}, bf16[256,2048]{1,0:T(8,128)(2,1)}, u32[]{:S(2)}, u32[]{:S(2)}) collective-permute-start(bf16[256,2048]{1,0:T(8,128)(2,1)} %attend.1), channel_id=1, source_target_pairs={{0,4},{4,0},{8,12},{12,8},{16,20},{20,16},{24,28},{28,24},{1,5},{5... | collective-permute-start | bytes 3145736 | tf_op jit(solution)/shard_map/ppermute | solution.py:41
  450.2 29.5 %collective-permute-start.23 = (bf16[144,2048]{1,0:T(8,128)(2,1)S(1)}, bf16[144,2048]{1,0:T(8,128)(2,1)S(1)}, u32[]{:S(2)}, u32[]{:S(2)}) collective-permute-start(bf16[144,2048]{1,0:T(8,128)(2,1)S(1)} %get-tuple-element.101), channel_id=1, source_target_pairs={{0,24},{4,28},{8,16},{12,20},{16,8},{20,12},{24,0},{28,4},{1,25},{... | collective-permute-start | bytes 1769480 | tf_op jit(solution)/shard_map/ppermute | solution.py:41
  452.6 26.4 %collective-permute-start.22 = (bf16[144,2048]{1,0:T(8,128)(2,1)S(1)}, bf16[144,2048]{1,0:T(8,128)(2,1)S(1)}, u32[]{:S(2)}, u32[]{:S(2)}) collective-permute-start(bf16[144,2048]{1,0:T(8,128)(2,1)S(1)} %get-tuple-element.102), channel_id=1, source_target_pairs={{0,16},{4,20},{8,24},{12,28},{16,0},{20,4},{24,8},{28,12},{1,17},{... | collective-permute-start | bytes 1769480 | tf_op jit(solution)/shard_map/ppermute | solution.py:41
  479.0 27.1 %collective-permute-start.21 = (bf16[144,2048]{1,0:T(8,128)(2,1)S(1)}, bf16[144,2048]{1,0:T(8,128)(2,1)S(1)}, u32[]{:S(2)}, u32[]{:S(2)}) collective-permute-start(bf16[144,2048]{1,0:T(8,128)(2,1)S(1)} %get-tuple-element.103), channel_id=1, source_target_pairs={{0,8},{4,12},{8,0},{12,4},{16,24},{20,28},{24,16},{28,20},{1,9},{5... | collective-permute-start | bytes 1769480 | tf_op jit(solution)/shard_map/ppermute | solution.py:41
  479.7 41.8 %collective-permute-start.17 = (bf16[144,2048]{1,0:T(8,128)(2,1)}, bf16[144,2048]{1,0:T(8,128)(2,1)}, u32[]{:S(2)}, u32[]{:S(2)}) collective-permute-start(bf16[144,2048]{1,0:T(8,128)(2,1)} %get-tuple-element.109), channel_id=1, source_target_pairs={{0,24},{4,28},{8,16},{12,20},{16,8},{20,12},{24,0},{28,4},{1,25},{... | collective-permute-start | bytes 1769480 | tf_op jit(solution)/shard_map/ppermute | solution.py:41
  506.0 14.0 %collective-permute-start.16 = (bf16[144,2048]{1,0:T(8,128)(2,1)}, bf16[144,2048]{1,0:T(8,128)(2,1)}, u32[]{:S(2)}, u32[]{:S(2)}) collective-permute-start(bf16[144,2048]{1,0:T(8,128)(2,1)} %get-tuple-element.110), channel_id=1, source_target_pairs={{0,16},{4,20},{8,24},{12,28},{16,0},{20,4},{24,8},{28,12},{1,17},{... | collective-permute-start | bytes 1769480 | tf_op jit(solution)/shard_map/ppermute | solution.py:41
  514.1 215.1 %all-reduce.11.cloned.1.call-start = ((), (), s32[]{:S(2)}) async-start(), calls=%async_computation.4 | async-start | bytes 4194304 | tf_op jit(solution)/shard_map/psum | solution.py:376
  520.1 13.0 %collective-permute-start.15 = (bf16[144,2048]{1,0:T(8,128)(2,1)}, bf16[144,2048]{1,0:T(8,128)(2,1)S(1)}, u32[]{:S(2)}, u32[]{:S(2)}) collective-permute-start(bf16[144,2048]{1,0:T(8,128)(2,1)} %get-tuple-element.111), channel_id=1, source_target_pairs={{0,8},{4,12},{8,0},{12,4},{16,24},{20,28},{24,16},{28,20},{1,9},{5... | collective-permute-start | bytes 1769480 | tf_op jit(solution)/shard_map/ppermute | solution.py:41
  521.4 18.3 %collective-permute-start.41 = (bf16[576,1408]{1,0:T(8,128)(2,1)S(1)}, bf16[576,1408]{1,0:T(8,128)(2,1)S(1)}, u32[]{:S(2)}, u32[]{:S(2)}) collective-permute-start(bf16[576,1408]{1,0:T(8,128)(2,1)S(1)} %copy-done.69), channel_id=1, source_target_pairs={{0,4},{4,0},{8,12},{12,8},{16,20},{20,16},{24,28},{28,24},{1,5},{5... | collective-permute-start | bytes 4866056 | tf_op jit(solution)/shard_map/ppermute | solution.py:41
  533.0 124.4 %collective-permute-start.39 = (bf16[576,2816]{1,0:T(8,128)(2,1)}, bf16[576,2816]{1,0:T(8,128)(2,1)}, u32[]{:S(2)}, u32[]{:S(2)}) collective-permute-start(bf16[576,2816]{1,0:T(8,128)(2,1)} %pad_maximum_fusion.1), channel_id=1, source_target_pairs={{0,4},{4,0},{8,12},{12,8},{16,20},{20,16},{24,28},{28,24},{1,5},{5... | collective-permute-start | bytes 9732104 | tf_op jit(solution)/shard_map/ppermute | solution.py:41
  605.1 7.6 collective-permute-start.24
  608.6 47.4 %collective-permute-start.38 = (bf16[576,1024]{1,0:T(8,128)(2,1)}, bf16[576,1024]{1,0:T(8,128)(2,1)}, u32[]{:S(2)}, u32[]{:S(2)}) collective-permute-start(bf16[576,1024]{1,0:T(8,128)(2,1)} %pad_maximum_fusion.15), channel_id=1, source_target_pairs={{0,4},{4,0},{8,12},{12,8},{16,20},{20,16},{24,28},{28,24},{1,5},{5... | collective-permute-start | bytes 3538952 | tf_op jit(solution)/shard_map/ppermute | solution.py:41
  613.2 14.4 %collective-permute-start.25 = (bf16[256,1024]{1,0:T(8,128)(2,1)S(1)}, bf16[256,1024]{1,0:T(8,128)(2,1)S(1)}, u32[]{:S(2)}, u32[]{:S(2)}) collective-permute-start(bf16[256,1024]{1,0:T(8,128)(2,1)S(1)} %slice.651), channel_id=1, source_target_pairs={{0,8},{4,12},{8,0},{12,4},{1,9},{5,13},{9,1},{13,5},{2,10},{6,14},... | collective-permute-start | bytes 1572872 | tf_op jit(solution)/shard_map/ppermute | solution.py:41
  616.3 27.1 %collective-permute-start.36 = (bf16[2,256,1024]{2,1,0:T(8,128)(2,1)}, bf16[2,256,1024]{2,1,0:T(8,128)(2,1)}, u32[]{:S(2)}, u32[]{:S(2)}) collective-permute-start(bf16[2,256,1024]{2,1,0:T(8,128)(2,1)} %bitcast.91), channel_id=1, source_target_pairs={{0,16},{4,20},{8,24},{12,28},{16,0},{20,4},{24,8},{28,12},{1,17},{... | collective-permute-start | bytes 3145736 | tf_op jit(solution)/shard_map/ppermute | solution.py:41
  627.6 25.2 %collective-permute-start.34 = (bf16[2,256,1024]{2,1,0:T(8,128)(2,1)}, bf16[2,256,1024]{2,1,0:T(8,128)(2,1)}, u32[]{:S(2)}, u32[]{:S(2)}) collective-permute-start(bf16[2,256,1024]{2,1,0:T(8,128)(2,1)} %slice_bitcast_fusion), channel_id=1, source_target_pairs={{0,8},{4,12},{8,0},{12,4},{16,24},{20,28},{24,16},{28,20},{1,9},{5... | collective-permute-start | bytes 3145736 | tf_op jit(solution)/shard_map/ppermute | solution.py:41
  643.4 48.6 %collective-permute-start.27 = (bf16[256,3072]{1,0:T(8,128)(2,1)}, bf16[256,3072]{1,0:T(8,128)(2,1)}, u32[]{:S(2)}, u32[]{:S(2)}) collective-permute-start(bf16[256,3072]{1,0:T(8,128)(2,1)} %pad_maximum_fusion.14), channel_id=1, source_target_pairs={{0,4},{4,0},{8,12},{12,8},{16,20},{20,16},{24,28},{28,24},{1,5},{5... | collective-permute-start | bytes 4718600 | tf_op jit(solution)/shard_map/ppermute | solution.py:41
  652.7 30.7 %collective-permute-start.37 = (bf16[256,1024]{1,0:T(8,128)(2,1)S(1)}, bf16[256,1024]{1,0:T(8,128)(2,1)S(1)}, u32[]{:S(2)}, u32[]{:S(2)}) collective-permute-start(bf16[256,1024]{1,0:T(8,128)(2,1)S(1)} %slice_bitcast_fusion.16), channel_id=1, source_target_pairs={{0,8},{4,12},{8,0},{12,4},{16,24},{20,28},{24,16},{28,20},{1,9},{5... | collective-permute-start | bytes 1572872 | tf_op jit(solution)/shard_map/ppermute | solution.py:41
  655.9 29.3 %collective-permute-start.35 = (bf16[256,1024]{1,0:T(8,128)(2,1)S(1)}, bf16[256,1024]{1,0:T(8,128)(2,1)S(1)}, u32[]{:S(2)}, u32[]{:S(2)}) collective-permute-start(bf16[256,1024]{1,0:T(8,128)(2,1)S(1)} %slice_bitcast_fusion.18), channel_id=1, source_target_pairs={{0,16},{4,20},{8,24},{12,28},{16,0},{20,4},{24,8},{28,12},{1,17},{... | collective-permute-start | bytes 1572872 | tf_op jit(solution)/shard_map/ppermute | solution.py:41
  678.5 151.1 %collective-permute-start.44 = (bf16[256,4224]{1,0:T(8,128)(2,1)}, bf16[256,4224]{1,0:T(8,128)(2,1)}, u32[]{:S(2)}, u32[]{:S(2)}) collective-permute-start(bf16[256,4224]{1,0:T(8,128)(2,1)} %pad_maximum_fusion.11), channel_id=1, source_target_pairs={{0,24},{4,28},{8,16},{12,20},{16,8},{20,12},{24,0},{28,4},{1,25},{... | collective-permute-start | bytes 6488072 | tf_op jit(solution)/shard_map/ppermute | solution.py:41
  683.5 146.1 %collective-permute-start.43 = (bf16[256,4224]{1,0:T(8,128)(2,1)}, bf16[256,4224]{1,0:T(8,128)(2,1)}, u32[]{:S(2)}, u32[]{:S(2)}) collective-permute-start(bf16[256,4224]{1,0:T(8,128)(2,1)} %pad_maximum_fusion.10), channel_id=1, source_target_pairs={{0,16},{4,20},{8,24},{12,28},{16,0},{20,4},{24,8},{28,12},{1,17},{... | collective-permute-start | bytes 6488072 | tf_op jit(solution)/shard_map/ppermute | solution.py:41
  685.2 144.4 %collective-permute-start.42 = (bf16[256,4224]{1,0:T(8,128)(2,1)}, bf16[256,4224]{1,0:T(8,128)(2,1)}, u32[]{:S(2)}, u32[]{:S(2)}) collective-permute-start(bf16[256,4224]{1,0:T(8,128)(2,1)} %pad_maximum_fusion.9), channel_id=1, source_target_pairs={{0,8},{4,12},{8,0},{12,4},{16,24},{20,28},{24,16},{28,20},{1,9},{5... | collective-permute-start | bytes 6488072 | tf_op jit(solution)/shard_map/ppermute | solution.py:41
  707.2 171.6 %collective-permute-start.30 = (bf16[2,256,1536]{1,2,0:T(8,128)(2,1)}, bf16[2,256,1536]{1,2,0:T(8,128)(2,1)}, u32[]{:S(2)}, u32[]{:S(2)}) collective-permute-start(bf16[2,256,1536]{1,2,0:T(8,128)(2,1)} %copy.115), channel_id=1, source_target_pairs={{0,16},{4,20},{8,24},{12,28},{16,0},{20,4},{24,8},{28,12},{1,17},{... | collective-permute-start | bytes 4718600 | tf_op jit(solution)/shard_map/ppermute | solution.py:41
  714.4 166.6 %collective-permute-start.28 = (bf16[2,256,1536]{1,2,0:T(8,128)(2,1)}, bf16[2,256,1536]{1,2,0:T(8,128)(2,1)}, u32[]{:S(2)}, u32[]{:S(2)}) collective-permute-start(bf16[2,256,1536]{1,2,0:T(8,128)(2,1)} %bitcast.274), channel_id=1, source_target_pairs={{0,8},{4,12},{8,0},{12,4},{16,24},{20,28},{24,16},{28,20},{1,9},{5... | collective-permute-start | bytes 4718600 | tf_op jit(solution)/shard_map/ppermute | solution.py:41
  880.9 17.6 %collective-permute-start.31 = (bf16[256,1536]{0,1:T(8,128)(2,1)S(1)}, bf16[256,1536]{0,1:T(8,128)(2,1)S(1)}, u32[]{:S(2)}, u32[]{:S(2)}) collective-permute-start(bf16[256,1536]{0,1:T(8,128)(2,1)S(1)} %slice_bitcast_fusion.2), channel_id=1, source_target_pairs={{0,8},{4,12},{8,0},{12,4},{16,24},{20,28},{24,16},{28,20},{1,9},{5... | collective-permute-start | bytes 2359304 | tf_op jit(solution)/shard_map/ppermute | solution.py:41
  883.1 18.9 %collective-permute-start.29 = (bf16[256,1536]{0,1:T(8,128)(2,1)S(1)}, bf16[256,1536]{0,1:T(8,128)(2,1)S(1)}, u32[]{:S(2)}, u32[]{:S(2)}) collective-permute-start(bf16[256,1536]{0,1:T(8,128)(2,1)S(1)} %slice_bitcast_fusion.4), channel_id=1, source_target_pairs={{0,16},{4,20},{8,24},{12,28},{16,0},{20,4},{24,8},{28,12},{1,17},{... | collective-permute-start | bytes 2359304 | tf_op jit(solution)/shard_map/ppermute | solution.py:41
  (76 other events, 869.2 us)
Sparse Core Ops, SparseCore 0:
  10.5 73.8 all-gather.4
  86.9 168.6 all-gather.2
  329.3 52.3 all-reduce.6
  514.2 49.3 all-reduce.8
  643.5 85.5 all-reduce.10

commit v2 on v1

v2 whole, which is shorter than its diff:
```python
import functools

import jax
import jax.numpy as jnp
from jax import lax
from jax.experimental import pallas as pl
from jax.experimental.pallas import tpu as pltpu
from jax.sharding import PartitionSpec as P

HD = 128
EPSILON = 1e-06
ROPE_BASE = 10000.0
MASKED = -1e30
GROUP = ("fsdp", "ctx")
BF = jnp.bfloat16
F32 = jnp.float32
VMEM_LIMIT = 56 * 1024 * 1024


def normalize(tensor, gain_vec):
    inverse = lax.rsqrt(jnp.mean(tensor * tensor, axis=-1, keepdims=True) + EPSILON)
    normed = tensor * inverse
    return (normed, inverse, normed * gain_vec)


def norm_back(grad_in, normed, inverse, gain_vec):
    scaled = grad_in * gain_vec
    inner_mean = jnp.mean(scaled * normed, axis=-1, keepdims=True)
    return (inverse * (scaled - normed * inner_mean), jnp.sum(grad_in * normed, axis=0))


def dot(a, b, ca, cb):
    return lax.dot_general(a, b, (((ca,), (cb,)), ((), ())), preferred_element_type=F32)


def turn(x, cos, sin):
    return x * cos + pltpu.roll(x, HD // 2, 1) * sin


def swap(x, mask, axes, count):
    return lax.ppermute(x, axes, [(i, i ^ mask) for i in range(count)])


def bits_of(count):
    return count.bit_length() - 1


def flip(value, mask):
    step = 1
    while step <= mask:
        if mask & step:
            value = value + step - 2 * step * ((value // step) % 2)
        step *= 2
    return value


def peer(ctx_count, mask):
    return {
        "fsdp": flip(lax.axis_index("fsdp"), mask // ctx_count),
        "ctx": flip(lax.axis_index("ctx"), mask % ctx_count),
    }


def greet(ctx_count, masks):
    barrier = pltpu.get_barrier_semaphore()
    for mask in masks:
        pl.semaphore_signal(
            barrier, inc=1, device_id=peer(ctx_count, mask), device_id_type=pl.DeviceIdType.MESH
        )
    pl.semaphore_wait(barrier, len(masks))


def window(ref, rows, cols):
    if cols is None:
        return ref.at[pl.ds(rows[0], rows[1])]
    return ref.at[pl.ds(rows[0], rows[1]), pl.ds(cols[0], cols[1])]


class Moves:
    def __init__(self, ctx_count, moves, arrays, send, recv, bounces=()):
        self.moves = moves
        self.onward = {}
        bounces = list(bounces)
        self.copies = []
        self.place = {m[1]: i for i, m in enumerate(moves)}
        self.started, self.came = set(), set()
        for i, (source, target, mask, _) in enumerate(moves):
            src = window(arrays[source[0]], *source[1:])
            dst = window(arrays[target[0]], *target[1:])
            if mask:
                copy = pltpu.make_async_remote_copy(
                    src_ref=src,
                    dst_ref=dst,
                    send_sem=send.at[i],
                    recv_sem=recv.at[i],
                    device_id=peer(ctx_count, mask),
                    device_id_type=pl.DeviceIdType.MESH,
                )
            else:
                bounce = bounces.pop(0)
                copy = pltpu.make_async_copy(src, bounce, recv.at[i])
                self.onward[i] = pltpu.make_async_copy(bounce, dst, send.at[i])
            self.copies.append(copy)

    def start(self, i):
        if i not in self.started:
            self.started.add(i)
            self.copies[i].start()

    def begin(self, count=None):
        for i, move in enumerate(self.moves[:count]):
            if not move[3]:
                self.start(i)

    def await_one(self, i):
        if i not in self.came:
            self.came.add(i)
            if i in self.onward:
                self.copies[i].wait()
                self.onward[i].start()
            else:
                self.copies[i].wait_recv()

    def settle(self, count):
        for i in range(count):
            if i in self.onward:
                self.await_one(i)
        for i in range(count):
            for target in self.moves[i][3]:
                self.await_one(self.place[target])
            self.start(i)
        for i in range(count):
            self.await_one(i)

    def finish(self):
        self.settle(len(self.moves))
        for i in range(len(self.moves)):
            if i in self.onward:
                self.onward[i].wait()
            else:
                self.copies[i].wait_send()


def masks_of(moves):
    return sorted({move[2] for move in moves if move[2]})


def move_kernel(ctx_count, moves, names_in, names_out, *refs):
    count = len(names_in) + len(names_out)
    refs, (send, recv, *bounces) = refs[:count], refs[count:]
    arrays = dict(zip(names_in, refs))
    arrays.update(zip(names_out, refs[len(names_in) :]))
    greet(ctx_count, masks_of(moves))
    run = Moves(ctx_count, moves, arrays, send, recv, bounces)
    run.begin()
    run.finish()


def move(name, number, ctx_count, moves, given, made):
    names_in = [n for n in given if n not in made] + [n for n in given if n in made]
    plain = [n for n in names_in if n not in made]
    names_out = list(made)
    any_spec = pl.BlockSpec(memory_space=pl.ANY)
    bounces = [
        pltpu.VMEM((source[1][1], (source[2] or (0, given[source[0]].shape[1]))[1]), BF)
        for source, _, mask, _ in moves
        if not mask
    ]
    return dict(
        zip(
            names_out,
            pl.pallas_call(
                functools.partial(
                    move_kernel,
                    ctx_count,
                    moves,
                    plain + ["old_" + n for n in names_in[len(plain) :]],
                    names_out,
                ),
                out_shape=[jax.ShapeDtypeStruct(shape, BF) for shape in made.values()],
                in_specs=[any_spec] * len(names_in),
                out_specs=[any_spec] * len(names_out),
                input_output_aliases={
                    names_in.index(n): names_out.index(n) for n in names_out if n in given
                },
                scratch_shapes=[pltpu.SemaphoreType.DMA((len(moves),))] * 2 + bounces,
                compiler_params=pltpu.CompilerParams(
                    collective_id=number, has_side_effects=True, vmem_limit_bytes=VMEM_LIMIT
                ),
                name=name,
            )(*[given[n] for n in names_in]),
        )
    )


def reduce_kernel(ctx_count, bits, part, pieces, grad_ref, out_ref, sums, got, send, recv):
    count, wide = grad_ref.shape[0] // part, grad_ref.shape[1]
    greet(ctx_count, sorted(1 << b for b in bits))
    half = wide // 2
    size = half // pieces
    number = [0]

    def copy(source, mask, block, cols):
        i = number[0]
        number[0] += 1
        rows = pl.ds(block * part, part)
        return pltpu.make_async_remote_copy(
            src_ref=source.at[rows, cols],
            dst_ref=got.at[rows, cols],
            send_sem=send.at[i],
            recv_sem=recv.at[i],
            device_id=peer(ctx_count, mask),
            device_id_type=pl.DeviceIdType.MESH,
        )

    lanes = []
    for piece in range(pieces):
        for side in range(2):
            order = bits if side == 0 else bits[::-1]
            cols = pl.ds(side * half + piece * size, size)
            lanes.append((order, cols))
    sent = []
    flying = []
    for order, cols in lanes:
        at = bits.index(order[0])
        copies = {j: copy(grad_ref, 1 << order[0], j, cols) for j in range(count) if j >> at & 1}
        for c in copies.values():
            c.start()
        flying.append(copies)
        sent += list(copies.values())
    left = [list(range(count)) for _ in lanes]
    for step in range(len(bits)):
        last = step == len(bits) - 1
        for n, (order, cols) in enumerate(lanes):
            at = bits.index(order[step])
            left[n] = [j for j in left[n] if not j >> at & 1]
            for j in left[n]:
                flying[n][j | 1 << at].wait_recv()
                rows = pl.ds(j * part, part)
                mine = grad_ref if step == 0 else sums
                total = mine[rows, cols].astype(F32) + got[
                    pl.ds((j | 1 << at) * part, part), cols
                ].astype(F32)
                if last:
                    out_ref[:, cols] = total
                else:
                    sums[rows, cols] = total.astype(BF)
            if not last:
                following = bits.index(order[step + 1])
                copies = {
                    j: copy(sums, 1 << order[step + 1], j, cols)
                    for j in left[n]
                    if j >> following & 1
                }
                for c in copies.values():
                    c.start()
                flying[n] = copies
                sent += list(copies.values())
    for c in sent:
        c.wait_send()


def reduce_grads(number, ctx_count, bits, part, grad):
    pieces = 4
    copies = 2 * pieces * (grad.shape[0] // part)
    full = pl.BlockSpec(memory_space=pltpu.VMEM)
    return pl.pallas_call(
        functools.partial(reduce_kernel, ctx_count, bits, part, pieces),
        out_shape=jax.ShapeDtypeStruct((part, grad.shape[1]), F32),
        in_specs=[full],
        out_specs=full,
        scratch_shapes=[pltpu.VMEM(grad.shape, BF)] * 2
        + [pltpu.SemaphoreType.DMA((copies,))] * 2,
        compiler_params=pltpu.CompilerParams(
            collective_id=number, has_side_effects=True, vmem_limit_bytes=VMEM_LIMIT
        ),
        name="reduce_grads",
    )(grad)


def project_kernel(h_ref, w_ref, cos_ref, sin_ref, out_ref):
    y = jnp.dot(h_ref[...], w_ref[...], preferred_element_type=F32)
    for head in range(y.shape[1] // HD):
        cols = slice(head * HD, (head + 1) * HD)
        out_ref[:, cols] = turn(y[:, cols], cos_ref[0], sin_ref[0]).astype(BF)


def project(hidden, weight, cos, sin, plain, cols, count):
    rows, width = hidden.shape
    tables = [
        jnp.stack([cos, jnp.ones_like(cos)]),
        jnp.stack([sin, jnp.zeros_like(sin)]),
    ]
    table_spec = pl.BlockSpec((1, rows, HD), lambda p: (p // plain, 0, 0))
    return pl.pallas_call(
        project_kernel,
        out_shape=jax.ShapeDtypeStruct((rows, count * cols), BF),
        grid=(count,),
        in_specs=[
            pl.BlockSpec((rows, width), lambda p: (0, 0)),
            pl.BlockSpec((width, cols), lambda p: (0, p)),
            table_spec,
            table_spec,
        ],
        out_specs=pl.BlockSpec((rows, cols), lambda p: (0, p)),
        compiler_params=pltpu.CompilerParams(vmem_limit_bytes=VMEM_LIMIT),
        name="project",
    )(hidden, weight, *tables)


def head_cols(index):
    return pl.ds(pl.multiple_of(index * HD, HD), HD)


def scores_of(place, queries, keys, segq, idxq, segk, idxk):
    slots = dot(place, queries, 1, 0).astype(BF)
    scores = dot(slots, keys, 1, 1) * (HD**-0.5)
    allowed = (segq == segk) & (idxk <= idxq)
    scores = jnp.where(allowed, scores, MASKED)
    top = jnp.max(scores, axis=-1, keepdims=True)
    exps = jnp.exp(scores - top)
    total = jnp.sum(exps, axis=-1, keepdims=True)
    return slots, exps, 1.0 / total


def attend_kernel(
    ctx_count,
    moves,
    first_moves,
    names_in,
    names_out,
    heads,
    qkv_ref,
    place_ref,
    segq_ref,
    idxq_ref,
    gate_ref,
    segk_ref,
    idxk_ref,
    *refs,
):
    experts, _, rows = place_ref.shape
    given, refs = refs[: len(names_in)], refs[len(names_in) :]
    mixed_ref, kv_ref = refs[:2]
    made, (send, recv) = refs[2:-2], refs[-2:]
    arrays = {"qkv": qkv_ref, "kv": kv_ref, **dict(zip(names_in, given)), **dict(zip(names_out, made))}
    greet(ctx_count, masks_of(moves))
    run = Moves(ctx_count, moves, arrays, send, recv)
    run.begin(first_moves)
    kv_ref[:rows] = qkv_ref[:, experts * heads * HD :]
    run.settle(first_moves)
    run.begin()

    def step(i, carry):
        h, e = i // experts, i % experts
        cols = head_cols(e * heads + h)
        place = place_ref[e]
        _, exps, inv = scores_of(
            place,
            qkv_ref[:, cols],
            kv_ref[:, head_cols(h)],
            segq_ref[e],
            idxq_ref[e],
            segk_ref[...],
            idxk_ref[...],
        )
        attn = dot(exps.astype(BF), kv_ref[:, head_cols(heads + h)], 1, 0) * inv
        mixed = (attn * gate_ref[e]).astype(BF)
        mixed_ref[:, cols] = dot(place, mixed, 0, 0).astype(BF)
        return carry

    lax.fori_loop(0, heads * experts, step, 0)
    run.finish()


def attend(number, ctx_count, heads, moves, given, made, qkv, place, *slots_and_keys):
    experts, _, rows = place.shape
    wide = heads * HD
    kv_moves = []
    order = [0]
    bits = range(bits_of(ctx_count))[::-1]
    for bit in bits:
        for at in range(len(order)):
            target = ("kv", ((at + len(order)) * rows, rows), None)
            if at:
                source = ("kv", (at * rows, rows), None)
                kv_moves.append((source, target, 1 << bit, (source,)))
            else:
                source = ("qkv", (0, rows), (experts * wide, 2 * wide))
                kv_moves.append((source, target, 1 << bit, ()))
        order = order + order
    names_in = [n for n in given if n not in made] + [n for n in given if n in made]
    names_out = list(made)
    any_spec = pl.BlockSpec(memory_space=pl.ANY)
    full = pl.BlockSpec(memory_space=pltpu.VMEM)
    moves = kv_moves + moves
    before = 2 + len(slots_and_keys)
    mixed, kv, *rest = pl.pallas_call(
        functools.partial(
            attend_kernel,
            ctx_count,
            moves,
            len(kv_moves),
            [n if n not in made else "old_" + n for n in names_in],
            names_out,
            heads,
        ),
        out_shape=[
            jax.ShapeDtypeStruct((rows, experts * wide), BF),
            jax.ShapeDtypeStruct((ctx_count * rows, 2 * wide), BF),
        ]
        + [jax.ShapeDtypeStruct(shape, BF) for shape in made.values()],
        in_specs=[full] * before + [any_spec] * len(names_in),
        out_specs=[full] * 2 + [any_spec] * len(names_out),
        input_output_aliases={
            before + names_in.index(n): 2 + names_out.index(n) for n in names_out if n in given
        },
        scratch_shapes=[pltpu.SemaphoreType.DMA((len(moves),))] * 2,
        compiler_params=pltpu.CompilerParams(
            collective_id=number, has_side_effects=True, vmem_limit_bytes=VMEM_LIMIT
        ),
        name="attend",
    )(qkv, place, *slots_and_keys, *[given[n] for n in names_in])
    return mixed, kv, dict(zip(names_out, rest))


def attend_back_kernel(
    ctx_count,
    moves,
    names_in,
    names_out,
    heads,
    qkv_ref,
    kv_ref,
    place_ref,
    segq_ref,
    idxq_ref,
    segk_ref,
    idxk_ref,
    grad_ref,
    cos_ref,
    sin_ref,
    *refs,
):
    experts, _, rows = place_ref.shape
    keys = kv_ref.shape[0]
    given, refs = refs[: len(names_in)], refs[len(names_in) :]
    out_ref = refs[0]
    made, (dk_acc, dv_acc, total, got, send, recv, pass_send, pass_recv) = refs[1:-8], refs[-8:]
    arrays = {**dict(zip(names_in, given)), **dict(zip(names_out, made))}
    bits = range(bits_of(ctx_count))
    greet(ctx_count, sorted({*masks_of(moves), *[1 << b for b in bits]}))
    run = Moves(ctx_count, moves, arrays, send, recv)
    run.begin()

    def head_copy(h, bit):
        size = keys >> (bit + 1)
        i = h * len(bits) + bit
        return pltpu.make_async_remote_copy(
            src_ref=total.at[h, pl.ds(size, size)],
            dst_ref=got.at[h, pl.ds(size, size)],
            send_sem=pass_send.at[i],
            recv_sem=pass_recv.at[i],
            device_id=peer(ctx_count, 1 << bit),
            device_id_type=pl.DeviceIdType.MESH,
        )

    def head_sum(h, bit):
        size = keys >> (bit + 1)
        head_copy(h, bit).wait_recv()
        mine = total[h, :size].astype(F32) + got[h, size : 2 * size].astype(F32)
        mine = mine.astype(BF)
        if bit + 1 < len(bits):
            total[h, :size] = mine
            head_copy(h, bit + 1).start()
        else:
            at = experts * heads * HD
            out_ref[:, at + h * HD : at + (h + 1) * HD] = mine[:, :HD]
            at += heads * HD
            out_ref[:, at + h * HD : at + (h + 1) * HD] = mine[:, HD:]

    for h in range(heads):
        dk_acc[...] = jnp.zeros_like(dk_acc)
        dv_acc[...] = jnp.zeros_like(dv_acc)

        def step(e, carry, h=h):
            cols = head_cols(e * heads + h)
            place = place_ref[e]
            k, v = kv_ref[:, h * HD : (h + 1) * HD], kv_ref[:, (heads + h) * HD : (heads + h + 1) * HD]
            slots, exps, inv = scores_of(
                place, qkv_ref[:, cols], k, segq_ref[e], idxq_ref[e], segk_ref[...], idxk_ref[...]
            )
            attn = dot(exps.astype(BF), v, 1, 0) * inv
            probs = exps * inv
            grad = dot(place, grad_ref[:, cols], 1, 0)
            delta = jnp.sum(grad * attn, axis=-1, keepdims=True)
            grad = grad.astype(BF)
            dv_acc[...] += dot(probs.astype(BF), grad, 0, 0)
            grad_probs = dot(grad, v, 1, 1)
            grad_scores = (probs * (grad_probs - delta)).astype(BF)
            dq = dot(grad_scores, k, 1, 0) * (HD**-0.5)
            dk_acc[...] += dot(grad_scores, slots, 0, 0) * (HD**-0.5)
            top = dq.astype(BF)
            low = (dq - top.astype(F32)).astype(BF)
            back = dot(place, top, 0, 0) + dot(place, low, 0, 0)
            out_ref[:, cols] = turn(back, cos_ref[:rows], -sin_ref[:rows]).astype(BF)
            return carry

        lax.fori_loop(0, experts, step, 0)
        total[h, :, :HD] = turn(dk_acc[...], cos_ref[...], -sin_ref[...]).astype(BF)
        total[h, :, HD:] = dv_acc[...].astype(BF)
        head_copy(h, 0).start()
        for bit in bits:
            if h - 1 - bit >= 0:
                head_sum(h - 1 - bit, bit)
    for h in range(heads, heads + len(bits)):
        for bit in bits:
            if 0 <= h - 1 - bit < heads:
                head_sum(h - 1 - bit, bit)
    for h in range(heads):
        for bit in bits:
            head_copy(h, bit).wait_send()
    run.finish()


def attend_back(number, ctx_count, heads, moves, given, made, qkv, kv, place, *others):
    rows, keys = qkv.shape[0], kv.shape[0]
    any_spec = pl.BlockSpec(memory_space=pl.ANY)
    full = pl.BlockSpec(memory_space=pltpu.VMEM)
    passes = heads * bits_of(ctx_count)
    out, *rest = pl.pallas_call(
        functools.partial(attend_back_kernel, ctx_count, moves, list(given), list(made), heads),
        out_shape=[jax.ShapeDtypeStruct(qkv.shape, BF)]
        + [jax.ShapeDtypeStruct(shape, BF) for shape in made.values()],
        in_specs=[full] * (3 + len(others)) + [any_spec] * len(given),
        out_specs=[full] + [any_spec] * len(made),
        scratch_shapes=[pltpu.VMEM((keys, HD), F32)] * 2
        + [pltpu.VMEM((heads, keys, 2 * HD), BF)] * 2
        + [pltpu.SemaphoreType.DMA((max(1, len(moves)),))] * 2
        + [pltpu.SemaphoreType.DMA((passes,))] * 2,
        compiler_params=pltpu.CompilerParams(
            collective_id=number, has_side_effects=True, vmem_limit_bytes=VMEM_LIMIT
        ),
        name="attend_back",
    )(qkv, kv, place, *others, *given.values())
    return out, dict(zip(made, rest))


def spread_kernel(experts, me_ref, *refs):
    blocks, (in_ref, down_ref) = refs[:experts], refs[experts:]
    units = down_ref.shape[2]
    for m in range(experts):

        @pl.when(me_ref[0] == m)
        def _():
            for e in range(experts):
                block = blocks[e ^ m]
                for c in range(2):
                    in_ref[:, e, c, :] = block[:, c * units : (c + 1) * units].astype(F32)
                down_ref[:, e, :] = block[:, 2 * units :].astype(F32)


def spread_grads(blocks, me, in_shape, down_shape):
    experts = len(blocks)
    step = min(32, in_shape[0])
    return pl.pallas_call(
        functools.partial(spread_kernel, experts),
        grid_spec=pltpu.PrefetchScalarGridSpec(
            num_scalar_prefetch=1,
            grid=(in_shape[0] // step,),
            in_specs=[pl.BlockSpec((step, blocks[0].shape[1]), lambda i, m: (i, 0))] * experts,
            out_specs=[
                pl.BlockSpec((step, *in_shape[1:]), lambda i, m: (i, 0, 0, 0)),
                pl.BlockSpec((step, *down_shape[1:]), lambda i, m: (i, 0, 0)),
            ],
        ),
        out_shape=[
            jax.ShapeDtypeStruct(in_shape, F32),
            jax.ShapeDtypeStruct(down_shape, F32),
        ],
        compiler_params=pltpu.CompilerParams(vmem_limit_bytes=VMEM_LIMIT),
        name="spread_grads",
    )(me.astype(jnp.int32).reshape(1), *blocks)


def places(routes, gates, experts, cap, room):
    rows = routes.shape[0]
    named = routes[:, :, None] == jnp.arange(experts, dtype=jnp.int32)[None, None, :]
    member = jnp.any(named, axis=1)
    gate = jnp.sum(jnp.where(named, gates[:, :, None], 0.0), axis=1)
    token = jnp.arange(rows, dtype=jnp.int32)
    earlier = (token[None, :] < token[:, None]).astype(BF)
    rank = dot(earlier, member.astype(BF), 1, 0).astype(jnp.int32)
    slot = jnp.where(member, rank, -1).T
    taken = slot[:, None, :] == jnp.arange(room, dtype=jnp.int32)[None, :, None]
    return taken, gate


def slot_sum(taken, values):
    return jnp.sum(jnp.where(taken, values, 0), axis=-1, keepdims=True)


def layer(
    counts,
    tokens,
    gain_attn,
    gain_mlp,
    w_kv,
    w_query,
    w_out_attn,
    w_in,
    w_down,
    segments,
    attn_routes,
    attn_gates,
    mlp_routes,
    mlp_gates,
    cotangent,
):
    fsdp_count, ctx_count, tp_count = counts
    group = fsdp_count * ctx_count
    me = lax.axis_index(GROUP)
    ctx_me = lax.axis_index("ctx")
    rows, width = tokens.shape[1:]
    cap = 9 * rows // 16
    room = -(-cap // 16) * 16
    part = width // group
    attn_experts = w_query.shape[1]
    experts = w_in.shape[1]
    share = group // experts
    expert_me = me // share
    hidden_units = w_down.shape[2]
    head_width = w_kv.shape[2]

    def piece(x, index, size=part, axis=1):
        return lax.dynamic_slice_in_dim(x, index * size, size, axis)

    def exchange(x, mask):
        return swap(x, mask, GROUP, group)

    def after(x, *events):
        return lax.optimization_barrier((x, *events))[0]

    def relative(x):
        return jnp.concatenate([piece(x, me ^ j) for j in range(group)], axis=1)

    high, second = group // 2, group // 4

    qkv_wide = (attn_experts + 2) * head_width
    attn_own = jnp.concatenate(
        [w_query.reshape(part, -1), w_kv.reshape(part, -1), w_out_attn.reshape(part, -1)], axis=1
    )
    attn_wide = attn_own.shape[1]
    gain_own = jnp.pad(
        jnp.concatenate([gain_attn, gain_mlp])[None, :], ((0, 15), (0, 0))
    )
    far_x, far_y = exchange(attn_own, high), exchange(attn_own, second)

    seg_row = segments[0]
    seq_total = seg_row.shape[0]
    ctx_bits = list(range(bits_of(ctx_count)))[::-1]
    key_order = [0]
    for bit in ctx_bits:
        key_order = key_order + [j | (1 << bit) for j in key_order]
    key_seg = jnp.concatenate([piece(seg_row, ctx_me ^ j, rows, 0) for j in key_order])
    key_idx = jnp.concatenate(
        [(ctx_me ^ j) * rows + jnp.arange(rows, dtype=jnp.int32) for j in key_order]
    )
    place_idx = jnp.arange(seq_total, dtype=jnp.int32)
    pos = jnp.sum(
        (seg_row[None, :] == key_seg[:, None]) & (place_idx[None, :] < key_idx[:, None]),
        axis=1,
        dtype=jnp.int32,
    ).astype(F32)
    frequency = ROPE_BASE ** (-(jnp.arange(HD // 2, dtype=F32) * 2.0) / HD)
    angles = pos[:, None] * frequency[None, :]
    cos_half, sin_half = jnp.cos(angles), jnp.sin(angles)
    cos = jnp.concatenate([cos_half, cos_half], axis=1)
    sin = jnp.concatenate([-sin_half, sin_half], axis=1)
    taken_attn, gate_attn = places(attn_routes[0], attn_gates[0], attn_experts, cap, room)
    place_attn = taken_attn.astype(BF)
    own_seg, own_idx = key_seg[:rows], key_idx[:rows]
    filled = jnp.any(taken_attn, axis=-1, keepdims=True)
    slot_seg = jnp.where(filled, slot_sum(taken_attn, own_seg), own_seg[0])
    slot_idx = jnp.where(filled, slot_sum(taken_attn, own_idx), own_idx[0])
    slot_gate = slot_sum(taken_attn, gate_attn.T[:, None, :])
    taken_mlp, gate_mlp = places(mlp_routes[0], mlp_gates[0], experts, cap, room)
    mine_first = [expert_me ^ k for k in range(experts)]
    place_mlp = jnp.concatenate([piece(taken_mlp, e, 1, 0) for e in mine_first]).astype(BF)
    inputs = relative(tokens[0]).astype(F32)
    grad_out = relative(cotangent[0])

    def expert_rows(k):
        in_rows = piece(w_in, expert_me ^ k, 1, 1).reshape(part, 2 * hidden_units)
        down_rows = piece(w_down, expert_me ^ k, 1, 1).reshape(part, hidden_units)
        return jnp.concatenate([in_rows, down_rows], axis=1)

    to_send = [expert_rows(k) for k in range(experts)]
    in_cols, down_cols = (0, 2 * hidden_units), (2 * hidden_units, hidden_units)
    weight_shapes = {"in": (width, 2 * hidden_units), "down": (width, hidden_units)}

    def weight_moves(k, first, size):
        moves = []
        for name, cols in (("in", in_cols), ("down", down_cols)):
            base = k * share * part + first
            source = (f"send{k}", (first, size), cols)
            landed = (name, (base, size), None)
            moves.append((source, landed, k * share, ()))
            for t in range(1, share):
                target = (name, (base + t * part, size), None)
                if k:
                    moves.append((landed, target, t, (landed,)))
                else:
                    moves.append((source, target, t, ()))
        return moves

    def many_weight_moves(cuts):
        return [m for cut in cuts for m in weight_moves(*cut)]

    near = [k for k in range(1, experts) if k & (k - 1) == 0]
    far = [k for k in range(1, experts) if k & (k - 1)]
    half_part = part // 2

    (attn_own, far_x, far_y, gain_own), to_send, tables = lax.optimization_barrier(
        (
            (attn_own, far_x, far_y, gain_own),
            to_send,
            (cos, sin, place_attn, slot_seg, slot_idx, slot_gate, place_mlp),
        )
    )
    cos, sin, place_attn, slot_seg, slot_idx, slot_gate, place_mlp = tables
    quarter = part // 4
    moves = []
    held = {0: [("own", 0, part, ())], high: [("far_x", 0, part, ())], second: [("far_y", 0, part, ())]}
    held[high | second] = []
    for i in (0, 2, 1, 3):
        source, mask = (("far_x", second), ("far_y", high))[i // 2]
        target = ("full", ((high | second) * part + i * quarter, quarter), None)
        moves.append(((source, (i * quarter, quarter), None), target, mask, ()))
        held[high | second].append(("full", i * quarter, quarter, (target,)))
    for j in (0, high, second):
        name = held[j][0][0]
        moves.append(((name, (0, part), None), ("full", (j * part, part), None), 0, ()))
    for j in range(group):
        moves.append((("gain_own", (0, 16), None), ("gains", (j * 16, 16), None), j, ()))
    moves += weight_moves(0, 0, part)
    for bit in range(bits_of(group) - 2)[::-1]:
        for j in list(held):
            there = []
            for name, at, size, needs in held[j]:
                source = (name, (at + j * part if name == "full" else at, size), None)
                target = ("full", ((j | 1 << bit) * part + at, size), None)
                moves.append((source, target, 1 << bit, needs))
                there.append(("full", at, size, (target,)))
            held[j | 1 << bit] = there
    made = move(
        "gather",
        1,
        ctx_count,
        moves,
        {"own": attn_own, "far_x": far_x, "far_y": far_y, "gain_own": gain_own, "send0": to_send[0]},
        {"full": (width, attn_wide), "gains": (16 * group, 2 * part), **weight_shapes},
    )
    attn_full, weights = made["full"], {n: made[n] for n in weight_shapes}
    gains = made["gains"].reshape(group, 16, 2 * part)[:, 0].astype(F32)
    gain_one, gain_two = gains[:, :part].reshape(1, width), gains[:, part:].reshape(1, width)
    qkv_full, out_full = attn_full[:, :qkv_wide], attn_full[:, qkv_wide:]
    normed_one, inverse_one, pre_one = normalize(inputs, gain_one)
    hidden_one = pre_one.astype(BF)
    qkv = project(hidden_one, attn_full, cos[:rows], sin[:rows], attn_experts + 1, head_width, attn_experts + 2)
    key_row = (key_seg[None, :], key_idx[None, :])
    heads = head_width // HD
    cuts = [(k, 0, half_part) for k in near]
    mixed, kv, weights = attend(
        2,
        ctx_count,
        heads,
        many_weight_moves(cuts),
        {**{f"send{k}": to_send[k] for k in near}, **weights},
        weight_shapes,
        qkv,
        place_attn,
        slot_seg,
        slot_idx,
        slot_gate,
        *key_row,
    )

    def turned(x, k):
        wide = share * part
        return jnp.concatenate(
            [x[:, (i ^ k) * wide : ((i ^ k) + 1) * wide] for i in range(experts)], axis=1
        )

    def pick(k, x):
        return dot(place_mlp[k], x, 1, 0).astype(BF)

    run = width // tp_count
    tp_me = lax.axis_index("tp")
    gate_high = gate_mlp.astype(BF)
    gate_low = (gate_mlp - gate_high.astype(F32)).astype(BF)
    gate_ride = jnp.pad(
        jnp.concatenate([gate_high, gate_low], axis=1), ((0, 0), (0, HD - 2 * experts))
    )
    grad_got = []
    for k in range(experts):
        sent = jnp.concatenate([piece(grad_out, tp_me ^ k, run), gate_ride], axis=1)
        slots = pick(k, sent)
        grad_got.append(exchange(slots, k * share) if k else slots)
    grad_got = jnp.concatenate(grad_got, axis=0)
    own_gate = jnp.tile(jnp.arange(experts) == expert_me, 2)
    slot_weight = jnp.sum(
        jnp.where(own_gate[None, :], grad_got[:, run : run + 2 * experts].astype(F32), 0.0),
        axis=1,
        keepdims=True,
    )
    grad_slots = lax.all_gather(grad_got[:, :run], "tp", axis=1, tiled=True)

    def send_weights(name, number, cuts, weights, slots=None):
        moves, given, made_shapes = [], {f"send{k}": to_send[k] for k, _, _ in cuts}, dict(weight_shapes)
        if slots is not None:
            made_shapes["slots"] = (experts * room, width)
            for k, x in enumerate(slots):
                given[f"slots{k}"] = x
                target = ("slots", (k * room, room), None)
                moves.append(((f"slots{k}", (0, room), None), target, k * share, ()))
        moves += many_weight_moves(cuts)
        made = move(name, number, ctx_count, moves, {**given, **weights}, made_shapes)
        return {n: made[n] for n in weight_shapes}, made.get("slots")

    branch = dot(mixed, out_full, 1, 1).astype(BF)
    branch_sum = lax.psum(branch, "tp")
    cuts = [(k, half_part, part - half_part) for k in near] + [(k, 0, half_part) for k in far]
    to_send, weights, _ = lax.optimization_barrier((to_send, weights, branch))
    weights, _ = send_weights("weights_two", 3, cuts, weights)
    resid = inputs + branch_sum.astype(F32)
    normed_two, inverse_two, pre_two = normalize(resid, gain_two)
    hidden_two = pre_two.astype(BF)
    slots = [pick(0, hidden_two)] + [turned(pick(k, hidden_two), k) for k in range(1, experts)]
    cuts = [(k, half_part, part - half_part) for k in far]
    weights, two_slots = send_weights("dispatch", 4, cuts, weights, slots)
    in_full, down_full = weights["in"], weights["down"]

    def send_back(x):
        slots = x.reshape(experts, room, width)
        return [slots[0]] + [exchange(slots[k], k * share) for k in range(1, experts)]

    def gathered_rows(got):
        got = [got[0]] + [turned(got[k], k) for k in range(1, experts)]
        return jnp.einsum(
            "kct,kcd->td", place_mlp, jnp.stack(got), preferred_element_type=F32
        ).astype(BF)

    gate_up = dot(two_slots, in_full, 1, 0)
    gate_part, up_part = gate_up[:, :hidden_units], gate_up[:, hidden_units:]
    sigmoid_gate = jax.nn.sigmoid(gate_part)
    silu_gate = gate_part * sigmoid_gate
    active = (silu_gate * up_part * slot_weight).astype(BF)
    mlp_slots = dot(active, down_full, 1, 1).astype(BF)
    mlp_back = send_back(mlp_slots)
    grad_active = dot(after(grad_slots, mlp_slots), down_full, 1, 0)
    scaled = grad_active * slot_weight
    grad_gate = scaled * up_part * sigmoid_gate * (1.0 + gate_part * (1.0 - sigmoid_gate))
    grad_up = scaled * silu_gate
    grad_gu = jnp.concatenate([grad_gate, grad_up], axis=1).astype(BF)
    back_two_slots = dot(grad_gu, in_full, 1, 1).astype(BF)
    two_back = send_back(after(back_two_slots, *mlp_back))

    def for_share(x, t):
        return jnp.concatenate(
            [x[:, (k * share + t) * part : (k * share + t + 1) * part] for k in range(experts)],
            axis=1,
        )

    def every_share(x, cut):
        got = [for_share(x, 0) if cut else x]
        for t in range(1, share):
            got.append(exchange(for_share(x, t) if cut else x, t))
        return jnp.concatenate(got, axis=0)

    grad_gu_late = after(grad_gu, back_two_slots)
    grad_in_w = dot(every_share(two_slots, True), every_share(grad_gu_late, False), 0, 0)
    grad_down_w = dot(every_share(grad_slots, True), every_share(active, False), 0, 0)
    expert_grads = jnp.concatenate([grad_in_w.astype(BF), grad_down_w.astype(BF)], axis=1)
    two_back = after(two_back, expert_grads)
    back_two = lax.psum(gathered_rows(two_back), "tp").astype(F32)
    grads_got = {0: expert_grads[:part]}

    def grad_moves(ks):
        return [
            (("grads", (k * part, part), None), (f"got{k}", (0, part), None), k * share, ())
            for k in ks
        ], {f"got{k}": (part, expert_grads.shape[1]) for k in ks}

    moves, made_shapes = grad_moves(near)
    made = move("grads_near", 5, ctx_count, moves, {"grads": expert_grads}, made_shapes)
    grads_got.update({k: made[f"got{k}"] for k in near})
    grads_near = [grads_got[k] for k in near]

    grad_resid_norm, gain_two_grad = norm_back(back_two, normed_two, inverse_two, gain_two)
    grad_resid = grad_out.astype(F32) + grad_resid_norm
    grad_branch = grad_resid.astype(BF)
    grad_mixed = dot(after(grad_branch, *grads_near), out_full, 1, 0)
    gate_wide = jnp.repeat(gate_attn, head_width, axis=1)
    grad_attn = (grad_mixed * gate_wide).astype(BF)
    moves, made_shapes = grad_moves(far)
    grad_qkv, made = attend_back(
        6,
        ctx_count,
        heads,
        moves,
        {"grads": expert_grads},
        made_shapes,
        qkv,
        kv,
        place_attn,
        slot_seg,
        slot_idx,
        *key_row,
        grad_attn,
        cos,
        sin,
    )
    grads_got.update({k: made[f"got{k}"] for k in far})
    mlp_total = lax.psum(gathered_rows(after(mlp_back, grad_attn)), "tp").astype(F32)
    back_one_part = dot(grad_qkv, qkv_full, 1, 1)
    back_one = lax.psum(back_one_part.astype(BF), "tp").astype(F32)
    grad_input_norm, gain_one_grad = norm_back(back_one, normed_one, inverse_one, gain_one)
    grad_tokens = relative((grad_resid + grad_input_norm).astype(BF))

    output = relative((resid + mlp_total).astype(BF))

    def both(x):
        return jnp.concatenate([x, exchange(x, 1)], axis=0)

    def both_cut(x):
        sides = [
            jnp.concatenate([x[:, j * part : (j + 1) * part] for j in range(side, group, 2)], axis=1)
            for side in range(2)
        ]
        return jnp.concatenate([sides[0], exchange(sides[1], 1)], axis=0)

    def reduced(x, bits, kind=BF):
        axes = sorted(bits)[::-1]
        x = x.reshape((2,) * len(bits) + (-1, x.shape[1]))
        for bit in bits:
            at = axes.index(bit)
            keep = lax.index_in_dim(x, 0, at, False).astype(F32)
            got = exchange(lax.index_in_dim(x, 1, at, False), 1 << bit).astype(F32)
            axes.remove(bit)
            x = keep + got
            if axes:
                x = x.astype(kind)
        return x

    upper = list(range(1, bits_of(group)))

    grad_outw = dot(both_cut(grad_branch), both(mixed), 0, 0).astype(BF)
    grad_qkvw = dot(both_cut(hidden_one), both(grad_qkv), 0, 0).astype(BF)
    grad_attnw = jnp.concatenate([grad_qkvw, grad_outw], axis=1)
    grad_attnw = reduce_grads(7, ctx_count, upper, part, grad_attnw)

    def planes(first, count):
        cut = grad_attnw[:, first * head_width : (first + count) * head_width]
        return cut.reshape(part, count, head_width)

    def gain_sum(x):
        return reduced(x.reshape(width, 1), [0] + upper, F32).reshape(part)

    return (
        output[None],
        grad_tokens[None],
        gain_sum(gain_one_grad),
        gain_sum(gain_two_grad),
        planes(attn_experts, 2),
        planes(0, attn_experts),
        planes(attn_experts + 2, attn_experts),
        *spread_grads([grads_got[k] for k in range(experts)], expert_me, w_in.shape, w_down.shape),
    )


def solution(mesh):
    rows = P("fsdp", "ctx", None)
    weight = P(GROUP, None, "tp")
    weight_in = P(GROUP, None, None, "tp")
    return jax.shard_map(
        functools.partial(layer, tuple(mesh.shape[a] for a in ("fsdp", "ctx", "tp"))),
        mesh=mesh,
        in_specs=(
            rows,
            P(GROUP),
            P(GROUP),
            weight,
            weight,
            weight,
            weight_in,
            weight,
            P("fsdp", None),
            rows,
            rows,
            rows,
            rows,
            rows,
        ),
        out_specs=(rows, rows, P(GROUP), P(GROUP), weight, weight, weight, weight_in, weight),
        check_vma=False,
    )
```

time: 921 us -> 741 us (0.80)
  Pallas kernels: 57.2 us -> 430 us
  waiting for transfers between devices: 363 us -> 37.3 us
  blocking collectives: 123 us -> 0 us
  local copies, waits for them, and re-layouts: 150 us -> 76.3 us
  starting transfers between devices: 41.8 us -> 21.9 us
  other arithmetic: 66.6 us -> 54.5 us
    pallas_call x2 -> x8, Pallas kernels: 47.3 us -> 420 us  [the longest x4 196 us: move(): pl.pallas_call(functools.partial(move_kernel, ctx_count, moves, plain + [...]
    ppermute x45 -> x25, waiting for transfers between devices: 273 us -> 37.2 us  [swap(): return lax.ppermute(x, axes, [(i, i ^ mask) for i in range(count)])]
    psum x1 -> x0, blocking collectives: 92.7 us -> none  [layer(): gain_grads = lax.psum(jnp.stack([gain_one_grad, gain_two_grad]), GROUP)]
    psum x3, waiting for transfers between devices: 75.8 us -> 0.02 us  [the longest x1 0.02 us: layer(): branch_sum = lax.psum(branch, 'tp')]
    unnamed x204 -> x187, local copies, waits for them, and re-layouts: 66.9 us -> 26.2 us
    all_gather x1 -> x0, blocking collectives: 29.9 us -> none  [layer(): lax.all_gather(jnp.stack([gain_attn, gain_mlp]), GROUP, axis=1, tiled=True)]
    dot_general x7 -> x2, matrix products: 25.9 us -> 3.95 us  [gathered_rows(): jnp.einsum('kct,kcd->td', place_mlp, jnp.stack(got), preferred_element_ty...]
    dot_general x10 -> x21, matrix products: 69.4 us -> 90.5 us  [dot(): lax.dot_general(a, b, (((ca,), (cb,)), ((), ())), preferred_element_type=...]
  transfers between devices with their start and end apart: 50 -> 29, of which waited for: 17 -> 8; matrix products, arithmetic and copies ran while one was open for 33% -> 23% of each run, Pallas kernels for 6% -> 46%
where the time goes in v2:
time: 741 us; the launch traced here: 730 us
  Pallas kernels  430 us (58%)
  matrix products  94.4 us (13%)
  local copies, waits for them, and re-layouts  76.3 us (10%)
  other arithmetic  54.5 us (7%)
  waiting for transfers between devices  37.3 us (5%)
  starting transfers between devices  21.9 us (3%)
  between operations  15.7 us (2%)
    pallas_call x4, Pallas kernels, move(): pl.pallas_call(functools.partial(move_kernel, ctx_count, moves, plain + [...  196 us
    pallas_call x1, Pallas kernels, reduce_grads(): pl.pallas_call(functools.partial(reduce_kernel, ctx_count, bits, part, pi...  93 us
    dot_general x21, matrix products, dot(): lax.dot_general(a, b, (((ca,), (cb,)), ((), ())), preferred_element_type=...  90.5 us
    pallas_call x1, Pallas kernels, attend_back(): pl.pallas_call(functools.partial(attend_back_kernel, ctx_count, moves, li...  70.9 us
    pallas_call x1, Pallas kernels, attend(): pl.pallas_call(functools.partial(attend_kernel, ctx_count, moves, len(kv_...  48.4 us
    ppermute x25, waiting for transfers between devices, swap(): return lax.ppermute(x, axes, [(i, i ^ mask) for i in range(count)])  37.2 us
    unnamed x187, local copies, waits for them, and re-layouts  26.2 us
    ppermute x25, starting transfers between devices, swap(): return lax.ppermute(x, axes, [(i, i ^ mask) for i in range(count)])  21.8 us
  transfers between devices with their start and end apart: 29, of which 8 were waited for; matrix products, arithmetic and copies ran while one was open for 23% of the time, Pallas kernels for 46%

profile of v2, /device:TPU:0, one launch (start us, length us, event | category | flops | bytes accessed | tf_op | source)
XLA Modules:
  0.0 730.2 jit_solution(15258340554523963140)
XLA Ops:
  7.2 1.6 copy.105
  12.1 2.9 collective-permute-start
  16.7 7.3 %constant_dynamic-slice_fusion.13 = (bf16[256,1,1408]{2,1,0:T(2,128)(2,1)}, bf16[256,1,1408]{2,1,0:T(2,128)(2,1)}, bf16[256,1,1408]{2,1,0:T(2,128)(2,1)}, bf16[256,1,1408]{2,1,0:T(2,128)(2,1)}) fusion(bf16[256,4,1408]{2,1,0:T(4,128)(2,1)S(1)} %copy-done.3, s32[]{:T(128)S(6)} %select_n.169, s32[]{:T(128)S(6)} %select_n.168, s32[]{:T(128)S(6)} %select_n.167, ...), kind=kLoop, calls=%fused_computation.259 | loop fusion | bytes 5767184 | tf_op jit(solution)/shard_map/dynamic_slice | solution.py:636
  24.1 5.6 constant_dynamic-slice_fusion.14
  39.4 3.1 fusion.125
  51.1 3.2 copy_bitcast_fusion.2
  68.8 3.4 collective-permute-done.refs_1_
  73.7 35.4 %gather.1 = (bf16[2048,5120]{1,0:T(8,128)(2,1)}, bf16[128,512]{1,0:T(8,128)(2,1)}, bf16[2048,2816]{1,0:T(8,128)(2,1)}, bf16[2048,1408]{1,0:T(8,128)(2,1)}) custom-call(bf16[256,5120]{1,0:T(8,128)(2,1)} %constant_dynamic-update-slice_fusion.refs_0_, bf16[256,5120]{1,0:T(8,128)(2,1)} %collective-permute-done.refs_1_, ...), custom_call_target="tpu_custom_call" | custom-call | tf_op jit(solution)/shard_map/gather/pallas_call | solution.py:172
  116.4 9.9 %project.1.qkv_ref = bf16[256,3072]{1,0:T(8,128)(2,1)} custom-call(bf16[256,2048]{1,0:T(8,128)(2,1)} %fusion.82.h_ref, bf16[2048,5120]{1,0:T(8,128)(2,1)} %get-tuple-element.66.w_ref, f32[2,256,128]{2,1,0:T(8,128)} %stack.43.cos_ref, f32[2,256,128]{2,1,0:T(8,128)} %stack.45.sin_ref), custom_call_target="tpu_custom_call" | custom-call | tf_op jit(solution)/shard_map/project/pallas_call | solution.py:295
  126.3 48.4 %attend.1 = (bf16[256,2048]{1,0:T(8,128)(2,1)}, bf16[1024,1024]{1,0:T(8,128)(2,1)}, bf16[2048,2816]{1,0:T(8,128)(2,1)}, bf16[2048,1408]{1,0:T(8,128)(2,1)}) custom-call(bf16[256,3072]{1,0:T(8,128)(2,1)} %project.1.qkv_ref, bf16[4,144,256]{2,1,0:T(8,128)(2,1)} %get-tuple-element.69.place_ref, ...), custom_call_target="tpu_custom_call", output_to_operand_aliasing={{2}: (9, {}), {3}: (10, {})} | custom-call | tf_op jit(solution)/shard_map/attend/pallas_call | solution.py:398
  174.7 7.1 fusion.33
  185.7 1.5 collective-permute-start.4
  187.3 56.6 %weights_two.1 = (bf16[2048,2816]{1,0:T(8,128)(2,1)}, bf16[2048,1408]{1,0:T(8,128)(2,1)}) custom-call(bf16[256,4224]{1,0:T(8,128)(2,1)} %pad_maximum_fusion.4.refs_0_, bf16[256,4224]{1,0:T(8,128)(2,1)} %pad_maximum_fusion.5.refs_1_, bf16[256,4224]{1,0:T(8,128)(2,1)} %pad_maximum_fusion.6.refs_2_.refs_0_, ...), custom_call_target="tpu_custom_call", output_to_operand_aliasing={{0}: (4, {}), {1}: (3, {})} | custom-call | tf_op jit(solution)/shard_map/weights_two/pallas_call | solution.py:172
  245.3 1.7 multiply_reduce_fusion
  252.4 54.4 %dispatch.1 = (bf16[2048,2816]{1,0:T(8,128)(2,1)}, bf16[2048,1408]{1,0:T(8,128)(2,1)}, bf16[576,2048]{1,0:T(8,128)(2,1)}) custom-call(bf16[256,4224]{1,0:T(8,128)(2,1)} %pad_maximum_fusion.6.refs_2_.refs_0_, bf16[144,2048]{1,0:T(8,128)(2,1)} %convolution_convert_fusion.8.refs_1_, ...), custom_call_target="tpu_custom_call", output_to_operand_aliasing={{0}: (5, {}), {1}: (6, {})} | custom-call | tf_op jit(solution)/shard_map/dispatch/pallas_call | solution.py:172
  306.9 11.0 %fusion.189 = f32[576,2816]{1,0:T(8,128)S(1)} fusion(bf16[576,2048]{1,0:T(8,128)(2,1)} %get-tuple-element.89, bf16[2048,2816]{1,0:T(8,128)(2,1)} %get-tuple-element.90), kind=kOutput, calls=%fused_computation.345 | convolution fusion | flops 6643777536 | bytes 20381696 | tf_op jit(solution)/shard_map/dot_general | solution.py:33
  318.8 2.4 copy-done.10
  323.5 5.1 convolution_convert_fusion.4
  328.6 9.8 %multiply_convert_fusion.1 = (bf16[576,1408]{1,0:T(8,128)(2,1)S(1)}, bf16[576,1408]{1,0:T(8,128)(2,1)S(1)}) fusion(f32[576,2816]{1,0:T(8,128)} %copy-done.10, f32[576]{0:T(1024)S(1)} %select_reduce_fusion.3, bf16[576,2048]{1,0:T(8,128)(2,1)} %all-gather.2.cloned.1.call-done, bf16[2048,1408]{1,0:T(8,128)(2,1)} %get-tuple-element.91), kind=kOutput, calls=%fused_computation.27 | convolution fusion | flops 3333242880 | bytes 17860864 | tf_op jit(solution)/shard_map/dot_general | solution.py:33
  338.6 10.1 %convolution_convert_fusion.3 = bf16[576,2048]{1,0:T(8,128)(2,1)S(1)} fusion(bf16[2048,2816]{1,0:T(8,128)(2,1)} %get-tuple-element.90, bf16[576,1408]{1,0:T(8,128)(2,1)S(1)} %get-tuple-element.122, bf16[576,1408]{1,0:T(8,128)(2,1)S(1)} %get-tuple-element.121), kind=kOutput, calls=%fused_computation.41 | convolution fusion | flops 6651445248 | bytes 17137664 | tf_op jit(solution)/shard_map/dot_general | solution.py:33
  353.4 12.2 %collective-permute-done.5 = bf16[144,2048]{1,0:T(8,128)(2,1)S(1)} collective-permute-done((bf16[144,2048]{1,0:T(8,128)(2,1)S(1)}, bf16[144,2048]{1,0:T(8,128)(2,1)S(1)}, u32[]{:S(2)}, u32[]{:S(2)}) %collective-permute-start.5) | collective-permute-done | bytes 589856 | tf_op jit(solution)/shard_map/ppermute | solution.py:41
  368.3 12.7 %collective-permute-done.7 = bf16[144,2048]{1,0:T(8,128)(2,1)S(1)} collective-permute-done((bf16[144,2048]{1,0:T(8,128)(2,1)S(1)}, bf16[144,2048]{1,0:T(8,128)(2,1)S(1)}, u32[]{:S(2)}, u32[]{:S(2)}) %collective-permute-start.7) | collective-permute-done | bytes 589856 | tf_op jit(solution)/shard_map/ppermute | solution.py:41
  385.7 4.3 convolution_convert_fusion.2
  392.1 13.2 %fusion.10 = bf16[1024,2816]{1,0:T(8,128)(2,1)S(1)} fusion(bf16[576,2816]{1,0:T(8,128)(2,1)} %copy-done.70, bf16[576,2816]{1,0:T(8,128)(2,1)S(1)} %pad_maximum_fusion.2, bf16[576,1024]{1,0:T(8,128)(2,1)} %copy-done.72, bf16[576,256]{1,0:T(8,128)(2,1)S(1)} %get-tuple-element.138, bf16[576,256]{1,0:T(8,128)(2,1)} %get-tuple-element.139, ...), kind=kOutput, calls=%fused_computation.15 | convolution fusion | flops 6671433728 | bytes 14614528 | tf_op jit(solution)/shard_map/dot_general | solution.py:33
  405.4 4.6 pad_maximum_fusion.refs_0_
  410.8 2.0 fusion.31
  415.0 2.2 copy.114
  419.4 49.3 %grads_near.1 = (bf16[256,4224]{1,0:T(8,128)(2,1)}, bf16[256,4224]{1,0:T(8,128)(2,1)}) custom-call(bf16[1024,4224]{1,0:T(8,128)(2,1)} %pad_maximum_fusion.refs_0_), custom_call_target="tpu_custom_call" | custom-call | tf_op jit(solution)/shard_map/grads_near/pallas_call | solution.py:172
  468.7 2.9 fusion.74.refs_0_
  471.5 2.2 fusion.81
  475.7 6.7 fusion.28.grad_ref
  482.5 70.9 %attend_back.1 = (bf16[256,3072]{1,0:T(8,128)(2,1)}, bf16[256,4224]{1,0:T(8,128)(2,1)}) custom-call(bf16[256,3072]{1,0:T(8,128)(2,1)} %project.1.qkv_ref, bf16[1024,1024]{1,0:T(8,128)(2,1)} %get-tuple-element.106.kv_ref, bf16[4,144,256]{2,1,0:T(8,128)(2,1)} %get-tuple-element.69.place_ref, s32[4,144,1]{2,1,0:T(8,128)} %copy.91.segq_ref, ...), custom_call_target="tpu_custom_call" | custom-call | tf_op jit(solution)/shard_map/attend_back/pallas_call | solution.py:531
  553.4 9.5 %fusion.36 = bf16[256,2048]{1,0:T(8,128)(2,1)} fusion(bf16[256,3072]{1,0:T(8,128)(2,1)} %get-tuple-element.107, bf16[2048,5120]{1,0:T(8,128)(2,1)} %get-tuple-element.66.w_ref), kind=kOutput, calls=%fused_computation.53 | convolution fusion | flops 3221749760 | bytes 15204352 | tf_op jit(solution)/shard_map/dot_general | solution.py:33
  566.5 2.9 collective-permute-done.19
  570.1 2.0 fusion.32
  572.1 12.0 %spread_grads.1 = (f32[256,4,2,1408]{3,2,1,0:T(2,128)}, f32[256,4,1408]{2,1,0:T(4,128)}) custom-call(s32[1]{0:T(128)} %bitcast.72.me_ref, bf16[256,4224]{1,0:T(8,128)(2,1)} %fusion.74.refs_0_, bf16[256,4224]{1,0:T(8,128)(2,1)} %get-tuple-element.99.refs_1_, bf16[256,4224]{1,0:T(8,128)(2,1)} %get-tuple-element.100.refs_2_, ...), custom_call_target="tpu_custom_call" | custom-call | tf_op jit(solution)/shard_map/spread_grads/pallas_call | solution.py:566
  584.8 4.2 convolution_convert_fusion.1
  589.1 5.0 convolution_convert_fusion
  594.2 7.9 %pad_maximum_fusion.1.grad_ref = bf16[1024,5120]{1,0:T(8,128)(2,1)} fusion(bf16[1024,2048]{1,0:T(8,128)(2,1)S(1)} %convolution_convert_fusion.1, bf16[1024,3072]{1,0:T(8,128)(2,1)S(1)} %convolution_convert_fusion), kind=kLoop, calls=%fused_computation.4 | loop fusion | flops 20971520 | bytes 20971520 | tf_op jit(solution)/shard_map/concatenate | solution.py:960
  602.0 93.0 %reduce_grads.1 = f32[256,5120]{1,0:T(8,128)} custom-call(bf16[1024,5120]{1,0:T(8,128)(2,1)} %pad_maximum_fusion.1.grad_ref), custom_call_target="tpu_custom_call" | custom-call | tf_op jit(solution)/shard_map/reduce_grads/pallas_call | solution.py:267
  695.0 4.7 fusion.173
  699.8 3.6 reshape.214
  703.4 4.0 reshape.215
  707.4 1.9 reshape.213
  709.2 2.1 fusion.84
  711.5 3.5 fusion.77
  717.1 2.2 collective-permute-done.16
  720.7 2.1 collective-permute-done.17
  (357 shorter events, 89.6 us)
Async XLA Ops:
  7.2 238.1 %all-reduce.9.cloned.1.call-start = ((), (), s32[]{:S(2)}) async-start(), calls=%async_computation | async-start | bytes 2097152 | tf_op jit(solution)/shard_map/psum | solution.py:832
  12.1 60.1 %collective-permute-start = (bf16[256,5120]{1,0:T(8,128)(2,1)}, bf16[256,5120]{1,0:T(8,128)(2,1)}, u32[]{:S(2)}, u32[]{:S(2)}) collective-permute-start(bf16[256,5120]{1,0:T(8,128)(2,1)} %constant_dynamic-update-slice_fusion.refs_0_), channel_id=1, source_target_pairs={{0,16},{4,20},{8,24},{12,28},{16,0},{20,4},{24,8},{28,12},{1,17},{... | collective-permute-start | bytes 7864328 | tf_op jit(solution)/shard_map/ppermute | solution.py:41
  15.1 58.6 %collective-permute-start.1 = (bf16[256,5120]{1,0:T(8,128)(2,1)}, bf16[256,5120]{1,0:T(8,128)(2,1)}, u32[]{:S(2)}, u32[]{:S(2)}) collective-permute-start(bf16[256,5120]{1,0:T(8,128)(2,1)} %constant_dynamic-update-slice_fusion.refs_0_), channel_id=1, source_target_pairs={{0,8},{4,12},{8,0},{12,4},{16,24},{20,28},{24,16},{28,20},{1,9},{5... | collective-permute-start | bytes 7864328 | tf_op jit(solution)/shard_map/ppermute | solution.py:41
  34.9 8.6 %copy-start.65 = (f32[1,256,2]{1,2,0:T(2,128)S(1)}, f32[1,256,2]{1,2,0:T(2,128)}, u32[]{:S(2)}) copy-start(f32[1,256,2]{1,2,0:T(2,128)} %param.24) | copy-start | bytes 6148
  34.9 9.5 %copy-start.68 = (bf16[256]{0:T(256)(128)(2,1)S(1)}, bf16[256]{0:T(256)(128)(2,1)}, u32[]{:S(2)}) copy-start(bf16[256]{0:T(256)(128)(2,1)} %param.16) | copy-start | bytes 1540
  34.9 9.5 %copy-start.69 = (bf16[256]{0:T(256)(128)(2,1)S(1)}, bf16[256]{0:T(256)(128)(2,1)}, u32[]{:S(2)}) copy-start(bf16[256]{0:T(256)(128)(2,1)} %param.15) | copy-start | bytes 1540
  34.9 9.5 %copy-start.27 = (bf16[1,256,2048]{2,1,0:T(8,128)(2,1)S(1)}, bf16[1,256,2048]{2,1,0:T(8,128)(2,1)}, u32[]{:S(2)}) copy-start(bf16[1,256,2048]{2,1,0:T(8,128)(2,1)} %param.14) | copy-start | bytes 3145732
  49.4 424.4 %copy-start.6 = (bf16[256,2048]{1,0:T(8,128)(2,1)}, bf16[256,2048]{1,0:T(8,128)(2,1)S(1)}, u32[]{:S(2)}) copy-start(bf16[256,2048]{1,0:T(8,128)(2,1)S(1)} %bitcast_dynamic-update-slice_fusion) | copy-start | bytes 3145732
  60.4 50.5 %copy-start.20 = (f32[1024,128]{1,0:T(8,128)}, f32[1024,128]{1,0:T(8,128)S(1)}, u32[]{:S(2)}) copy-start(f32[1024,128]{1,0:T(8,128)S(1)} %pad_maximum_fusion.16.sin_ref) | copy-start | bytes 1572868
  73.7 39.1 %copy-start.55 = (f32[4,144]{1,0:T(4,128)S(1)}, f32[4,144]{1,0:T(4,128)}, u32[]{:S(2)}) copy-start(f32[4,144]{1,0:T(4,128)} %select_reduce_fusion) | copy-start | bytes 6916
  73.7 39.9 %copy-start.60 = (f32[256]{0:T(256)S(1)}, f32[256]{0:T(256)}, u32[]{:S(2)}) copy-start(f32[256]{0:T(256)} %add_rsqrt_fusion.1) | copy-start | bytes 3076
  110.0 16.3 %copy-start.48 = (f32[1,2,8,128]{3,1,2,0:T(2,128)}, f32[1,2,8,128]{3,1,2,0:T(2,128)S(1)}, u32[]{:S(2)}) copy-start(f32[1,2,8,128]{3,1,2,0:T(2,128)S(1)} %copy.112) | copy-start | bytes 24580
  181.8 146.8 %all-gather.2.cloned.1.call-start = ((), (), s32[]{:S(2)}) async-start(), calls=%async_computation.1 | async-start | bytes 2949120 | tf_op jit(solution)/shard_map/all_gather | solution.py:817
  182.1 62.0 %collective-permute-start.2 = (bf16[144,640]{1,0:T(8,128)(2,1)S(1)}, bf16[144,640]{1,0:T(8,128)(2,1)S(1)}, u32[]{:S(2)}, u32[]{:S(2)}) collective-permute-start(bf16[144,640]{1,0:T(8,128)(2,1)S(1)} %convolution_convert_fusion.11), channel_id=1, source_target_pairs={{0,8},{4,12},{8,0},{12,4},{16,24},{20,28},{24,16},{28,20},{1,9},{5... | collective-permute-start | bytes 552968 | tf_op jit(solution)/shard_map/ppermute | solution.py:41
  184.8 59.3 %collective-permute-start.3 = (bf16[144,640]{1,0:T(8,128)(2,1)S(1)}, bf16[144,640]{1,0:T(8,128)(2,1)S(1)}, u32[]{:S(2)}, u32[]{:S(2)}) collective-permute-start(bf16[144,640]{1,0:T(8,128)(2,1)S(1)} %convolution_convert_fusion.10), channel_id=1, source_target_pairs={{0,16},{4,20},{8,24},{12,28},{16,0},{20,4},{24,8},{28,12},{1,17},{... | collective-permute-start | bytes 552968 | tf_op jit(solution)/shard_map/ppermute | solution.py:41
  185.7 58.4 %collective-permute-start.4 = (bf16[144,640]{1,0:T(8,128)(2,1)S(1)}, bf16[144,640]{1,0:T(8,128)(2,1)S(1)}, u32[]{:S(2)}, u32[]{:S(2)}) collective-permute-start(bf16[144,640]{1,0:T(8,128)(2,1)S(1)} %convolution_convert_fusion.9), channel_id=1, source_target_pairs={{0,24},{4,28},{8,16},{12,20},{16,8},{20,12},{24,0},{28,4},{1,25},{... | collective-permute-start | bytes 552968 | tf_op jit(solution)/shard_map/ppermute | solution.py:41
  245.0 226.5 %all-reduce.11.cloned.1.call-start = ((), (), s32[]{:S(2)}) async-start(), calls=%async_computation.2 | async-start | bytes 2097152 | tf_op jit(solution)/shard_map/psum | solution.py:886
  338.6 10.6 %copy-start.23 = (bf16[576,2048]{1,0:T(8,128)(2,1)S(1)}, bf16[576,2048]{1,0:T(8,128)(2,1)}, u32[]{:S(2)}) copy-start(bf16[576,2048]{1,0:T(8,128)(2,1)} %convolution_convert_fusion.4) | copy-start | bytes 7077892
  348.8 41.3 %collective-permute-start.12 = (bf16[576,2816]{1,0:T(8,128)(2,1)S(1)}, bf16[576,2816]{1,0:T(8,128)(2,1)S(1)}, u32[]{:S(2)}, u32[]{:S(2)}) collective-permute-start(bf16[576,2816]{1,0:T(8,128)(2,1)S(1)} %pad_maximum_fusion.2), channel_id=1, source_target_pairs={{0,4},{4,0},{8,12},{12,8},{16,20},{20,16},{24,28},{28,24},{1,5},{5... | collective-permute-start | bytes 9732104 | tf_op jit(solution)/shard_map/ppermute | solution.py:41
  350.2 15.4 %collective-permute-start.5 = (bf16[144,2048]{1,0:T(8,128)(2,1)S(1)}, bf16[144,2048]{1,0:T(8,128)(2,1)S(1)}, u32[]{:S(2)}, u32[]{:S(2)}) collective-permute-start(bf16[144,2048]{1,0:T(8,128)(2,1)S(1)} %get-tuple-element.155), channel_id=1, source_target_pairs={{0,8},{4,12},{8,0},{12,4},{16,24},{20,28},{24,16},{28,20},{1,9},{5... | collective-permute-start | bytes 1769480 | tf_op jit(solution)/shard_map/ppermute | solution.py:41
  351.7 31.9 %collective-permute-start.14 = (bf16[576,1408]{1,0:T(8,128)(2,1)S(1)}, bf16[576,1408]{1,0:T(8,128)(2,1)S(1)}, u32[]{:S(2)}, u32[]{:S(2)}) collective-permute-start(bf16[576,1408]{1,0:T(8,128)(2,1)S(1)} %copy-done.26), channel_id=1, source_target_pairs={{0,4},{4,0},{8,12},{12,8},{16,20},{20,16},{24,28},{28,24},{1,5},{5... | collective-permute-start | bytes 4866056 | tf_op jit(solution)/shard_map/ppermute | solution.py:41
  351.9 15.2 %copy-start.22 = (bf16[576,2048]{1,0:T(8,128)(2,1)S(1)}, bf16[576,2048]{1,0:T(8,128)(2,1)}, u32[]{:S(2)}) copy-start(bf16[576,2048]{1,0:T(8,128)(2,1)} %get-tuple-element.89) | copy-start | bytes 7077892
  352.1 33.0 %collective-permute-start.13 = (bf16[576,1024]{1,0:T(8,128)(2,1)S(1)}, bf16[576,1024]{1,0:T(8,128)(2,1)S(1)}, u32[]{:S(2)}, u32[]{:S(2)}) collective-permute-start(bf16[576,1024]{1,0:T(8,128)(2,1)S(1)} %pad_maximum_fusion.8), channel_id=1, source_target_pairs={{0,4},{4,0},{8,12},{12,8},{16,20},{20,16},{24,28},{28,24},{1,5},{5... | collective-permute-start | bytes 3538952 | tf_op jit(solution)/shard_map/ppermute | solution.py:41
  352.6 15.6 %collective-permute-start.6 = (bf16[144,2048]{1,0:T(8,128)(2,1)S(1)}, bf16[144,2048]{1,0:T(8,128)(2,1)S(1)}, u32[]{:S(2)}, u32[]{:S(2)}) collective-permute-start(bf16[144,2048]{1,0:T(8,128)(2,1)S(1)} %get-tuple-element.154), channel_id=1, source_target_pairs={{0,16},{4,20},{8,24},{12,28},{16,0},{20,4},{24,8},{28,12},{1,17},{... | collective-permute-start | bytes 1769480 | tf_op jit(solution)/shard_map/ppermute | solution.py:41
  365.6 15.4 %collective-permute-start.7 = (bf16[144,2048]{1,0:T(8,128)(2,1)S(1)}, bf16[144,2048]{1,0:T(8,128)(2,1)S(1)}, u32[]{:S(2)}, u32[]{:S(2)}) collective-permute-start(bf16[144,2048]{1,0:T(8,128)(2,1)S(1)} %get-tuple-element.153), channel_id=1, source_target_pairs={{0,24},{4,28},{8,16},{12,20},{16,8},{20,12},{24,0},{28,4},{1,25},{... | collective-permute-start | bytes 1769480 | tf_op jit(solution)/shard_map/ppermute | solution.py:41
  368.2 13.9 %copy-start.33 = (bf16[144,2048]{1,0:T(8,128)(2,1)}, bf16[144,2048]{1,0:T(8,128)(2,1)S(1)}, u32[]{:S(2)}) copy-start(bf16[144,2048]{1,0:T(8,128)(2,1)S(1)} %collective-permute-done.6) | copy-start | bytes 1769476
  368.2 21.8 %collective-permute-start.11 = (bf16[576,1024]{1,0:T(8,128)(2,1)S(1)}, bf16[576,1024]{1,0:T(8,128)(2,1)S(1)}, u32[]{:S(2)}, u32[]{:S(2)}) collective-permute-start(bf16[576,1024]{1,0:T(8,128)(2,1)S(1)} %pad_maximum_fusion.7), channel_id=1, source_target_pairs={{0,4},{4,0},{8,12},{12,8},{16,20},{20,16},{24,28},{28,24},{1,5},{5... | collective-permute-start | bytes 3538952 | tf_op jit(solution)/shard_map/ppermute | solution.py:41
  382.1 28.4 %collective-permute-start.10 = (bf16[144,2048]{1,0:T(8,128)(2,1)S(1)}, bf16[144,2048]{1,0:T(8,128)(2,1)S(1)}, u32[]{:S(2)}, u32[]{:S(2)}) collective-permute-start(bf16[144,2048]{1,0:T(8,128)(2,1)S(1)} %get-tuple-element.149), channel_id=1, source_target_pairs={{0,24},{4,28},{8,16},{12,20},{16,8},{20,12},{24,0},{28,4},{1,25},{... | collective-permute-start | bytes 1769480 | tf_op jit(solution)/shard_map/ppermute | solution.py:41
  383.6 26.9 %collective-permute-start.8 = (bf16[144,2048]{1,0:T(8,128)(2,1)S(1)}, bf16[144,2048]{1,0:T(8,128)(2,1)S(1)}, u32[]{:S(2)}, u32[]{:S(2)}) collective-permute-start(bf16[144,2048]{1,0:T(8,128)(2,1)S(1)} %get-tuple-element.151), channel_id=1, source_target_pairs={{0,8},{4,12},{8,0},{12,4},{16,24},{20,28},{24,16},{28,20},{1,9},{5... | collective-permute-start | bytes 1769480 | tf_op jit(solution)/shard_map/ppermute | solution.py:41
  385.1 25.4 %collective-permute-start.9 = (bf16[144,2048]{1,0:T(8,128)(2,1)S(1)}, bf16[144,2048]{1,0:T(8,128)(2,1)S(1)}, u32[]{:S(2)}, u32[]{:S(2)}) collective-permute-start(bf16[144,2048]{1,0:T(8,128)(2,1)S(1)} %get-tuple-element.150), channel_id=1, source_target_pairs={{0,16},{4,20},{8,24},{12,28},{16,0},{20,4},{24,8},{28,12},{1,17},{... | collective-permute-start | bytes 1769480 | tf_op jit(solution)/shard_map/ppermute | solution.py:41
  390.0 15.4 %copy-start.4 = (bf16[1024,1408]{1,0:T(8,128)(2,1)}, bf16[1024,1408]{1,0:T(8,128)(2,1)S(1)}, u32[]{:S(2)}) copy-start(bf16[1024,1408]{1,0:T(8,128)(2,1)S(1)} %convolution_convert_fusion.2) | copy-start | bytes 8650756
  412.8 296.4 %all-reduce.13.cloned.1.call-start = ((), (), s32[]{:S(2)}) async-start(), calls=%async_computation.3 | async-start | bytes 4194304 | tf_op jit(solution)/shard_map/psum | solution.py:925
  417.2 167.5 %collective-permute-start.24 = (bf16[256,2048]{1,0:T(8,128)(2,1)}, bf16[256,2048]{1,0:T(8,128)(2,1)}, u32[]{:S(2)}, u32[]{:S(2)}) collective-permute-start(bf16[256,2048]{1,0:T(8,128)(2,1)} %get-tuple-element.77), channel_id=1, source_target_pairs={{0,4},{4,0},{8,12},{12,8},{16,20},{20,16},{24,28},{28,24},{1,5},{5... | collective-permute-start | bytes 3145736 | tf_op jit(solution)/shard_map/ppermute | solution.py:41
  418.8 49.8 %copy-start.5 = (bf16[1024,1408]{1,0:T(8,128)(2,1)S(1)}, bf16[1024,1408]{1,0:T(8,128)(2,1)}, u32[]{:S(2)}) copy-start(bf16[1024,1408]{1,0:T(8,128)(2,1)} %copy-done.4) | copy-start | bytes 8650756
  418.9 170.2 %collective-permute-start.21 = (bf16[256,1024]{1,0:T(8,128)(2,1)}, bf16[256,1024]{1,0:T(8,128)(2,1)}, u32[]{:S(2)}, u32[]{:S(2)}) collective-permute-start(bf16[256,1024]{1,0:T(8,128)(2,1)} %pad_maximum_fusion.17), channel_id=1, source_target_pairs={{0,4},{4,0},{8,12},{12,8},{16,20},{20,16},{24,28},{28,24},{1,5},{5... | collective-permute-start | bytes 1572872 | tf_op jit(solution)/shard_map/ppermute | solution.py:41
  553.4 11.1 %copy-start.32 = (bf16[144,2048]{1,0:T(8,128)(2,1)S(1)}, bf16[144,2048]{1,0:T(8,128)(2,1)}, u32[]{:S(2)}) copy-start(bf16[144,2048]{1,0:T(8,128)(2,1)} %copy-done.31) | copy-start | bytes 1769476
  553.4 35.7 %collective-permute-start.22 = (bf16[256,3072]{1,0:T(8,128)(2,1)}, bf16[256,3072]{1,0:T(8,128)(2,1)}, u32[]{:S(2)}, u32[]{:S(2)}) collective-permute-start(bf16[256,3072]{1,0:T(8,128)(2,1)} %get-tuple-element.107), channel_id=1, source_target_pairs={{0,4},{4,0},{8,12},{12,8},{16,20},{20,16},{24,28},{28,24},{1,5},{5... | collective-permute-start | bytes 4718600 | tf_op jit(solution)/shard_map/ppermute | solution.py:41
  563.8 20.9 %collective-permute-start.23 = (bf16[256,1024]{1,0:T(8,128)(2,1)}, bf16[256,1024]{1,0:T(8,128)(2,1)}, u32[]{:S(2)}, u32[]{:S(2)}) collective-permute-start(bf16[256,1024]{1,0:T(8,128)(2,1)} %pad_maximum_fusion.18), channel_id=1, source_target_pairs={{0,4},{4,0},{8,12},{12,8},{16,20},{20,16},{24,28},{28,24},{1,5},{5... | collective-permute-start | bytes 1572872 | tf_op jit(solution)/shard_map/ppermute | solution.py:41
  564.3 1.5 collective-permute-start.18
  565.8 3.6 collective-permute-start.19
  569.5 14.7 %collective-permute-start.20 = (f32[256,1]{0,1:T(1,128)S(1)}, f32[256,1]{0,1:T(1,128)S(1)}, u32[]{:S(2)}, u32[]{:S(2)}) collective-permute-start(f32[256,1]{0,1:T(1,128)S(1)} %slice_bitcast_fusion.12), channel_id=1, source_target_pairs={{0,16},{4,20},{8,24},{12,28},{16,0},{20,4},{24,8},{28,12},{1,17},{... | collective-permute-start | bytes 3080 | tf_op jit(solution)/shard_map/ppermute | solution.py:41
  572.1 12.6 %copy-start.44 = (bf16[256,256]{1,0:T(8,128)(2,1)S(1)}, bf16[256,256]{1,0:T(8,128)(2,1)}, u32[]{:S(2)}) copy-start(bf16[256,256]{1,0:T(8,128)(2,1)} %get-tuple-element.167) | copy-start | bytes 393220
  572.1 12.6 %copy-start.45 = (bf16[256,256]{1,0:T(8,128)(2,1)S(1)}, bf16[256,256]{1,0:T(8,128)(2,1)}, u32[]{:S(2)}) copy-start(bf16[256,256]{1,0:T(8,128)(2,1)} %get-tuple-element.172) | copy-start | bytes 393220
  572.1 12.6 %copy-start.46 = (bf16[256,256]{1,0:T(8,128)(2,1)S(1)}, bf16[256,256]{1,0:T(8,128)(2,1)}, u32[]{:S(2)}) copy-start(bf16[256,256]{1,0:T(8,128)(2,1)} %get-tuple-element.173) | copy-start | bytes 393220
  572.1 12.6 %copy-start.47 = (bf16[256,256]{1,0:T(8,128)(2,1)S(1)}, bf16[256,256]{1,0:T(8,128)(2,1)}, u32[]{:S(2)}) copy-start(bf16[256,256]{1,0:T(8,128)(2,1)} %get-tuple-element.174) | copy-start | bytes 393220
  711.4 4.2 collective-permute-start.15
  715.6 3.7 collective-permute-start.16
  719.3 3.6 collective-permute-start.17
  (55 other events, 184.9 us)
Sparse Core Ops, SparseCore 0:
  181.9 52.1 all-reduce.8
  245.1 50.7 all-gather.1
  413.0 52.0 all-reduce.10
  572.2 87.3 all-reduce.12

commit v3 on v2

--- a/solution.py
+++ b/solution.py
@@ -17,10 +17,9 @@
 VMEM_LIMIT = 56 * 1024 * 1024
 
 
-def normalize(tensor, gain_vec):
+def normalize(tensor):
     inverse = lax.rsqrt(jnp.mean(tensor * tensor, axis=-1, keepdims=True) + EPSILON)
-    normed = tensor * inverse
-    return (normed, inverse, normed * gain_vec)
+    return (tensor * inverse, inverse)
 
 
 def norm_back(grad_in, normed, inverse, gain_vec):
@@ -96,6 +95,8 @@
                     device_id=peer(ctx_count, mask),
                     device_id_type=pl.DeviceIdType.MESH,
                 )
+            elif mask is None:
+                copy = pltpu.make_async_copy(src, dst, recv.at[i])
             else:
                 bounce = bounces.pop(0)
                 copy = pltpu.make_async_copy(src, bounce, recv.at[i])
@@ -118,18 +119,20 @@
             if i in self.onward:
                 self.copies[i].wait()
                 self.onward[i].start()
+            elif self.moves[i][2] is None:
+                self.copies[i].wait()
             else:
                 self.copies[i].wait_recv()
 
-    def settle(self, count):
-        for i in range(count):
+    def settle(self, count, first=0):
+        for i in range(first, count):
             if i in self.onward:
                 self.await_one(i)
-        for i in range(count):
+        for i in range(first, count):
             for target in self.moves[i][3]:
                 self.await_one(self.place[target])
             self.start(i)
-        for i in range(count):
+        for i in range(first, count):
             self.await_one(i)
 
     def finish(self):
@@ -137,7 +140,7 @@
         for i in range(len(self.moves)):
             if i in self.onward:
                 self.onward[i].wait()
-            else:
+            elif self.moves[i][2] is not None:
                 self.copies[i].wait_send()
 
 
@@ -193,119 +196,321 @@
     )
 
 
-def reduce_kernel(ctx_count, bits, part, pieces, grad_ref, out_ref, sums, got, send, recv):
-    count, wide = grad_ref.shape[0] // part, grad_ref.shape[1]
-    greet(ctx_count, sorted(1 << b for b in bits))
-    half = wide // 2
-    size = half // pieces
+def attn_grads_kernel(
+    ctx_count,
+    bits,
+    part,
+    cols,
+    hidden_ref,
+    branch_ref,
+    qkv_ref,
+    mixed_ref,
+    out_ref,
+    hidden,
+    branch,
+    hidden_odd,
+    branch_odd,
+    right,
+    grads,
+    got,
+    send,
+    recv,
+    pass_send,
+    pass_recv,
+):
+    rows, width = hidden_ref.shape
+    count = width // part // 2
+    planes = right.shape[1] // cols
+    first = qkv_ref.shape[1]
+    greet(ctx_count, [1, *[1 << b for b in bits]])
+    arrays = {
+        "hidden_odd": hidden_odd,
+        "branch_odd": branch_odd,
+        "qkv_in": qkv_ref,
+        "mixed_in": mixed_ref,
+        "hidden": hidden,
+        "branch": branch,
+        "right": right,
+    }
+    theirs = (rows, rows)
+    moves = [
+        (("mixed_in", (0, rows), None), ("right", theirs, (first, mixed_ref.shape[1])), 1, ()),
+        (("branch_odd", (0, rows), None), ("branch", theirs, None), 1, ()),
+        (("qkv_in", (0, rows), None), ("right", theirs, (0, first)), 1, ()),
+        (("hidden_odd", (0, rows), None), ("hidden", theirs, None), 1, ()),
+    ]
+    run = Moves(ctx_count, moves, arrays, pass_send, pass_recv)
+    for given, even_side, odd_side in (
+        (branch_ref, branch, branch_odd),
+        (hidden_ref, hidden, hidden_odd),
+    ):
+        for j in range(count):
+            block = slice(j * part, (j + 1) * part)
+            even_side[:rows, block] = given[:, 2 * j * part : (2 * j + 1) * part]
+            odd_side[:, block] = given[:, (2 * j + 1) * part : (2 * j + 2) * part]
+    run.begin()
+    right[:rows, :first] = qkv_ref[...]
+    right[:rows, first:] = mixed_ref[...]
     number = [0]
 
-    def copy(source, mask, block, cols):
+    def copy(mask, block, plane):
         i = number[0]
         number[0] += 1
-        rows = pl.ds(block * part, part)
+        window_of = (pl.ds(block * part, part), pl.ds(plane * cols, cols))
         return pltpu.make_async_remote_copy(
-            src_ref=source.at[rows, cols],
-            dst_ref=got.at[rows, cols],
+            src_ref=grads.at[window_of],
+            dst_ref=got.at[window_of],
             send_sem=send.at[i],
             recv_sem=recv.at[i],
             device_id=peer(ctx_count, mask),
             device_id_type=pl.DeviceIdType.MESH,
         )
 
+    sent, flying, left = [], {}, {}
+
+    def send_half(plane, order, step):
+        at = bits.index(order[step])
+        flying[plane] = {
+            j: copy(1 << order[step], j, plane) for j in left[plane] if j >> at & 1
+        }
+        for c in flying[plane].values():
+            c.start()
+        sent.extend(flying[plane].values())
+
     lanes = []
-    for piece in range(pieces):
-        for side in range(2):
-            order = bits if side == 0 else bits[::-1]
-            cols = pl.ds(side * half + piece * size, size)
-            lanes.append((order, cols))
-    sent = []
-    flying = []
-    for order, cols in lanes:
-        at = bits.index(order[0])
-        copies = {j: copy(grad_ref, 1 << order[0], j, cols) for j in range(count) if j >> at & 1}
-        for c in copies.values():
-            c.start()
-        flying.append(copies)
-        sent += list(copies.values())
-    left = [list(range(count)) for _ in lanes]
+    late = first // cols
+    for n, plane in enumerate([*range(late, planes), *range(late)]):
+        lanes.append((plane, bits if n % 2 else bits[::-1]))
+    for plane, order in lanes:
+        run.settle(2 if plane >= late else 4)
+        at = pl.ds(plane * cols, cols)
+        left_side = hidden if plane < late else branch
+        grads[:, at] = dot(left_side[...], right[:, at], 0, 0).astype(BF)
+        left[plane] = list(range(count))
+        send_half(plane, order, 0)
     for step in range(len(bits)):
-        last = step == len(bits) - 1
-        for n, (order, cols) in enumerate(lanes):
+        for plane, order in lanes:
             at = bits.index(order[step])
-            left[n] = [j for j in left[n] if not j >> at & 1]
-            for j in left[n]:
-                flying[n][j | 1 << at].wait_recv()
-                rows = pl.ds(j * part, part)
-                mine = grad_ref if step == 0 else sums
-                total = mine[rows, cols].astype(F32) + got[
-                    pl.ds((j | 1 << at) * part, part), cols
-                ].astype(F32)
-                if last:
-                    out_ref[:, cols] = total
+            left[plane] = [j for j in left[plane] if not j >> at & 1]
+            across = pl.ds(plane * cols, cols)
+            for j in left[plane]:
+                flying[plane][j | 1 << at].wait_recv()
+                down, other = pl.ds(j * part, part), pl.ds((j | 1 << at) * part, part)
+                total = grads[down, across].astype(F32) + got[other, across].astype(F32)
+                if step == len(bits) - 1:
+                    out_ref[:, across] = total
                 else:
-                    sums[rows, cols] = total.astype(BF)
-            if not last:
-                following = bits.index(order[step + 1])
-                copies = {
-                    j: copy(sums, 1 << order[step + 1], j, cols)
-                    for j in left[n]
-                    if j >> following & 1
-                }
-                for c in copies.values():
-                    c.start()
-                flying[n] = copies
-                sent += list(copies.values())
+                    grads[down, across] = total.astype(BF)
+            if step < len(bits) - 1:
+                send_half(plane, order, step + 1)
+    run.finish()
     for c in sent:
         c.wait_send()
 
 
-def reduce_grads(number, ctx_count, bits, part, grad):
-    pieces = 4
-    copies = 2 * pieces * (grad.shape[0] // part)
+def attn_grads(number, ctx_count, bits, part, cols, hidden, branch, qkv, mixed):
+    rows, width = hidden.shape
+    wide = qkv.shape[1] + mixed.shape[1]
+    copies = (wide // cols) * (width // part // 2)
     full = pl.BlockSpec(memory_space=pltpu.VMEM)
     return pl.pallas_call(
-        functools.partial(reduce_kernel, ctx_count, bits, part, pieces),
-        out_shape=jax.ShapeDtypeStruct((part, grad.shape[1]), F32),
-        in_specs=[full],
+        functools.partial(attn_grads_kernel, ctx_count, bits, part, cols),
+        out_shape=jax.ShapeDtypeStruct((part, wide), F32),
+        in_specs=[full] * 4,
         out_specs=full,
-        scratch_shapes=[pltpu.VMEM(grad.shape, BF)] * 2
-        + [pltpu.SemaphoreType.DMA((copies,))] * 2,
+        scratch_shapes=[pltpu.VMEM((2 * rows, width // 2), BF)] * 2
+        + [pltpu.VMEM((rows, width // 2), BF)] * 2
+        + [pltpu.VMEM((2 * rows, wide), BF)]
+        + [pltpu.VMEM((width // 2, wide), BF)] * 2
+        + [pltpu.SemaphoreType.DMA((copies,))] * 2
+        + [pltpu.SemaphoreType.DMA((4,))] * 2,
         compiler_params=pltpu.CompilerParams(
             collective_id=number, has_side_effects=True, vmem_limit_bytes=VMEM_LIMIT
         ),
-        name="reduce_grads",
+        name="attn_grads",
+    )(hidden, branch, qkv, mixed)
+
+
+def lay_kernel(grad_ref, *out_refs):
+    at = 0
+    for ref in out_refs:
+        for p in range(ref.shape[1]):
+            ref[:, p, :] = grad_ref[:, at : at + ref.shape[2]]
+            at += ref.shape[2]
+
+
+def lay_out(grad, shapes):
+    step = min(64, grad.shape[0])
+    return pl.pallas_call(
+        lay_kernel,
+        grid=(grad.shape[0] // step,),
+        in_specs=[pl.BlockSpec((step, grad.shape[1]), lambda i: (i, 0))],
+        out_specs=[pl.BlockSpec((step, *shape[1:]), lambda i: (i, 0, 0)) for shape in shapes],
+        out_shape=[jax.ShapeDtypeStruct(shape, F32) for shape in shapes],
+        compiler_params=pltpu.CompilerParams(vmem_limit_bytes=VMEM_LIMIT),
+        name="lay_out",
     )(grad)
 
 
-def project_kernel(h_ref, w_ref, cos_ref, sin_ref, out_ref):
-    y = jnp.dot(h_ref[...], w_ref[...], preferred_element_type=F32)
-    for head in range(y.shape[1] // HD):
-        cols = slice(head * HD, (head + 1) * HD)
-        out_ref[:, cols] = turn(y[:, cols], cos_ref[0], sin_ref[0]).astype(BF)
-
-
-def project(hidden, weight, cos, sin, plain, cols, count):
-    rows, width = hidden.shape
-    tables = [
-        jnp.stack([cos, jnp.ones_like(cos)]),
-        jnp.stack([sin, jnp.zeros_like(sin)]),
-    ]
-    table_spec = pl.BlockSpec((1, rows, HD), lambda p: (p // plain, 0, 0))
+def gain_kernel(ctx_count, group, gain_ref, out_ref, got, send, recv):
+    greet(ctx_count, range(1, group))
+    copies = []
+    for j in range(1, group):
+        rows = pl.ds(j * 8, 8)
+        copies.append(
+            pltpu.make_async_remote_copy(
+                src_ref=gain_ref.at[rows],
+                dst_ref=got.at[rows],
+                send_sem=send.at[j],
+                recv_sem=recv.at[j],
+                device_id=peer(ctx_count, j),
+                device_id_type=pl.DeviceIdType.MESH,
+            )
+        )
+        copies[-1].start()
+    total = gain_ref[:8]
+    for j, copy in enumerate(copies):
+        copy.wait_recv()
+        total = total + got[(j + 1) * 8 : (j + 2) * 8]
+    out_ref[...] = total
+    for copy in copies:
+        copy.wait_send()
+
+
+def gain_sums(number, ctx_count, group, gains):
+    count, part = len(gains), gains[0].shape[0] // group
+    laid = jnp.stack([g.reshape(group, part) for g in gains], axis=1)
+    laid = jnp.pad(laid, ((0, 0), (0, 8 - count), (0, 0))).reshape(group * 8, part)
+    full = pl.BlockSpec(memory_space=pltpu.VMEM)
+    total = pl.pallas_call(
+        functools.partial(gain_kernel, ctx_count, group),
+        out_shape=jax.ShapeDtypeStruct((8, part), F32),
+        in_specs=[full],
+        out_specs=full,
+        scratch_shapes=[pltpu.VMEM((group * 8, part), F32)]
+        + [pltpu.SemaphoreType.DMA((group,))] * 2,
+        compiler_params=pltpu.CompilerParams(collective_id=number, has_side_effects=True),
+        name="gain_sums",
+    )(laid)
+    return [total[i] for i in range(count)]
+
+
+def expert_grads_kernel(
+    ctx_count,
+    experts,
+    share,
+    part,
+    moves,
+    two_ref,
+    down_ref,
+    gu_ref,
+    active_ref,
+    back_ref,
+    place_ref,
+    grads_ref,
+    out_ref,
+    back_got,
+    two_out,
+    down_out,
+    two_got,
+    down_got,
+    gu_got,
+    active_got,
+    send,
+    recv,
+):
+    slots, width = two_ref.shape
+    units = active_ref.shape[1]
+    room = slots // experts
+    run = Moves(
+        ctx_count,
+        moves,
+        {
+            "two": two_out,
+            "down": down_out,
+            "gu": gu_ref,
+            "active": active_ref,
+            "back": back_ref,
+            "back_got": back_got,
+            "two_got": two_got,
+            "down_got": down_got,
+            "gu_got": gu_got,
+            "active_got": active_got,
+        },
+        send,
+        recv,
+    )
+    greet(ctx_count, masks_of(moves))
+    for t in range(1, share):
+        rows = slice((t - 1) * slots, t * slots)
+        for k in range(experts):
+            at = (k * share + t) * part
+            two_out[rows, k * part : (k + 1) * part] = two_ref[:, at : at + part]
+            down_out[rows, k * part : (k + 1) * part] = down_ref[:, at : at + part]
+    run.begin()
+    for i in range(experts - 1, len(moves)):
+        run.await_one(i)
+    for k in range(experts):
+        rows = pl.ds(k * part, part)
+        own, other = slice(k * share * part, (k * share + 1) * part), slice(k * part, (k + 1) * part)
+        for cols, left, left_got, right, right_got in (
+            (pl.ds(0, 2 * units), two_ref, two_got, gu_ref, gu_got),
+            (pl.ds(2 * units, units), down_ref, down_got, active_ref, active_got),
+        ):
+            total = dot(left[:, own], right[...], 0, 0)
+            if share > 1:
+                total = total + dot(left_got[:, other], right_got[...], 0, 0)
+            grads_ref[rows, cols] = total.astype(BF)
+    run.finish()
+    run_of = width // experts
+    for i in range(experts):
+        total = dot(place_ref[0], back_ref[:room, i * run_of : (i + 1) * run_of], 0, 0)
+        for k in range(1, experts):
+            at = (i ^ k) * run_of
+            total = total + dot(
+                place_ref[k], back_got[k * room : (k + 1) * room, at : at + run_of], 0, 0
+            )
+        out_ref[:, i * run_of : (i + 1) * run_of] = total.astype(BF)
+
+
+def expert_grads_of(number, ctx_count, experts, share, part, two, down, gu, active, back, place):
+    slots, width = two.shape
+    room, units = slots // experts, active.shape[1]
+    moves = []
+    for k in range(1, experts):
+        moves.append(
+            (("back", (k * room, room), None), ("back_got", (k * room, room), None), k * share, ())
+        )
+    for t in range(1, share):
+        rows = ((t - 1) * slots, slots)
+        for name in ("gu", "active"):
+            moves.append(((name, (0, slots), None), (name + "_got", rows, None), t, ()))
+        for name in ("two", "down"):
+            moves.append(((name, rows, None), (name + "_got", rows, None), t, ()))
+    others = max(1, share - 1) * slots
+    full = pl.BlockSpec(memory_space=pltpu.VMEM)
     return pl.pallas_call(
-        project_kernel,
-        out_shape=jax.ShapeDtypeStruct((rows, count * cols), BF),
-        grid=(count,),
-        in_specs=[
-            pl.BlockSpec((rows, width), lambda p: (0, 0)),
-            pl.BlockSpec((width, cols), lambda p: (0, p)),
-            table_spec,
-            table_spec,
+        functools.partial(
+            expert_grads_kernel, ctx_count, experts, share, part, moves
+        ),
+        out_shape=[
+            jax.ShapeDtypeStruct((experts * part, 3 * units), BF),
+            jax.ShapeDtypeStruct((place.shape[2], width), BF),
         ],
-        out_specs=pl.BlockSpec((rows, cols), lambda p: (0, p)),
-        compiler_params=pltpu.CompilerParams(vmem_limit_bytes=VMEM_LIMIT),
-        name="project",
-    )(hidden, weight, *tables)
+        in_specs=[full] * 6,
+        out_specs=[full] * 2,
+        scratch_shapes=[
+            pltpu.VMEM((slots, width), BF),
+            *[pltpu.VMEM((others, experts * part), BF)] * 4,
+            pltpu.VMEM((others, 2 * units), BF),
+            pltpu.VMEM((others, units), BF),
+        ]
+        + [pltpu.SemaphoreType.DMA((len(moves),))] * 2,
+        compiler_params=pltpu.CompilerParams(
+            collective_id=number, has_side_effects=True, vmem_limit_bytes=VMEM_LIMIT
+        ),
+        name="expert_grads",
+    )(two, down, gu, active, back, place)
 
 
 def head_cols(index):
@@ -323,14 +528,18 @@
     return slots, exps, 1.0 / total
 
 
-def attend_kernel(
+def front_kernel(
     ctx_count,
     moves,
-    first_moves,
+    marks,
     names_in,
     names_out,
     heads,
-    qkv_ref,
+    part,
+    normed_ref,
+    gain_ref,
+    cos_ref,
+    sin_ref,
     place_ref,
     segq_ref,
     idxq_ref,
@@ -340,16 +549,51 @@
     *refs,
 ):
     experts, _, rows = place_ref.shape
+    width = normed_ref.shape[1]
+    wide = heads * HD
+    group = width // part
     given, refs = refs[: len(names_in)], refs[len(names_in) :]
-    mixed_ref, kv_ref = refs[:2]
-    made, (send, recv) = refs[2:-2], refs[-2:]
-    arrays = {"qkv": qkv_ref, "kv": kv_ref, **dict(zip(names_in, given)), **dict(zip(names_out, made))}
+    gains_ref, hidden_ref, qkv_ref, kv_ref, mixed_ref, branch_ref = refs[:6]
+    refs = refs[6:]
+    made, (full, send, recv, *bounces) = refs[: len(names_out)], refs[len(names_out) :]
+    arrays = {
+        "gain_own": gain_ref,
+        "gains": gains_ref,
+        "full": full,
+        "qkv": qkv_ref,
+        "kv": kv_ref,
+        **dict(zip(names_in, given)),
+        **dict(zip(names_out, made)),
+    }
     greet(ctx_count, masks_of(moves))
-    run = Moves(ctx_count, moves, arrays, send, recv)
-    run.begin(first_moves)
-    kv_ref[:rows] = qkv_ref[:, experts * heads * HD :]
-    run.settle(first_moves)
+    run = Moves(ctx_count, moves, arrays, send, recv, bounces)
+    gains_done, first_done, rest_done, keys_done = marks
+    run.begin(rest_done)
+    gains_ref[:16] = gain_ref[...]
+    run.settle(gains_done)
+    for j in range(group):
+        cols = slice(j * part, (j + 1) * part)
+        gain = gains_ref[j * 16 : (j + 1) * 16].astype(F32)[:1, :part]
+        hidden_ref[:, cols] = (normed_ref[:, cols] * gain).astype(BF)
+    run.settle(first_done, gains_done)
+    cos, sin = cos_ref[...], sin_ref[...]
+
+    def project(plane):
+        y = dot(hidden_ref[...], full[:, plane * wide : (plane + 1) * wide], 1, 0)
+        for head in range(heads):
+            cols = slice(head * HD, (head + 1) * HD)
+            at = slice(plane * wide + head * HD, plane * wide + (head + 1) * HD)
+            z = y[:, cols]
+            qkv_ref[:, at] = (turn(z, cos, sin) if plane <= experts else z).astype(BF)
+
+    project(experts)
+    project(experts + 1)
+    run.begin(keys_done)
+    kv_ref[:rows] = qkv_ref[:, experts * wide :]
     run.begin()
+    for plane in range(experts):
+        project(plane)
+    run.settle(keys_done, rest_done)
 
     def step(i, carry):
         h, e = i // experts, i % experts
@@ -370,16 +614,23 @@
         return carry
 
     lax.fori_loop(0, heads * experts, step, 0)
+    run.settle(rest_done, first_done)
+    for j in range(group):
+        rows_at = slice(j * part, (j + 1) * part)
+        branch_ref[:, rows_at] = dot(mixed_ref[...], full[rows_at, (experts + 2) * wide :], 1, 1).astype(BF)
     run.finish()
 
 
-def attend(number, ctx_count, heads, moves, given, made, qkv, place, *slots_and_keys):
+def front(number, ctx_count, heads, part, moves, later, given, made, small):
+    normed, gain_own, place = small[0], small[1], small[4]
     experts, _, rows = place.shape
+    width = normed.shape[1]
     wide = heads * HD
+    group = width // part
+    full_wide = 2 * (experts + 1) * wide
     kv_moves = []
     order = [0]
-    bits = range(bits_of(ctx_count))[::-1]
-    for bit in bits:
+    for bit in range(bits_of(ctx_count))[::-1]:
         for at in range(len(order)):
             target = ("kv", ((at + len(order)) * rows, rows), None)
             if at:
@@ -389,39 +640,48 @@
                 source = ("qkv", (0, rows), (experts * wide, 2 * wide))
                 kv_moves.append((source, target, 1 << bit, ()))
         order = order + order
-    names_in = [n for n in given if n not in made] + [n for n in given if n in made]
-    names_out = list(made)
+    gains_moves, first_moves, rest_moves = moves
+    marks = [len(gains_moves)]
+    for more in (first_moves, rest_moves, kv_moves):
+        marks.append(marks[-1] + len(more))
+    whole = ("full", (0, width), None)
+    landed = tuple(m[1] for m in first_moves + rest_moves if m[1][0] == "full")
+    keep = [(whole, ("kept", (0, width), None), None, landed)]
+    moves = gains_moves + first_moves + rest_moves + kv_moves + later + keep
+    names_in, names_out = list(given), [*made, "kept"]
+    shapes_out = [*made.values(), (width, full_wide)]
     any_spec = pl.BlockSpec(memory_space=pl.ANY)
     full = pl.BlockSpec(memory_space=pltpu.VMEM)
-    moves = kv_moves + moves
-    before = 2 + len(slots_and_keys)
-    mixed, kv, *rest = pl.pallas_call(
+    small_out = [
+        ((16 * group, gain_own.shape[1]), BF),
+        ((rows, width), BF),
+        ((rows, (experts + 2) * wide), BF),
+        ((ctx_count * rows, 2 * wide), BF),
+        ((rows, experts * wide), BF),
+        ((rows, width), BF),
+    ]
+    bounces = [
+        pltpu.VMEM((source[1][1], (source[2] or (0, given[source[0]].shape[1]))[1]), BF)
+        for source, _, mask, _ in moves
+        if mask == 0
+    ]
+    out = pl.pallas_call(
         functools.partial(
-            attend_kernel,
-            ctx_count,
-            moves,
-            len(kv_moves),
-            [n if n not in made else "old_" + n for n in names_in],
-            names_out,
-            heads,
+            front_kernel, ctx_count, moves, marks, names_in, names_out, heads, part
         ),
-        out_shape=[
-            jax.ShapeDtypeStruct((rows, experts * wide), BF),
-            jax.ShapeDtypeStruct((ctx_count * rows, 2 * wide), BF),
-        ]
-        + [jax.ShapeDtypeStruct(shape, BF) for shape in made.values()],
-        in_specs=[full] * before + [any_spec] * len(names_in),
-        out_specs=[full] * 2 + [any_spec] * len(names_out),
-        input_output_aliases={
-            before + names_in.index(n): 2 + names_out.index(n) for n in names_out if n in given
-        },
-        scratch_shapes=[pltpu.SemaphoreType.DMA((len(moves),))] * 2,
+        out_shape=[jax.ShapeDtypeStruct(*x) for x in small_out]
+        + [jax.ShapeDtypeStruct(shape, BF) for shape in shapes_out],
+        in_specs=[full] * len(small) + [any_spec] * len(names_in),
+        out_specs=[full] * len(small_out) + [any_spec] * len(names_out),
+        scratch_shapes=[pltpu.VMEM((width, full_wide), BF)]
+        + [pltpu.SemaphoreType.DMA((len(moves),))] * 2
+        + bounces,
         compiler_params=pltpu.CompilerParams(
             collective_id=number, has_side_effects=True, vmem_limit_bytes=VMEM_LIMIT
         ),
-        name="attend",
-    )(qkv, place, *slots_and_keys, *[given[n] for n in names_in])
-    return mixed, kv, dict(zip(names_out, rest))
+        name="front",
+    )(*small, *given.values())
+    return out[: len(small_out)], dict(zip(names_out, out[len(small_out) :]))
 
 
 def attend_back_kernel(
@@ -721,70 +981,76 @@
     far = [k for k in range(1, experts) if k & (k - 1)]
     half_part = part // 2
 
+    normed_one, inverse_one = normalize(inputs)
     (attn_own, far_x, far_y, gain_own), to_send, tables = lax.optimization_barrier(
         (
             (attn_own, far_x, far_y, gain_own),
             to_send,
-            (cos, sin, place_attn, slot_seg, slot_idx, slot_gate, place_mlp),
+            (normed_one, cos, sin, place_attn, slot_seg, slot_idx, slot_gate, place_mlp),
         )
     )
-    cos, sin, place_attn, slot_seg, slot_idx, slot_gate, place_mlp = tables
+    normed_one, cos, sin, place_attn, slot_seg, slot_idx, slot_gate, place_mlp = tables
     quarter = part // 4
-    moves = []
-    held = {0: [("own", 0, part, ())], high: [("far_x", 0, part, ())], second: [("far_y", 0, part, ())]}
-    held[high | second] = []
-    for i in (0, 2, 1, 3):
-        source, mask = (("far_x", second), ("far_y", high))[i // 2]
-        target = ("full", ((high | second) * part + i * quarter, quarter), None)
-        moves.append(((source, (i * quarter, quarter), None), target, mask, ()))
-        held[high | second].append(("full", i * quarter, quarter, (target,)))
-    for j in (0, high, second):
-        name = held[j][0][0]
-        moves.append(((name, (0, part), None), ("full", (j * part, part), None), 0, ()))
-    for j in range(group):
-        moves.append((("gain_own", (0, 16), None), ("gains", (j * 16, 16), None), j, ()))
-    moves += weight_moves(0, 0, part)
-    for bit in range(bits_of(group) - 2)[::-1]:
-        for j in list(held):
-            there = []
-            for name, at, size, needs in held[j]:
-                source = (name, (at + j * part if name == "full" else at, size), None)
-                target = ("full", ((j | 1 << bit) * part + at, size), None)
-                moves.append((source, target, 1 << bit, needs))
-                there.append(("full", at, size, (target,)))
-            held[j | 1 << bit] = there
-    made = move(
-        "gather",
+    gather_moves = []
+    for cols in ((0, qkv_wide), (qkv_wide, attn_wide - qkv_wide)):
+        moves = []
+        held = {0: [("own", 0, part, ())], high: [("far_x", 0, part, ())], second: [("far_y", 0, part, ())]}
+        held[high | second] = []
+        for i in (0, 2, 1, 3):
+            source, mask = (("far_x", second), ("far_y", high))[i // 2]
+            target = ("full", ((high | second) * part + i * quarter, quarter), cols)
+            moves.append(((source, (i * quarter, quarter), cols), target, mask, ()))
+            held[high | second].append(("full", i * quarter, quarter, (target,)))
+        for j in (0, high, second):
+            name = held[j][0][0]
+            moves.append(((name, (0, part), cols), ("full", (j * part, part), cols), None, ()))
+        for bit in range(bits_of(group) - 2)[::-1]:
+            for j in list(held):
+                there = []
+                for name, at, size, needs in held[j]:
+                    source = (name, (at + j * part if name == "full" else at, size), cols)
+                    target = ("full", ((j | 1 << bit) * part + at, size), cols)
+                    moves.append((source, target, 1 << bit, needs))
+                    there.append(("full", at, size, (target,)))
+                held[j | 1 << bit] = there
+        gather_moves.append(moves)
+    gain_moves = [
+        (("gain_own", (0, 16), None), ("gains", (j * 16, 16), None), j, ())
+        for j in range(1, group)
+    ]
+    key_row = (key_seg[None, :], key_idx[None, :])
+    heads = head_width // HD
+    later = weight_moves(0, 0, part) + many_weight_moves([(k, 0, half_part) for k in near])
+    (gains, hidden_one, qkv, kv, mixed, branch), made = front(
         1,
         ctx_count,
-        moves,
-        {"own": attn_own, "far_x": far_x, "far_y": far_y, "gain_own": gain_own, "send0": to_send[0]},
-        {"full": (width, attn_wide), "gains": (16 * group, 2 * part), **weight_shapes},
-    )
-    attn_full, weights = made["full"], {n: made[n] for n in weight_shapes}
-    gains = made["gains"].reshape(group, 16, 2 * part)[:, 0].astype(F32)
+        heads,
+        part,
+        (gain_moves, *gather_moves),
+        later,
+        {
+            "own": attn_own,
+            "far_x": far_x,
+            "far_y": far_y,
+            **{f"send{k}": to_send[k] for k in [0, *near]},
+        },
+        weight_shapes,
+        (
+            normed_one,
+            gain_own,
+            cos[:rows],
+            sin[:rows],
+            place_attn,
+            slot_seg,
+            slot_idx,
+            slot_gate,
+            *key_row,
+        ),
+    )
+    attn_full, weights = made["kept"], {n: made[n] for n in weight_shapes}
+    gains = gains.reshape(group, 16, 2 * part)[:, 0].astype(F32)
     gain_one, gain_two = gains[:, :part].reshape(1, width), gains[:, part:].reshape(1, width)
     qkv_full, out_full = attn_full[:, :qkv_wide], attn_full[:, qkv_wide:]
-    normed_one, inverse_one, pre_one = normalize(inputs, gain_one)
-    hidden_one = pre_one.astype(BF)
-    qkv = project(hidden_one, attn_full, cos[:rows], sin[:rows], attn_experts + 1, head_width, attn_experts + 2)
-    key_row = (key_seg[None, :], key_idx[None, :])
-    heads = head_width // HD
-    cuts = [(k, 0, half_part) for k in near]
-    mixed, kv, weights = attend(
-        2,
-        ctx_count,
-        heads,
-        many_weight_moves(cuts),
-        {**{f"send{k}": to_send[k] for k in near}, **weights},
-        weight_shapes,
-        qkv,
-        place_attn,
-        slot_seg,
-        slot_idx,
-        slot_gate,
-        *key_row,
-    )
 
     def turned(x, k):
         wide = share * part
@@ -828,14 +1094,13 @@
         made = move(name, number, ctx_count, moves, {**given, **weights}, made_shapes)
         return {n: made[n] for n in weight_shapes}, made.get("slots")
 
-    branch = dot(mixed, out_full, 1, 1).astype(BF)
     branch_sum = lax.psum(branch, "tp")
     cuts = [(k, half_part, part - half_part) for k in near] + [(k, 0, half_part) for k in far]
     to_send, weights, _ = lax.optimization_barrier((to_send, weights, branch))
     weights, _ = send_weights("weights_two", 3, cuts, weights)
     resid = inputs + branch_sum.astype(F32)
-    normed_two, inverse_two, pre_two = normalize(resid, gain_two)
-    hidden_two = pre_two.astype(BF)
+    normed_two, inverse_two = normalize(resid)
+    hidden_two = (normed_two * gain_two).astype(BF)
     slots = [pick(0, hidden_two)] + [turned(pick(k, hidden_two), k) for k in range(1, experts)]
     cuts = [(k, half_part, part - half_part) for k in far]
     weights, two_slots = send_weights("dispatch", 4, cuts, weights, slots)
@@ -864,26 +1129,20 @@
     grad_up = scaled * silu_gate
     grad_gu = jnp.concatenate([grad_gate, grad_up], axis=1).astype(BF)
     back_two_slots = dot(grad_gu, in_full, 1, 1).astype(BF)
-    two_back = send_back(after(back_two_slots, *mlp_back))
-
-    def for_share(x, t):
-        return jnp.concatenate(
-            [x[:, (k * share + t) * part : (k * share + t + 1) * part] for k in range(experts)],
-            axis=1,
-        )
-
-    def every_share(x, cut):
-        got = [for_share(x, 0) if cut else x]
-        for t in range(1, share):
-            got.append(exchange(for_share(x, t) if cut else x, t))
-        return jnp.concatenate(got, axis=0)
-
-    grad_gu_late = after(grad_gu, back_two_slots)
-    grad_in_w = dot(every_share(two_slots, True), every_share(grad_gu_late, False), 0, 0)
-    grad_down_w = dot(every_share(grad_slots, True), every_share(active, False), 0, 0)
-    expert_grads = jnp.concatenate([grad_in_w.astype(BF), grad_down_w.astype(BF)], axis=1)
-    two_back = after(two_back, expert_grads)
-    back_two = lax.psum(gathered_rows(two_back), "tp").astype(F32)
+    expert_grads, back_two_part = expert_grads_of(
+        8,
+        ctx_count,
+        experts,
+        share,
+        part,
+        two_slots,
+        grad_slots,
+        grad_gu,
+        active,
+        after(back_two_slots, *mlp_back),
+        place_mlp,
+    )
+    back_two = lax.psum(back_two_part, "tp").astype(F32)
     grads_got = {0: expert_grads[:part]}
 
     def grad_moves(ks):
@@ -930,51 +1189,22 @@
 
     output = relative((resid + mlp_total).astype(BF))
 
-    def both(x):
-        return jnp.concatenate([x, exchange(x, 1)], axis=0)
-
-    def both_cut(x):
-        sides = [
-            jnp.concatenate([x[:, j * part : (j + 1) * part] for j in range(side, group, 2)], axis=1)
-            for side in range(2)
-        ]
-        return jnp.concatenate([sides[0], exchange(sides[1], 1)], axis=0)
-
-    def reduced(x, bits, kind=BF):
-        axes = sorted(bits)[::-1]
-        x = x.reshape((2,) * len(bits) + (-1, x.shape[1]))
-        for bit in bits:
-            at = axes.index(bit)
-            keep = lax.index_in_dim(x, 0, at, False).astype(F32)
-            got = exchange(lax.index_in_dim(x, 1, at, False), 1 << bit).astype(F32)
-            axes.remove(bit)
-            x = keep + got
-            if axes:
-                x = x.astype(kind)
-        return x
-
     upper = list(range(1, bits_of(group)))
-
-    grad_outw = dot(both_cut(grad_branch), both(mixed), 0, 0).astype(BF)
-    grad_qkvw = dot(both_cut(hidden_one), both(grad_qkv), 0, 0).astype(BF)
-    grad_attnw = jnp.concatenate([grad_qkvw, grad_outw], axis=1)
-    grad_attnw = reduce_grads(7, ctx_count, upper, part, grad_attnw)
-
-    def planes(first, count):
-        cut = grad_attnw[:, first * head_width : (first + count) * head_width]
-        return cut.reshape(part, count, head_width)
-
-    def gain_sum(x):
-        return reduced(x.reshape(width, 1), [0] + upper, F32).reshape(part)
+    grad_attnw = attn_grads(
+        7, ctx_count, upper, part, head_width, hidden_one, grad_branch, grad_qkv, mixed
+    )
+    grad_query_w, grad_kv_w, grad_out_w = lay_out(
+        grad_attnw, (w_query.shape, w_kv.shape, w_out_attn.shape)
+    )
+    gain_grads = gain_sums(9, ctx_count, group, [gain_one_grad, gain_two_grad])
 
     return (
         output[None],
         grad_tokens[None],
-        gain_sum(gain_one_grad),
-        gain_sum(gain_two_grad),
-        planes(attn_experts, 2),
-        planes(0, attn_experts),
-        planes(attn_experts + 2, attn_experts),
+        *gain_grads,
+        grad_kv_w,
+        grad_query_w,
+        grad_out_w,
         *spread_grads([grads_got[k] for k in range(experts)], expert_me, w_in.shape, w_down.shape),
     )
 

time: 741 us -> 672 us (0.907)
  Pallas kernels: 430 us -> 470 us
  matrix products: 94.4 us -> 58.4 us
  waiting for transfers between devices: 37.3 us -> 7.82 us
  other arithmetic: 54.5 us -> 36.4 us
  local copies, waits for them, and re-layouts: 76.3 us -> 64.7 us
  starting transfers between devices: 21.9 us -> 12.2 us
    pallas_call x3 -> x5, Pallas kernels: 151 us -> 226 us  [the longest x1 97.5 us: attn_grads(): pl.pallas_call(functools.partial(attn_grads_kernel, ctx_count, bits, part...]
    pallas_call x4 -> x3, Pallas kernels: 196 us -> 161 us  [move(): pl.pallas_call(functools.partial(move_kernel, ctx_count, moves, plain + [...]
    dot_general x21 -> x16, matrix products: 90.5 us -> 56.4 us  [dot(): lax.dot_general(a, b, (((ca,), (cb,)), ((), ())), preferred_element_type=...]
    ppermute x25 -> x8, waiting for transfers between devices: 37.2 us -> 6.65 us  [swap(): return lax.ppermute(x, axes, [(i, i ^ mask) for i in range(count)])]
    concatenate x7 -> x0, other arithmetic: 17.3 us -> none  [the longest x1 7.87 us: layer(): grad_attnw = jnp.concatenate([grad_qkvw, grad_outw], axis=1)]
    ppermute x25 -> x8, starting transfers between devices: 21.8 us -> 11.7 us  [swap(): return lax.ppermute(x, axes, [(i, i ^ mask) for i in range(count)])]
    reshape x3 -> x0, local copies, waits for them, and re-layouts: 9.45 us -> none  [planes(): return cut.reshape(part, count, head_width)]
    unnamed x187 -> x125, local copies, waits for them, and re-layouts: 26.2 us -> 27.6 us
  transfers between devices with their start and end apart: 29 -> 12, of which waited for: 8 -> 4; matrix products, arithmetic and copies ran while one was open for 23% -> 16% of each run, Pallas kernels for 46% -> 41%
where the time goes in v3:
time: 672 us; the launch traced here: 665 us
  Pallas kernels  470 us (70%)
  local copies, waits for them, and re-layouts  64.7 us (10%)
  matrix products  58.4 us (9%)
  other arithmetic  36.4 us (5%)
  between operations  15.1 us (2%)
  starting transfers between devices  12.2 us (2%)
  waiting for transfers between devices  7.82 us (1%)
    pallas_call x3, Pallas kernels, move(): pl.pallas_call(functools.partial(move_kernel, ctx_count, moves, plain + [...  161 us
    pallas_call x1, Pallas kernels, attn_grads(): pl.pallas_call(functools.partial(attn_grads_kernel, ctx_count, bits, part...  97.5 us
    pallas_call x1, Pallas kernels, front(): pl.pallas_call(functools.partial(front_kernel, ctx_count, moves, marks, n...  80 us
    pallas_call x1, Pallas kernels, attend_back(): pl.pallas_call(functools.partial(attend_back_kernel, ctx_count, moves, li...  71.9 us
    dot_general x16, matrix products, dot(): lax.dot_general(a, b, (((ca,), (cb,)), ((), ())), preferred_element_type=...  56.4 us
    pallas_call x1, Pallas kernels, expert_grads_of(): pl.pallas_call(functools.partial(expert_grads_kernel, ctx_count, experts,...  36.6 us
    unnamed x125, local copies, waits for them, and re-layouts  27.6 us
    dynamic_slice x5, local copies, waits for them, and re-layouts, piece(): return lax.dynamic_slice_in_dim(x, index * size, size, axis)  13.9 us
  transfers between devices with their start and end apart: 12, of which 4 were waited for; matrix products, arithmetic and copies ran while one was open for 16% of the time, Pallas kernels for 41%

profile of v3, /device:TPU:0, one launch (start us, length us, event | category | flops | bytes accessed | tf_op | source)
XLA Modules:
  0.0 664.9 jit_solution(7926910147232234613)
XLA Ops:
  7.2 1.5 copy.91
  12.6 2.9 collective-permute-start
  15.5 1.5 collective-permute-start.1
  17.2 7.3 %constant_dynamic-slice_fusion.13 = (bf16[256,1,1408]{2,1,0:T(2,128)(2,1)}, bf16[256,1,1408]{2,1,0:T(2,128)(2,1)}, bf16[256,1,1408]{2,1,0:T(2,128)(2,1)}, bf16[256,1,1408]{2,1,0:T(2,128)(2,1)}) fusion(bf16[256,4,1408]{2,1,0:T(4,128)(2,1)S(1)} %copy-done.4, s32[]{:T(128)S(6)} %select_n.169, s32[]{:T(128)S(6)} %select_n.168, s32[]{:T(128)S(6)} %select_n.167, ...), kind=kLoop, calls=%fused_computation.180 | loop fusion | bytes 5767184 | tf_op jit(solution)/shard_map/dynamic_slice | solution.py:896
  24.5 5.6 constant_dynamic-slice_fusion.14
  37.1 1.5 convert_multiply_fusion.normed_ref
  41.0 3.3 fusion.55
  54.0 3.2 copy_bitcast_fusion.2
  61.3 1.4 pad_maximum_fusion.12.sin_ref
  62.8 1.5 pad_maximum_fusion.1.refs_3_
  65.2 1.5 pad_maximum_fusion.2.refs_4_.refs_0_
  67.6 1.5 pad_maximum_fusion.3.refs_5_.refs_1_
  69.6 1.5 pad_maximum_fusion.4.refs_2_.refs_0_
  71.1 1.6 collective-permute-done.refs_1_
  72.7 1.5 collective-permute-done.1.refs_2_
  74.2 1.6 slice.151.cos_ref
  79.1 80.0 %front.1 = (bf16[128,512]{1,0:T(8,128)(2,1)}, bf16[256,2048]{1,0:T(8,128)(2,1)}, bf16[256,3072]{1,0:T(8,128)(2,1)}, bf16[1024,1024]{1,0:T(8,128)(2,1)}, bf16[256...) custom-call(f32[256,2048]{1,0:T(8,128)} %convert_multiply_fusion.nor, ...), custom_call_target="tpu_custom_call" | custom-call | tf_op jit(solution)/shard_map/front/pallas_call | solution.py:668
  160.3 2.5 collective-permute-start.4
  165.4 57.6 %weights_two.1 = (bf16[2048,2816]{1,0:T(8,128)(2,1)}, bf16[2048,1408]{1,0:T(8,128)(2,1)}) custom-call(bf16[256,4224]{1,0:T(8,128)(2,1)} %pad_maximum_fusion.2.refs_4_.refs_0_, bf16[256,4224]{1,0:T(8,128)(2,1)} %pad_maximum_fusion.3.refs_5_.refs_1_, ...), custom_call_target="tpu_custom_call", output_to_operand_aliasing={{0}: (4, {}), {1}: (3, {})} | custom-call | tf_op jit(solution)/shard_map/weights_two/pallas_call | solution.py:175
  224.8 1.7 multiply_reduce_fusion
  232.0 54.5 %dispatch.1 = (bf16[2048,2816]{1,0:T(8,128)(2,1)}, bf16[2048,1408]{1,0:T(8,128)(2,1)}, bf16[576,2048]{1,0:T(8,128)(2,1)}) custom-call(bf16[256,4224]{1,0:T(8,128)(2,1)} %pad_maximum_fusion.4.refs_2_.refs_0_, bf16[144,2048]{1,0:T(8,128)(2,1)} %convolution_convert_fusion.5.refs_1_, ...), custom_call_target="tpu_custom_call", output_to_operand_aliasing={{0}: (5, {}), {1}: (6, {})} | custom-call | tf_op jit(solution)/shard_map/dispatch/pallas_call | solution.py:175
  286.5 11.0 %fusion.101 = f32[576,2816]{1,0:T(8,128)S(1)} fusion(bf16[576,2048]{1,0:T(8,128)(2,1)} %get-tuple-element.89.two_ref, bf16[2048,2816]{1,0:T(8,128)(2,1)} %get-tuple-element.90), kind=kOutput, calls=%fused_computation.235 | convolution fusion | flops 6643777536 | bytes 20381696 | tf_op jit(solution)/shard_map/dot_general | solution.py:32
  298.4 2.4 copy-done.10
  300.8 2.3 copy-done.3
  303.1 4.1 convolution_convert_fusion.1
  307.2 1.5 fusion.93
  309.2 1.5 collective-permute-start.6
  310.7 1.5 collective-permute-start.7
  312.2 9.8 %multiply_convert_fusion.1 = (bf16[576,1408]{1,0:T(8,128)(2,1)S(1)}, bf16[576,1408]{1,0:T(8,128)(2,1)S(1)}) fusion(f32[576,2816]{1,0:T(8,128)} %copy-done.10, f32[576]{0:T(1024)S(1)} %select_reduce_fusion.3, bf16[576,2048]{1,0:T(8,128)(2,1)} %all-gather.2.cloned.1.call-done.down_ref, bf16[2048,1408]{1,0:T(8,128)(2,1)} %get-tuple-element.91), kind=kOutput, calls=%fused_computation.10 | convolution fusion | flops 3333242880 | bytes 17860864 | tf_op jit(solution)/shard_map/dot_general | solution.py:32
  322.0 10.9 %convolution_convert_fusion.back_ref = bf16[576,2048]{1,0:T(8,128)(2,1)} fusion(bf16[2048,2816]{1,0:T(8,128)(2,1)} %get-tuple-element.90, bf16[576,1408]{1,0:T(8,128)(2,1)S(1)} %get-tuple-element.126, bf16[576,1408]{1,0:T(8,128)(2,1)S(1)} %get-tuple-element.125), kind=kOutput, calls=%fused_computation.17 | convolution fusion | flops 6651445248 | bytes 17137664 | tf_op jit(solution)/shard_map/dot_general | solution.py:32
  332.9 1.9 pad_maximum_fusion.gu_ref
  334.9 3.6 collective-permute-done.7
  338.4 36.6 %expert_grads.1 = (bf16[1024,4224]{1,0:T(8,128)(2,1)}, bf16[256,2048]{1,0:T(8,128)(2,1)}) custom-call(bf16[576,2048]{1,0:T(8,128)(2,1)} %get-tuple-element.89.two_ref, bf16[576,2048]{1,0:T(8,128)(2,1)} %all-gather.2.cloned.1.call-done.down_ref, bf16[576,2816]{1,0:T(8,128)(2,1)} %pad_maximum_fusion.gu_ref, bf16[576,1408]{1,0:T(8,128)(2,1)} %copy-done.9, ...), custom_call_target="tpu_custom_call" | custom-call | tf_op jit(solution)/shard_map/expert_grads/pallas_call | solution.py:492
  375.6 2.2 copy.99
  377.8 48.4 %grads_near.1 = (bf16[256,4224]{1,0:T(8,128)(2,1)}, bf16[256,4224]{1,0:T(8,128)(2,1)}) custom-call(bf16[1024,4224]{1,0:T(8,128)(2,1)} %get-tuple-element.95.refs_0_), custom_call_target="tpu_custom_call" | custom-call | tf_op jit(solution)/shard_map/grads_near/pallas_call | solution.py:175
  427.3 2.2 fusion.34
  431.2 6.7 %fusion.9.grad_ref = bf16[256,2048]{1,0:T(8,128)(2,1)} fusion(f32[256,2048]{1,0:T(8,128)S(1)} %bitcast.160, bf16[256,2048]{1,0:T(8,128)(2,1)S(1)} %fusion.92.branch_ref, bf16[2048,5120]{1,0:T(8,128)(2,1)} %get-tuple-element.99), kind=kOutput, calls=%fused_computation.25 | convolution fusion | flops 2148532224 | bytes 12582912 | tf_op jit(solution)/shard_map/dot_general | solution.py:32
  441.4 71.9 %attend_back.1 = (bf16[256,3072]{1,0:T(8,128)(2,1)}, bf16[256,4224]{1,0:T(8,128)(2,1)}) custom-call(bf16[256,3072]{1,0:T(8,128)(2,1)} %get-tuple-element.104.qkv_ref, bf16[1024,1024]{1,0:T(8,128)(2,1)} %get-tuple-element.105.kv_ref, bf16[4,144,256]{2,1,0:T(8,128)(2,1)} %get-tuple-element.66.place_ref, s32[4,144,1]{2,1,0:T(8,128)} %copy.79.segq_ref, ...), custom_call_target="tpu_custom_call" | custom-call | tf_op jit(solution)/shard_map/attend_back/pallas_call | solution.py:791
  513.3 9.5 %fusion.13 = bf16[256,2048]{1,0:T(8,128)(2,1)} fusion(bf16[256,3072]{1,0:T(8,128)(2,1)} %get-tuple-element.106.qkv_ref, bf16[2048,5120]{1,0:T(8,128)(2,1)} %get-tuple-element.99), kind=kOutput, calls=%fused_computation.27 | convolution fusion | flops 3221749760 | bytes 15204352 | tf_op jit(solution)/shard_map/dot_general | solution.py:32
  524.0 2.0 fusion.12
  526.0 3.1 slice.192.refs_0_
  529.1 97.5 %attn_grads.1.grad_ref = f32[256,5120]{1,0:T(8,128)} custom-call(bf16[256,2048]{1,0:T(8,128)(2,1)} %get-tuple-element.107.hidden_ref, bf16[256,2048]{1,0:T(8,128)(2,1)} %copy-done.17, bf16[256,3072]{1,0:T(8,128)(2,1)} %get-tuple-element.106.qkv_ref, bf16[256,2048]{1,0:T(8,128)(2,1)} %get-tuple-element.108.mixed_ref), custom_call_target="tpu_custom_call" | custom-call | tf_op jit(solution)/shard_map/attn_grads/pallas_call | solution.py:316
  626.6 5.4 lay_out.1
  632.0 11.9 %spread_grads.1 = (f32[256,4,2,1408]{3,2,1,0:T(2,128)}, f32[256,4,1408]{2,1,0:T(4,128)}) custom-call(s32[1]{0:T(128)} %bitcast.56.me_ref, bf16[256,4224]{1,0:T(8,128)(2,1)} %slice.192.refs_0_, bf16[256,4224]{1,0:T(8,128)(2,1)} %get-tuple-element.96.refs_1_, bf16[256,4224]{1,0:T(8,128)(2,1)} %get-tuple-element.97.refs_2_, ...), custom_call_target="tpu_custom_call" | custom-call | tf_op jit(solution)/shard_map/spread_grads/pallas_call | solution.py:826
  643.9 2.0 fusion.35
  646.1 3.0 fusion.30
  650.5 6.3 gain_sums.1
  656.8 1.3 fusion.100
  (219 shorter events, 53.9 us)
Async XLA Ops:
  7.2 217.6 %all-reduce.8.cloned.1.call-start = ((), (), s32[]{:S(2)}) async-start(), calls=%async_computation | async-start | bytes 2097152 | tf_op jit(solution)/shard_map/psum | solution.py:1097
  7.2 2.6 copy-start.28
  10.7 6.4 copy-start.40
  10.7 6.4 copy-start.41
  10.7 6.5 copy-start.4
  12.6 60.1 %collective-permute-start = (bf16[256,5120]{1,0:T(8,128)(2,1)}, bf16[256,5120]{1,0:T(8,128)(2,1)}, u32[]{:S(2)}, u32[]{:S(2)}) collective-permute-start(bf16[256,5120]{1,0:T(8,128)(2,1)} %constant_dynamic-update-slice_fusion.refs_0_), channel_id=1, source_target_pairs={{0,16},{4,20},{8,24},{12,28},{16,0},{20,4},{24,8},{28,12},{1,17},{... | collective-permute-start | bytes 7864328 | tf_op jit(solution)/shard_map/ppermute | solution.py:40
  15.5 58.6 %collective-permute-start.1 = (bf16[256,5120]{1,0:T(8,128)(2,1)}, bf16[256,5120]{1,0:T(8,128)(2,1)}, u32[]{:S(2)}, u32[]{:S(2)}) collective-permute-start(bf16[256,5120]{1,0:T(8,128)(2,1)} %constant_dynamic-update-slice_fusion.refs_0_), channel_id=1, source_target_pairs={{0,8},{4,12},{8,0},{12,4},{16,24},{20,28},{24,16},{28,20},{1,9},{5... | collective-permute-start | bytes 7864328 | tf_op jit(solution)/shard_map/ppermute | solution.py:40
  36.8 2.3 copy-start.37
  38.6 6.7 %copy-start.35 = (s32[1,256,2]{1,2,0:T(2,128)S(1)}, s32[1,256,2]{1,2,0:T(2,128)}, u32[]{:S(2)}) copy-start(s32[1,256,2]{1,2,0:T(2,128)} %param.23) | copy-start | bytes 6148
  38.6 6.9 %copy-start.36 = (s32[1,256,2]{1,2,0:T(2,128)S(1)}, s32[1,256,2]{1,2,0:T(2,128)}, u32[]{:S(2)}) copy-start(s32[1,256,2]{1,2,0:T(2,128)} %param.25) | copy-start | bytes 6148
  38.6 7.6 %copy-start.38 = (f32[1,256,2]{1,2,0:T(2,128)S(1)}, f32[1,256,2]{1,2,0:T(2,128)}, u32[]{:S(2)}) copy-start(f32[1,256,2]{1,2,0:T(2,128)} %param.24) | copy-start | bytes 6148
  38.6 7.9 %copy-start.39 = (f32[1,256,2]{1,2,0:T(2,128)S(1)}, f32[1,256,2]{1,2,0:T(2,128)}, u32[]{:S(2)}) copy-start(f32[1,256,2]{1,2,0:T(2,128)} %param.26) | copy-start | bytes 6148
  39.8 10.5 %copy-start.31 = (s32[1024]{0:T(1024)}, s32[1024]{0:T(1024)S(1)}, u32[]{:S(2)}) copy-start(s32[1024]{0:T(1024)S(1)} %get-tuple-element.184) | copy-start | bytes 12292
  39.8 10.5 %copy-start.32 = (s32[1024]{0:T(1024)}, s32[1024]{0:T(1024)S(1)}, u32[]{:S(2)}) copy-start(s32[1024]{0:T(1024)S(1)} %get-tuple-element.185) | copy-start | bytes 12292
  53.1 376.5 %copy-start.5 = (bf16[256,2048]{1,0:T(8,128)(2,1)}, bf16[256,2048]{1,0:T(8,128)(2,1)S(1)}, u32[]{:S(2)}) copy-start(bf16[256,2048]{1,0:T(8,128)(2,1)S(1)} %bitcast_dynamic-update-slice_fusion) | copy-start | bytes 3145732
  53.9 3.2 copy-start.11
  53.9 3.2 copy-start.12
  58.2 4.5 copy-start.16
  58.2 4.5 copy-start.20
  59.1 169.8 %copy-start.22 = (bf16[4,144,256]{2,1,0:T(8,128)(2,1)}, bf16[4,144,256]{2,1,0:T(8,128)(2,1)S(1)}, u32[]{:S(2)}) copy-start(bf16[4,144,256]{2,1,0:T(8,128)(2,1)S(1)} %get-tuple-element.77.place_ref) | copy-start | bytes 884740
  62.7 13.0 %copy-start.21 = (f32[1024,128]{1,0:T(8,128)}, f32[1024,128]{1,0:T(8,128)S(1)}, u32[]{:S(2)}) copy-start(f32[1024,128]{1,0:T(8,128)S(1)} %pad_maximum_fusion.12.sin_ref) | copy-start | bytes 1572868
  62.7 2.3 copy-start.15
  62.8 2.5 copy-start.18
  65.2 2.0 copy-start.14
  65.2 2.3 copy-start.19
  67.6 2.0 copy-start.13
  79.1 81.0 %copy-start.30 = (bf16[256,512]{1,0:T(8,128)(2,1)S(1)}, bf16[256,512]{1,0:T(8,128)(2,1)}, u32[]{:S(2)}) copy-start(bf16[256,512]{1,0:T(8,128)(2,1)} %get-tuple-element.142) | copy-start | bytes 786436
  159.1 5.5 copy-start.29
  159.1 153.1 %all-gather.2.cloned.1.call-start = ((), (), s32[]{:S(2)}) async-start(), calls=%async_computation.1 | async-start | bytes 2949120 | tf_op jit(solution)/shard_map/all_gather | solution.py:1083
  160.3 63.0 %collective-permute-start.4 = (bf16[144,640]{1,0:T(8,128)(2,1)S(1)}, bf16[144,640]{1,0:T(8,128)(2,1)S(1)}, u32[]{:S(2)}, u32[]{:S(2)}) collective-permute-start(bf16[144,640]{1,0:T(8,128)(2,1)S(1)} %convolution_convert_fusion.6), channel_id=1, source_target_pairs={{0,24},{4,28},{8,16},{12,20},{16,8},{20,12},{24,0},{28,4},{1,25},{... | collective-permute-start | bytes 552968 | tf_op jit(solution)/shard_map/ppermute | solution.py:40
  163.9 59.3 %collective-permute-start.3 = (bf16[144,640]{1,0:T(8,128)(2,1)S(1)}, bf16[144,640]{1,0:T(8,128)(2,1)S(1)}, u32[]{:S(2)}, u32[]{:S(2)}) collective-permute-start(bf16[144,640]{1,0:T(8,128)(2,1)S(1)} %convolution_convert_fusion.7), channel_id=1, source_target_pairs={{0,16},{4,20},{8,24},{12,28},{16,0},{20,4},{24,8},{28,12},{1,17},{... | collective-permute-start | bytes 552968 | tf_op jit(solution)/shard_map/ppermute | solution.py:40
  164.8 58.5 %collective-permute-start.2 = (bf16[144,640]{1,0:T(8,128)(2,1)S(1)}, bf16[144,640]{1,0:T(8,128)(2,1)S(1)}, u32[]{:S(2)}, u32[]{:S(2)}) collective-permute-start(bf16[144,640]{1,0:T(8,128)(2,1)S(1)} %convolution_convert_fusion.8), channel_id=1, source_target_pairs={{0,8},{4,12},{8,0},{12,4},{16,24},{20,28},{24,16},{28,20},{1,9},{5... | collective-permute-start | bytes 552968 | tf_op jit(solution)/shard_map/ppermute | solution.py:40
  224.1 203.2 %all-reduce.10.cloned.1.call-start = ((), (), s32[]{:S(2)}) async-start(), calls=%async_computation.2 | async-start | bytes 2097152 | tf_op jit(solution)/shard_map/psum | solution.py:1145
  297.5 3.3 copy-start.10
  297.5 5.6 copy-start.3
  300.8 6.4 copy-start.9
  308.7 26.2 %collective-permute-start.5 = (bf16[144,2048]{1,0:T(8,128)(2,1)}, bf16[144,2048]{1,0:T(8,128)(2,1)}, u32[]{:S(2)}, u32[]{:S(2)}) collective-permute-start(bf16[144,2048]{1,0:T(8,128)(2,1)} %get-tuple-element.137), channel_id=1, source_target_pairs={{0,8},{4,12},{8,0},{12,4},{16,24},{20,28},{24,16},{28,20},{1,9},{5... | collective-permute-start | bytes 1769480 | tf_op jit(solution)/shard_map/ppermute | solution.py:40
  309.2 25.6 %collective-permute-start.6 = (bf16[144,2048]{1,0:T(8,128)(2,1)}, bf16[144,2048]{1,0:T(8,128)(2,1)}, u32[]{:S(2)}, u32[]{:S(2)}) collective-permute-start(bf16[144,2048]{1,0:T(8,128)(2,1)} %get-tuple-element.136), channel_id=1, source_target_pairs={{0,16},{4,20},{8,24},{12,28},{16,0},{20,4},{24,8},{28,12},{1,17},{... | collective-permute-start | bytes 1769480 | tf_op jit(solution)/shard_map/ppermute | solution.py:40
  310.7 27.7 %collective-permute-start.7 = (bf16[144,2048]{1,0:T(8,128)(2,1)}, bf16[144,2048]{1,0:T(8,128)(2,1)}, u32[]{:S(2)}, u32[]{:S(2)}) collective-permute-start(bf16[144,2048]{1,0:T(8,128)(2,1)} %get-tuple-element.135), channel_id=1, source_target_pairs={{0,24},{4,28},{8,16},{12,20},{16,8},{20,12},{24,0},{28,4},{1,25},{... | collective-permute-start | bytes 1769480 | tf_op jit(solution)/shard_map/ppermute | solution.py:40
  375.1 268.8 %all-reduce.12.cloned.1.call-start = ((), (), s32[]{:S(2)}) async-start(), calls=%async_computation.3 | async-start | bytes 4194304 | tf_op jit(solution)/shard_map/psum | solution.py:1184
  427.3 2.3 copy-start.7
  430.7 7.3 %copy-start.17 = (bf16[256,2048]{1,0:T(8,128)(2,1)}, bf16[256,2048]{1,0:T(8,128)(2,1)S(1)}, u32[]{:S(2)}) copy-start(bf16[256,2048]{1,0:T(8,128)(2,1)S(1)} %fusion.92.branch_ref) | copy-start | bytes 3145732
  632.0 11.9 %copy-start = (f32[256,2048]{1,0:T(8,128)S(1)}, f32[256,2048]{1,0:T(8,128)}, u32[]{:S(2)}) copy-start(f32[256,2048]{1,0:T(8,128)} %convert_multiply_fusion.normed_ref) | copy-start | bytes 6291460
  643.9 2.0 copy-start.2
  643.9 2.1 copy-start.6
  643.9 2.2 copy-start.8
  649.4 8.8 %copy-start.34 = (bf16[256,2048]{1,0:T(8,128)(2,1)}, bf16[256,2048]{1,0:T(8,128)(2,1)S(1)}, u32[]{:S(2)}) copy-start(bf16[256,2048]{1,0:T(8,128)(2,1)S(1)} %dynamic-slice_dynamic-update-slice_fusion.8) | copy-start | bytes 3145732
  649.7 8.5 %copy-start.33 = (bf16[256,2048]{1,0:T(8,128)(2,1)}, bf16[256,2048]{1,0:T(8,128)(2,1)S(1)}, u32[]{:S(2)}) copy-start(bf16[256,2048]{1,0:T(8,128)(2,1)S(1)} %dynamic-slice_dynamic-update-slice_fusion) | copy-start | bytes 3145732
  (6 other events, 8.7 us)
Sparse Core Ops, SparseCore 0:
  159.2 53.0 all-reduce.7
  224.3 50.8 all-gather.1
  375.2 52.0 all-reduce.9
  526.1 85.8 all-reduce.11

commit v4 on v3

--- a/solution.py
+++ b/solution.py
@@ -54,6 +54,8 @@
 
 
 def peer(ctx_count, mask):
+    if mask < 0:
+        return {"tp": flip(lax.axis_index("tp"), -mask)}
     return {
         "fsdp": flip(lax.axis_index("fsdp"), mask // ctx_count),
         "ctx": flip(lax.axis_index("ctx"), mask % ctx_count),
@@ -69,21 +71,28 @@
     pl.semaphore_wait(barrier, len(masks))
 
 
+def run_cols(size, flips=0):
+    return pl.ds(pl.multiple_of(flip(lax.axis_index("tp"), flips) * size, size), size)
+
+
 def window(ref, rows, cols):
     if cols is None:
         return ref.at[pl.ds(rows[0], rows[1])]
+    if cols[0] == "tp":
+        return ref.at[pl.ds(rows[0], rows[1]), run_cols(cols[1])]
     return ref.at[pl.ds(rows[0], rows[1]), pl.ds(cols[0], cols[1])]
 
 
 class Moves:
-    def __init__(self, ctx_count, moves, arrays, send, recv, bounces=()):
+    def __init__(self, ctx_count, moves, arrays, send, recv, bounces=(), base=0):
         self.moves = moves
         self.onward = {}
         bounces = list(bounces)
         self.copies = []
         self.place = {m[1]: i for i, m in enumerate(moves)}
         self.started, self.came = set(), set()
-        for i, (source, target, mask, _) in enumerate(moves):
+        for at, (source, target, mask, _) in enumerate(moves):
+            i = base + at
             src = window(arrays[source[0]], *source[1:])
             dst = window(arrays[target[0]], *target[1:])
             if mask:
@@ -100,7 +109,7 @@
             else:
                 bounce = bounces.pop(0)
                 copy = pltpu.make_async_copy(src, bounce, recv.at[i])
-                self.onward[i] = pltpu.make_async_copy(bounce, dst, send.at[i])
+                self.onward[at] = pltpu.make_async_copy(bounce, dst, send.at[i])
             self.copies.append(copy)
 
     def start(self, i):
@@ -124,7 +133,8 @@
             else:
                 self.copies[i].wait_recv()
 
-    def settle(self, count, first=0):
+    def settle(self, count=None, first=0):
+        count = len(self.moves) if count is None else count
         for i in range(first, count):
             if i in self.onward:
                 self.await_one(i)
@@ -136,7 +146,7 @@
             self.await_one(i)
 
     def finish(self):
-        self.settle(len(self.moves))
+        self.settle()
         for i in range(len(self.moves)):
             if i in self.onward:
                 self.onward[i].wait()
@@ -331,6 +341,35 @@
     )(hidden, branch, qkv, mixed)
 
 
+def turn_kernel(me_ref, *refs):
+    half = len(refs) // 2
+    for given, made in zip(refs[:half], refs[half:]):
+        made[...] = given[...]
+
+
+def in_order(me, arrays, group):
+    rows, width = arrays[0].shape
+    part = width // group
+    if part % HD:
+        return [
+            jnp.concatenate(
+                [lax.dynamic_slice_in_dim(x, (me ^ j) * part, part, 1) for j in range(group)], axis=1
+            )
+            for x in arrays
+        ]
+    return pl.pallas_call(
+        turn_kernel,
+        grid_spec=pltpu.PrefetchScalarGridSpec(
+            num_scalar_prefetch=1,
+            grid=(group,),
+            in_specs=[pl.BlockSpec((rows, part), lambda j, m: (0, m[0] ^ j))] * len(arrays),
+            out_specs=[pl.BlockSpec((rows, part), lambda j, m: (0, j))] * len(arrays),
+        ),
+        out_shape=[jax.ShapeDtypeStruct((rows, width), x.dtype) for x in arrays],
+        name="in_order",
+    )(me.astype(jnp.int32).reshape(1), *arrays)
+
+
 def lay_kernel(grad_ref, *out_refs):
     at = 0
     for ref in out_refs:
@@ -395,122 +434,254 @@
     return [total[i] for i in range(count)]
 
 
-def expert_grads_kernel(
+def chunks(total, size):
+    return [(at, min(size, total - at)) for at in range(0, total, size)]
+
+
+def experts_kernel(
     ctx_count,
     experts,
     share,
     part,
-    moves,
-    two_ref,
+    groups,
+    far_names,
+    tokens_ref,
+    branch_ref,
+    gain_ref,
+    place_ref,
+    dy_run_ref,
+    weight_ref,
+    in_ref,
     down_ref,
-    gu_ref,
-    active_ref,
-    back_ref,
-    place_ref,
-    grads_ref,
-    out_ref,
-    back_got,
-    two_out,
-    down_out,
-    two_got,
-    down_got,
-    gu_got,
-    active_got,
-    send,
-    recv,
+    *refs,
 ):
-    slots, width = two_ref.shape
-    units = active_ref.shape[1]
-    room = slots // experts
-    run = Moves(
-        ctx_count,
-        moves,
-        {
-            "two": two_out,
-            "down": down_out,
-            "gu": gu_ref,
-            "active": active_ref,
-            "back": back_ref,
-            "back_got": back_got,
-            "two_got": two_got,
-            "down_got": down_got,
-            "gu_got": gu_got,
-            "active_got": active_got,
-        },
+    far_refs, refs = refs[: len(far_names)], refs[len(far_names) :]
+    grads_in, grads_down, mlp_part, two_part = refs[:4]
+    (
+        win,
+        wdown,
+        two,
+        slots_out,
+        mlp_got,
+        back_out,
+        back_got,
+        gate,
+        up,
+        active,
+        gu,
+        two_out,
+        dy_out,
+        two_got,
+        dy_got,
+        gu_got,
+        active_got,
+        dy_ref,
         send,
         recv,
+    ) = refs[4:]
+    slots, width = two.shape
+    units = active.shape[1]
+    room, run = slots // experts, width // experts
+    arrays = dict(
+        zip(far_names, far_refs),
+        grads_in=grads_in,
+        grads_down=grads_down,
+        win=win,
+        wdown=wdown,
+        dy_run=dy_run_ref,
+        dy=dy_ref,
+        two=two,
+        slots_out=slots_out,
+        mlp_got=mlp_got,
+        back_out=back_out,
+        back_got=back_got,
+        active=active,
+        gu=gu,
+        two_out=two_out,
+        dy_out=dy_out,
+        two_got=two_got,
+        dy_got=dy_got,
+        gu_got=gu_got,
+        active_got=active_got,
+        **{"in": in_ref, "down": down_ref},
     )
-    greet(ctx_count, masks_of(moves))
+    runs, base = {}, 0
+    for name, moves in groups.items():
+        runs[name] = Moves(ctx_count, moves, arrays, send, recv, (), base)
+        base += len(moves)
+    greet(ctx_count, masks_of([m for moves in groups.values() for m in moves]))
+    runs["load_in"].begin()
+    runs["load_down"].begin()
+    runs["far_in"].begin()
+    runs["dy"].begin()
+    dy_ref[:, run_cols(run)] = dy_run_ref[...]
+    x = tokens_ref[...].astype(F32) + branch_ref[...].astype(F32)
+    inverse = lax.rsqrt(jnp.mean(x * x, axis=-1, keepdims=True) + EPSILON)
+    hidden = (x * inverse * gain_ref[...]).astype(BF)
+    for k in range(experts)[::-1]:
+        rows = slice(k * room, (k + 1) * room)
+        picked = dot(place_ref[k], hidden, 1, 0).astype(BF)
+        if k == 0:
+            two[rows] = picked
+            continue
+        for i in range(experts):
+            slots_out[rows, i * run : (i + 1) * run] = picked[:, (i ^ k) * run : ((i ^ k) + 1) * run]
+        runs["slots"].start(k - 1)
+    runs["far_down"].begin()
+    runs["slots"].settle()
     for t in range(1, share):
         rows = slice((t - 1) * slots, t * slots)
         for k in range(experts):
             at = (k * share + t) * part
-            two_out[rows, k * part : (k + 1) * part] = two_ref[:, at : at + part]
-            down_out[rows, k * part : (k + 1) * part] = down_ref[:, at : at + part]
-    run.begin()
-    for i in range(experts - 1, len(moves)):
-        run.await_one(i)
+            two_out[rows, k * part : (k + 1) * part] = two[:, at : at + part]
+    runs["share_two"].begin()
+    runs["load_in"].settle()
+    runs["far_in"].settle()
+    weight = weight_ref[...]
+    for at, size in chunks(units, 256):
+        cols = slice(at, at + size)
+        g = dot(two[...], win[:, cols], 1, 0)
+        u = dot(two[...], win[:, units + at : units + at + size], 1, 0)
+        silu = g * (1.0 / (1.0 + jnp.exp(-g)))
+        active[:, cols] = (silu * u * weight).astype(BF)
+        gate[:, cols] = g.astype(BF)
+        up[:, cols] = u.astype(BF)
+    runs["share_active"].begin()
+    runs["load_down"].settle()
+    runs["far_down"].settle()
+    runs["slots"].finish()
+    runs["dy"].settle()
+    for t in range(1, share):
+        rows = slice((t - 1) * slots, t * slots)
+        for k in range(experts):
+            at = (k * share + t) * part
+            dy_out[rows, k * part : (k + 1) * part] = dy_ref[:, at : at + part]
+    runs["share_dy"].begin()
+    for i in range(experts):
+        cols = slice(i * run, (i + 1) * run)
+        slots_out[:, cols] = dot(active[...], wdown[cols], 1, 1).astype(BF)
+        for k in range(1, experts):
+            runs["mlp"].start(i * (experts - 1) + k - 1)
+    for at, size in chunks(units, 256):
+        cols = slice(at, at + size)
+        grad = dot(dy_ref[...], wdown[:, cols], 1, 0) * weight
+        g, u = gate[:, cols].astype(F32), up[:, cols].astype(F32)
+        sigmoid = 1.0 / (1.0 + jnp.exp(-g))
+        gu[:, cols] = (grad * u * sigmoid * (1.0 + g * (1.0 - sigmoid))).astype(BF)
+        gu[:, units + at : units + at + size] = (grad * g * sigmoid).astype(BF)
+    runs["share_gu"].begin()
+    for i in range(experts):
+        cols = slice(i * run, (i + 1) * run)
+        back_out[:, cols] = dot(gu[...], win[cols], 1, 1).astype(BF)
+        for k in range(1, experts):
+            runs["back"].start(i * (experts - 1) + k - 1)
+    for name in ("dy", "far_in", "far_down", "share_two", "share_dy", "share_active", "share_gu"):
+        runs[name].finish()
     for k in range(experts):
-        rows = pl.ds(k * part, part)
-        own, other = slice(k * share * part, (k * share + 1) * part), slice(k * part, (k + 1) * part)
-        for cols, left, left_got, right, right_got in (
-            (pl.ds(0, 2 * units), two_ref, two_got, gu_ref, gu_got),
-            (pl.ds(2 * units, units), down_ref, down_got, active_ref, active_got),
+        rows = slice(k * part, (k + 1) * part)
+        own = slice(k * share * part, (k * share + 1) * part)
+        for out, left, left_got, right, right_got in (
+            (win, two, two_got, gu, gu_got),
+            (wdown, dy_ref, dy_got, active, active_got),
         ):
-            total = dot(left[:, own], right[...], 0, 0)
-            if share > 1:
-                total = total + dot(left_got[:, other], right_got[...], 0, 0)
-            grads_ref[rows, cols] = total.astype(BF)
-    run.finish()
-    run_of = width // experts
-    for i in range(experts):
-        total = dot(place_ref[0], back_ref[:room, i * run_of : (i + 1) * run_of], 0, 0)
-        for k in range(1, experts):
-            at = (i ^ k) * run_of
-            total = total + dot(
-                place_ref[k], back_got[k * room : (k + 1) * room, at : at + run_of], 0, 0
-            )
-        out_ref[:, i * run_of : (i + 1) * run_of] = total.astype(BF)
-
-
-def expert_grads_of(number, ctx_count, experts, share, part, two, down, gu, active, back, place):
-    slots, width = two.shape
-    room, units = slots // experts, active.shape[1]
-    moves = []
-    for k in range(1, experts):
-        moves.append(
-            (("back", (k * room, room), None), ("back_got", (k * room, room), None), k * share, ())
-        )
-    for t in range(1, share):
-        rows = ((t - 1) * slots, slots)
-        for name in ("gu", "active"):
-            moves.append(((name, (0, slots), None), (name + "_got", rows, None), t, ()))
-        for name in ("two", "down"):
-            moves.append(((name, rows, None), (name + "_got", rows, None), t, ()))
+            for at, size in chunks(right.shape[1], 512):
+                cols = slice(at, at + size)
+                total = dot(left[:, own], right[:, cols], 0, 0)
+                if share > 1:
+                    total = total + dot(left_got[:, rows], right_got[:, cols], 0, 0)
+                out[rows, cols] = total.astype(BF)
+        runs["out"].start(2 * k)
+        runs["out"].start(2 * k + 1)
+    for name, own, got, part_ref in (
+        ("mlp", slots_out, mlp_got, mlp_part),
+        ("back", back_out, back_got, two_part),
+    ):
+        runs[name].settle()
+        for i in range(experts):
+            total = dot(place_ref[0], own[:room, i * run : (i + 1) * run], 0, 0)
+            for k in range(1, experts):
+                at = (i ^ k) * run
+                total = total + dot(
+                    place_ref[k], got[k * room : (k + 1) * room, at : at + run], 0, 0
+                )
+            part_ref[:, i * run : (i + 1) * run] = total.astype(BF)
+        runs[name].finish()
+    runs["out"].finish()
+
+
+def run_experts(
+    number, ctx_count, tp_count, experts, share, part, fetched, far_moves, far, weights, tokens, *small
+):
+    place = small[2]
+    room, rows = place.shape[1:]
+    slots, width = experts * room, tokens.shape[1]
+    units = weights["down"].shape[1]
+    run = width // experts
     others = max(1, share - 1) * slots
+    groups = {
+        "dy": [
+            (("dy_run", (0, slots), None), ("dy", (0, slots), ("tp", run)), -r, ())
+            for r in range(1, tp_count)
+        ],
+        "slots": [
+            (("slots_out", (k * room, room), None), ("two", (k * room, room), None), k * share, ())
+            for k in range(1, experts)
+        ],
+        "load_in": [(("in", r, None), ("win", r, None), None, ()) for r in fetched],
+        "load_down": [(("down", r, None), ("wdown", r, None), None, ()) for r in fetched],
+        "far_in": [m for m in far_moves if m[1][0] == "win"],
+        "far_down": [m for m in far_moves if m[1][0] == "wdown"],
+    }
+    for name in ("two", "dy", "active", "gu"):
+        groups["share_" + name] = []
+        for t in range(1, share):
+            rows_at = ((t - 1) * slots, slots)
+            if name in ("two", "dy"):
+                source = (name + "_out", rows_at, None)
+            else:
+                source = (name, (0, slots), None)
+            groups["share_" + name].append((source, (name + "_got", rows_at, None), t, ()))
+    for name, source in (("mlp", "slots_out"), ("back", "back_out")):
+        groups[name] = []
+        for i in range(experts):
+            for k in range(1, experts):
+                at = ((k * room, room), (i * run, run))
+                groups[name].append(((source, *at), (name + "_got", *at), k * share, ()))
+    groups["out"] = []
+    for k in range(experts):
+        r = (k * part, part)
+        groups["out"].append((("win", r, None), ("grads_in", r, None), None, ()))
+        groups["out"].append((("wdown", r, None), ("grads_down", r, None), None, ()))
+    total = sum(len(moves) for moves in groups.values())
     full = pl.BlockSpec(memory_space=pltpu.VMEM)
+    any_spec = pl.BlockSpec(memory_space=pl.ANY)
     return pl.pallas_call(
-        functools.partial(
-            expert_grads_kernel, ctx_count, experts, share, part, moves
-        ),
+        functools.partial(experts_kernel, ctx_count, experts, share, part, groups, list(far)),
         out_shape=[
-            jax.ShapeDtypeStruct((experts * part, 3 * units), BF),
-            jax.ShapeDtypeStruct((place.shape[2], width), BF),
+            jax.ShapeDtypeStruct((experts * part, 2 * units), BF),
+            jax.ShapeDtypeStruct((experts * part, units), BF),
+            jax.ShapeDtypeStruct((rows, width), BF),
+            jax.ShapeDtypeStruct((rows, width), BF),
         ],
-        in_specs=[full] * 6,
-        out_specs=[full] * 2,
+        in_specs=[full] * 6 + [any_spec] * (2 + len(far)),
+        out_specs=[any_spec] * 2 + [full] * 2,
         scratch_shapes=[
-            pltpu.VMEM((slots, width), BF),
+            pltpu.VMEM((width, 2 * units), BF),
+            pltpu.VMEM((width, units), BF),
+            *[pltpu.VMEM((slots, width), BF)] * 5,
+            *[pltpu.VMEM((slots, units), BF)] * 3,
+            pltpu.VMEM((slots, 2 * units), BF),
             *[pltpu.VMEM((others, experts * part), BF)] * 4,
             pltpu.VMEM((others, 2 * units), BF),
             pltpu.VMEM((others, units), BF),
+            pltpu.VMEM((slots, width), BF),
         ]
-        + [pltpu.SemaphoreType.DMA((len(moves),))] * 2,
+        + [pltpu.SemaphoreType.DMA((total,))] * 2,
         compiler_params=pltpu.CompilerParams(
             collective_id=number, has_side_effects=True, vmem_limit_bytes=VMEM_LIMIT
         ),
-        name="expert_grads",
-    )(two, down, gu, active, back, place)
+        name="experts",
+    )(tokens, *small, weights["in"], weights["down"], *far.values())
 
 
 def head_cols(index):
@@ -546,20 +717,25 @@
     gate_ref,
     segk_ref,
     idxk_ref,
+    dy_ref,
+    ride_ref,
+    place_mlp_ref,
     *refs,
 ):
-    experts, _, rows = place_ref.shape
+    experts, room, rows = place_ref.shape
     width = normed_ref.shape[1]
     wide = heads * HD
     group = width // part
     given, refs = refs[: len(names_in)], refs[len(names_in) :]
-    gains_ref, hidden_ref, qkv_ref, kv_ref, mixed_ref, branch_ref = refs[:6]
-    refs = refs[6:]
-    made, (full, send, recv, *bounces) = refs[: len(names_out)], refs[len(names_out) :]
+    gains_ref, hidden_ref, qkv_ref, kv_ref, mixed_ref, branch_ref, slots_ref = refs[:7]
+    refs = refs[7:]
+    made, (full, picked, send, recv, *bounces) = refs[: len(names_out)], refs[len(names_out) :]
     arrays = {
         "gain_own": gain_ref,
         "gains": gains_ref,
         "full": full,
+        "picked": picked,
+        "slots": slots_ref,
         "qkv": qkv_ref,
         "kv": kv_ref,
         **dict(zip(names_in, given)),
@@ -567,7 +743,14 @@
     }
     greet(ctx_count, masks_of(moves))
     run = Moves(ctx_count, moves, arrays, send, recv, bounces)
-    gains_done, first_done, rest_done, keys_done = marks
+    gains_done, first_done, rest_done, keys_done, dy_done = marks
+    run_of = dy_ref.shape[1] // experts
+    for k in range(experts):
+        rows_at = slice(k * room, (k + 1) * room)
+        side = slots_ref if k == 0 else picked
+        cols = run_cols(run_of, k)
+        side[rows_at, :run_of] = dot(place_mlp_ref[k], dy_ref[:, cols], 1, 0).astype(BF)
+        side[rows_at, run_of:] = dot(place_mlp_ref[k], ride_ref[...], 1, 0).astype(BF)
     run.begin(rest_done)
     gains_ref[:16] = gain_ref[...]
     run.settle(gains_done)
@@ -593,6 +776,8 @@
     run.begin()
     for plane in range(experts):
         project(plane)
+    run.settle(rest_done, first_done)
+    run.start(len(moves) - 1)
     run.settle(keys_done, rest_done)
 
     def step(i, carry):
@@ -614,7 +799,6 @@
         return carry
 
     lax.fori_loop(0, heads * experts, step, 0)
-    run.settle(rest_done, first_done)
     for j in range(group):
         rows_at = slice(j * part, (j + 1) * part)
         branch_ref[:, rows_at] = dot(mixed_ref[...], full[rows_at, (experts + 2) * wide :], 1, 1).astype(BF)
@@ -640,14 +824,15 @@
                 source = ("qkv", (0, rows), (experts * wide, 2 * wide))
                 kv_moves.append((source, target, 1 << bit, ()))
         order = order + order
-    gains_moves, first_moves, rest_moves = moves
+    gains_moves, first_moves, rest_moves, dy_moves = moves
     marks = [len(gains_moves)]
-    for more in (first_moves, rest_moves, kv_moves):
+    for more in (first_moves, rest_moves, kv_moves, dy_moves):
         marks.append(marks[-1] + len(more))
     whole = ("full", (0, width), None)
     landed = tuple(m[1] for m in first_moves + rest_moves if m[1][0] == "full")
     keep = [(whole, ("kept", (0, width), None), None, landed)]
-    moves = gains_moves + first_moves + rest_moves + kv_moves + later + keep
+    moves = gains_moves + first_moves + rest_moves + kv_moves + dy_moves + later + keep
+    slots_shape = (experts * place.shape[1], width // experts + HD)
     names_in, names_out = list(given), [*made, "kept"]
     shapes_out = [*made.values(), (width, full_wide)]
     any_spec = pl.BlockSpec(memory_space=pl.ANY)
@@ -659,6 +844,7 @@
         ((ctx_count * rows, 2 * wide), BF),
         ((rows, experts * wide), BF),
         ((rows, width), BF),
+        (slots_shape, BF),
     ]
     bounces = [
         pltpu.VMEM((source[1][1], (source[2] or (0, given[source[0]].shape[1]))[1]), BF)
@@ -673,7 +859,7 @@
         + [jax.ShapeDtypeStruct(shape, BF) for shape in shapes_out],
         in_specs=[full] * len(small) + [any_spec] * len(names_in),
         out_specs=[full] * len(small_out) + [any_spec] * len(names_out),
-        scratch_shapes=[pltpu.VMEM((width, full_wide), BF)]
+        scratch_shapes=[pltpu.VMEM((width, full_wide), BF), pltpu.VMEM(slots_shape, BF)]
         + [pltpu.SemaphoreType.DMA((len(moves),))] * 2
         + bounces,
         compiler_params=pltpu.CompilerParams(
@@ -690,6 +876,13 @@
     names_in,
     names_out,
     heads,
+    part,
+    tokens_ref,
+    branch_ref,
+    gain_ref,
+    back_ref,
+    dy_ref,
+    gate_ref,
     qkv_ref,
     kv_ref,
     place_ref,
@@ -697,21 +890,45 @@
     idxq_ref,
     segk_ref,
     idxk_ref,
-    grad_ref,
     cos_ref,
     sin_ref,
+    weight_ref,
     *refs,
 ):
     experts, _, rows = place_ref.shape
     keys = kv_ref.shape[0]
+    wide = heads * HD
+    width = tokens_ref.shape[1]
     given, refs = refs[: len(names_in)], refs[len(names_in) :]
-    out_ref = refs[0]
-    made, (dk_acc, dv_acc, total, got, send, recv, pass_send, pass_recv) = refs[1:-8], refs[-8:]
+    out_ref, resid_ref, grad_branch_ref, gain_out_ref, back_one_ref = refs[:5]
+    made, refs = refs[5 : 5 + len(names_out)], refs[5 + len(names_out) :]
+    full, grad_ref, back_acc, dk_acc, dv_acc, total, got, send, recv, pass_send, pass_recv, load = refs
     arrays = {**dict(zip(names_in, given)), **dict(zip(names_out, made))}
     bits = range(bits_of(ctx_count))
     greet(ctx_count, sorted({*masks_of(moves), *[1 << b for b in bits]}))
     run = Moves(ctx_count, moves, arrays, send, recv)
     run.begin()
+    edge = (experts + 2) * wide
+    loads = []
+    for i, cols in enumerate((pl.ds(edge, experts * wide), pl.ds(0, edge))):
+        loads.append(pltpu.make_async_copy(weight_ref.at[:, cols], full.at[:, cols], load.at[i]))
+        loads[-1].start()
+
+    x = tokens_ref[...].astype(F32) + branch_ref[...].astype(F32)
+    inverse = lax.rsqrt(jnp.mean(x * x, axis=-1, keepdims=True) + EPSILON)
+    normed = x * inverse
+    back = back_ref[...].astype(F32)
+    gain_out_ref[...] = jnp.sum(back * normed, axis=0, keepdims=True)
+    scaled = back * gain_ref[...]
+    inner = jnp.mean(scaled * normed, axis=-1, keepdims=True)
+    resid = dy_ref[...].astype(F32) + inverse * (scaled - normed * inner)
+    resid_ref[...] = resid
+    grad_branch_ref[...] = resid.astype(BF)
+    loads[0].wait()
+    for e in range(experts):
+        cols = slice(edge + e * wide, edge + (e + 1) * wide)
+        mixed = dot(grad_branch_ref[...], full[:, cols], 1, 0)
+        grad_ref[:, e * wide : (e + 1) * wide] = (mixed * gate_ref[:, e : e + 1]).astype(BF)
 
     def head_copy(h, bit):
         size = keys >> (bit + 1)
@@ -734,9 +951,9 @@
             total[h, :size] = mine
             head_copy(h, bit + 1).start()
         else:
-            at = experts * heads * HD
+            at = experts * wide
             out_ref[:, at + h * HD : at + (h + 1) * HD] = mine[:, :HD]
-            at += heads * HD
+            at += wide
             out_ref[:, at + h * HD : at + (h + 1) * HD] = mine[:, HD:]
 
     for h in range(heads):
@@ -762,48 +979,73 @@
             dk_acc[...] += dot(grad_scores, slots, 0, 0) * (HD**-0.5)
             top = dq.astype(BF)
             low = (dq - top.astype(F32)).astype(BF)
-            back = dot(place, top, 0, 0) + dot(place, low, 0, 0)
-            out_ref[:, cols] = turn(back, cos_ref[:rows], -sin_ref[:rows]).astype(BF)
+            back_q = dot(place, top, 0, 0) + dot(place, low, 0, 0)
+            out_ref[:, cols] = turn(back_q, cos_ref[:rows], -sin_ref[:rows]).astype(BF)
             return carry
 
         lax.fori_loop(0, experts, step, 0)
         total[h, :, :HD] = turn(dk_acc[...], cos_ref[...], -sin_ref[...]).astype(BF)
         total[h, :, HD:] = dv_acc[...].astype(BF)
         head_copy(h, 0).start()
-        for bit in bits:
-            if h - 1 - bit >= 0:
-                head_sum(h - 1 - bit, bit)
-    for h in range(heads, heads + len(bits)):
-        for bit in bits:
-            if 0 <= h - 1 - bit < heads:
-                head_sum(h - 1 - bit, bit)
+        if h:
+            head_sum(h - 1, 0)
+    head_sum(heads - 1, 0)
+    loads[1].wait()
+    queries = experts * wide
+    for j in range(width // part):
+        rows_at = slice(j * part, (j + 1) * part)
+        back_acc[:, rows_at] = dot(out_ref[:, :queries], full[rows_at, :queries], 1, 1)
+    for bit in bits[1:]:
+        for h in range(heads):
+            head_sum(h, bit)
+    for j in range(width // part):
+        rows_at = slice(j * part, (j + 1) * part)
+        keyed = dot(out_ref[:, queries:], full[rows_at, queries:edge], 1, 1)
+        back_one_ref[:, rows_at] = (back_acc[:, rows_at] + keyed).astype(BF)
     for h in range(heads):
         for bit in bits:
             head_copy(h, bit).wait_send()
     run.finish()
 
 
-def attend_back(number, ctx_count, heads, moves, given, made, qkv, kv, place, *others):
-    rows, keys = qkv.shape[0], kv.shape[0]
+def attend_back(number, ctx_count, heads, part, moves, given, made, weight, *small):
+    tokens, qkv, kv = small[0], small[6], small[7]
+    rows, width = tokens.shape
+    keys = kv.shape[0]
     any_spec = pl.BlockSpec(memory_space=pl.ANY)
     full = pl.BlockSpec(memory_space=pltpu.VMEM)
     passes = heads * bits_of(ctx_count)
-    out, *rest = pl.pallas_call(
-        functools.partial(attend_back_kernel, ctx_count, moves, list(given), list(made), heads),
-        out_shape=[jax.ShapeDtypeStruct(qkv.shape, BF)]
+    small_out = [
+        (qkv.shape, BF),
+        ((rows, width), F32),
+        ((rows, width), BF),
+        ((1, width), F32),
+        ((rows, width), BF),
+    ]
+    out = pl.pallas_call(
+        functools.partial(
+            attend_back_kernel, ctx_count, moves, list(given), list(made), heads, part
+        ),
+        out_shape=[jax.ShapeDtypeStruct(*x) for x in small_out]
         + [jax.ShapeDtypeStruct(shape, BF) for shape in made.values()],
-        in_specs=[full] * (3 + len(others)) + [any_spec] * len(given),
-        out_specs=[full] + [any_spec] * len(made),
-        scratch_shapes=[pltpu.VMEM((keys, HD), F32)] * 2
+        in_specs=[full] * len(small) + [any_spec] * (1 + len(given)),
+        out_specs=[full] * len(small_out) + [any_spec] * len(made),
+        scratch_shapes=[
+            pltpu.VMEM(weight.shape, BF),
+            pltpu.VMEM((rows, weight.shape[1] - qkv.shape[1]), BF),
+            pltpu.VMEM((rows, width), F32),
+        ]
+        + [pltpu.VMEM((keys, HD), F32)] * 2
         + [pltpu.VMEM((heads, keys, 2 * HD), BF)] * 2
         + [pltpu.SemaphoreType.DMA((max(1, len(moves)),))] * 2
-        + [pltpu.SemaphoreType.DMA((passes,))] * 2,
+        + [pltpu.SemaphoreType.DMA((passes,))] * 2
+        + [pltpu.SemaphoreType.DMA((2,))],
         compiler_params=pltpu.CompilerParams(
             collective_id=number, has_side_effects=True, vmem_limit_bytes=VMEM_LIMIT
         ),
         name="attend_back",
-    )(qkv, kv, place, *others, *given.values())
-    return out, dict(zip(made, rest))
+    )(*small, weight, *given.values())
+    return out[: len(small_out)], dict(zip(made, out[len(small_out) :]))
 
 
 def spread_kernel(experts, me_ref, *refs):
@@ -901,9 +1143,6 @@
     def after(x, *events):
         return lax.optimization_barrier((x, *events))[0]
 
-    def relative(x):
-        return jnp.concatenate([piece(x, me ^ j) for j in range(group)], axis=1)
-
     high, second = group // 2, group // 4
 
     qkv_wide = (attn_experts + 2) * head_width
@@ -947,27 +1186,32 @@
     taken_mlp, gate_mlp = places(mlp_routes[0], mlp_gates[0], experts, cap, room)
     mine_first = [expert_me ^ k for k in range(experts)]
     place_mlp = jnp.concatenate([piece(taken_mlp, e, 1, 0) for e in mine_first]).astype(BF)
-    inputs = relative(tokens[0]).astype(F32)
-    grad_out = relative(cotangent[0])
+    tokens_rel, grad_out = in_order(me, [tokens[0], cotangent[0]], group)
+    inputs = tokens_rel.astype(F32)
 
     def expert_rows(k):
-        in_rows = piece(w_in, expert_me ^ k, 1, 1).reshape(part, 2 * hidden_units)
-        down_rows = piece(w_down, expert_me ^ k, 1, 1).reshape(part, hidden_units)
-        return jnp.concatenate([in_rows, down_rows], axis=1)
+        in_rows = piece(w_in, expert_me ^ k, 1, 1)
+        down_rows = piece(w_down, expert_me ^ k, 1, 1)
+        return [in_rows[:, 0, 0], in_rows[:, 0, 1], down_rows[:, 0]]
 
     to_send = [expert_rows(k) for k in range(experts)]
+
+    def given_sends(ks):
+        return {f"send{k}{c}": x for k in ks for c, x in enumerate(to_send[k])}
+
     in_cols, down_cols = (0, 2 * hidden_units), (2 * hidden_units, hidden_units)
     weight_shapes = {"in": (width, 2 * hidden_units), "down": (width, hidden_units)}
 
-    def weight_moves(k, first, size):
+    def weight_moves(k, first, size, prefix=""):
         moves = []
-        for name, cols in (("in", in_cols), ("down", down_cols)):
+        sides = (("in", (0, hidden_units)), ("in", (hidden_units, hidden_units)), ("down", None))
+        for c, (name, cols) in enumerate(sides):
             base = k * share * part + first
-            source = (f"send{k}", (first, size), cols)
-            landed = (name, (base, size), None)
+            source = (f"send{k}{c}", (first, size), None)
+            landed = (prefix + name, (base, size), cols)
             moves.append((source, landed, k * share, ()))
             for t in range(1, share):
-                target = (name, (base + t * part, size), None)
+                target = (prefix + name, (base + t * part, size), cols)
                 if k:
                     moves.append((landed, target, t, (landed,)))
                 else:
@@ -1021,18 +1265,27 @@
     key_row = (key_seg[None, :], key_idx[None, :])
     heads = head_width // HD
     later = weight_moves(0, 0, part) + many_weight_moves([(k, 0, half_part) for k in near])
-    (gains, hidden_one, qkv, kv, mixed, branch), made = front(
+    gate_high = gate_mlp.astype(BF)
+    gate_low = (gate_mlp - gate_high.astype(F32)).astype(BF)
+    gate_ride = jnp.pad(
+        jnp.concatenate([gate_high, gate_low], axis=1), ((0, 0), (0, HD - 2 * experts))
+    )
+    dy_moves = [
+        (("picked", (k * room, room), None), ("slots", (k * room, room), None), k * share, ())
+        for k in range(1, experts)
+    ]
+    (gains, hidden_one, qkv, kv, mixed, branch, dy_got), made = front(
         1,
         ctx_count,
         heads,
         part,
-        (gain_moves, *gather_moves),
+        (gain_moves, *gather_moves, dy_moves),
         later,
         {
             "own": attn_own,
             "far_x": far_x,
             "far_y": far_y,
-            **{f"send{k}": to_send[k] for k in [0, *near]},
+            **given_sends([0, *near]),
         },
         weight_shapes,
         (
@@ -1045,149 +1298,109 @@
             slot_idx,
             slot_gate,
             *key_row,
+            grad_out,
+            gate_ride,
+            place_mlp,
         ),
     )
     attn_full, weights = made["kept"], {n: made[n] for n in weight_shapes}
     gains = gains.reshape(group, 16, 2 * part)[:, 0].astype(F32)
     gain_one, gain_two = gains[:, :part].reshape(1, width), gains[:, part:].reshape(1, width)
-    qkv_full, out_full = attn_full[:, :qkv_wide], attn_full[:, qkv_wide:]
-
-    def turned(x, k):
-        wide = share * part
-        return jnp.concatenate(
-            [x[:, (i ^ k) * wide : ((i ^ k) + 1) * wide] for i in range(experts)], axis=1
-        )
-
-    def pick(k, x):
-        return dot(place_mlp[k], x, 1, 0).astype(BF)
-
-    run = width // tp_count
-    tp_me = lax.axis_index("tp")
-    gate_high = gate_mlp.astype(BF)
-    gate_low = (gate_mlp - gate_high.astype(F32)).astype(BF)
-    gate_ride = jnp.pad(
-        jnp.concatenate([gate_high, gate_low], axis=1), ((0, 0), (0, HD - 2 * experts))
-    )
-    grad_got = []
-    for k in range(experts):
-        sent = jnp.concatenate([piece(grad_out, tp_me ^ k, run), gate_ride], axis=1)
-        slots = pick(k, sent)
-        grad_got.append(exchange(slots, k * share) if k else slots)
-    grad_got = jnp.concatenate(grad_got, axis=0)
+
+    run = width // experts
     own_gate = jnp.tile(jnp.arange(experts) == expert_me, 2)
     slot_weight = jnp.sum(
-        jnp.where(own_gate[None, :], grad_got[:, run : run + 2 * experts].astype(F32), 0.0),
+        jnp.where(own_gate[None, :], dy_got[:, run : run + 2 * experts].astype(F32), 0.0),
         axis=1,
         keepdims=True,
     )
-    grad_slots = lax.all_gather(grad_got[:, :run], "tp", axis=1, tiled=True)
-
-    def send_weights(name, number, cuts, weights, slots=None):
-        moves, given, made_shapes = [], {f"send{k}": to_send[k] for k, _, _ in cuts}, dict(weight_shapes)
-        if slots is not None:
-            made_shapes["slots"] = (experts * room, width)
-            for k, x in enumerate(slots):
-                given[f"slots{k}"] = x
-                target = ("slots", (k * room, room), None)
-                moves.append(((f"slots{k}", (0, room), None), target, k * share, ()))
-        moves += many_weight_moves(cuts)
-        made = move(name, number, ctx_count, moves, {**given, **weights}, made_shapes)
-        return {n: made[n] for n in weight_shapes}, made.get("slots")
+    grad_slots = dy_got[:, :run]
 
     branch_sum = lax.psum(branch, "tp")
     cuts = [(k, half_part, part - half_part) for k in near] + [(k, 0, half_part) for k in far]
     to_send, weights, _ = lax.optimization_barrier((to_send, weights, branch))
-    weights, _ = send_weights("weights_two", 3, cuts, weights)
-    resid = inputs + branch_sum.astype(F32)
-    normed_two, inverse_two = normalize(resid)
-    hidden_two = (normed_two * gain_two).astype(BF)
-    slots = [pick(0, hidden_two)] + [turned(pick(k, hidden_two), k) for k in range(1, experts)]
-    cuts = [(k, half_part, part - half_part) for k in far]
-    weights, two_slots = send_weights("dispatch", 4, cuts, weights, slots)
-    in_full, down_full = weights["in"], weights["down"]
-
-    def send_back(x):
-        slots = x.reshape(experts, room, width)
-        return [slots[0]] + [exchange(slots[k], k * share) for k in range(1, experts)]
-
-    def gathered_rows(got):
-        got = [got[0]] + [turned(got[k], k) for k in range(1, experts)]
-        return jnp.einsum(
-            "kct,kcd->td", place_mlp, jnp.stack(got), preferred_element_type=F32
-        ).astype(BF)
-
-    gate_up = dot(two_slots, in_full, 1, 0)
-    gate_part, up_part = gate_up[:, :hidden_units], gate_up[:, hidden_units:]
-    sigmoid_gate = jax.nn.sigmoid(gate_part)
-    silu_gate = gate_part * sigmoid_gate
-    active = (silu_gate * up_part * slot_weight).astype(BF)
-    mlp_slots = dot(active, down_full, 1, 1).astype(BF)
-    mlp_back = send_back(mlp_slots)
-    grad_active = dot(after(grad_slots, mlp_slots), down_full, 1, 0)
-    scaled = grad_active * slot_weight
-    grad_gate = scaled * up_part * sigmoid_gate * (1.0 + gate_part * (1.0 - sigmoid_gate))
-    grad_up = scaled * silu_gate
-    grad_gu = jnp.concatenate([grad_gate, grad_up], axis=1).astype(BF)
-    back_two_slots = dot(grad_gu, in_full, 1, 1).astype(BF)
-    expert_grads, back_two_part = expert_grads_of(
-        8,
+    given = {**given_sends([*near, *far]), **weights}
+    weights = move("weights_two", 3, ctx_count, many_weight_moves(cuts), given, weight_shapes)
+    fetched, far_moves = [], []
+    for j in range(group):
+        size = half_part if j // share in far else part
+        if fetched and sum(fetched[-1]) == j * part:
+            fetched[-1] = (fetched[-1][0], fetched[-1][1] + size)
+        else:
+            fetched.append((j * part, size))
+    for k in far:
+        far_moves += weight_moves(k, half_part, part - half_part, "w")
+    grads_in, grads_down, mlp_part, back_two_part = run_experts(
+        4,
         ctx_count,
+        tp_count,
         experts,
         share,
         part,
-        two_slots,
+        fetched,
+        far_moves,
+        given_sends(far),
+        weights,
+        tokens_rel,
+        branch_sum,
+        gain_two,
+        place_mlp,
         grad_slots,
-        grad_gu,
-        active,
-        after(back_two_slots, *mlp_back),
-        place_mlp,
+        slot_weight,
     )
-    back_two = lax.psum(back_two_part, "tp").astype(F32)
-    grads_got = {0: expert_grads[:part]}
+    back_two = lax.psum(back_two_part, "tp")
+    grads_got = {0: jnp.concatenate([grads_in[:part], grads_down[:part]], axis=1)}
 
     def grad_moves(ks):
-        return [
-            (("grads", (k * part, part), None), (f"got{k}", (0, part), None), k * share, ())
-            for k in ks
-        ], {f"got{k}": (part, expert_grads.shape[1]) for k in ks}
+        moves = []
+        for k in ks:
+            rows_at = (k * part, part)
+            for name, cols in (("grads_in", in_cols), ("grads_down", down_cols)):
+                target = (f"got{k}", (0, part), cols)
+                moves.append(((name, rows_at, None), target, k * share, ()))
+        return moves, {f"got{k}": (part, 3 * hidden_units) for k in ks}
 
     moves, made_shapes = grad_moves(near)
-    made = move("grads_near", 5, ctx_count, moves, {"grads": expert_grads}, made_shapes)
+    grads_in, grads_down, _ = lax.optimization_barrier((grads_in, grads_down, back_two_part))
+    given = {"grads_in": grads_in, "grads_down": grads_down}
+    made = move("grads_near", 5, ctx_count, moves, given, made_shapes)
     grads_got.update({k: made[f"got{k}"] for k in near})
     grads_near = [grads_got[k] for k in near]
 
-    grad_resid_norm, gain_two_grad = norm_back(back_two, normed_two, inverse_two, gain_two)
-    grad_resid = grad_out.astype(F32) + grad_resid_norm
-    grad_branch = grad_resid.astype(BF)
-    grad_mixed = dot(after(grad_branch, *grads_near), out_full, 1, 0)
-    gate_wide = jnp.repeat(gate_attn, head_width, axis=1)
-    grad_attn = (grad_mixed * gate_wide).astype(BF)
     moves, made_shapes = grad_moves(far)
-    grad_qkv, made = attend_back(
+    back_two, given, _ = lax.optimization_barrier((back_two, given, grads_near))
+    (grad_qkv, grad_resid, grad_branch, gain_two_grad, back_one_part), made = attend_back(
         6,
         ctx_count,
         heads,
+        part,
         moves,
-        {"grads": expert_grads},
+        given,
         made_shapes,
+        attn_full,
+        tokens_rel,
+        branch_sum,
+        gain_two,
+        back_two,
+        grad_out,
+        gate_attn,
         qkv,
         kv,
         place_attn,
         slot_seg,
         slot_idx,
         *key_row,
-        grad_attn,
         cos,
         sin,
     )
     grads_got.update({k: made[f"got{k}"] for k in far})
-    mlp_total = lax.psum(gathered_rows(after(mlp_back, grad_attn)), "tp").astype(F32)
-    back_one_part = dot(grad_qkv, qkv_full, 1, 1)
-    back_one = lax.psum(back_one_part.astype(BF), "tp").astype(F32)
+    mlp_total = lax.psum(mlp_part, "tp").astype(F32)
+    back_one = lax.psum(back_one_part, "tp").astype(F32)
     grad_input_norm, gain_one_grad = norm_back(back_one, normed_one, inverse_one, gain_one)
-    grad_tokens = relative((grad_resid + grad_input_norm).astype(BF))
-
-    output = relative((resid + mlp_total).astype(BF))
+    grad_tokens = (grad_resid + grad_input_norm).astype(BF)
+
+    resid = inputs + branch_sum.astype(F32)
+    output, grad_tokens = in_order(me, [(resid + mlp_total).astype(BF), grad_tokens], group)
 
     upper = list(range(1, bits_of(group)))
     grad_attnw = attn_grads(
@@ -1196,7 +1409,7 @@
     grad_query_w, grad_kv_w, grad_out_w = lay_out(
         grad_attnw, (w_query.shape, w_kv.shape, w_out_attn.shape)
     )
-    gain_grads = gain_sums(9, ctx_count, group, [gain_one_grad, gain_two_grad])
+    gain_grads = gain_sums(9, ctx_count, group, [gain_one_grad, gain_two_grad[0]])
 
     return (
         output[None],

time: 672 us -> 622 us (0.926)
  matrix products: 58.4 us -> 0.32 us
  Pallas kernels: 470 us -> 513 us
  local copies, waits for them, and re-layouts: 64.7 us -> 48.8 us
  other arithmetic: 36.4 us -> 23 us
  starting transfers between devices: 12.2 us -> 5.39 us
    pallas_call x1 -> x3, Pallas kernels: 36.6 us -> 134 us  [the longest x1 123 us: run_experts(): pl.pallas_call(functools.partial(experts_kernel, ctx_count, experts, shar...]
    pallas_call x3 -> x2, Pallas kernels: 161 us -> 102 us  [move(): pl.pallas_call(functools.partial(move_kernel, ctx_count, moves, plain + [...]
    dot_general x16 -> x2, matrix products: 56.4 us -> 0.32 us  [dot(): lax.dot_general(a, b, (((ca,), (cb,)), ((), ())), preferred_element_type=...]
    unnamed x125 -> x50, local copies, waits for them, and re-layouts: 27.6 us -> 6.14 us
    concatenate x9 -> x1, other arithmetic: 11.4 us -> 1.57 us  [layer(): jnp.concatenate([grads_in[:part], grads_down[:part]], axis=1)]
    slice x8 -> x5, local copies, waits for them, and re-layouts: 8.14 us -> 17.1 us  [the longest x1 11.7 us: expert_rows(): return [in_rows[:, 0, 0], in_rows[:, 0, 1], down_rows[:, 0]]]
    squeeze x0 -> x6, local copies, waits for them, and re-layouts: none -> 7.77 us  [expert_rows(): return [in_rows[:, 0, 0], in_rows[:, 0, 1], down_rows[:, 0]]]
    dynamic_slice x5 -> x3, local copies, waits for them, and re-layouts: 13.9 us -> 6.3 us  [piece(): return lax.dynamic_slice_in_dim(x, index * size, size, axis)]
  transfers between devices with their start and end apart: 12 -> 5, of which waited for: 4 -> 2; matrix products, arithmetic and copies ran while one was open for 16% -> 8% of each run, Pallas kernels for 41% -> 37%
where the time goes in v4:
time: 622 us; the launch traced here: 613 us
  Pallas kernels  513 us (82%)
  local copies, waits for them, and re-layouts  48.8 us (8%)
  other arithmetic  23 us (4%)
  between operations  14.5 us (2%)
  waiting for transfers between devices  8.53 us (1%)
    pallas_call x1, Pallas kernels, run_experts(): pl.pallas_call(functools.partial(experts_kernel, ctx_count, experts, shar...  123 us
    pallas_call x2, Pallas kernels, move(): pl.pallas_call(functools.partial(move_kernel, ctx_count, moves, plain + [...  102 us
    pallas_call x1, Pallas kernels, attn_grads(): pl.pallas_call(functools.partial(attn_grads_kernel, ctx_count, bits, part...  99.1 us
    pallas_call x1, Pallas kernels, front(): pl.pallas_call(functools.partial(front_kernel, ctx_count, moves, marks, n...  85.2 us
    pallas_call x1, Pallas kernels, attend_back(): pl.pallas_call(functools.partial(attend_back_kernel, ctx_count, moves, li...  68.5 us
  transfers between devices with their start and end apart: 5, of which 2 were waited for; matrix products, arithmetic and copies ran while one was open for 8% of the time, Pallas kernels for 37%

profile of v4, /device:TPU:0, one launch (start us, length us, event | category | flops | bytes accessed | tf_op | source)
XLA Modules:
  0.0 613.4 jit_solution(4438569173771686169)
XLA Ops:
  7.2 1.5 copy.135
  8.8 1.0 constant_dynamic-update-slice_fusion.2
  11.5 1.0 constant_dynamic-update-slice_fusion.refs_0_
  12.6 2.9 collective-permute-start
  15.5 1.5 collective-permute-start.1
  18.0 1.2 convert_reduce_fusion
  19.2 3.1 fusion.15
  22.3 1.0 pad_maximum_fusion.1.cos_ref
  23.3 5.7 in_order.2
  29.1 1.5 fusion.8
  30.6 2.8 convert_multiply_fusion.normed_ref
  33.5 11.7 %constant_dynamic-slice_fusion.14 = (bf16[256,1,1,1408]{3,2,1,0:T(2,128)(2,1)S(1)}, bf16[256,1,1,1408]{3,2,1,0:T(2,128)(2,1)S(1)}, bf16[256,1,1,1408]{3,2,1,0:T(...) fusion(bf16[256,4,2,1408]{3,2,1,0:T(2,128)(2,1)} %param.20, ...), kind=kLoop, calls=%fused_computation.80 | loop fusion | bytes 11534356 | tf_op jit(solution)/shard_map/slice | solution.py:1195
  45.2 1.3 copy_bitcast_fusion.1
  46.6 1.3 copy_bitcast_fusion.4
  47.9 1.3 copy_bitcast_fusion.7
  49.6 1.0 fusion.13
  53.3 1.3 select_bitcast_fusion
  54.6 1.3 copy_bitcast_fusion.10
  55.9 1.0 copy-done.2
  56.9 6.2 %constant_dynamic-slice_fusion.13 = (bf16[256,1,1408]{2,1,0:T(2,128)(2,1)S(1)}, bf16[256,1,1408]{2,1,0:T(2,128)(2,1)S(1)}, bf16[256,1,1408]{2,1,0:T(2,128)(2,1)S(1)}, bf16[256,1,1408]{2,1,0:T(2,128)(2,1)S(1)}) fusion(bf16[256,4,1408]{2,1,0:T(4,128)(2,1)S(1)} %copy-done.2, s32[]{:T(128)S(6)} %select_n.101, s32[]{:T(128)S(6)} %select_n.100, s32[]{:T(128)S(6)} %select_n.99, ...), kind=kLoop, calls=%fused_computation.79 | loop fusion | bytes 5767184 | tf_op jit(solution)/shard_map/dynamic_slice | solution.py:1138
  63.2 1.3 copy_bitcast_fusion
  64.5 1.3 copy_bitcast_fusion.6
  65.7 7.0 %collective-permute-done.refs_1_ = bf16[256,5120]{1,0:T(8,128)(2,1)} collective-permute-done((bf16[256,5120]{1,0:T(8,128)(2,1)}, bf16[256,5120]{1,0:T(8,128)(2,1)}, u32[]{:S(2)}, u32[]{:S(2)}) %collective-permute-start) | collective-permute-done | bytes 2621472 | tf_op jit(solution)/shard_map/ppermute | solution.py:40
  72.7 1.5 collective-permute-done.1.refs_2_
  74.2 0.9 copy.109.segq_ref
  75.1 0.9 copy.110.idxq_ref
  75.9 0.9 copy.111.gate_ref
  76.9 1.6 slice.74.cos_ref
  79.1 85.2 %front.1 = (bf16[128,512]{1,0:T(8,128)(2,1)}, bf16[256,2048]{1,0:T(8,128)(2,1)}, bf16[256,3072]{1,0:T(8,128)(2,1)}, bf16[1024,1024]{1,0:T(8,128)(2,1)}, bf16[256...) custom-call(f32[256,2048]{1,0:T(8,128)} %convert_multiply_fusion.nor, ...), custom_call_target="tpu_custom_call" | custom-call | tf_op jit(solution)/shard_map/front/pallas_call | solution.py:854
  164.8 1.9 slice.78.dy_run_ref
  166.7 1.1 select_reduce_fusion.3
  167.8 0.9 broadcast_in_dim.137.weight_ref
  170.1 52.6 %weights_two.1 = (bf16[2048,2816]{1,0:T(8,128)(2,1)}, bf16[2048,1408]{1,0:T(8,128)(2,1)}) custom-call(bf16[256,1408]{1,0:T(8,128)(2,1)} %get-tuple-element.113.refs_6_.refs_0_, bf16[256,1408]{1,0:T(8,128)(2,1)} %get-tuple-element.114.refs_7_.refs_1_, ...), custom_call_target="tpu_custom_call", output_to_operand_aliasing={{0}: (10, {}), {1}: (9, {})} | custom-call | tf_op jit(solution)/shard_map/weights_two/pallas_call | solution.py:185
  222.8 122.6 %experts.1 = (bf16[1024,2816]{1,0:T(8,128)(2,1)}, bf16[1024,1408]{1,0:T(8,128)(2,1)}, bf16[256,2048]{1,0:T(8,128)(2,1)}, bf16[256,2048]{1,0:T(8,128)(2,1)}) custom-call(bf16[256,2048]{1,0:T(8,128)(2,1)} %get-tuple-element.82.tokens_ref, bf16[256,2048]{1,0:T(8,128)(2,1)} %all-reduce.8.cloned.1.call-done.branch_ref, f32[1,2048]{1,0:T(1,128)} %bitcast.90, ...), custom_call_target="tpu_custom_call" | custom-call | tf_op jit(solution)/shard_map/experts/pallas_call | solution.py:658
  346.7 49.7 %grads_near.1 = (bf16[256,4224]{1,0:T(8,128)(2,1)}, bf16[256,4224]{1,0:T(8,128)(2,1)}) custom-call(bf16[1024,2816]{1,0:T(8,128)(2,1)} %get-tuple-element.139.refs_0_.refs_1_, bf16[1024,1408]{1,0:T(8,128)(2,1)} %get-tuple-element.138.refs_1_.refs_0_), custom_call_target="tpu_custom_call" | custom-call | tf_op jit(solution)/shard_map/grads_near/pallas_call | solution.py:185
  396.4 68.5 %attend_back.1 = (bf16[256,3072]{1,0:T(8,128)(2,1)}, f32[256,2048]{1,0:T(8,128)}, bf16[256,2048]{1,0:T(8,128)(2,1)}, f32[1,2048]{1,0:T(1,128)}, bf16[256,2048]{1,0:T(8,128)(2,1)}, /*index=5*/bf16[256,4224]{1,0:T(8,128)(2,1)}) custom-call(bf16[256,2048]{1,0:T(8,128)(2,1)} %get-tuple-element.82.tokens_ref, ...), custom_call_target="tpu_custom_call" | custom-call | tf_op jit(solution)/shard_map/attend_back/pallas_call | solution.py:1025
  464.9 1.5 slice.83
  466.4 1.2 slice.84
  467.6 1.6 pad_maximum_fusion.refs_0_
  469.1 99.1 %attn_grads.1.grad_ref = f32[256,5120]{1,0:T(8,128)} custom-call(bf16[256,2048]{1,0:T(8,128)(2,1)} %get-tuple-element.145.hidden_ref, bf16[256,2048]{1,0:T(8,128)(2,1)} %get-tuple-element.146.branch_ref, bf16[256,3072]{1,0:T(8,128)(2,1)} %get-tuple-element.147.qkv_ref, bf16[256,2048]{1,0:T(8,128)(2,1)} %get-tuple-element.148.mixed_ref), custom_call_target="tpu_custom_call" | custom-call | tf_op jit(solution)/shard_map/attn_grads/pallas_call | solution.py:326
  568.3 5.4 lay_out.1
  573.7 11.9 %spread_grads.1 = (f32[256,4,2,1408]{3,2,1,0:T(2,128)}, f32[256,4,1408]{2,1,0:T(4,128)}) custom-call(s32[1]{0:T(128)} %bitcast.44.me_ref, bf16[256,4224]{1,0:T(8,128)(2,1)} %pad_maximum_fusion.refs_0_, bf16[256,4224]{1,0:T(8,128)(2,1)} %get-tuple-element.132.refs_1_, bf16[256,4224]{1,0:T(8,128)(2,1)} %get-tuple-element.133.refs_2_, ...), custom_call_target="tpu_custom_call" | custom-call | tf_op jit(solution)/shard_map/spread_grads/pallas_call | solution.py:1068
  585.6 2.0 fusion.7
  588.3 6.3 %gain_sums.1 = f32[8,256]{1,0:T(8,128)} custom-call(f32[64,256]{1,0:T(8,128)} %fusion.16.gain_ref), custom_call_target="tpu_custom_call" | custom-call | tf_op jit(solution)/shard_map/gain_sums/pallas_call | solution.py:424
  594.6 1.3 fusion.20
  596.0 3.3 fusion.6.refs_1_
  599.3 1.5 fusion.10.refs_0_
  600.9 5.7 in_order.3
  (94 shorter events, 10.5 us)
Async XLA Ops:
  7.2 215.6 %all-reduce.8.cloned.1.call-start = ((), (), s32[]{:S(2)}) async-start(), calls=%async_computation | async-start | bytes 2097152 | tf_op jit(solution)/shard_map/psum | solution.py:1319
  7.2 2.6 copy-start.10
  8.8 1.6 copy-start.8
  10.7 6.4 %copy-start.15 = (s32[1,256,2]{1,2,0:T(2,128)S(1)}, s32[1,256,2]{1,2,0:T(2,128)}, u32[]{:S(2)}) copy-start(s32[1,256,2]{1,2,0:T(2,128)} %param.25) | copy-start | bytes 6148
  10.7 6.7 %copy-start.14 = (s32[1,256,2]{1,2,0:T(2,128)S(1)}, s32[1,256,2]{1,2,0:T(2,128)}, u32[]{:S(2)}) copy-start(s32[1,256,2]{1,2,0:T(2,128)} %param.23) | copy-start | bytes 6148
  10.7 6.9 %copy-start.16 = (s32[1,1024]{1,0:T(1,128)S(1)}, s32[1,1024]{1,0:T(1,128)}, u32[]{:S(2)}) copy-start(s32[1,1024]{1,0:T(1,128)} %param.22) | copy-start | bytes 12292
  12.6 60.1 %collective-permute-start = (bf16[256,5120]{1,0:T(8,128)(2,1)}, bf16[256,5120]{1,0:T(8,128)(2,1)}, u32[]{:S(2)}, u32[]{:S(2)}) collective-permute-start(bf16[256,5120]{1,0:T(8,128)(2,1)} %constant_dynamic-update-slice_fusion.refs_0_), channel_id=1, source_target_pairs={{0,16},{4,20},{8,24},{12,28},{16,0},{20,4},{24,8},{28,12},{1,17},{... | collective-permute-start | bytes 7864328 | tf_op jit(solution)/shard_map/ppermute | solution.py:40
  15.5 58.6 %collective-permute-start.1 = (bf16[256,5120]{1,0:T(8,128)(2,1)}, bf16[256,5120]{1,0:T(8,128)(2,1)}, u32[]{:S(2)}, u32[]{:S(2)}) collective-permute-start(bf16[256,5120]{1,0:T(8,128)(2,1)} %constant_dynamic-update-slice_fusion.refs_0_), channel_id=1, source_target_pairs={{0,8},{4,12},{8,0},{12,4},{16,24},{20,28},{24,16},{28,20},{1,9},{5... | collective-permute-start | bytes 7864328 | tf_op jit(solution)/shard_map/ppermute | solution.py:40
  18.0 11.1 %copy-start.11 = (s32[1024]{0:T(1024)}, s32[1024]{0:T(1024)S(1)}, u32[]{:S(2)}) copy-start(s32[1024]{0:T(1024)S(1)} %get-tuple-element.194) | copy-start | bytes 12292
  18.0 11.1 %copy-start.12 = (s32[1024]{0:T(1024)}, s32[1024]{0:T(1024)S(1)}, u32[]{:S(2)}) copy-start(s32[1024]{0:T(1024)S(1)} %get-tuple-element.195) | copy-start | bytes 12292
  29.1 4.3 copy-start.17
  29.1 4.3 copy-start.18
  47.9 1.3 copy-start.6
  47.9 1.5 copy-start.7
  49.2 1.4 copy-start.19
  49.2 1.4 copy-start.20
  49.5 28.9 %copy-start.5 = (f32[1024,128]{1,0:T(8,128)}, f32[1024,128]{1,0:T(8,128)S(1)}, u32[]{:S(2)}) copy-start(f32[1024,128]{1,0:T(8,128)S(1)} %pad_maximum_fusion.2.sin_ref) | copy-start | bytes 1572868
  54.6 2.3 copy-start.2
  164.3 232.2 %all-reduce.10.cloned.1.call-start = ((), (), s32[]{:S(2)}) async-start(), calls=%async_computation.1 | async-start | bytes 2097152 | tf_op jit(solution)/shard_map/psum | solution.py:1351
  345.4 240.2 %all-reduce.12.cloned.1.call-start = ((), (), s32[]{:S(2)}) async-start(), calls=%async_computation.2 | async-start | bytes 4194304 | tf_op jit(solution)/shard_map/psum | solution.py:1397
  573.7 11.9 %copy-start = (f32[256,2048]{1,0:T(8,128)S(1)}, f32[256,2048]{1,0:T(8,128)}, u32[]{:S(2)}) copy-start(f32[256,2048]{1,0:T(8,128)} %convert_multiply_fusion.normed_ref) | copy-start | bytes 6291460
  585.6 2.1 copy-start.13
  585.6 10.4 %copy-start.4 = (bf16[256,2048]{1,0:T(8,128)(2,1)S(1)}, bf16[256,2048]{1,0:T(8,128)(2,1)}, u32[]{:S(2)}) copy-start(bf16[256,2048]{1,0:T(8,128)(2,1)} %get-tuple-element.160) | copy-start | bytes 3145732
  596.0 3.4 copy-start.1
  596.0 3.4 copy-start.3
  596.0 3.4 copy-start.9
Sparse Core Ops, SparseCore 0:
  164.4 53.0 all-reduce.7
  345.5 49.9 all-reduce.9
  465.0 86.1 all-reduce.11

commit v5 on v4

--- a/solution.py
+++ b/solution.py
@@ -11,7 +11,9 @@
 EPSILON = 1e-06
 ROPE_BASE = 10000.0
 MASKED = -1e30
-GROUP = ("fsdp", "ctx")
+FSDP, CTX, TP = "fsdp", "ctx", "tp"
+GROUP = (FSDP, CTX)
+FULL = "full"
 BF = jnp.bfloat16
 F32 = jnp.float32
 VMEM_LIMIT = 56 * 1024 * 1024
@@ -55,10 +57,10 @@
 
 def peer(ctx_count, mask):
     if mask < 0:
-        return {"tp": flip(lax.axis_index("tp"), -mask)}
+        return {TP: flip(lax.axis_index(TP), -mask)}
     return {
-        "fsdp": flip(lax.axis_index("fsdp"), mask // ctx_count),
-        "ctx": flip(lax.axis_index("ctx"), mask % ctx_count),
+        FSDP: flip(lax.axis_index(FSDP), mask // ctx_count),
+        CTX: flip(lax.axis_index(CTX), mask % ctx_count),
     }
 
 
@@ -72,15 +74,23 @@
 
 
 def run_cols(size, flips=0):
-    return pl.ds(pl.multiple_of(flip(lax.axis_index("tp"), flips) * size, size), size)
+    return pl.ds(pl.multiple_of(flip(lax.axis_index(TP), flips) * size, size), size)
 
 
 def window(ref, rows, cols):
+    if rows[0] == TP:
+        return ref.at[run_cols(rows[1], rows[2])]
     if cols is None:
         return ref.at[pl.ds(rows[0], rows[1])]
-    if cols[0] == "tp":
-        return ref.at[pl.ds(rows[0], rows[1]), run_cols(cols[1])]
+    if cols[0] == TP:
+        return ref.at[pl.ds(rows[0], rows[1]), run_cols(*cols[1:3])]
     return ref.at[pl.ds(rows[0], rows[1]), pl.ds(cols[0], cols[1])]
+
+
+def gain_of(gains_ref, which, part):
+    rows = gains_ref[...].astype(F32)
+    cols = slice(which * part, (which + 1) * part)
+    return jnp.concatenate([rows[at : at + 1, cols] for at in range(0, rows.shape[0], 16)], axis=1)
 
 
 class Moves:
@@ -90,7 +100,7 @@
         bounces = list(bounces)
         self.copies = []
         self.place = {m[1]: i for i, m in enumerate(moves)}
-        self.started, self.came = set(), set()
+        self.started, self.came, self.sent = set(), set(), set()
         for at, (source, target, mask, _) in enumerate(moves):
             i = base + at
             src = window(arrays[source[0]], *source[1:])
@@ -133,6 +143,11 @@
             else:
                 self.copies[i].wait_recv()
 
+    def await_sent(self, i):
+        if i not in self.sent:
+            self.sent.add(i)
+            self.copies[i].wait_send()
+
     def settle(self, count=None, first=0):
         count = len(self.moves) if count is None else count
         for i in range(first, count):
@@ -151,7 +166,7 @@
             if i in self.onward:
                 self.onward[i].wait()
             elif self.moves[i][2] is not None:
-                self.copies[i].wait_send()
+                self.await_sent(i)
 
 
 def masks_of(moves):
@@ -208,6 +223,7 @@
 
 def attn_grads_kernel(
     ctx_count,
+    groups,
     bits,
     part,
     cols,
@@ -215,7 +231,22 @@
     branch_ref,
     qkv_ref,
     mixed_ref,
+    back_ref,
+    tokens_ref,
+    gain_ref,
+    resid_ref,
+    gain_two_ref,
+    mlp_ref,
+    place_ref,
     out_ref,
+    grad_tokens_ref,
+    gain_out_ref,
+    mlp_sum_ref,
+    mlp_got,
+    back_got,
+    back_sum,
+    gain_send,
+    gain_got,
     hidden,
     branch,
     hidden_odd,
@@ -232,24 +263,34 @@
     count = width // part // 2
     planes = right.shape[1] // cols
     first = qkv_ref.shape[1]
-    greet(ctx_count, [1, *[1 << b for b in bits]])
-    arrays = {
-        "hidden_odd": hidden_odd,
-        "branch_odd": branch_odd,
-        "qkv_in": qkv_ref,
-        "mixed_in": mixed_ref,
-        "hidden": hidden,
-        "branch": branch,
-        "right": right,
-    }
-    theirs = (rows, rows)
-    moves = [
-        (("mixed_in", (0, rows), None), ("right", theirs, (first, mixed_ref.shape[1])), 1, ()),
-        (("branch_odd", (0, rows), None), ("branch", theirs, None), 1, ()),
-        (("qkv_in", (0, rows), None), ("right", theirs, (0, first)), 1, ()),
-        (("hidden_odd", (0, rows), None), ("hidden", theirs, None), 1, ()),
-    ]
-    run = Moves(ctx_count, moves, arrays, pass_send, pass_recv)
+    group = width // part
+    run_rows = groups["spread"][0][0][1][1]
+    greet(ctx_count, masks_of([m for moves in groups.values() for m in moves]))
+    arrays = dict(
+        back=back_ref,
+        back_got=back_got,
+        back_sum=back_sum,
+        mlp=mlp_ref,
+        mlp_got=mlp_got,
+        mlp_sum=mlp_sum_ref,
+        gain_send=gain_send,
+        gain_got=gain_got,
+        hidden_odd=hidden_odd,
+        branch_odd=branch_odd,
+        qkv_in=qkv_ref,
+        mixed_in=mixed_ref,
+        hidden=hidden,
+        branch=branch,
+        right=right,
+    )
+    runs, base = {}, 0
+    for name, moves in groups.items():
+        if name != "sums":
+            runs[name] = Moves(ctx_count, moves, arrays, pass_send, pass_recv, (), base)
+        base += len(moves)
+    run = runs["share"]
+    runs["reduce"].begin()
+    runs["mlp"].begin()
     for given, even_side, odd_side in (
         (branch_ref, branch, branch_odd),
         (hidden_ref, hidden, hidden_odd),
@@ -298,8 +339,48 @@
         grads[:, at] = dot(left_side[...], right[:, at], 0, 0).astype(BF)
         left[plane] = list(range(count))
         send_half(plane, order, 0)
+    def sum_back():
+        runs["reduce"].settle()
+        own = run_cols(run_rows)
+        total = back_ref[own].astype(F32)
+        for r in range(len(groups["reduce"])):
+            total = total + back_got[r * run_rows : (r + 1) * run_rows].astype(F32)
+        back_sum[own] = total.astype(BF)
+        runs["spread"].begin()
+
+    def sum_mlp():
+        runs["mlp"].settle()
+        room = mlp_ref.shape[0] // place_ref.shape[0]
+        total = dot(place_ref[0], mlp_ref[:room], 0, 0)
+        for k in range(1, place_ref.shape[0]):
+            total = total + dot(place_ref[k], mlp_got[k * room : (k + 1) * room], 0, 0)
+        mlp_sum_ref[:, run_cols(mlp_ref.shape[1])] = total.astype(BF)
+        runs["mlp_spread"].begin()
+
+    def norm_back():
+        runs["spread"].settle()
+        x = tokens_ref[...].astype(F32)
+        inverse = lax.rsqrt(jnp.mean(x * x, axis=-1, keepdims=True) + EPSILON)
+        normed = x * inverse
+        back = back_sum[...].astype(F32)
+        gain_grad = jnp.sum(back * normed, axis=0, keepdims=True)
+        scaled = back * gain_of(gain_ref, 0, part)
+        inner = jnp.mean(scaled * normed, axis=-1, keepdims=True)
+        grad_tokens_ref[...] = (resid_ref[...] + inverse * (scaled - normed * inner)).astype(BF)
+        gain_send[...] = jnp.zeros_like(gain_send)
+        for j in range(group):
+            block = slice(j * part, (j + 1) * part)
+            gain_send[j * 8 : j * 8 + 1] = gain_grad[:, block]
+            gain_send[j * 8 + 1 : j * 8 + 2] = gain_two_ref[:, block]
+        runs["gains"].begin()
+
     for step in range(len(bits)):
-        for plane, order in lanes:
+        for n, (plane, order) in enumerate(lanes):
+            if step == 0 and n == len(lanes) // 2:
+                sum_mlp()
+                sum_back()
+            if step == 0 and n == len(lanes) - 1:
+                norm_back()
             at = bits.index(order[step])
             left[plane] = [j for j in left[plane] if not j >> at & 1]
             across = pl.ds(plane * cols, cols)
@@ -313,32 +394,86 @@
                     grads[down, across] = total.astype(BF)
             if step < len(bits) - 1:
                 send_half(plane, order, step + 1)
-    run.finish()
+    runs["gains"].settle()
+    gains = gain_send[:8]
+    for j in range(1, group):
+        gains = gains + gain_got[j * 8 : (j + 1) * 8]
+    gain_out_ref[...] = gains
+    for moves in runs.values():
+        moves.finish()
     for c in sent:
         c.wait_send()
 
 
-def attn_grads(number, ctx_count, bits, part, cols, hidden, branch, qkv, mixed):
+def attn_grads(number, ctx_count, tp_count, bits, part, cols, hidden, branch, qkv, mixed, *others):
     rows, width = hidden.shape
+    group = width // part
+    first = qkv.shape[1]
+    theirs = (rows, rows)
+    run_rows = rows // tp_count
+    mlp, place = others[-2:]
+    experts, room = place.shape[:2]
+    run = mlp.shape[1]
+    groups = {
+        "mlp": [
+            (("mlp", (k * room, room), None), ("mlp_got", (k * room, room), None), k * group // experts, ())
+            for k in range(1, experts)
+        ],
+        "mlp_spread": [
+            (("mlp_sum", (0, rows), (TP, run)), ("mlp_sum", (0, rows), (TP, run, 0, r)), -r, ())
+            for r in range(1, tp_count)
+        ],
+        "reduce": [
+            (("back", (TP, run_rows, r), None), ("back_got", ((r - 1) * run_rows, run_rows), None), -r, ())
+            for r in range(1, tp_count)
+        ],
+        "spread": [
+            (("back_sum", (TP, run_rows, 0), None), ("back_sum", (TP, run_rows, 0), r), -r, ())
+            for r in range(1, tp_count)
+        ],
+        "gains": [
+            (("gain_send", (j * 8, 8), None), ("gain_got", (j * 8, 8), None), j, ())
+            for j in range(1, group)
+        ],
+        "share": [
+            (("mixed_in", (0, rows), None), ("right", theirs, (first, mixed.shape[1])), 1, ()),
+            (("branch_odd", (0, rows), None), ("branch", theirs, None), 1, ()),
+            (("qkv_in", (0, rows), None), ("right", theirs, (0, first)), 1, ()),
+            (("hidden_odd", (0, rows), None), ("hidden", theirs, None), 1, ()),
+        ],
+        "sums": [((), (), 1 << b, ()) for b in bits],
+    }
     wide = qkv.shape[1] + mixed.shape[1]
     copies = (wide // cols) * (width // part // 2)
+    passes = sum(len(moves) for moves in groups.values())
     full = pl.BlockSpec(memory_space=pltpu.VMEM)
     return pl.pallas_call(
-        functools.partial(attn_grads_kernel, ctx_count, bits, part, cols),
-        out_shape=jax.ShapeDtypeStruct((part, wide), F32),
-        in_specs=[full] * 4,
-        out_specs=full,
-        scratch_shapes=[pltpu.VMEM((2 * rows, width // 2), BF)] * 2
+        functools.partial(attn_grads_kernel, ctx_count, groups, bits, part, cols),
+        out_shape=[
+            jax.ShapeDtypeStruct((part, wide), F32),
+            jax.ShapeDtypeStruct((rows, width), BF),
+            jax.ShapeDtypeStruct((8, part), F32),
+            jax.ShapeDtypeStruct((rows, width), BF),
+        ],
+        in_specs=[full] * (4 + len(others)),
+        out_specs=[full] * 4,
+        scratch_shapes=[
+            pltpu.VMEM(mlp.shape, BF),
+            pltpu.VMEM(((tp_count - 1) * run_rows, width), BF),
+            pltpu.VMEM((rows, width), BF),
+            *[pltpu.VMEM((group * 8, part), F32)] * 2,
+        ]
+        + [pltpu.VMEM((2 * rows, width // 2), BF)] * 2
         + [pltpu.VMEM((rows, width // 2), BF)] * 2
         + [pltpu.VMEM((2 * rows, wide), BF)]
         + [pltpu.VMEM((width // 2, wide), BF)] * 2
         + [pltpu.SemaphoreType.DMA((copies,))] * 2
-        + [pltpu.SemaphoreType.DMA((4,))] * 2,
+        + [pltpu.SemaphoreType.DMA((passes,))] * 2,
         compiler_params=pltpu.CompilerParams(
             collective_id=number, has_side_effects=True, vmem_limit_bytes=VMEM_LIMIT
         ),
         name="attn_grads",
-    )(hidden, branch, qkv, mixed)
+    )(hidden, branch, qkv, mixed, *others)
 
 
 def turn_kernel(me_ref, *refs):
@@ -370,6 +505,35 @@
     )(me.astype(jnp.int32).reshape(1), *arrays)
 
 
+def last_kernel(group, me_ref, *refs):
+    tokens, branch, mlp, grad, out_ref, grad_out_ref = refs
+    width = tokens.shape[1]
+    part = width // group
+    total = (tokens[...].astype(F32) + branch[...].astype(F32) + mlp[...].astype(F32)).astype(BF)
+    for j in range(group):
+        cols = slice(j * part, (j + 1) * part)
+        at = pl.ds(pl.multiple_of((me_ref[0] ^ j) * part, part), part)
+        out_ref[:, at] = total[:, cols]
+        grad_out_ref[:, at] = grad[:, cols]
+
+
+def last(me, group, tokens, branch, mlp, grad):
+    rows, width = tokens.shape
+    if width // group % HD:
+        total = tokens.astype(F32) + branch.astype(F32) + mlp.astype(F32)
+        return in_order(me, [total.astype(BF), grad], group)
+    whole = pl.BlockSpec((rows, width), lambda i, m: (0, 0))
+    return pl.pallas_call(
+        functools.partial(last_kernel, group),
+        grid_spec=pltpu.PrefetchScalarGridSpec(
+            num_scalar_prefetch=1, grid=(1,), in_specs=[whole] * 4, out_specs=[whole] * 2
+        ),
+        out_shape=[jax.ShapeDtypeStruct((rows, width), BF)] * 2,
+        compiler_params=pltpu.CompilerParams(vmem_limit_bytes=VMEM_LIMIT),
+        name="last",
+    )(me.astype(jnp.int32).reshape(1), tokens, branch, mlp, grad)
+
+
 def lay_kernel(grad_ref, *out_refs):
     at = 0
     for ref in out_refs:
@@ -389,49 +553,6 @@
         compiler_params=pltpu.CompilerParams(vmem_limit_bytes=VMEM_LIMIT),
         name="lay_out",
     )(grad)
-
-
-def gain_kernel(ctx_count, group, gain_ref, out_ref, got, send, recv):
-    greet(ctx_count, range(1, group))
-    copies = []
-    for j in range(1, group):
-        rows = pl.ds(j * 8, 8)
-        copies.append(
-            pltpu.make_async_remote_copy(
-                src_ref=gain_ref.at[rows],
-                dst_ref=got.at[rows],
-                send_sem=send.at[j],
-                recv_sem=recv.at[j],
-                device_id=peer(ctx_count, j),
-                device_id_type=pl.DeviceIdType.MESH,
-            )
-        )
-        copies[-1].start()
-    total = gain_ref[:8]
-    for j, copy in enumerate(copies):
-        copy.wait_recv()
-        total = total + got[(j + 1) * 8 : (j + 2) * 8]
-    out_ref[...] = total
-    for copy in copies:
-        copy.wait_send()
-
-
-def gain_sums(number, ctx_count, group, gains):
-    count, part = len(gains), gains[0].shape[0] // group
-    laid = jnp.stack([g.reshape(group, part) for g in gains], axis=1)
-    laid = jnp.pad(laid, ((0, 0), (0, 8 - count), (0, 0))).reshape(group * 8, part)
-    full = pl.BlockSpec(memory_space=pltpu.VMEM)
-    total = pl.pallas_call(
-        functools.partial(gain_kernel, ctx_count, group),
-        out_shape=jax.ShapeDtypeStruct((8, part), F32),
-        in_specs=[full],
-        out_specs=full,
-        scratch_shapes=[pltpu.VMEM((group * 8, part), F32)]
-        + [pltpu.SemaphoreType.DMA((group,))] * 2,
-        compiler_params=pltpu.CompilerParams(collective_id=number, has_side_effects=True),
-        name="gain_sums",
-    )(laid)
-    return [total[i] for i in range(count)]
 
 
 def chunks(total, size):
@@ -450,23 +571,20 @@
     gain_ref,
     place_ref,
     dy_run_ref,
-    weight_ref,
+    rides_ref,
     in_ref,
     down_ref,
     *refs,
 ):
     far_refs, refs = refs[: len(far_names)], refs[len(far_names) :]
-    grads_in, grads_down, mlp_part, two_part = refs[:4]
+    grads_in, grads_down, mlp_ref, two_part = refs[:4]
     (
         win,
         wdown,
         two,
         slots_out,
-        mlp_got,
         back_out,
         back_got,
-        gate,
-        up,
         active,
         gu,
         two_out,
@@ -484,15 +602,14 @@
     room, run = slots // experts, width // experts
     arrays = dict(
         zip(far_names, far_refs),
-        grads_in=grads_in,
-        grads_down=grads_down,
+        gin=grads_in,
+        gdown=grads_down,
         win=win,
         wdown=wdown,
         dy_run=dy_run_ref,
         dy=dy_ref,
         two=two,
         slots_out=slots_out,
-        mlp_got=mlp_got,
         back_out=back_out,
         back_got=back_got,
         active=active,
@@ -503,22 +620,30 @@
         dy_got=dy_got,
         gu_got=gu_got,
         active_got=active_got,
-        **{"in": in_ref, "down": down_ref},
+        down=down_ref,
+        **{"in": in_ref},
     )
     runs, base = {}, 0
     for name, moves in groups.items():
         runs[name] = Moves(ctx_count, moves, arrays, send, recv, (), base)
         base += len(moves)
     greet(ctx_count, masks_of([m for moves in groups.values() for m in moves]))
-    runs["load_in"].begin()
-    runs["load_down"].begin()
-    runs["far_in"].begin()
-    runs["dy"].begin()
+    stages = list_stages(experts)
+    runs["load", "in"].begin()
+    runs["load", "down"].begin()
+    runs["far", "in"].begin()
+    runs["far", "down"].begin()
+    for stage in range(len(stages)):
+        runs["dy", stage].begin()
     dy_ref[:, run_cols(run)] = dy_run_ref[...]
     x = tokens_ref[...].astype(F32) + branch_ref[...].astype(F32)
     inverse = lax.rsqrt(jnp.mean(x * x, axis=-1, keepdims=True) + EPSILON)
-    hidden = (x * inverse * gain_ref[...]).astype(BF)
-    for k in range(experts)[::-1]:
+    hidden = (x * inverse * gain_of(gain_ref, 1, part)).astype(BF)
+    mine = flip(lax.axis_index(FSDP), 0) * ctx_count + lax.axis_index(CTX)
+    lane = lax.broadcasted_iota(jnp.int32, (1, HD), 1)
+    chosen = (lane % experts == mine // share) & (lane < 2 * experts)
+    weights = jnp.sum(jnp.where(chosen, rides_ref[...].astype(F32), 0.0), axis=1, keepdims=True)
+    for k in [*range(1, experts), 0]:
         rows = slice(k * room, (k + 1) * room)
         picked = dot(place_ref[k], hidden, 1, 0).astype(BF)
         if k == 0:
@@ -527,56 +652,54 @@
         for i in range(experts):
             slots_out[rows, i * run : (i + 1) * run] = picked[:, (i ^ k) * run : ((i ^ k) + 1) * run]
         runs["slots"].start(k - 1)
-    runs["far_down"].begin()
-    runs["slots"].settle()
-    for t in range(1, share):
-        rows = slice((t - 1) * slots, t * slots)
-        for k in range(experts):
-            at = (k * share + t) * part
-            two_out[rows, k * part : (k + 1) * part] = two[:, at : at + part]
-    runs["share_two"].begin()
-    runs["load_in"].settle()
-    runs["far_in"].settle()
-    weight = weight_ref[...]
-    for at, size in chunks(units, 256):
-        cols = slice(at, at + size)
-        g = dot(two[...], win[:, cols], 1, 0)
-        u = dot(two[...], win[:, units + at : units + at + size], 1, 0)
-        silu = g * (1.0 / (1.0 + jnp.exp(-g)))
-        active[:, cols] = (silu * u * weight).astype(BF)
-        gate[:, cols] = g.astype(BF)
-        up[:, cols] = u.astype(BF)
-    runs["share_active"].begin()
-    runs["load_down"].settle()
-    runs["far_down"].settle()
-    runs["slots"].finish()
-    runs["dy"].settle()
-    for t in range(1, share):
-        rows = slice((t - 1) * slots, t * slots)
-        for k in range(experts):
-            at = (k * share + t) * part
-            dy_out[rows, k * part : (k + 1) * part] = dy_ref[:, at : at + part]
-    runs["share_dy"].begin()
-    for i in range(experts):
-        cols = slice(i * run, (i + 1) * run)
-        slots_out[:, cols] = dot(active[...], wdown[cols], 1, 1).astype(BF)
-        for k in range(1, experts):
-            runs["mlp"].start(i * (experts - 1) + k - 1)
-    for at, size in chunks(units, 256):
-        cols = slice(at, at + size)
-        grad = dot(dy_ref[...], wdown[:, cols], 1, 0) * weight
-        g, u = gate[:, cols].astype(F32), up[:, cols].astype(F32)
-        sigmoid = 1.0 / (1.0 + jnp.exp(-g))
-        gu[:, cols] = (grad * u * sigmoid * (1.0 + g * (1.0 - sigmoid))).astype(BF)
-        gu[:, units + at : units + at + size] = (grad * g * sigmoid).astype(BF)
-    runs["share_gu"].begin()
-    for i in range(experts):
-        cols = slice(i * run, (i + 1) * run)
-        back_out[:, cols] = dot(gu[...], win[cols], 1, 1).astype(BF)
-        for k in range(1, experts):
-            runs["back"].start(i * (experts - 1) + k - 1)
-    for name in ("dy", "far_in", "far_down", "share_two", "share_dy", "share_active", "share_gu"):
-        runs[name].finish()
+    for move in ("load", "far"):
+        for name in ("in", "down"):
+            runs[move, name].settle()
+    for stage, ks in enumerate(stages):
+        rows = slice(ks[0] * room, (ks[-1] + 1) * room)
+        for k in ks:
+            if k:
+                runs["slots"].await_one(k - 1)
+        runs["dy", stage].settle()
+        for t in range(1, share):
+            out_rows = slice((t - 1) * slots + rows.start, (t - 1) * slots + rows.stop)
+            for k in range(experts):
+                block = slice(k * part, (k + 1) * part)
+                at = slice((k * share + t) * part, (k * share + t + 1) * part)
+                two_out[out_rows, block] = two[rows, at]
+                dy_out[out_rows, block] = dy_ref[rows, at]
+        runs["two", stage, 0].begin()
+        runs["dy", stage, 0].begin()
+        two_rows, grad_rows = two[rows], dy_ref[rows]
+        weight = weights[rows]
+        for at, size in chunks(units, 256):
+            cols = slice(at, at + size)
+            g = dot(two_rows, win[:, cols], 1, 0)
+            u = dot(two_rows, win[:, units + at : units + at + size], 1, 0)
+            sigmoid = 1.0 / (1.0 + jnp.exp(-g))
+            silu = g * sigmoid
+            active[rows, cols] = (silu * u * weight).astype(BF)
+            grad = dot(grad_rows, wdown[:, cols], 1, 0) * weight
+            gu[rows, cols] = (grad * u * (sigmoid * (1.0 + g * (1.0 - sigmoid)))).astype(BF)
+            gu[rows, units + at : units + at + size] = (grad * silu).astype(BF)
+        runs["active", stage, 0].begin()
+        runs["gu", stage, 0].begin()
+        for i in range(experts):
+            cols = slice(i * run, (i + 1) * run)
+            back_out[rows, cols] = dot(gu[rows], win[cols], 1, 1).astype(BF)
+        for k in ks:
+            if k:
+                runs["back"].start(k - 1)
+        for i in range(experts):
+            cols = slice(i * run, (i + 1) * run)
+            out = dot(active[rows], wdown[cols], 1, 1).astype(BF)
+            for k in ks:
+                at = slice(k * room - rows.start, (k + 1) * room - rows.start)
+                turned = slice((i ^ k) * run, ((i ^ k) + 1) * run)
+                mlp_ref[k * room : (k + 1) * room, turned] = out[at]
+    for name in groups:
+        if isinstance(name, tuple) and name[0] != "load":
+            runs[name].finish()
     for k in range(experts):
         rows = slice(k * part, (k + 1) * part)
         own = slice(k * share * part, (k * share + 1) * part)
@@ -592,21 +715,21 @@
                 out[rows, cols] = total.astype(BF)
         runs["out"].start(2 * k)
         runs["out"].start(2 * k + 1)
-    for name, own, got, part_ref in (
-        ("mlp", slots_out, mlp_got, mlp_part),
-        ("back", back_out, back_got, two_part),
-    ):
-        runs[name].settle()
-        for i in range(experts):
-            total = dot(place_ref[0], own[:room, i * run : (i + 1) * run], 0, 0)
-            for k in range(1, experts):
-                at = (i ^ k) * run
-                total = total + dot(
-                    place_ref[k], got[k * room : (k + 1) * room, at : at + run], 0, 0
-                )
-            part_ref[:, i * run : (i + 1) * run] = total.astype(BF)
-        runs[name].finish()
+    runs["back"].settle()
+    for i in range(experts):
+        cols = slice(i * run, (i + 1) * run)
+        total = dot(place_ref[0], back_out[:room, cols], 0, 0)
+        for k in range(1, experts):
+            at = slice((i ^ k) * run, ((i ^ k) + 1) * run)
+            total = total + dot(place_ref[k], back_got[k * room : (k + 1) * room, at], 0, 0)
+        two_part[:, cols] = total.astype(BF)
+    runs["back"].finish()
     runs["out"].finish()
+    runs["slots"].finish()
+
+
+def list_stages(experts):
+    return [[0], list(range(1, experts - 1)), [experts - 1]]
 
 
 def run_experts(
@@ -619,39 +742,36 @@
     run = width // experts
     others = max(1, share - 1) * slots
     groups = {
-        "dy": [
-            (("dy_run", (0, slots), None), ("dy", (0, slots), ("tp", run)), -r, ())
-            for r in range(1, tp_count)
-        ],
         "slots": [
             (("slots_out", (k * room, room), None), ("two", (k * room, room), None), k * share, ())
             for k in range(1, experts)
         ],
-        "load_in": [(("in", r, None), ("win", r, None), None, ()) for r in fetched],
-        "load_down": [(("down", r, None), ("wdown", r, None), None, ()) for r in fetched],
-        "far_in": [m for m in far_moves if m[1][0] == "win"],
-        "far_down": [m for m in far_moves if m[1][0] == "wdown"],
+        ("load", "in"): [(("in", r, None), ("win", r, None), None, ()) for r in fetched],
+        ("load", "down"): [(("down", r, None), ("wdown", r, None), None, ()) for r in fetched],
+        ("far", "in"): [m for m in far_moves if m[1][0] == "win"],
+        ("far", "down"): [m for m in far_moves if m[1][0] == "wdown"],
     }
-    for name in ("two", "dy", "active", "gu"):
-        groups["share_" + name] = []
-        for t in range(1, share):
-            rows_at = ((t - 1) * slots, slots)
-            if name in ("two", "dy"):
-                source = (name + "_out", rows_at, None)
-            else:
-                source = (name, (0, slots), None)
-            groups["share_" + name].append((source, (name + "_got", rows_at, None), t, ()))
-    for name, source in (("mlp", "slots_out"), ("back", "back_out")):
-        groups[name] = []
-        for i in range(experts):
-            for k in range(1, experts):
-                at = ((k * room, room), (i * run, run))
-                groups[name].append(((source, *at), (name + "_got", *at), k * share, ()))
+    for stage, ks in enumerate(list_stages(experts)):
+        mine = (ks[0] * room, len(ks) * room)
+        groups["dy", stage] = [
+            (("dy_run", mine, None), ("dy", mine, (TP, run)), -r, ()) for r in range(1, tp_count)
+        ]
+        for name in ("two", "dy", "active", "gu"):
+            groups[name, stage, 0] = []
+            for t in range(1, share):
+                rows_at = ((t - 1) * slots + mine[0], mine[1])
+                source = (name + "_out", rows_at, None) if name in ("two", "dy") else (name, mine, None)
+                target = (name + "_got", rows_at, None)
+                groups[name, stage, 0].append((source, target, t, ()))
+    groups["back"] = [
+        (("back_out", (k * room, room), None), ("back_got", (k * room, room), None), k * share, ())
+        for k in range(1, experts)
+    ]
     groups["out"] = []
     for k in range(experts):
         r = (k * part, part)
-        groups["out"].append((("win", r, None), ("grads_in", r, None), None, ()))
-        groups["out"].append((("wdown", r, None), ("grads_down", r, None), None, ()))
+        groups["out"].append((("win", r, None), ("gin", r, None), None, ()))
+        groups["out"].append((("wdown", r, None), ("gdown", r, None), None, ()))
     total = sum(len(moves) for moves in groups.values())
     full = pl.BlockSpec(memory_space=pltpu.VMEM)
     any_spec = pl.BlockSpec(memory_space=pl.ANY)
@@ -660,7 +780,7 @@
         out_shape=[
             jax.ShapeDtypeStruct((experts * part, 2 * units), BF),
             jax.ShapeDtypeStruct((experts * part, units), BF),
-            jax.ShapeDtypeStruct((rows, width), BF),
+            jax.ShapeDtypeStruct((slots, width), BF),
             jax.ShapeDtypeStruct((rows, width), BF),
         ],
         in_specs=[full] * 6 + [any_spec] * (2 + len(far)),
@@ -668,8 +788,8 @@
         scratch_shapes=[
             pltpu.VMEM((width, 2 * units), BF),
             pltpu.VMEM((width, units), BF),
-            *[pltpu.VMEM((slots, width), BF)] * 5,
-            *[pltpu.VMEM((slots, units), BF)] * 3,
+            *[pltpu.VMEM((slots, width), BF)] * 4,
+            pltpu.VMEM((slots, units), BF),
             pltpu.VMEM((slots, 2 * units), BF),
             *[pltpu.VMEM((others, experts * part), BF)] * 4,
             pltpu.VMEM((others, 2 * units), BF),
@@ -688,7 +808,20 @@
     return pl.ds(pl.multiple_of(index * HD, HD), HD)
 
 
-def scores_of(place, queries, keys, segq, idxq, segk, idxk):
+def slot_table(place_ref, about_ref, out):
+    experts = place_ref.shape[0]
+    for e in range(experts):
+        found = dot(place_ref[e], about_ref[...], 1, 0)
+        filled = jnp.sum(place_ref[e].astype(F32), axis=1, keepdims=True)
+        found = jnp.where(filled > 0, found, about_ref[:1].astype(F32))
+        out[e, :, 0:1] = found[:, 0:1]
+        out[e, :, 1:2] = found[:, 1:2] * 32.0 + found[:, 2:3]
+        gate = found[:, 3 + e : 4 + e] + found[:, 3 + experts + e : 4 + experts + e]
+        out[e, :, 2:3] = gate * filled
+
+
+def scores_of(place, queries, keys, info, segk, idxk):
+    segq, idxq = info[:, 0:1], info[:, 1:2]
     slots = dot(place, queries, 1, 0).astype(BF)
     scores = dot(slots, keys, 1, 1) * (HD**-0.5)
     allowed = (segq == segk) & (idxk <= idxq)
@@ -707,14 +840,12 @@
     names_out,
     heads,
     part,
-    normed_ref,
+    tokens_ref,
     gain_ref,
     cos_ref,
     sin_ref,
     place_ref,
-    segq_ref,
-    idxq_ref,
-    gate_ref,
+    about_ref,
     segk_ref,
     idxk_ref,
     dy_ref,
@@ -723,43 +854,48 @@
     *refs,
 ):
     experts, room, rows = place_ref.shape
-    width = normed_ref.shape[1]
+    width = tokens_ref.shape[1]
     wide = heads * HD
     group = width // part
     given, refs = refs[: len(names_in)], refs[len(names_in) :]
-    gains_ref, hidden_ref, qkv_ref, kv_ref, mixed_ref, branch_ref, slots_ref = refs[:7]
-    refs = refs[7:]
-    made, (full, picked, send, recv, *bounces) = refs[: len(names_out)], refs[len(names_out) :]
-    arrays = {
-        "gain_own": gain_ref,
-        "gains": gains_ref,
-        "full": full,
-        "picked": picked,
-        "slots": slots_ref,
-        "qkv": qkv_ref,
-        "kv": kv_ref,
-        **dict(zip(names_in, given)),
-        **dict(zip(names_out, made)),
-    }
+    gains_ref, hidden_ref, qkv_ref, kv_ref, mixed_ref, branch_ref, slots_ref, rides_ref = refs[:8]
+    refs = refs[8:]
+    made, (full, picked, picked_ride, slot_info, send, recv, *bounces) = refs[: len(names_out)], refs[len(names_out) :]
+    arrays = dict(
+        gain_own=gain_ref,
+        gains=gains_ref,
+        picked=picked,
+        slots=slots_ref,
+        picked_ride=picked_ride,
+        rides=rides_ref,
+        qkv=qkv_ref,
+        kv=kv_ref,
+        full=full,
+    )
+    arrays.update(zip(names_in, given))
+    arrays.update(zip(names_out, made))
     greet(ctx_count, masks_of(moves))
     run = Moves(ctx_count, moves, arrays, send, recv, bounces)
-    gains_done, first_done, rest_done, keys_done, dy_done = marks
+    gains_done, first_done, second_done, rest_done, keys_done, dy_done = marks
     run_of = dy_ref.shape[1] // experts
     for k in range(experts):
         rows_at = slice(k * room, (k + 1) * room)
-        side = slots_ref if k == 0 else picked
         cols = run_cols(run_of, k)
-        side[rows_at, :run_of] = dot(place_mlp_ref[k], dy_ref[:, cols], 1, 0).astype(BF)
-        side[rows_at, run_of:] = dot(place_mlp_ref[k], ride_ref[...], 1, 0).astype(BF)
-    run.begin(rest_done)
+        slots = dot(place_mlp_ref[k], dy_ref[:, cols], 1, 0).astype(BF)
+        rides = dot(place_mlp_ref[k], ride_ref[...], 1, 0).astype(BF)
+        if k:
+            picked[rows_at], picked_ride[rows_at] = slots, rides
+        else:
+            slots_ref[rows_at], rides_ref[rows_at] = slots, rides
+    run.begin(second_done)
     gains_ref[:16] = gain_ref[...]
+    slot_table(place_ref, about_ref, slot_info)
+    x = tokens_ref[...].astype(F32)
+    normed = x * lax.rsqrt(jnp.mean(x * x, axis=-1, keepdims=True) + EPSILON)
     run.settle(gains_done)
-    for j in range(group):
-        cols = slice(j * part, (j + 1) * part)
-        gain = gains_ref[j * 16 : (j + 1) * 16].astype(F32)[:1, :part]
-        hidden_ref[:, cols] = (normed_ref[:, cols] * gain).astype(BF)
+    hidden_ref[...] = (normed * gain_of(gains_ref, 0, part)).astype(BF)
     run.settle(first_done, gains_done)
-    cos, sin = cos_ref[...], sin_ref[...]
+    cos, sin = cos_ref[:rows], sin_ref[:rows]
 
     def project(plane):
         y = dot(hidden_ref[...], full[:, plane * wide : (plane + 1) * wide], 1, 0)
@@ -771,14 +907,17 @@
 
     project(experts)
     project(experts + 1)
-    run.begin(keys_done)
+    for i in range(rest_done, keys_done):
+        if not moves[i][3]:
+            run.start(i)
     kv_ref[:rows] = qkv_ref[:, experts * wide :]
     run.begin()
+    run.settle(second_done, first_done)
     for plane in range(experts):
         project(plane)
-    run.settle(rest_done, first_done)
+    run.settle(keys_done, rest_done)
+    run.settle(rest_done, second_done)
     run.start(len(moves) - 1)
-    run.settle(keys_done, rest_done)
 
     def step(i, carry):
         h, e = i // experts, i % experts
@@ -788,13 +927,12 @@
             place,
             qkv_ref[:, cols],
             kv_ref[:, head_cols(h)],
-            segq_ref[e],
-            idxq_ref[e],
+            slot_info[e],
             segk_ref[...],
             idxk_ref[...],
         )
         attn = dot(exps.astype(BF), kv_ref[:, head_cols(heads + h)], 1, 0) * inv
-        mixed = (attn * gate_ref[e]).astype(BF)
+        mixed = (attn * slot_info[e][:, 2:3]).astype(BF)
         mixed_ref[:, cols] = dot(place, mixed, 0, 0).astype(BF)
         return carry
 
@@ -806,9 +944,9 @@
 
 
 def front(number, ctx_count, heads, part, moves, later, given, made, small):
-    normed, gain_own, place = small[0], small[1], small[4]
-    experts, _, rows = place.shape
-    width = normed.shape[1]
+    tokens, gain_own, place = small[0], small[1], small[4]
+    experts, room, rows = place.shape
+    width = tokens.shape[1]
     wide = heads * HD
     group = width // part
     full_wide = 2 * (experts + 1) * wide
@@ -824,15 +962,17 @@
                 source = ("qkv", (0, rows), (experts * wide, 2 * wide))
                 kv_moves.append((source, target, 1 << bit, ()))
         order = order + order
-    gains_moves, first_moves, rest_moves, dy_moves = moves
+    gains_moves, first_moves, second_moves, rest_moves, dy_moves = moves
     marks = [len(gains_moves)]
-    for more in (first_moves, rest_moves, kv_moves, dy_moves):
+    for more in (first_moves, second_moves, rest_moves, kv_moves, dy_moves):
         marks.append(marks[-1] + len(more))
-    whole = ("full", (0, width), None)
-    landed = tuple(m[1] for m in first_moves + rest_moves if m[1][0] == "full")
+    whole = (FULL, (0, width), None)
+    gathered = first_moves + second_moves + rest_moves
+    landed = tuple(m[1] for m in gathered)
     keep = [(whole, ("kept", (0, width), None), None, landed)]
-    moves = gains_moves + first_moves + rest_moves + kv_moves + dy_moves + later + keep
-    slots_shape = (experts * place.shape[1], width // experts + HD)
+    moves = gains_moves + gathered + kv_moves + dy_moves + later + keep
+    slots_shape = (experts * place.shape[1], width // experts)
+    rides_shape = (experts * place.shape[1], HD)
     names_in, names_out = list(given), [*made, "kept"]
     shapes_out = [*made.values(), (width, full_wide)]
     any_spec = pl.BlockSpec(memory_space=pl.ANY)
@@ -845,6 +985,7 @@
         ((rows, experts * wide), BF),
         ((rows, width), BF),
         (slots_shape, BF),
+        (rides_shape, BF),
     ]
     bounces = [
         pltpu.VMEM((source[1][1], (source[2] or (0, given[source[0]].shape[1]))[1]), BF)
@@ -859,7 +1000,12 @@
         + [jax.ShapeDtypeStruct(shape, BF) for shape in shapes_out],
         in_specs=[full] * len(small) + [any_spec] * len(names_in),
         out_specs=[full] * len(small_out) + [any_spec] * len(names_out),
-        scratch_shapes=[pltpu.VMEM((width, full_wide), BF), pltpu.VMEM(slots_shape, BF)]
+        scratch_shapes=[
+            pltpu.VMEM((width, full_wide), BF),
+            pltpu.VMEM(slots_shape, BF),
+            pltpu.VMEM(rides_shape, BF),
+            pltpu.VMEM((experts, room, HD), F32),
+        ]
         + [pltpu.SemaphoreType.DMA((len(moves),))] * 2
         + bounces,
         compiler_params=pltpu.CompilerParams(
@@ -886,8 +1032,7 @@
     qkv_ref,
     kv_ref,
     place_ref,
-    segq_ref,
-    idxq_ref,
+    about_ref,
     segk_ref,
     idxk_ref,
     cos_ref,
@@ -900,14 +1045,32 @@
     wide = heads * HD
     width = tokens_ref.shape[1]
     given, refs = refs[: len(names_in)], refs[len(names_in) :]
-    out_ref, resid_ref, grad_branch_ref, gain_out_ref, back_one_ref = refs[:5]
-    made, refs = refs[5 : 5 + len(names_out)], refs[5 + len(names_out) :]
-    full, grad_ref, back_acc, dk_acc, dv_acc, total, got, send, recv, pass_send, pass_recv, load = refs
+    out_ref, resid_ref, grad_branch_ref, gain_out_ref, back_one_ref, mlp_out_ref = refs[:6]
+    made, refs = refs[6 : 6 + len(names_out)], refs[6 + len(names_out) :]
+    (
+        full,
+        grad_ref,
+        back_acc,
+        dk_acc,
+        dv_acc,
+        total,
+        got,
+        mlp_mine,
+        mlp_got,
+        slot_info,
+        send,
+        recv,
+        pass_send,
+        pass_recv,
+        load,
+    ) = refs
     arrays = {**dict(zip(names_in, given)), **dict(zip(names_out, made))}
+    arrays.update(mlp_mine=mlp_mine, mlp_got=mlp_got)
     bits = range(bits_of(ctx_count))
     greet(ctx_count, sorted({*masks_of(moves), *[1 << b for b in bits]}))
     run = Moves(ctx_count, moves, arrays, send, recv)
     run.begin()
+    slot_table(place_ref, about_ref, slot_info)
     edge = (experts + 2) * wide
     loads = []
     for i, cols in enumerate((pl.ds(edge, experts * wide), pl.ds(0, edge))):
@@ -919,7 +1082,7 @@
     normed = x * inverse
     back = back_ref[...].astype(F32)
     gain_out_ref[...] = jnp.sum(back * normed, axis=0, keepdims=True)
-    scaled = back * gain_ref[...]
+    scaled = back * gain_of(gain_ref, 1, part)
     inner = jnp.mean(scaled * normed, axis=-1, keepdims=True)
     resid = dy_ref[...].astype(F32) + inverse * (scaled - normed * inner)
     resid_ref[...] = resid
@@ -965,7 +1128,7 @@
             place = place_ref[e]
             k, v = kv_ref[:, h * HD : (h + 1) * HD], kv_ref[:, (heads + h) * HD : (heads + h + 1) * HD]
             slots, exps, inv = scores_of(
-                place, qkv_ref[:, cols], k, segq_ref[e], idxq_ref[e], segk_ref[...], idxk_ref[...]
+                place, qkv_ref[:, cols], k, slot_info[e], segk_ref[...], idxk_ref[...]
             )
             attn = dot(exps.astype(BF), v, 1, 0) * inv
             probs = exps * inv
@@ -1002,25 +1165,40 @@
         rows_at = slice(j * part, (j + 1) * part)
         keyed = dot(out_ref[:, queries:], full[rows_at, queries:edge], 1, 1)
         back_one_ref[:, rows_at] = (back_acc[:, rows_at] + keyed).astype(BF)
+    runs_mlp = [i for i, m in enumerate(moves) if m[0][0] == "mlp"]
+    for i in runs_mlp:
+        run.await_one(i)
+    mlp_total = mlp_mine[...].astype(F32)
+    for r in range(len(runs_mlp) - 1):
+        mlp_total = mlp_total + mlp_got[r * mlp_mine.shape[0] : (r + 1) * mlp_mine.shape[0]].astype(F32)
+    mlp_out_ref[...] = mlp_total.astype(BF)
     for h in range(heads):
         for bit in bits:
             head_copy(h, bit).wait_send()
     run.finish()
 
 
-def attend_back(number, ctx_count, heads, part, moves, given, made, weight, *small):
+def attend_back(number, ctx_count, tp_count, heads, part, moves, given, made, weight, *small):
     tokens, qkv, kv = small[0], small[6], small[7]
     rows, width = tokens.shape
     keys = kv.shape[0]
     any_spec = pl.BlockSpec(memory_space=pl.ANY)
     full = pl.BlockSpec(memory_space=pltpu.VMEM)
     passes = heads * bits_of(ctx_count)
+    slots, run = given["mlp"].shape[0], width // tp_count
+    every = (0, slots)
+    mlp_moves = [(("mlp", every, (TP, run)), ("mlp_mine", every, None), None, ())]
+    for r in range(1, tp_count):
+        target = ("mlp_got", ((r - 1) * slots, slots), None)
+        mlp_moves.append((("mlp", every, (TP, run, r)), target, -r, ()))
+    moves = mlp_moves + moves
     small_out = [
         (qkv.shape, BF),
         ((rows, width), F32),
         ((rows, width), BF),
         ((1, width), F32),
         ((rows, width), BF),
+        ((slots, run), BF),
     ]
     out = pl.pallas_call(
         functools.partial(
@@ -1030,6 +1208,9 @@
         + [jax.ShapeDtypeStruct(shape, BF) for shape in made.values()],
         in_specs=[full] * len(small) + [any_spec] * (1 + len(given)),
         out_specs=[full] * len(small_out) + [any_spec] * len(made),
+        input_output_aliases={
+            len(small) + 1 + list(given).index(n): len(small_out) + i for i, n in enumerate(made)
+        },
         scratch_shapes=[
             pltpu.VMEM(weight.shape, BF),
             pltpu.VMEM((rows, weight.shape[1] - qkv.shape[1]), BF),
@@ -1037,7 +1218,9 @@
         ]
         + [pltpu.VMEM((keys, HD), F32)] * 2
         + [pltpu.VMEM((heads, keys, 2 * HD), BF)] * 2
-        + [pltpu.SemaphoreType.DMA((max(1, len(moves)),))] * 2
+        + [pltpu.VMEM((slots, run), BF), pltpu.VMEM(((tp_count - 1) * slots, run), BF)]
+        + [pltpu.VMEM((*small[8].shape[:2], HD), F32)]
+        + [pltpu.SemaphoreType.DMA((len(moves),))] * 2
         + [pltpu.SemaphoreType.DMA((passes,))] * 2
         + [pltpu.SemaphoreType.DMA((2,))],
         compiler_params=pltpu.CompilerParams(
@@ -1049,28 +1232,33 @@
 
 
 def spread_kernel(experts, me_ref, *refs):
-    blocks, (in_ref, down_ref) = refs[:experts], refs[experts:]
+    from_in, from_down = refs[:experts], refs[experts : 2 * experts]
+    in_ref, down_ref = refs[2 * experts :]
     units = down_ref.shape[2]
     for m in range(experts):
 
         @pl.when(me_ref[0] == m)
         def _():
             for e in range(experts):
-                block = blocks[e ^ m]
                 for c in range(2):
-                    in_ref[:, e, c, :] = block[:, c * units : (c + 1) * units].astype(F32)
-                down_ref[:, e, :] = block[:, 2 * units :].astype(F32)
-
-
-def spread_grads(blocks, me, in_shape, down_shape):
-    experts = len(blocks)
-    step = min(32, in_shape[0])
+                    in_ref[:, e, c, :] = from_in[e ^ m][:, c * units : (c + 1) * units].astype(F32)
+                down_ref[:, e, :] = from_down[e ^ m][...].astype(F32)
+
+
+def spread_grads(from_in, from_down, me, in_shape, down_shape):
+    experts = len(from_in)
+    step = min(64, in_shape[0])
+
+    def rows_of(width):
+        return pl.BlockSpec((step, width), lambda i, m: (i, 0))
+
     return pl.pallas_call(
         functools.partial(spread_kernel, experts),
         grid_spec=pltpu.PrefetchScalarGridSpec(
             num_scalar_prefetch=1,
             grid=(in_shape[0] // step,),
-            in_specs=[pl.BlockSpec((step, blocks[0].shape[1]), lambda i, m: (i, 0))] * experts,
+            in_specs=[rows_of(from_in[0].shape[1])] * experts
+            + [rows_of(from_down[0].shape[1])] * experts,
             out_specs=[
                 pl.BlockSpec((step, *in_shape[1:]), lambda i, m: (i, 0, 0, 0)),
                 pl.BlockSpec((step, *down_shape[1:]), lambda i, m: (i, 0, 0)),
@@ -1082,7 +1270,7 @@
         ],
         compiler_params=pltpu.CompilerParams(vmem_limit_bytes=VMEM_LIMIT),
         name="spread_grads",
-    )(me.astype(jnp.int32).reshape(1), *blocks)
+    )(me.astype(jnp.int32).reshape(1), *from_in, *from_down)
 
 
 def places(routes, gates, experts, cap, room):
@@ -1098,8 +1286,9 @@
     return taken, gate
 
 
-def slot_sum(taken, values):
-    return jnp.sum(jnp.where(taken, values, 0), axis=-1, keepdims=True)
+def split(x):
+    high = x.astype(BF)
+    return high, (x - high.astype(F32)).astype(BF)
 
 
 def layer(
@@ -1122,7 +1311,7 @@
     fsdp_count, ctx_count, tp_count = counts
     group = fsdp_count * ctx_count
     me = lax.axis_index(GROUP)
-    ctx_me = lax.axis_index("ctx")
+    ctx_me = lax.axis_index(CTX)
     rows, width = tokens.shape[1:]
     cap = 9 * rows // 16
     room = -(-cap // 16) * 16
@@ -1145,15 +1334,13 @@
 
     high, second = group // 2, group // 4
 
-    qkv_wide = (attn_experts + 2) * head_width
-    attn_own = jnp.concatenate(
-        [w_query.reshape(part, -1), w_kv.reshape(part, -1), w_out_attn.reshape(part, -1)], axis=1
-    )
-    attn_wide = attn_own.shape[1]
-    gain_own = jnp.pad(
-        jnp.concatenate([gain_attn, gain_mlp])[None, :], ((0, 15), (0, 0))
-    )
-    far_x, far_y = exchange(attn_own, high), exchange(attn_own, second)
+    gain_own = jnp.pad(jnp.concatenate([gain_attn, gain_mlp])[None, :], ((0, 15), (0, 0)))
+    kv_out_own = jnp.concatenate([w_kv.reshape(part, -1), w_out_attn.reshape(part, -1)], axis=1)
+    attn_own = [w_query.reshape(part, -1), kv_out_own]
+    far_x, far_y = [], []
+    for own in attn_own:
+        far_x.append(exchange(own, high))
+        far_y.append(exchange(own, second))
 
     seg_row = segments[0]
     seq_total = seg_row.shape[0]
@@ -1179,15 +1366,15 @@
     taken_attn, gate_attn = places(attn_routes[0], attn_gates[0], attn_experts, cap, room)
     place_attn = taken_attn.astype(BF)
     own_seg, own_idx = key_seg[:rows], key_idx[:rows]
-    filled = jnp.any(taken_attn, axis=-1, keepdims=True)
-    slot_seg = jnp.where(filled, slot_sum(taken_attn, own_seg), own_seg[0])
-    slot_idx = jnp.where(filled, slot_sum(taken_attn, own_idx), own_idx[0])
-    slot_gate = slot_sum(taken_attn, gate_attn.T[:, None, :])
+    gate_high, gate_low = split(gate_attn)
+    about = [own_seg[:, None], (own_idx // 32)[:, None], (own_idx % 32)[:, None], gate_high, gate_low]
+    about = jnp.concatenate([x.astype(BF) for x in about], axis=1)
+    about = jnp.pad(about, ((0, 0), (0, HD - about.shape[1])))
+    key_row = (key_seg.astype(F32)[None, :], key_idx.astype(F32)[None, :])
     taken_mlp, gate_mlp = places(mlp_routes[0], mlp_gates[0], experts, cap, room)
     mine_first = [expert_me ^ k for k in range(experts)]
     place_mlp = jnp.concatenate([piece(taken_mlp, e, 1, 0) for e in mine_first]).astype(BF)
     tokens_rel, grad_out = in_order(me, [tokens[0], cotangent[0]], group)
-    inputs = tokens_rel.astype(F32)
 
     def expert_rows(k):
         in_rows = piece(w_in, expert_me ^ k, 1, 1)
@@ -1197,7 +1384,7 @@
     to_send = [expert_rows(k) for k in range(experts)]
 
     def given_sends(ks):
-        return {f"send{k}{c}": x for k in ks for c, x in enumerate(to_send[k])}
+        return {("send", k, c): x for k in ks for c, x in enumerate(to_send[k])}
 
     in_cols, down_cols = (0, 2 * hidden_units), (2 * hidden_units, hidden_units)
     weight_shapes = {"in": (width, 2 * hidden_units), "down": (width, hidden_units)}
@@ -1207,7 +1394,7 @@
         sides = (("in", (0, hidden_units)), ("in", (hidden_units, hidden_units)), ("down", None))
         for c, (name, cols) in enumerate(sides):
             base = k * share * part + first
-            source = (f"send{k}{c}", (first, size), None)
+            source = (("send", k, c), (first, size), None)
             landed = (prefix + name, (base, size), cols)
             moves.append((source, landed, k * share, ()))
             for t in range(1, share):
@@ -1225,56 +1412,58 @@
     far = [k for k in range(1, experts) if k & (k - 1)]
     half_part = part // 2
 
-    normed_one, inverse_one = normalize(inputs)
-    (attn_own, far_x, far_y, gain_own), to_send, tables = lax.optimization_barrier(
-        (
-            (attn_own, far_x, far_y, gain_own),
-            to_send,
-            (normed_one, cos, sin, place_attn, slot_seg, slot_idx, slot_gate, place_mlp),
-        )
-    )
-    normed_one, cos, sin, place_attn, slot_seg, slot_idx, slot_gate, place_mlp = tables
-    quarter = part // 4
+    far_x, to_send = lax.optimization_barrier((far_x, to_send))
+    cut = max(16, part * 3 // 8 // 16 * 16)
     gather_moves = []
-    for cols in ((0, qkv_wide), (qkv_wide, attn_wide - qkv_wide)):
+    queries, two_planes = attn_experts * head_width, 2 * head_width
+    for n, first, size_of, edge in (
+        (1, 0, two_planes, queries),
+        (0, 0, queries, 0),
+        (1, two_planes, queries, queries + two_planes),
+    ):
+        cols, own_cols = (edge, size_of), (first, size_of)
         moves = []
-        held = {0: [("own", 0, part, ())], high: [("far_x", 0, part, ())], second: [("far_y", 0, part, ())]}
-        held[high | second] = []
-        for i in (0, 2, 1, 3):
-            source, mask = (("far_x", second), ("far_y", high))[i // 2]
-            target = ("full", ((high | second) * part + i * quarter, quarter), cols)
-            moves.append(((source, (i * quarter, quarter), cols), target, mask, ()))
-            held[high | second].append(("full", i * quarter, quarter, (target,)))
+        held = {0: [(("own", n), 0, part, ())], high: [(("x", n), 0, part, ())], second: [(("y", n), 0, part, ())]}
+        corner = []
+        for side, mask, low, top in ((("x", n), second, 0, cut), (("y", n), high, cut, part)):
+            half = (top - low) // 32 * 16
+            for at, size in ((low, half), (low + half, top - low - half)):
+                if size:
+                    target = (FULL, ((high | second) * part + at, size), cols)
+                    corner.append(((side, (at, size), own_cols), target, mask, ()))
+        corner = corner[::2] + corner[1::2]
+        moves += corner
+        held[high | second] = [(FULL, t[1][0] - (high | second) * part, t[1][1], (t,)) for _, t, _, _ in corner]
         for j in (0, high, second):
-            name = held[j][0][0]
-            moves.append(((name, (0, part), cols), ("full", (j * part, part), cols), None, ()))
+            source = (held[j][0][0], (0, part), own_cols)
+            moves.append((source, (FULL, (j * part, part), cols), None, ()))
         for bit in range(bits_of(group) - 2)[::-1]:
             for j in list(held):
                 there = []
                 for name, at, size, needs in held[j]:
-                    source = (name, (at + j * part if name == "full" else at, size), cols)
-                    target = ("full", ((j | 1 << bit) * part + at, size), cols)
+                    if name == FULL:
+                        source = (name, (at + j * part, size), cols)
+                    else:
+                        source = (name, (at, size), own_cols)
+                    target = (FULL, ((j | 1 << bit) * part + at, size), cols)
                     moves.append((source, target, 1 << bit, needs))
-                    there.append(("full", at, size, (target,)))
+                    there.append((FULL, at, size, (target,)))
                 held[j | 1 << bit] = there
         gather_moves.append(moves)
     gain_moves = [
         (("gain_own", (0, 16), None), ("gains", (j * 16, 16), None), j, ())
         for j in range(1, group)
     ]
-    key_row = (key_seg[None, :], key_idx[None, :])
     heads = head_width // HD
     later = weight_moves(0, 0, part) + many_weight_moves([(k, 0, half_part) for k in near])
-    gate_high = gate_mlp.astype(BF)
-    gate_low = (gate_mlp - gate_high.astype(F32)).astype(BF)
-    gate_ride = jnp.pad(
-        jnp.concatenate([gate_high, gate_low], axis=1), ((0, 0), (0, HD - 2 * experts))
-    )
+    gate_ride = jnp.concatenate(split(gate_mlp), axis=1)
+    gate_ride = jnp.pad(gate_ride, ((0, 0), (0, HD - 2 * experts)))
     dy_moves = [
-        (("picked", (k * room, room), None), ("slots", (k * room, room), None), k * share, ())
+        ((name, (k * room, room), None), (target, (k * room, room), None), k * share, ())
         for k in range(1, experts)
+        for name, target in (("picked", "slots"), ("picked_ride", "rides"))
     ]
-    (gains, hidden_one, qkv, kv, mixed, branch, dy_got), made = front(
+    (gains, hidden_one, qkv, kv, mixed, branch, dy_run, dy_rides), made = front(
         1,
         ctx_count,
         heads,
@@ -1282,21 +1471,19 @@
         (gain_moves, *gather_moves, dy_moves),
         later,
         {
-            "own": attn_own,
-            "far_x": far_x,
-            "far_y": far_y,
+            **{("own", n): x for n, x in enumerate(attn_own)},
+            **{("x", n): x for n, x in enumerate(far_x)},
+            **{("y", n): x for n, x in enumerate(far_y)},
             **given_sends([0, *near]),
         },
         weight_shapes,
         (
-            normed_one,
+            tokens_rel,
             gain_own,
-            cos[:rows],
-            sin[:rows],
+            cos,
+            sin,
             place_attn,
-            slot_seg,
-            slot_idx,
-            slot_gate,
+            about,
             *key_row,
             grad_out,
             gate_ride,
@@ -1304,19 +1491,7 @@
         ),
     )
     attn_full, weights = made["kept"], {n: made[n] for n in weight_shapes}
-    gains = gains.reshape(group, 16, 2 * part)[:, 0].astype(F32)
-    gain_one, gain_two = gains[:, :part].reshape(1, width), gains[:, part:].reshape(1, width)
-
-    run = width // experts
-    own_gate = jnp.tile(jnp.arange(experts) == expert_me, 2)
-    slot_weight = jnp.sum(
-        jnp.where(own_gate[None, :], dy_got[:, run : run + 2 * experts].astype(F32), 0.0),
-        axis=1,
-        keepdims=True,
-    )
-    grad_slots = dy_got[:, :run]
-
-    branch_sum = lax.psum(branch, "tp")
+    branch_sum = lax.psum(branch, TP)
     cuts = [(k, half_part, part - half_part) for k in near] + [(k, 0, half_part) for k in far]
     to_send, weights, _ = lax.optimization_barrier((to_send, weights, branch))
     given = {**given_sends([*near, *far]), **weights}
@@ -1330,7 +1505,7 @@
             fetched.append((j * part, size))
     for k in far:
         far_moves += weight_moves(k, half_part, part - half_part, "w")
-    grads_in, grads_down, mlp_part, back_two_part = run_experts(
+    grads_in, grads_down, mlp_slots, back_two_part = run_experts(
         4,
         ctx_count,
         tp_count,
@@ -1343,35 +1518,46 @@
         weights,
         tokens_rel,
         branch_sum,
-        gain_two,
+        gains,
         place_mlp,
-        grad_slots,
-        slot_weight,
+        dy_run,
+        dy_rides,
     )
-    back_two = lax.psum(back_two_part, "tp")
-    grads_got = {0: jnp.concatenate([grads_in[:part], grads_down[:part]], axis=1)}
-
-    def grad_moves(ks):
+    back_two = lax.psum(back_two_part, TP)
+    got_in, got_down = {0: grads_in}, {0: grads_down}
+
+    def grad_moves(ks, cuts, first=0):
         moves = []
-        for k in ks:
-            rows_at = (k * part, part)
-            for name, cols in (("grads_in", in_cols), ("grads_down", down_cols)):
-                target = (f"got{k}", (0, part), cols)
-                moves.append(((name, rows_at, None), target, k * share, ()))
-        return moves, {f"got{k}": (part, 3 * hidden_units) for k in ks}
-
-    moves, made_shapes = grad_moves(near)
+        for at in range(first, part, part // cuts):
+            for k in ks:
+                for name in ("in", "down"):
+                    source = (name, (k * part + at, part // cuts), None)
+                    target = ((name, k), (at, part // cuts), None)
+                    moves.append((source, target, k * share, ()))
+        made_shapes = {("in", k): (part, 2 * hidden_units) for k in ks}
+        return moves, {**made_shapes, **{("down", k): (part, hidden_units) for k in ks}}
+
+    def keep_grads(made, ks):
+        got_in.update({k: made[("in", k)] for k in ks})
+        got_down.update({k: made[("down", k)] for k in ks})
+
+    moves, made_shapes = grad_moves(near, 1)
+    early, early_shapes = grad_moves(far, 4)
+    moves += early[: len(early) // 4]
+    made_shapes.update(early_shapes)
     grads_in, grads_down, _ = lax.optimization_barrier((grads_in, grads_down, back_two_part))
-    given = {"grads_in": grads_in, "grads_down": grads_down}
+    given = {"in": grads_in, "down": grads_down}
     made = move("grads_near", 5, ctx_count, moves, given, made_shapes)
-    grads_got.update({k: made[f"got{k}"] for k in near})
-    grads_near = [grads_got[k] for k in near]
-
-    moves, made_shapes = grad_moves(far)
-    back_two, given, _ = lax.optimization_barrier((back_two, given, grads_near))
-    (grad_qkv, grad_resid, grad_branch, gain_two_grad, back_one_part), made = attend_back(
+    keep_grads(made, near)
+
+    moves, made_shapes = grad_moves(far, 4, part // 4)
+    back_two, given, made = lax.optimization_barrier((back_two, given, made))
+    given.update({name: made[name] for name in made_shapes})
+    given["mlp"] = mlp_slots
+    (grad_qkv, grad_resid, grad_branch, gain_two_grad, back_one_part, mlp_run), made = attend_back(
         6,
         ctx_count,
+        tp_count,
         heads,
         part,
         moves,
@@ -1380,54 +1566,68 @@
         attn_full,
         tokens_rel,
         branch_sum,
-        gain_two,
+        gains,
         back_two,
         grad_out,
         gate_attn,
         qkv,
         kv,
         place_attn,
-        slot_seg,
-        slot_idx,
+        about,
         *key_row,
         cos,
         sin,
     )
-    grads_got.update({k: made[f"got{k}"] for k in far})
-    mlp_total = lax.psum(mlp_part, "tp").astype(F32)
-    back_one = lax.psum(back_one_part, "tp").astype(F32)
-    grad_input_norm, gain_one_grad = norm_back(back_one, normed_one, inverse_one, gain_one)
-    grad_tokens = (grad_resid + grad_input_norm).astype(BF)
-
-    resid = inputs + branch_sum.astype(F32)
-    output, grad_tokens = in_order(me, [(resid + mlp_total).astype(BF), grad_tokens], group)
-
+    keep_grads(made, far)
     upper = list(range(1, bits_of(group)))
-    grad_attnw = attn_grads(
-        7, ctx_count, upper, part, head_width, hidden_one, grad_branch, grad_qkv, mixed
+    grad_attnw, grad_tokens, gain_grads, mlp_sum = attn_grads(
+        7,
+        ctx_count,
+        tp_count,
+        upper,
+        part,
+        head_width,
+        hidden_one,
+        grad_branch,
+        grad_qkv,
+        mixed,
+        back_one_part,
+        tokens_rel,
+        gains,
+        grad_resid,
+        gain_two_grad,
+        mlp_run,
+        place_mlp,
     )
+    output, grad_tokens = last(me, group, tokens_rel, branch_sum, mlp_sum, grad_tokens)
     grad_query_w, grad_kv_w, grad_out_w = lay_out(
         grad_attnw, (w_query.shape, w_kv.shape, w_out_attn.shape)
     )
-    gain_grads = gain_sums(9, ctx_count, group, [gain_one_grad, gain_two_grad[0]])
 
     return (
         output[None],
         grad_tokens[None],
-        *gain_grads,
+        gain_grads[0],
+        gain_grads[1],
         grad_kv_w,
         grad_query_w,
         grad_out_w,
-        *spread_grads([grads_got[k] for k in range(experts)], expert_me, w_in.shape, w_down.shape),
+        *spread_grads(
+            [got_in[k] for k in range(experts)],
+            [got_down[k] for k in range(experts)],
+            expert_me,
+            w_in.shape,
+            w_down.shape,
+        ),
     )
 
 
 def solution(mesh):
-    rows = P("fsdp", "ctx", None)
-    weight = P(GROUP, None, "tp")
-    weight_in = P(GROUP, None, None, "tp")
+    rows = P(FSDP, CTX, None)
+    weight = P(GROUP, None, TP)
+    weight_in = P(GROUP, None, None, TP)
     return jax.shard_map(
-        functools.partial(layer, tuple(mesh.shape[a] for a in ("fsdp", "ctx", "tp"))),
+        functools.partial(layer, tuple(mesh.shape[a] for a in (FSDP, CTX, TP))),
         mesh=mesh,
         in_specs=(
             rows,
@@ -1438,7 +1638,7 @@
             weight,
             weight_in,
             weight,
-            P("fsdp", None),
+            P(FSDP, None),
             rows,
             rows,
             rows,

time: 622 us -> 561 us (0.902)
  Pallas kernels: 513 us -> 474 us
  other arithmetic: 23 us -> 8.52 us
  local copies, waits for them, and re-layouts: 48.8 us -> 39.1 us
    pallas_call x1, Pallas kernels: 123 us -> 84.9 us  [run_experts(): pl.pallas_call(functools.partial(experts_kernel, ctx_count, experts, shar...]
    pallas_call x2, Pallas kernels: 102 us -> 114 us  [move(): pl.pallas_call(functools.partial(move_kernel, ctx_count, moves, plain + [...]
    slice x9 -> x1, local copies, waits for them, and re-layouts: 10 us -> 1.34 us  [layer(): gain_grads[1]]
    pallas_call x1, Pallas kernels: 68.5 us -> 61.6 us  [attend_back(): pl.pallas_call(functools.partial(attend_back_kernel, ctx_count, moves, li...]
  transfers between devices with their start and end apart: 5 -> 6, of which waited for: 2 -> 2; matrix products, arithmetic and copies ran while one was open for 8% -> 7% of each run, Pallas kernels for 37% -> 22%
where the time goes in v5:
time: 561 us; the launch traced here: 550 us
  Pallas kernels  474 us (84%)
  local copies, waits for them, and re-layouts  39.1 us (7%)
  between operations  15.1 us (3%)
  other arithmetic  8.52 us (2%)
  waiting for transfers between devices  6.86 us (1%)
    pallas_call x2, Pallas kernels, move(): pl.pallas_call(functools.partial(move_kernel, ctx_count, moves, plain + [...  114 us
    pallas_call x1, Pallas kernels, attn_grads(): pl.pallas_call(functools.partial(attn_grads_kernel, ctx_count, groups, bi...  107 us
    pallas_call x1, Pallas kernels, run_experts(): pl.pallas_call(functools.partial(experts_kernel, ctx_count, experts, shar...  84.9 us
    pallas_call x1, Pallas kernels, front(): pl.pallas_call(functools.partial(front_kernel, ctx_count, moves, marks, n...  80.2 us
    pallas_call x1, Pallas kernels, attend_back(): pl.pallas_call(functools.partial(attend_back_kernel, ctx_count, moves, li...  61.6 us
    slice x1, local copies, waits for them, and re-layouts, expert_rows(): return [in_rows[:, 0, 0], in_rows[:, 0, 1], down_rows[:, 0]]  11.7 us
  transfers between devices with their start and end apart: 6, of which 2 were waited for; matrix products, arithmetic and copies ran while one was open for 7% of the time, Pallas kernels for 22%

profile of v5, /device:TPU:0, one launch (start us, length us, event | category | flops | bytes accessed | tf_op | source)
XLA Modules:
  0.0 550.2 jit_solution(12782807187356483984)
XLA Ops:
  7.2 1.2 copy.92
  8.4 0.8 constant_dynamic-update-slice_fusion.1
  9.3 0.3 copy.93
  9.6 1.0 constant_dynamic-update-slice_fusion.refs_1_
  10.6 2.9 collective-permute-start.1
  13.5 1.5 collective-permute-start.3
  15.1 1.2 copy.91
  16.3 0.5 collective-permute-start
  16.9 0.6 fusion.7
  17.9 7.3 %constant_dynamic-slice_fusion.4 = (bf16[256,1,1408]{2,1,0:T(2,128)(2,1)}, bf16[256,1,1408]{2,1,0:T(2,128)(2,1)}, bf16[256,1,1408]{2,1,0:T(2,128)(2,1)}, bf16[256,1,1408]{2,1,0:T(2,128)(2,1)}) fusion(bf16[256,4,1408]{2,1,0:T(4,128)(2,1)S(1)} %copy-done, s32[]{:T(128)S(6)} %select_n.92, s32[]{:T(128)S(6)} %select_n.91, s32[]{:T(128)S(6)} %select_n.90, ...), kind=kLoop, calls=%fused_computation.41 | loop fusion | bytes 5767184 | tf_op jit(solution)/shard_map/dynamic_slice | solution.py:1327
  25.3 0.8 fusion.1
  26.2 0.5 copy-done.10
  26.7 1.2 convert_reduce_fusion
  28.0 3.0 fusion.4
  31.0 1.0 pad_maximum_fusion.cos_ref
  32.0 0.6 copy-done.8
  33.0 0.6 pad.13.about_ref
  33.7 0.6 pad.14.ride_ref
  34.3 0.6 pad.12.gain_ref
  34.9 11.7 %constant_dynamic-slice_fusion.5 = (bf16[256,1,1,1408]{3,2,1,0:T(2,128)(2,1)S(1)}, bf16[256,1,1,1408]{3,2,1,0:T(2,128)(2,1)S(1)}, bf16[256,1,1,1408]{3,2,1,0:T(2...) fusion(bf16[256,4,2,1408]{3,2,1,0:T(2,128)(2,1)} %param.20, ...), kind=kLoop, calls=%fused_computation.42 | loop fusion | bytes 11534356 | tf_op jit(solution)/shard_map/slice | solution.py:1382
  46.7 1.3 copy_bitcast_fusion.1
  48.0 1.3 copy_bitcast_fusion.4
  49.3 1.3 copy_bitcast_fusion.7
  50.6 1.0 pad_maximum_fusion.1.sin_ref
  51.6 6.2 %in_order.1 = (bf16[256,2048]{1,0:T(8,128)(2,1)}, bf16[256,2048]{1,0:T(8,128)(2,1)}) custom-call(s32[1]{0:T(128)} %bitcast.me_ref, bf16[256,2048]{1,0:T(8,128)(2,1)} %bitcast.61, bf16[256,2048]{1,0:T(8,128)(2,1)} %bitcast.62), custom_call_target="tpu_custom_call" | custom-call | tf_op jit(solution)/shard_map/in_order/pallas_call | solution.py:495
  57.9 0.6 add_convert_fusion.1
  58.6 0.9 fusion.3
  59.5 1.3 copy_bitcast_fusion.10
  60.8 0.6 copy-done.3
  61.4 0.4 copy-done.4
  61.8 1.3 copy_bitcast_fusion
  63.1 0.6 copy-done.1
  63.7 0.4 copy-done.2
  64.1 1.3 copy_bitcast_fusion.6
  65.4 5.3 collective-permute-done.refs_2_
  70.7 1.5 collective-permute-done.2.refs_4_
  72.2 80.2 %front.1 = (bf16[128,512]{1,0:T(8,128)(2,1)}, bf16[256,2048]{1,0:T(8,128)(2,1)}, bf16[256,3072]{1,0:T(8,128)(2,1)}, bf16[1024,1024]{1,0:T(8,128)(2,1)}, bf16[256...) custom-call(bf16[256,2048]{1,0:T(8,128)(2,1)} %get-tuple-element.85., ...), custom_call_target="tpu_custom_call" | custom-call | tf_op jit(solution)/shard_map/front/pallas_call | solution.py:995
  152.4 0.2 all-reduce.8.cloned.1.call-start
  152.7 52.7 %weights_two.1 = (bf16[2048,2816]{1,0:T(8,128)(2,1)}, bf16[2048,1408]{1,0:T(8,128)(2,1)}) custom-call(bf16[256,1408]{1,0:T(8,128)(2,1)} %get-tuple-element.108.refs_9_.refs_0_, bf16[256,1408]{1,0:T(8,128)(2,1)} %get-tuple-element.109.refs_10_.refs_1_, ...), custom_call_target="tpu_custom_call", output_to_operand_aliasing={{0}: (10, {}), {1}: (9, {})} | custom-call | tf_op jit(solution)/shard_map/weights_two/pallas_call | solution.py:200
  205.4 84.9 %experts.1 = (bf16[1024,2816]{1,0:T(8,128)(2,1)}, bf16[1024,1408]{1,0:T(8,128)(2,1)}, bf16[576,2048]{1,0:T(8,128)(2,1)}, bf16[256,2048]{1,0:T(8,128)(2,1)}) custom-call(bf16[256,2048]{1,0:T(8,128)(2,1)} %get-tuple-element.85.tokens_ref.refs_0_, bf16[256,2048]{1,0:T(8,128)(2,1)} %all-reduce.6.cloned.1.call-done.branch_ref.refs_1_, ...), custom_call_target="tpu_custom_call" | custom-call | tf_op jit(solution)/shard_map/experts/pallas_call | solution.py:778
  290.4 0.8 copy.74.gate_ref
  291.2 61.6 %grads_near.1 = (bf16[256,2816]{1,0:T(8,128)(2,1)}, bf16[256,2816]{1,0:T(8,128)(2,1)}, bf16[256,1408]{1,0:T(8,128)(2,1)}, bf16[256,1408]{1,0:T(8,128)(2,1)}, bf1...) custom-call(bf16[1024,2816]{1,0:T(8,128)(2,1)} %get-tuple-element.137.refs_0_.refs_1_, ...), custom_call_target="tpu_custom_call" | custom-call | tf_op jit(solution)/shard_map/grads_near/pallas_call | solution.py:200
  352.8 61.6 %attend_back.1 = (bf16[256,3072]{1,0:T(8,128)(2,1)}, f32[256,2048]{1,0:T(8,128)}, bf16[256,2048]{1,0:T(8,128)(2,1)}, f32[1,2048]{1,0:T(1,128)}, bf16[256,2048]{1...) custom-call(bf16[256,2048]{1,0:T(8,128)(2,1)} %get-tuple-element.85., ...), custom_call_target="tpu_custom_call", output_to_operand_aliasing={{6}: (17, {}), {7}: (18, {})} | custom-call | tf_op jit(solution)/shard_map/attend_back/pallas_call | solution.py:1203
  414.4 106.9 %attn_grads.1 = (f32[256,5120]{1,0:T(8,128)}, bf16[256,2048]{1,0:T(8,128)(2,1)}, f32[8,256]{1,0:T(8,128)}, bf16[256,2048]{1,0:T(8,128)(2,1)}) custom-call(bf16[256,2048]{1,0:T(8,128)(2,1)} %get-tuple-element.99.hidden_ref, bf16[256,2048]{1,0:T(8,128)(2,1)} %get-tuple-element.141.branch_ref, bf16[256,3072]{1,0:T(8,128)(2,1)} %get-tuple-element.142.qkv_ref, ...), custom_call_target="tpu_custom_call" | custom-call | tf_op jit(solution)/shard_map/attn_grads/pallas_call | solution.py:450
  521.3 5.4 lay_out.1
  526.7 1.3 fusion.9
  528.1 10.8 %spread_grads.1 = (f32[256,4,2,1408]{3,2,1,0:T(2,128)}, f32[256,4,1408]{2,1,0:T(4,128)}) custom-call(s32[1]{0:T(128)} %bitcast.35.me_ref, bf16[1024,2816]{1,0:T(8,128)(2,1)} %get-tuple-element.137.refs_0_.refs_1_, bf16[256,2816]{1,0:T(8,128)(2,1)} %get-tuple-element.129.refs_1_, bf16[256,2816]{1,0:T(8,128)(2,1)} %get-tuple-element.130.refs_2_, ...), custom_call_target="tpu_custom_call" | custom-call | tf_op jit(solution)/shard_map/spread_grads/pallas_call | solution.py:1255
  538.9 4.0 last.1
  (101 shorter events, 1.1 us)
Async XLA Ops:
  7.2 2.1 copy-start.6
  7.2 198.2 %all-reduce.6.cloned.1.call-start = ((), (), s32[]{:S(2)}) async-start(), calls=%async_computation | async-start | bytes 2097152 | tf_op jit(solution)/shard_map/psum | solution.py:1494
  9.5 5.5 %copy-start.7 = (bf16[256,4,512]{2,1,0:T(4,128)(2,1)S(1)}, bf16[256,4,512]{2,1,0:T(4,128)(2,1)}, u32[]{:S(2)}) copy-start(bf16[256,4,512]{2,1,0:T(4,128)(2,1)} %param.18) | copy-start | bytes 3145732
  9.5 8.3 %copy-start = (bf16[256,4,1408]{2,1,0:T(4,128)(2,1)S(1)}, bf16[256,4,1408]{2,1,0:T(4,128)(2,1)}, u32[]{:S(2)}) copy-start(bf16[256,4,1408]{2,1,0:T(4,128)(2,1)} %param.21) | copy-start | bytes 8650756
  10.6 6.9 %copy-start.20 = (s32[1,256,2]{1,2,0:T(2,128)S(1)}, s32[1,256,2]{1,2,0:T(2,128)}, u32[]{:S(2)}) copy-start(s32[1,256,2]{1,2,0:T(2,128)} %param.25) | copy-start | bytes 6148
  10.6 60.1 %collective-permute-start.1 = (bf16[256,3072]{1,0:T(8,128)(2,1)}, bf16[256,3072]{1,0:T(8,128)(2,1)}, u32[]{:S(2)}, u32[]{:S(2)}) collective-permute-start(bf16[256,3072]{1,0:T(8,128)(2,1)} %constant_dynamic-update-slice_fusion.refs_1_), channel_id=1, source_target_pairs={{0,16},{4,20},{8,24},{12,28},{16,0},{20,4},{24,8},{28,12},{1,17},{... | collective-permute-start | bytes 4718600 | tf_op jit(solution)/shard_map/ppermute | solution.py:42
  13.5 58.6 %collective-permute-start.3 = (bf16[256,3072]{1,0:T(8,128)(2,1)}, bf16[256,3072]{1,0:T(8,128)(2,1)}, u32[]{:S(2)}, u32[]{:S(2)}) collective-permute-start(bf16[256,3072]{1,0:T(8,128)(2,1)} %constant_dynamic-update-slice_fusion.refs_1_), channel_id=1, source_target_pairs={{0,8},{4,12},{8,0},{12,4},{16,24},{20,28},{24,16},{28,20},{1,9},{5... | collective-permute-start | bytes 4718600 | tf_op jit(solution)/shard_map/ppermute | solution.py:42
  16.3 54.4 %collective-permute-start = (bf16[256,2048]{1,0:T(8,128)(2,1)}, bf16[256,2048]{1,0:T(8,128)(2,1)}, u32[]{:S(2)}, u32[]{:S(2)}) collective-permute-start(bf16[256,2048]{1,0:T(8,128)(2,1)} %bitcast.37.refs_0_), channel_id=1, source_target_pairs={{0,16},{4,20},{8,24},{12,28},{16,0},{20,4},{24,8},{28,12},{1,17},{... | collective-permute-start | bytes 3145736 | tf_op jit(solution)/shard_map/ppermute | solution.py:42
  16.8 55.3 %collective-permute-start.2 = (bf16[256,2048]{1,0:T(8,128)(2,1)}, bf16[256,2048]{1,0:T(8,128)(2,1)}, u32[]{:S(2)}, u32[]{:S(2)}) collective-permute-start(bf16[256,2048]{1,0:T(8,128)(2,1)} %bitcast.37.refs_0_), channel_id=1, source_target_pairs={{0,8},{4,12},{8,0},{12,4},{16,24},{20,28},{24,16},{28,20},{1,9},{5... | collective-permute-start | bytes 3145736 | tf_op jit(solution)/shard_map/ppermute | solution.py:42
  16.9 9.3 %copy-start.23 = (s32[256]{0:T(256)}, s32[256]{0:T(256)S(1)}, u32[]{:S(2)}) copy-start(s32[256]{0:T(256)S(1)} %iota_add_fusion.4) | copy-start | bytes 3076
  16.9 9.3 %copy-start.25 = (s32[256]{0:T(256)}, s32[256]{0:T(256)S(1)}, u32[]{:S(2)}) copy-start(s32[256]{0:T(256)S(1)} %iota_add_fusion.1) | copy-start | bytes 3076
  16.9 9.3 %copy-start.27 = (s32[256]{0:T(256)}, s32[256]{0:T(256)S(1)}, u32[]{:S(2)}) copy-start(s32[256]{0:T(256)S(1)} %iota_add_fusion.2) | copy-start | bytes 3076
  16.9 9.3 %copy-start.29 = (s32[256]{0:T(256)}, s32[256]{0:T(256)S(1)}, u32[]{:S(2)}) copy-start(s32[256]{0:T(256)S(1)} %iota_add_fusion.3) | copy-start | bytes 3076
  17.8 7.4 %copy-start.18 = (s32[1,256,2]{1,2,0:T(2,128)S(1)}, s32[1,256,2]{1,2,0:T(2,128)}, u32[]{:S(2)}) copy-start(s32[1,256,2]{1,2,0:T(2,128)} %param.23) | copy-start | bytes 6148
  17.9 8.3 %copy-start.31 = (s32[1,1024]{1,0:T(1,128)S(1)}, s32[1,1024]{1,0:T(1,128)}, u32[]{:S(2)}) copy-start(s32[1,1024]{1,0:T(1,128)} %param.22) | copy-start | bytes 12292
  25.2 6.7 %copy-start.19 = (s32[1,256,2]{1,2,0:T(2,128)S(1)}, s32[1,256,2]{1,2,0:T(2,128)}, u32[]{:S(2)}) copy-start(s32[1,256,2]{1,2,0:T(2,128)} %param.23) | copy-start | bytes 6148
  25.2 6.7 %copy-start.34 = (f32[1,256,2]{1,2,0:T(2,128)S(1)}, f32[1,256,2]{1,2,0:T(2,128)}, u32[]{:S(2)}) copy-start(f32[1,256,2]{1,2,0:T(2,128)} %param.24) | copy-start | bytes 6148
  25.2 7.3 %copy-start.32 = (bf16[256,1]{0,1:T(2,128)(2,1)S(1)}, bf16[256,1]{0,1:T(2,128)(2,1)}, u32[]{:S(2)}) copy-start(bf16[256,1]{0,1:T(2,128)(2,1)} %get-tuple-element.195) | copy-start | bytes 1540
  25.3 7.3 %copy-start.33 = (bf16[256,1]{0,1:T(2,128)(2,1)S(1)}, bf16[256,1]{0,1:T(2,128)(2,1)}, u32[]{:S(2)}) copy-start(bf16[256,1]{0,1:T(2,128)(2,1)} %get-tuple-element.196) | copy-start | bytes 1540
  25.3 7.5 %copy-start.21 = (s32[1,256,2]{1,2,0:T(2,128)S(1)}, s32[1,256,2]{1,2,0:T(2,128)}, u32[]{:S(2)}) copy-start(s32[1,256,2]{1,2,0:T(2,128)} %param.25) | copy-start | bytes 6148
  25.3 7.5 %copy-start.35 = (f32[1,256,2]{1,2,0:T(2,128)S(1)}, f32[1,256,2]{1,2,0:T(2,128)}, u32[]{:S(2)}) copy-start(f32[1,256,2]{1,2,0:T(2,128)} %param.26) | copy-start | bytes 6148
  26.1 0.6 copy-start.10
  26.1 0.6 copy-start.12
  26.1 0.6 copy-start.14
  26.1 0.6 copy-start.16
  28.0 6.3 %copy-start.36 = (bf16[256]{0:T(256)(128)(2,1)S(1)}, bf16[256]{0:T(256)(128)(2,1)}, u32[]{:S(2)}) copy-start(bf16[256]{0:T(256)(128)(2,1)} %param.16) | copy-start | bytes 1540
  28.0 6.3 %copy-start.37 = (bf16[256]{0:T(256)(128)(2,1)S(1)}, bf16[256]{0:T(256)(128)(2,1)}, u32[]{:S(2)}) copy-start(bf16[256]{0:T(256)(128)(2,1)} %param.15) | copy-start | bytes 1540
  32.0 0.6 copy-start.8
  49.3 1.3 copy-start.5
  51.6 6.3 %copy-start.11 = (s32[1,256]{1,0:T(1,128)S(1)}, s32[1,256]{1,0:T(1,128)}, u32[]{:S(2)}) copy-start(s32[1,256]{1,0:T(1,128)} %copy-done.10) | copy-start | bytes 3076
  51.6 6.3 %copy-start.13 = (s32[1,256]{1,0:T(1,128)S(1)}, s32[1,256]{1,0:T(1,128)}, u32[]{:S(2)}) copy-start(s32[1,256]{1,0:T(1,128)} %copy-done.12) | copy-start | bytes 3076
  51.6 6.3 %copy-start.15 = (s32[1,256]{1,0:T(1,128)S(1)}, s32[1,256]{1,0:T(1,128)}, u32[]{:S(2)}) copy-start(s32[1,256]{1,0:T(1,128)} %copy-done.14) | copy-start | bytes 3076
  51.6 6.3 %copy-start.17 = (s32[1,256]{1,0:T(1,128)S(1)}, s32[1,256]{1,0:T(1,128)}, u32[]{:S(2)}) copy-start(s32[1,256]{1,0:T(1,128)} %copy-done.16) | copy-start | bytes 3076
  51.6 6.3 %copy-start.24 = (s32[256]{0:T(256)S(1)}, s32[256]{0:T(256)}, u32[]{:S(2)}) copy-start(s32[256]{0:T(256)} %copy-done.23) | copy-start | bytes 3076
  51.6 6.3 %copy-start.26 = (s32[256]{0:T(256)S(1)}, s32[256]{0:T(256)}, u32[]{:S(2)}) copy-start(s32[256]{0:T(256)} %copy-done.25) | copy-start | bytes 3076
  51.6 6.3 %copy-start.28 = (s32[256]{0:T(256)S(1)}, s32[256]{0:T(256)}, u32[]{:S(2)}) copy-start(s32[256]{0:T(256)} %copy-done.27) | copy-start | bytes 3076
  51.6 6.3 %copy-start.30 = (s32[256]{0:T(256)S(1)}, s32[256]{0:T(256)}, u32[]{:S(2)}) copy-start(s32[256]{0:T(256)} %copy-done.29) | copy-start | bytes 3076
  51.6 6.9 %copy-start.22 = (s32[4,256]{1,0:T(4,128)S(1)}, s32[4,256]{1,0:T(4,128)}, u32[]{:S(2)}) copy-start(s32[4,256]{1,0:T(4,128)} %fusion.1) | copy-start | bytes 12292
  59.5 1.9 copy-start.3
  59.5 2.3 copy-start.4
  61.8 1.9 copy-start.1
  61.8 2.3 copy-start.2
  152.4 200.4 %all-reduce.8.cloned.1.call-start = ((), (), s32[]{:S(2)}) async-start(), calls=%async_computation.1 | async-start | bytes 2097152 | tf_op jit(solution)/shard_map/psum | solution.py:1526
  205.4 85.0 %copy-start.9 = (f32[256,4]{0,1:T(4,128)S(1)}, f32[256,4]{0,1:T(4,128)}, u32[]{:S(2)}) copy-start(f32[256,4]{0,1:T(4,128)} %copy-done.8) | copy-start | bytes 12292
Sparse Core Ops, SparseCore 0:
  152.6 51.2 all-reduce.5
  290.5 57.0 all-reduce.7

commit v6 on v5

--- a/solution.py
+++ b/solution.py
@@ -147,6 +147,12 @@
         if i not in self.sent:
             self.sent.add(i)
             self.copies[i].wait_send()
+
+    def kick(self, first, count):
+        for i in range(first, count):
+            for target in self.moves[i][3]:
+                self.await_one(self.place[target])
+            self.start(i)
 
     def settle(self, count=None, first=0):
         count = len(self.moves) if count is None else count
@@ -221,6 +227,14 @@
     )
 
 
+def lanes_of(planes, late, bits):
+    lanes = []
+    for n, plane in enumerate([*range(late, planes), *range(late)]):
+        lanes.append((plane, bits if n % 2 else bits[::-1]))
+    last = lanes[-6:]
+    return lanes, [p for p, _ in last[::2]] + [p for p, _ in last[1::2]]
+
+
 def attn_grads_kernel(
     ctx_count,
     groups,
@@ -239,6 +253,8 @@
     mlp_ref,
     place_ref,
     out_ref,
+    keep_ref,
+    give_ref,
     grad_tokens_ref,
     gain_out_ref,
     mlp_sum_ref,
@@ -328,10 +344,8 @@
             c.start()
         sent.extend(flying[plane].values())
 
-    lanes = []
     late = first // cols
-    for n, plane in enumerate([*range(late, planes), *range(late)]):
-        lanes.append((plane, bits if n % 2 else bits[::-1]))
+    lanes, last_lanes = lanes_of(planes, late, bits)
     for plane, order in lanes:
         run.settle(2 if plane >= late else 4)
         at = pl.ds(plane * cols, cols)
@@ -376,10 +390,12 @@
 
     for step in range(len(bits)):
         for n, (plane, order) in enumerate(lanes):
-            if step == 0 and n == len(lanes) // 2:
+            if step == len(bits) - 1 and plane in last_lanes:
+                continue
+            if step == 0 and n == len(lanes) * 2 // 5:
+                sum_back()
                 sum_mlp()
-                sum_back()
-            if step == 0 and n == len(lanes) - 1:
+            if step == 1 and n == min(2, len(lanes) - 1):
                 norm_back()
             at = bits.index(order[step])
             left[plane] = [j for j in left[plane] if not j >> at & 1]
@@ -389,10 +405,18 @@
                 down, other = pl.ds(j * part, part), pl.ds((j | 1 << at) * part, part)
                 total = grads[down, across].astype(F32) + got[other, across].astype(F32)
                 if step == len(bits) - 1:
-                    out_ref[:, across] = total
+                    at_out = sum(p not in last_lanes for p in range(plane))
+                    out_ref[:, at_out * cols : (at_out + 1) * cols] = total
+                elif step == len(bits) - 2 and plane in last_lanes:
+                    at_last = last_lanes.index(plane)
+                    there = slice(at_last * cols, (at_last + 1) * cols)
+                    if j:
+                        give_ref[:, there] = total.astype(BF)
+                    else:
+                        keep_ref[:, there] = total
                 else:
                     grads[down, across] = total.astype(BF)
-            if step < len(bits) - 1:
+            if step < len(bits) - 1 and not (step == len(bits) - 2 and plane in last_lanes):
                 send_half(plane, order, step + 1)
     runs["gains"].settle()
     gains = gain_send[:8]
@@ -450,13 +474,15 @@
     return pl.pallas_call(
         functools.partial(attn_grads_kernel, ctx_count, groups, bits, part, cols),
         out_shape=[
-            jax.ShapeDtypeStruct((part, wide), F32),
+            jax.ShapeDtypeStruct((part, wide - 6 * cols), F32),
+            jax.ShapeDtypeStruct((part, 6 * cols), F32),
+            jax.ShapeDtypeStruct((part, 6 * cols), BF),
             jax.ShapeDtypeStruct((rows, width), BF),
             jax.ShapeDtypeStruct((8, part), F32),
             jax.ShapeDtypeStruct((rows, width), BF),
         ],
         in_specs=[full] * (4 + len(others)),
-        out_specs=[full] * 4,
+        out_specs=[full] * 6,
         scratch_shapes=[
             pltpu.VMEM(mlp.shape, BF),
             pltpu.VMEM(((tp_count - 1) * run_rows, width), BF),
@@ -534,25 +560,35 @@
     )(me.astype(jnp.int32).reshape(1), tokens, branch, mlp, grad)
 
 
-def lay_kernel(grad_ref, *out_refs):
-    at = 0
+def lay_kernel(last, grad_ref, keep_ref, one_ref, two_ref, *out_refs):
+    plane = early = 0
+    half = len(last) // 2
     for ref in out_refs:
+        cols = ref.shape[2]
         for p in range(ref.shape[1]):
-            ref[:, p, :] = grad_ref[:, at : at + ref.shape[2]]
-            at += ref.shape[2]
-
-
-def lay_out(grad, shapes):
-    step = min(64, grad.shape[0])
+            if plane in last:
+                at = last.index(plane)
+                got_ref = (one_ref, two_ref)[at // half]
+                got = got_ref[:, at % half * cols : (at % half + 1) * cols].astype(F32)
+                ref[:, p, :] = keep_ref[:, at * cols : (at + 1) * cols] + got
+            else:
+                ref[:, p, :] = grad_ref[:, early * cols : (early + 1) * cols]
+                early += 1
+            plane += 1
+
+
+def lay_out(last, arrays, shapes):
+    rows = arrays[0].shape[0]
+    step = min(64, rows)
     return pl.pallas_call(
-        lay_kernel,
-        grid=(grad.shape[0] // step,),
-        in_specs=[pl.BlockSpec((step, grad.shape[1]), lambda i: (i, 0))],
+        functools.partial(lay_kernel, last),
+        grid=(rows // step,),
+        in_specs=[pl.BlockSpec((step, x.shape[1]), lambda i: (i, 0)) for x in arrays],
         out_specs=[pl.BlockSpec((step, *shape[1:]), lambda i: (i, 0, 0)) for shape in shapes],
         out_shape=[jax.ShapeDtypeStruct(shape, F32) for shape in shapes],
         compiler_params=pltpu.CompilerParams(vmem_limit_bytes=VMEM_LIMIT),
         name="lay_out",
-    )(grad)
+    )(*arrays)
 
 
 def chunks(total, size):
@@ -570,14 +606,14 @@
     branch_ref,
     gain_ref,
     place_ref,
-    dy_run_ref,
+    dy_ref,
     rides_ref,
     in_ref,
     down_ref,
     *refs,
 ):
     far_refs, refs = refs[: len(far_names)], refs[len(far_names) :]
-    grads_in, grads_down, mlp_ref, two_part = refs[:4]
+    grads_in, grads_down, mlp_ref, two_part, mlp_first = refs[:5]
     (
         win,
         wdown,
@@ -593,21 +629,20 @@
         dy_got,
         gu_got,
         active_got,
-        dy_ref,
         send,
         recv,
-    ) = refs[4:]
+    ) = refs[5:]
     slots, width = two.shape
     units = active.shape[1]
     room, run = slots // experts, width // experts
     arrays = dict(
         zip(far_names, far_refs),
+        mlp=mlp_ref,
+        mlp_first=mlp_first,
         gin=grads_in,
         gdown=grads_down,
         win=win,
         wdown=wdown,
-        dy_run=dy_run_ref,
-        dy=dy_ref,
         two=two,
         slots_out=slots_out,
         back_out=back_out,
@@ -633,9 +668,6 @@
     runs["load", "down"].begin()
     runs["far", "in"].begin()
     runs["far", "down"].begin()
-    for stage in range(len(stages)):
-        runs["dy", stage].begin()
-    dy_ref[:, run_cols(run)] = dy_run_ref[...]
     x = tokens_ref[...].astype(F32) + branch_ref[...].astype(F32)
     inverse = lax.rsqrt(jnp.mean(x * x, axis=-1, keepdims=True) + EPSILON)
     hidden = (x * inverse * gain_of(gain_ref, 1, part)).astype(BF)
@@ -660,7 +692,6 @@
         for k in ks:
             if k:
                 runs["slots"].await_one(k - 1)
-        runs["dy", stage].settle()
         for t in range(1, share):
             out_rows = slice((t - 1) * slots + rows.start, (t - 1) * slots + rows.stop)
             for k in range(experts):
@@ -697,6 +728,9 @@
                 at = slice(k * room - rows.start, (k + 1) * room - rows.start)
                 turned = slice((i ^ k) * run, ((i ^ k) + 1) * run)
                 mlp_ref[k * room : (k + 1) * room, turned] = out[at]
+        if stage < 2:
+            for r in range(len(groups["mlp"]) // 2):
+                runs["mlp"].start(2 * r + stage)
     for name in groups:
         if isinstance(name, tuple) and name[0] != "load":
             runs[name].finish()
@@ -725,6 +759,7 @@
         two_part[:, cols] = total.astype(BF)
     runs["back"].finish()
     runs["out"].finish()
+    runs["mlp"].finish()
     runs["slots"].finish()
 
 
@@ -753,9 +788,6 @@
     }
     for stage, ks in enumerate(list_stages(experts)):
         mine = (ks[0] * room, len(ks) * room)
-        groups["dy", stage] = [
-            (("dy_run", mine, None), ("dy", mine, (TP, run)), -r, ()) for r in range(1, tp_count)
-        ]
         for name in ("two", "dy", "active", "gu"):
             groups[name, stage, 0] = []
             for t in range(1, share):
@@ -766,6 +798,11 @@
     groups["back"] = [
         (("back_out", (k * room, room), None), ("back_got", (k * room, room), None), k * share, ())
         for k in range(1, experts)
+    ]
+    groups["mlp"] = [
+        (("mlp", (k * room, room), (TP, run, r)), ("mlp_first", ((2 * r - 2 + k) * room, room), None), -r, ())
+        for r in range(1, tp_count)
+        for k in range(2)
     ]
     groups["out"] = []
     for k in range(experts):
@@ -782,9 +819,10 @@
             jax.ShapeDtypeStruct((experts * part, units), BF),
             jax.ShapeDtypeStruct((slots, width), BF),
             jax.ShapeDtypeStruct((rows, width), BF),
+            jax.ShapeDtypeStruct(((tp_count - 1) * 2 * room, run), BF),
         ],
         in_specs=[full] * 6 + [any_spec] * (2 + len(far)),
-        out_specs=[any_spec] * 2 + [full] * 2,
+        out_specs=[any_spec] * 2 + [full] * 3,
         scratch_shapes=[
             pltpu.VMEM((width, 2 * units), BF),
             pltpu.VMEM((width, units), BF),
@@ -794,7 +832,6 @@
             *[pltpu.VMEM((others, experts * part), BF)] * 4,
             pltpu.VMEM((others, 2 * units), BF),
             pltpu.VMEM((others, units), BF),
-            pltpu.VMEM((slots, width), BF),
         ]
         + [pltpu.SemaphoreType.DMA((total,))] * 2,
         compiler_params=pltpu.CompilerParams(
@@ -858,9 +895,9 @@
     wide = heads * HD
     group = width // part
     given, refs = refs[: len(names_in)], refs[len(names_in) :]
-    gains_ref, hidden_ref, qkv_ref, kv_ref, mixed_ref, branch_ref, slots_ref, rides_ref = refs[:8]
+    gains_ref, hidden_ref, qkv_ref, kv_ref, mixed_ref, branch_ref, dy_out, rides_ref = refs[:8]
     refs = refs[8:]
-    made, (full, picked, picked_ride, slot_info, send, recv, *bounces) = refs[: len(names_out)], refs[len(names_out) :]
+    made, (full, slots_ref, picked, picked_ride, slot_info, send, recv, *bounces) = refs[: len(names_out)], refs[len(names_out) :]
     arrays = dict(
         gain_own=gain_ref,
         gains=gains_ref,
@@ -868,6 +905,7 @@
         slots=slots_ref,
         picked_ride=picked_ride,
         rides=rides_ref,
+        dy=dy_out,
         qkv=qkv_ref,
         kv=kv_ref,
         full=full,
@@ -876,7 +914,7 @@
     arrays.update(zip(names_out, made))
     greet(ctx_count, masks_of(moves))
     run = Moves(ctx_count, moves, arrays, send, recv, bounces)
-    gains_done, first_done, second_done, rest_done, keys_done, dy_done = marks
+    gains_done, first_done, second_done, rest_done, keys_done, dy_done, spread_done = marks
     run_of = dy_ref.shape[1] // experts
     for k in range(experts):
         rows_at = slice(k * room, (k + 1) * room)
@@ -887,6 +925,8 @@
             picked[rows_at], picked_ride[rows_at] = slots, rides
         else:
             slots_ref[rows_at], rides_ref[rows_at] = slots, rides
+    for i in range(keys_done, dy_done):
+        run.start(i)
     run.begin(second_done)
     gains_ref[:16] = gain_ref[...]
     slot_table(place_ref, about_ref, slot_info)
@@ -895,6 +935,8 @@
     run.settle(gains_done)
     hidden_ref[...] = (normed * gain_of(gains_ref, 0, part)).astype(BF)
     run.settle(first_done, gains_done)
+    run.kick(dy_done, spread_done)
+    dy_out[:, run_cols(run_of)] = slots_ref[...]
     cos, sin = cos_ref[:rows], sin_ref[:rows]
 
     def project(plane):
@@ -962,15 +1004,15 @@
                 source = ("qkv", (0, rows), (experts * wide, 2 * wide))
                 kv_moves.append((source, target, 1 << bit, ()))
         order = order + order
-    gains_moves, first_moves, second_moves, rest_moves, dy_moves = moves
+    gains_moves, first_moves, second_moves, rest_moves, dy_moves, dy_spread = moves
     marks = [len(gains_moves)]
-    for more in (first_moves, second_moves, rest_moves, kv_moves, dy_moves):
+    for more in (first_moves, second_moves, rest_moves, kv_moves, dy_moves, dy_spread):
         marks.append(marks[-1] + len(more))
     whole = (FULL, (0, width), None)
     gathered = first_moves + second_moves + rest_moves
     landed = tuple(m[1] for m in gathered)
     keep = [(whole, ("kept", (0, width), None), None, landed)]
-    moves = gains_moves + gathered + kv_moves + dy_moves + later + keep
+    moves = gains_moves + gathered + kv_moves + dy_moves + dy_spread + later + keep
     slots_shape = (experts * place.shape[1], width // experts)
     rides_shape = (experts * place.shape[1], HD)
     names_in, names_out = list(given), [*made, "kept"]
@@ -984,7 +1026,7 @@
         ((ctx_count * rows, 2 * wide), BF),
         ((rows, experts * wide), BF),
         ((rows, width), BF),
-        (slots_shape, BF),
+        ((slots_shape[0], width), BF),
         (rides_shape, BF),
     ]
     bounces = [
@@ -1002,7 +1044,7 @@
         out_specs=[full] * len(small_out) + [any_spec] * len(names_out),
         scratch_shapes=[
             pltpu.VMEM((width, full_wide), BF),
-            pltpu.VMEM(slots_shape, BF),
+            *[pltpu.VMEM(slots_shape, BF)] * 2,
             pltpu.VMEM(rides_shape, BF),
             pltpu.VMEM((experts, room, HD), F32),
         ]
@@ -1037,6 +1079,7 @@
     idxk_ref,
     cos_ref,
     sin_ref,
+    mlp_first_ref,
     weight_ref,
     *refs,
 ):
@@ -1168,10 +1211,13 @@
     runs_mlp = [i for i, m in enumerate(moves) if m[0][0] == "mlp"]
     for i in runs_mlp:
         run.await_one(i)
-    mlp_total = mlp_mine[...].astype(F32)
-    for r in range(len(runs_mlp) - 1):
-        mlp_total = mlp_total + mlp_got[r * mlp_mine.shape[0] : (r + 1) * mlp_mine.shape[0]].astype(F32)
-    mlp_out_ref[...] = mlp_total.astype(BF)
+    slots, others = mlp_mine.shape[0], len(runs_mlp) - 1
+    first = mlp_first_ref.shape[0] // others
+    for low, top, came, size in ((0, first, mlp_first_ref, first), (first, slots, mlp_got, slots)):
+        mlp_total = mlp_mine[low:top].astype(F32)
+        for r in range(others):
+            mlp_total = mlp_total + came[r * size + low : r * size + top].astype(F32)
+        mlp_out_ref[low:top] = mlp_total.astype(BF)
     for h in range(heads):
         for bit in bits:
             head_copy(h, bit).wait_send()
@@ -1186,11 +1232,12 @@
     full = pl.BlockSpec(memory_space=pltpu.VMEM)
     passes = heads * bits_of(ctx_count)
     slots, run = given["mlp"].shape[0], width // tp_count
-    every = (0, slots)
-    mlp_moves = [(("mlp", every, (TP, run)), ("mlp_mine", every, None), None, ())]
+    first = small[-1].shape[0] // (tp_count - 1)
+    mlp_moves = [(("mlp", (0, slots), (TP, run)), ("mlp_mine", (0, slots), None), None, ())]
     for r in range(1, tp_count):
-        target = ("mlp_got", ((r - 1) * slots, slots), None)
-        mlp_moves.append((("mlp", every, (TP, run, r)), target, -r, ()))
+        source = ("mlp", (first, slots - first), (TP, run, r))
+        target = ("mlp_got", ((r - 1) * slots + first, slots - first), None)
+        mlp_moves.append((source, target, -r, ()))
     moves = mlp_moves + moves
     small_out = [
         (qkv.shape, BF),
@@ -1463,12 +1510,19 @@
         for k in range(1, experts)
         for name, target in (("picked", "slots"), ("picked_ride", "rides"))
     ]
-    (gains, hidden_one, qkv, kv, mixed, branch, dy_run, dy_rides), made = front(
+    dy_spread, run = [], width // tp_count
+    for k in range(experts):
+        mine = (k * room, room)
+        needs = ((("slots", mine, None)),) if k else ()
+        for r in range(1, tp_count):
+            source, target = ("slots", mine, None), ("dy", mine, (TP, run, 0, r))
+            dy_spread.append((source, target, -r, needs))
+    (gains, hidden_one, qkv, kv, mixed, branch, dy_slots, dy_rides), made = front(
         1,
         ctx_count,
         heads,
         part,
-        (gain_moves, *gather_moves, dy_moves),
+        (gain_moves, *gather_moves, dy_moves, dy_spread),
         later,
         {
             **{("own", n): x for n, x in enumerate(attn_own)},
@@ -1505,7 +1559,7 @@
             fetched.append((j * part, size))
     for k in far:
         far_moves += weight_moves(k, half_part, part - half_part, "w")
-    grads_in, grads_down, mlp_slots, back_two_part = run_experts(
+    grads_in, grads_down, mlp_slots, back_two_part, mlp_first = run_experts(
         4,
         ctx_count,
         tp_count,
@@ -1520,7 +1574,7 @@
         branch_sum,
         gains,
         place_mlp,
-        dy_run,
+        dy_slots,
         dy_rides,
     )
     back_two = lax.psum(back_two_part, TP)
@@ -1577,10 +1631,11 @@
         *key_row,
         cos,
         sin,
+        mlp_first,
     )
     keep_grads(made, far)
     upper = list(range(1, bits_of(group)))
-    grad_attnw, grad_tokens, gain_grads, mlp_sum = attn_grads(
+    grad_attnw, kept, given, grad_tokens, gain_grads, mlp_sum = attn_grads(
         7,
         ctx_count,
         tp_count,
@@ -1599,11 +1654,25 @@
         mlp_run,
         place_mlp,
     )
+    planes = attn_experts * 2 + 2
+    lanes, last_lanes = lanes_of(planes, attn_experts + 2, upper)
+    half = given.shape[1] // 2
+    came = []
+    for i in range(2):
+        bit = dict(lanes)[last_lanes[3 * i]][-1]
+        came.append(exchange(given[:, i * half : (i + 1) * half], 1 << bit))
     output, grad_tokens = last(me, group, tokens_rel, branch_sum, mlp_sum, grad_tokens)
+    grad_in_out, grad_down_out = spread_grads(
+        [got_in[k] for k in range(experts)],
+        [got_down[k] for k in range(experts)],
+        expert_me,
+        w_in.shape,
+        w_down.shape,
+    )
+    came, _ = lax.optimization_barrier((came, (output, grad_in_out)))
     grad_query_w, grad_kv_w, grad_out_w = lay_out(
-        grad_attnw, (w_query.shape, w_kv.shape, w_out_attn.shape)
+        last_lanes, [grad_attnw, kept, *came], (w_query.shape, w_kv.shape, w_out_attn.shape)
     )
-
     return (
         output[None],
         grad_tokens[None],
@@ -1612,13 +1681,8 @@
         grad_kv_w,
         grad_query_w,
         grad_out_w,
-        *spread_grads(
-            [got_in[k] for k in range(experts)],
-            [got_down[k] for k in range(experts)],
-            expert_me,
-            w_in.shape,
-            w_down.shape,
-        ),
+        grad_in_out,
+        grad_down_out,
     )
 
 

time: 561 us -> 542 us (0.966)
  Pallas kernels: 474 us -> 453 us
    pallas_call x1, Pallas kernels: 107 us -> 86.7 us  [attn_grads(): pl.pallas_call(functools.partial(attn_grads_kernel, ctx_count, groups, bi...]
  transfers between devices with their start and end apart: 6 -> 8, of which waited for: 2 -> 4; matrix products, arithmetic and copies ran while one was open for 7% -> 8% of each run, Pallas kernels for 22% -> 25%
where the time goes in v6:
time: 542 us; the launch traced here: 535 us
  Pallas kernels  453 us (84%)
  local copies, waits for them, and re-layouts  41.5 us (8%)
  between operations  15.1 us (3%)
  waiting for transfers between devices  8.76 us (2%)
  other arithmetic  8.58 us (2%)
  starting transfers between devices  7.22 us (1%)
    pallas_call x2, Pallas kernels, move(): pl.pallas_call(functools.partial(move_kernel, ctx_count, moves, plain + [...  114 us
    pallas_call x1, Pallas kernels, attn_grads(): pl.pallas_call(functools.partial(attn_grads_kernel, ctx_count, groups, bi...  86.7 us
    pallas_call x1, Pallas kernels, run_experts(): pl.pallas_call(functools.partial(experts_kernel, ctx_count, experts, shar...  86.5 us
    pallas_call x1, Pallas kernels, front(): pl.pallas_call(functools.partial(front_kernel, ctx_count, moves, marks, n...  80.9 us
    pallas_call x1, Pallas kernels, attend_back(): pl.pallas_call(functools.partial(attend_back_kernel, ctx_count, moves, li...  57.9 us
    slice x1, local copies, waits for them, and re-layouts, expert_rows(): return [in_rows[:, 0, 0], in_rows[:, 0, 1], down_rows[:, 0]]  11.7 us
  transfers between devices with their start and end apart: 8, of which 4 were waited for; matrix products, arithmetic and copies ran while one was open for 8% of the time, Pallas kernels for 25%

profile of v6, /device:TPU:0, one launch (start us, length us, event | category | flops | bytes accessed | tf_op | source)
XLA Modules:
  0.0 535.0 jit_solution(2840162583162229050)
XLA Ops:
  7.2 1.2 copy.92
  8.4 0.8 constant_dynamic-update-slice_fusion.1
  9.6 1.0 constant_dynamic-update-slice_fusion.refs_1_
  10.6 2.9 collective-permute-start.1
  13.5 1.5 collective-permute-start.3
  15.1 1.2 copy.91
  16.3 0.5 collective-permute-start
  16.9 0.6 fusion.7
  17.9 7.3 %constant_dynamic-slice_fusion.4 = (bf16[256,1,1408]{2,1,0:T(2,128)(2,1)}, bf16[256,1,1408]{2,1,0:T(2,128)(2,1)}, bf16[256,1,1408]{2,1,0:T(2,128)(2,1)}, bf16[256,1,1408]{2,1,0:T(2,128)(2,1)}) fusion(bf16[256,4,1408]{2,1,0:T(4,128)(2,1)S(1)} %copy-done, s32[]{:T(128)S(6)} %select_n.92, s32[]{:T(128)S(6)} %select_n.91, s32[]{:T(128)S(6)} %select_n.90, ...), kind=kLoop, calls=%fused_computation.41 | loop fusion | bytes 5767184 | tf_op jit(solution)/shard_map/dynamic_slice | solution.py:1374
  25.3 0.8 fusion.1
  26.2 0.5 copy-done.12
  26.7 1.2 convert_reduce_fusion
  28.0 3.0 fusion.4
  31.0 1.0 pad_maximum_fusion.cos_ref
  32.0 0.6 copy-done.10
  33.0 0.6 pad.13.about_ref
  33.7 0.7 pad.14.ride_ref
  34.3 0.6 pad.12.gain_ref
  34.9 11.7 %constant_dynamic-slice_fusion.5 = (bf16[256,1,1,1408]{3,2,1,0:T(2,128)(2,1)S(1)}, bf16[256,1,1,1408]{3,2,1,0:T(2,128)(2,1)S(1)}, bf16[256,1,1,1408]{3,2,1,0:T(2...) fusion(bf16[256,4,2,1408]{3,2,1,0:T(2,128)(2,1)} %param.20, ...), kind=kLoop, calls=%fused_computation.42 | loop fusion | bytes 11534356 | tf_op jit(solution)/shard_map/slice | solution.py:1429
  46.7 1.3 copy_bitcast_fusion.1
  47.9 1.3 copy_bitcast_fusion.4
  49.3 1.3 copy_bitcast_fusion.7
  50.6 1.0 pad_maximum_fusion.1.sin_ref
  51.7 6.2 %in_order.1 = (bf16[256,2048]{1,0:T(8,128)(2,1)}, bf16[256,2048]{1,0:T(8,128)(2,1)}) custom-call(s32[1]{0:T(128)} %bitcast.me_ref, bf16[256,2048]{1,0:T(8,128)(2,1)} %bitcast.61, bf16[256,2048]{1,0:T(8,128)(2,1)} %bitcast.62), custom_call_target="tpu_custom_call" | custom-call | tf_op jit(solution)/shard_map/in_order/pallas_call | solution.py:521
  58.0 0.6 add_convert_fusion.1
  58.6 0.9 fusion.3
  59.5 1.3 copy_bitcast_fusion.10
  60.8 0.6 copy-done.3
  61.8 1.3 copy_bitcast_fusion
  63.2 0.6 copy-done.1
  64.2 1.3 copy_bitcast_fusion.6
  65.4 5.3 collective-permute-done.refs_2_
  70.7 1.5 collective-permute-done.2.refs_4_
  72.2 80.9 %front.1 = (bf16[128,512]{1,0:T(8,128)(2,1)}, bf16[256,2048]{1,0:T(8,128)(2,1)}, bf16[256,3072]{1,0:T(8,128)(2,1)}, bf16[1024,1024]{1,0:T(8,128)(2,1)}, bf16[256...) custom-call(bf16[256,2048]{1,0:T(8,128)(2,1)} %get-tuple-element.90., ...), custom_call_target="tpu_custom_call" | custom-call | tf_op jit(solution)/shard_map/front/pallas_call | solution.py:1037
  153.4 52.7 %weights_two.1 = (bf16[2048,2816]{1,0:T(8,128)(2,1)}, bf16[2048,1408]{1,0:T(8,128)(2,1)}) custom-call(bf16[256,1408]{1,0:T(8,128)(2,1)} %get-tuple-element.113.refs_9_.refs_0_, bf16[256,1408]{1,0:T(8,128)(2,1)} %get-tuple-element.114.refs_10_.refs_1_, ...), custom_call_target="tpu_custom_call", output_to_operand_aliasing={{0}: (10, {}), {1}: (9, {})} | custom-call | tf_op jit(solution)/shard_map/weights_two/pallas_call | solution.py:206
  206.1 86.5 %experts.1 = (bf16[1024,2816]{1,0:T(8,128)(2,1)}, bf16[1024,1408]{1,0:T(8,128)(2,1)}, bf16[576,2048]{1,0:T(8,128)(2,1)}, bf16[256,2048]{1,0:T(8,128)(2,1)}, bf16[864,512]{1,0:T(8,128)(2,1)}) custom-call(bf16[256,2048]{1,0:T(8,128)(2,1)} %get-tuple-element.90.tokens_ref.refs_0_, bf16[256,2048]{1,0:T(8,128)(2,1)} %all-reduce.6.cloned.1.call-done.branch_ref.refs_1_, ...), custom_call_target="tpu_custom_call" | custom-call | tf_op jit(solution)/shard_map/experts/pallas_call | solution.py:815
  292.6 0.8 copy.74.gate_ref
  293.4 61.5 %grads_near.1 = (bf16[256,2816]{1,0:T(8,128)(2,1)}, bf16[256,2816]{1,0:T(8,128)(2,1)}, bf16[256,1408]{1,0:T(8,128)(2,1)}, bf16[256,1408]{1,0:T(8,128)(2,1)}, bf1...) custom-call(bf16[1024,2816]{1,0:T(8,128)(2,1)} %get-tuple-element.143.refs_0_.refs_1_, ...), custom_call_target="tpu_custom_call" | custom-call | tf_op jit(solution)/shard_map/grads_near/pallas_call | solution.py:206
  355.0 57.9 %attend_back.1 = (bf16[256,3072]{1,0:T(8,128)(2,1)}, f32[256,2048]{1,0:T(8,128)}, bf16[256,2048]{1,0:T(8,128)(2,1)}, f32[1,2048]{1,0:T(1,128)}, bf16[256,2048]{1...) custom-call(bf16[256,2048]{1,0:T(8,128)(2,1)} %get-tuple-element.90., ...), custom_call_target="tpu_custom_call", output_to_operand_aliasing={{6}: (18, {}), {7}: (19, {})} | custom-call | tf_op jit(solution)/shard_map/attend_back/pallas_call | solution.py:1250
  412.9 86.7 %attn_grads.1 = (f32[256,2048]{1,0:T(8,128)}, f32[256,3072]{1,0:T(8,128)}, bf16[256,3072]{1,0:T(8,128)(2,1)}, bf16[256,2048]{1,0:T(8,128)(2,1)}, f32[8,256]{1,0:T(8,128)}, /*index=5*/bf16[256,2048]{1,0:T(8,128)(2,1)}) custom-call(bf16[256,2048]{1,0:T(8,128)(2,1)} %get-tuple-element.104.hidden_ref, bf16[256,2048]{1,0:T(8,128)(2,1)} %get-tuple-element.147.branch_ref, ...), custom_call_target="tpu_custom_call" | custom-call | tf_op jit(solution)/shard_map/attn_grads/pallas_call | solution.py:474
  499.6 1.5 fusion.9
  501.1 0.8 collective-permute-start.4
  501.9 1.2 collective-permute-start.5
  503.1 10.8 %spread_grads.1 = (f32[256,4,2,1408]{3,2,1,0:T(2,128)}, f32[256,4,1408]{2,1,0:T(4,128)}) custom-call(s32[1]{0:T(128)} %bitcast.35.me_ref, bf16[1024,2816]{1,0:T(8,128)(2,1)} %get-tuple-element.143.refs_0_.refs_1_, bf16[256,2816]{1,0:T(8,128)(2,1)} %get-tuple-element.134.refs_1_, bf16[256,2816]{1,0:T(8,128)(2,1)} %get-tuple-element.135.refs_2_, ...), custom_call_target="tpu_custom_call" | custom-call | tf_op jit(solution)/shard_map/spread_grads/pallas_call | solution.py:1302
  513.9 4.0 last.1
  517.9 1.3 fusion.10
  519.2 1.5 collective-permute-done.4.one_ref
  522.1 5.6 %lay_out.1 = (f32[256,4,512]{2,1,0:T(4,128)}, f32[256,2,512]{2,1,0:T(2,128)}, f32[256,4,512]{2,1,0:T(4,128)}) custom-call(f32[256,2048]{1,0:T(8,128)} %get-tuple-element.159.grad_ref, f32[256,3072]{1,0:T(8,128)} %get-tuple-element.160.keep_ref, bf16[256,1536]{1,0:T(8,128)(2,1)} %copy-done.8, bf16[256,1536]{1,0:T(8,128)(2,1)} %copy-done.9), custom_call_target="tpu_custom_call" | custom-call | tf_op jit(solution)/shard_map/lay_out/pallas_call | solution.py:583
  (110 shorter events, 3.8 us)
Async XLA Ops:
  7.2 2.1 copy-start.6
  7.2 198.9 %all-reduce.6.cloned.1.call-start = ((), (), s32[]{:S(2)}) async-start(), calls=%async_computation | async-start | bytes 2097152 | tf_op jit(solution)/shard_map/psum | solution.py:1548
  9.5 5.5 %copy-start.7 = (bf16[256,4,512]{2,1,0:T(4,128)(2,1)S(1)}, bf16[256,4,512]{2,1,0:T(4,128)(2,1)}, u32[]{:S(2)}) copy-start(bf16[256,4,512]{2,1,0:T(4,128)(2,1)} %param.18) | copy-start | bytes 3145732
  9.5 8.3 %copy-start = (bf16[256,4,1408]{2,1,0:T(4,128)(2,1)S(1)}, bf16[256,4,1408]{2,1,0:T(4,128)(2,1)}, u32[]{:S(2)}) copy-start(bf16[256,4,1408]{2,1,0:T(4,128)(2,1)} %param.21) | copy-start | bytes 8650756
  10.6 6.9 %copy-start.22 = (s32[1,256,2]{1,2,0:T(2,128)S(1)}, s32[1,256,2]{1,2,0:T(2,128)}, u32[]{:S(2)}) copy-start(s32[1,256,2]{1,2,0:T(2,128)} %param.25) | copy-start | bytes 6148
  10.6 60.1 %collective-permute-start.1 = (bf16[256,3072]{1,0:T(8,128)(2,1)}, bf16[256,3072]{1,0:T(8,128)(2,1)}, u32[]{:S(2)}, u32[]{:S(2)}) collective-permute-start(bf16[256,3072]{1,0:T(8,128)(2,1)} %constant_dynamic-update-slice_fusion.refs_1_), channel_id=1, source_target_pairs={{0,16},{4,20},{8,24},{12,28},{16,0},{20,4},{24,8},{28,12},{1,17},{... | collective-permute-start | bytes 4718600 | tf_op jit(solution)/shard_map/ppermute | solution.py:42
  13.5 58.6 %collective-permute-start.3 = (bf16[256,3072]{1,0:T(8,128)(2,1)}, bf16[256,3072]{1,0:T(8,128)(2,1)}, u32[]{:S(2)}, u32[]{:S(2)}) collective-permute-start(bf16[256,3072]{1,0:T(8,128)(2,1)} %constant_dynamic-update-slice_fusion.refs_1_), channel_id=1, source_target_pairs={{0,8},{4,12},{8,0},{12,4},{16,24},{20,28},{24,16},{28,20},{1,9},{5... | collective-permute-start | bytes 4718600 | tf_op jit(solution)/shard_map/ppermute | solution.py:42
  16.3 54.4 %collective-permute-start = (bf16[256,2048]{1,0:T(8,128)(2,1)}, bf16[256,2048]{1,0:T(8,128)(2,1)}, u32[]{:S(2)}, u32[]{:S(2)}) collective-permute-start(bf16[256,2048]{1,0:T(8,128)(2,1)} %bitcast.37.refs_0_), channel_id=1, source_target_pairs={{0,16},{4,20},{8,24},{12,28},{16,0},{20,4},{24,8},{28,12},{1,17},{... | collective-permute-start | bytes 3145736 | tf_op jit(solution)/shard_map/ppermute | solution.py:42
  16.8 55.3 %collective-permute-start.2 = (bf16[256,2048]{1,0:T(8,128)(2,1)}, bf16[256,2048]{1,0:T(8,128)(2,1)}, u32[]{:S(2)}, u32[]{:S(2)}) collective-permute-start(bf16[256,2048]{1,0:T(8,128)(2,1)} %bitcast.37.refs_0_), channel_id=1, source_target_pairs={{0,8},{4,12},{8,0},{12,4},{16,24},{20,28},{24,16},{28,20},{1,9},{5... | collective-permute-start | bytes 3145736 | tf_op jit(solution)/shard_map/ppermute | solution.py:42
  16.9 9.3 %copy-start.25 = (s32[256]{0:T(256)}, s32[256]{0:T(256)S(1)}, u32[]{:S(2)}) copy-start(s32[256]{0:T(256)S(1)} %iota_add_fusion.4) | copy-start | bytes 3076
  16.9 9.3 %copy-start.27 = (s32[256]{0:T(256)}, s32[256]{0:T(256)S(1)}, u32[]{:S(2)}) copy-start(s32[256]{0:T(256)S(1)} %iota_add_fusion.1) | copy-start | bytes 3076
  16.9 9.3 %copy-start.29 = (s32[256]{0:T(256)}, s32[256]{0:T(256)S(1)}, u32[]{:S(2)}) copy-start(s32[256]{0:T(256)S(1)} %iota_add_fusion.2) | copy-start | bytes 3076
  16.9 9.3 %copy-start.31 = (s32[256]{0:T(256)}, s32[256]{0:T(256)S(1)}, u32[]{:S(2)}) copy-start(s32[256]{0:T(256)S(1)} %iota_add_fusion.3) | copy-start | bytes 3076
  17.8 7.4 %copy-start.20 = (s32[1,256,2]{1,2,0:T(2,128)S(1)}, s32[1,256,2]{1,2,0:T(2,128)}, u32[]{:S(2)}) copy-start(s32[1,256,2]{1,2,0:T(2,128)} %param.23) | copy-start | bytes 6148
  17.9 8.3 %copy-start.33 = (s32[1,1024]{1,0:T(1,128)S(1)}, s32[1,1024]{1,0:T(1,128)}, u32[]{:S(2)}) copy-start(s32[1,1024]{1,0:T(1,128)} %param.22) | copy-start | bytes 12292
  25.2 6.7 %copy-start.21 = (s32[1,256,2]{1,2,0:T(2,128)S(1)}, s32[1,256,2]{1,2,0:T(2,128)}, u32[]{:S(2)}) copy-start(s32[1,256,2]{1,2,0:T(2,128)} %param.23) | copy-start | bytes 6148
  25.2 6.7 %copy-start.36 = (f32[1,256,2]{1,2,0:T(2,128)S(1)}, f32[1,256,2]{1,2,0:T(2,128)}, u32[]{:S(2)}) copy-start(f32[1,256,2]{1,2,0:T(2,128)} %param.24) | copy-start | bytes 6148
  25.3 7.3 %copy-start.34 = (bf16[256,1]{0,1:T(2,128)(2,1)S(1)}, bf16[256,1]{0,1:T(2,128)(2,1)}, u32[]{:S(2)}) copy-start(bf16[256,1]{0,1:T(2,128)(2,1)} %get-tuple-element.207) | copy-start | bytes 1540
  25.3 7.3 %copy-start.35 = (bf16[256,1]{0,1:T(2,128)(2,1)S(1)}, bf16[256,1]{0,1:T(2,128)(2,1)}, u32[]{:S(2)}) copy-start(bf16[256,1]{0,1:T(2,128)(2,1)} %get-tuple-element.208) | copy-start | bytes 1540
  25.3 7.5 %copy-start.23 = (s32[1,256,2]{1,2,0:T(2,128)S(1)}, s32[1,256,2]{1,2,0:T(2,128)}, u32[]{:S(2)}) copy-start(s32[1,256,2]{1,2,0:T(2,128)} %param.25) | copy-start | bytes 6148
  25.3 7.5 %copy-start.37 = (f32[1,256,2]{1,2,0:T(2,128)S(1)}, f32[1,256,2]{1,2,0:T(2,128)}, u32[]{:S(2)}) copy-start(f32[1,256,2]{1,2,0:T(2,128)} %param.26) | copy-start | bytes 6148
  26.1 0.6 copy-start.12
  26.1 0.6 copy-start.14
  26.1 0.6 copy-start.16
  26.1 0.6 copy-start.18
  28.0 6.4 %copy-start.38 = (bf16[256]{0:T(256)(128)(2,1)S(1)}, bf16[256]{0:T(256)(128)(2,1)}, u32[]{:S(2)}) copy-start(bf16[256]{0:T(256)(128)(2,1)} %param.16) | copy-start | bytes 1540
  28.0 6.3 %copy-start.39 = (bf16[256]{0:T(256)(128)(2,1)S(1)}, bf16[256]{0:T(256)(128)(2,1)}, u32[]{:S(2)}) copy-start(bf16[256]{0:T(256)(128)(2,1)} %param.15) | copy-start | bytes 1540
  32.0 0.6 copy-start.10
  49.3 1.3 copy-start.5
  51.6 6.3 %copy-start.13 = (s32[1,256]{1,0:T(1,128)S(1)}, s32[1,256]{1,0:T(1,128)}, u32[]{:S(2)}) copy-start(s32[1,256]{1,0:T(1,128)} %copy-done.12) | copy-start | bytes 3076
  51.6 6.3 %copy-start.15 = (s32[1,256]{1,0:T(1,128)S(1)}, s32[1,256]{1,0:T(1,128)}, u32[]{:S(2)}) copy-start(s32[1,256]{1,0:T(1,128)} %copy-done.14) | copy-start | bytes 3076
  51.6 6.3 %copy-start.17 = (s32[1,256]{1,0:T(1,128)S(1)}, s32[1,256]{1,0:T(1,128)}, u32[]{:S(2)}) copy-start(s32[1,256]{1,0:T(1,128)} %copy-done.16) | copy-start | bytes 3076
  51.6 6.3 %copy-start.19 = (s32[1,256]{1,0:T(1,128)S(1)}, s32[1,256]{1,0:T(1,128)}, u32[]{:S(2)}) copy-start(s32[1,256]{1,0:T(1,128)} %copy-done.18) | copy-start | bytes 3076
  51.6 6.3 %copy-start.26 = (s32[256]{0:T(256)S(1)}, s32[256]{0:T(256)}, u32[]{:S(2)}) copy-start(s32[256]{0:T(256)} %copy-done.25) | copy-start | bytes 3076
  51.6 6.3 %copy-start.28 = (s32[256]{0:T(256)S(1)}, s32[256]{0:T(256)}, u32[]{:S(2)}) copy-start(s32[256]{0:T(256)} %copy-done.27) | copy-start | bytes 3076
  51.6 6.3 %copy-start.30 = (s32[256]{0:T(256)S(1)}, s32[256]{0:T(256)}, u32[]{:S(2)}) copy-start(s32[256]{0:T(256)} %copy-done.29) | copy-start | bytes 3076
  51.7 6.3 %copy-start.32 = (s32[256]{0:T(256)S(1)}, s32[256]{0:T(256)}, u32[]{:S(2)}) copy-start(s32[256]{0:T(256)} %copy-done.31) | copy-start | bytes 3076
  51.7 6.9 %copy-start.24 = (s32[4,256]{1,0:T(4,128)S(1)}, s32[4,256]{1,0:T(4,128)}, u32[]{:S(2)}) copy-start(s32[4,256]{1,0:T(4,128)} %fusion.1) | copy-start | bytes 12292
  59.5 1.9 copy-start.3
  59.5 2.3 copy-start.4
  61.8 1.9 copy-start.1
  61.8 2.3 copy-start.2
  153.2 201.8 %all-reduce.8.cloned.1.call-start = ((), (), s32[]{:S(2)}) async-start(), calls=%async_computation.1 | async-start | bytes 2097152 | tf_op jit(solution)/shard_map/psum | solution.py:1580
  206.1 86.5 %copy-start.11 = (f32[256,4]{0,1:T(4,128)S(1)}, f32[256,4]{0,1:T(4,128)}, u32[]{:S(2)}) copy-start(f32[256,4]{0,1:T(4,128)} %copy-done.10) | copy-start | bytes 12292
  501.1 19.6 %collective-permute-start.4 = (bf16[256,1536]{1,0:T(8,128)(2,1)S(1)}, bf16[256,1536]{1,0:T(8,128)(2,1)S(1)}, u32[]{:S(2)}, u32[]{:S(2)}) collective-permute-start(bf16[256,1536]{1,0:T(8,128)(2,1)S(1)} %get-tuple-element.190), channel_id=1, source_target_pairs={{0,8},{4,12},{8,0},{12,4},{16,24},{20,28},{24,16},{28,20},{1,9},{5... | collective-permute-start | bytes 2359304 | tf_op jit(solution)/shard_map/ppermute | solution.py:42
  501.9 19.3 %collective-permute-start.5 = (bf16[256,1536]{1,0:T(8,128)(2,1)S(1)}, bf16[256,1536]{1,0:T(8,128)(2,1)S(1)}, u32[]{:S(2)}, u32[]{:S(2)}) collective-permute-start(bf16[256,1536]{1,0:T(8,128)(2,1)S(1)} %get-tuple-element.189), channel_id=1, source_target_pairs={{0,16},{4,20},{8,24},{12,28},{16,0},{20,4},{24,8},{28,12},{1,17},{... | collective-permute-start | bytes 2359304 | tf_op jit(solution)/shard_map/ppermute | solution.py:42
  520.7 0.9 copy-start.8
  521.2 0.9 copy-start.9
Sparse Core Ops, SparseCore 0:
  153.3 52.0 all-reduce.5
  292.8 49.9 all-reduce.7

commit v7 on v6

--- a/solution.py
+++ b/solution.py
@@ -246,15 +246,16 @@
     qkv_ref,
     mixed_ref,
     back_ref,
-    tokens_ref,
+    tokens_any,
     gain_ref,
-    resid_ref,
+    resid_any,
     gain_two_ref,
     mlp_ref,
     place_ref,
     out_ref,
     keep_ref,
-    give_ref,
+    give_one_ref,
+    give_two_ref,
     grad_tokens_ref,
     gain_out_ref,
     mlp_sum_ref,
@@ -270,6 +271,9 @@
     right,
     grads,
     got,
+    tokens_ref,
+    resid_ref,
+    load,
     send,
     recv,
     pass_send,
@@ -305,6 +309,10 @@
             runs[name] = Moves(ctx_count, moves, arrays, pass_send, pass_recv, (), base)
         base += len(moves)
     run = runs["share"]
+    late_loads = []
+    for i, (far_ref, near_ref) in enumerate(((tokens_any, tokens_ref), (resid_any, resid_ref))):
+        late_loads.append(pltpu.make_async_copy(far_ref, near_ref, load.at[i]))
+        late_loads[-1].start()
     runs["reduce"].begin()
     runs["mlp"].begin()
     for given, even_side, odd_side in (
@@ -372,6 +380,8 @@
         runs["mlp_spread"].begin()
 
     def norm_back():
+        for late_load in late_loads:
+            late_load.wait()
         runs["spread"].settle()
         x = tokens_ref[...].astype(F32)
         inverse = lax.rsqrt(jnp.mean(x * x, axis=-1, keepdims=True) + EPSILON)
@@ -411,7 +421,10 @@
                     at_last = last_lanes.index(plane)
                     there = slice(at_last * cols, (at_last + 1) * cols)
                     if j:
-                        give_ref[:, there] = total.astype(BF)
+                        half = len(last_lanes) // 2
+                        give_ref = (give_one_ref, give_two_ref)[at_last // half]
+                        at_give = at_last % half * cols
+                        give_ref[:, at_give : at_give + cols] = total.astype(BF)
                     else:
                         keep_ref[:, there] = total
                 else:
@@ -476,13 +489,13 @@
         out_shape=[
             jax.ShapeDtypeStruct((part, wide - 6 * cols), F32),
             jax.ShapeDtypeStruct((part, 6 * cols), F32),
-            jax.ShapeDtypeStruct((part, 6 * cols), BF),
+            *[jax.ShapeDtypeStruct((part, 3 * cols), BF)] * 2,
             jax.ShapeDtypeStruct((rows, width), BF),
             jax.ShapeDtypeStruct((8, part), F32),
             jax.ShapeDtypeStruct((rows, width), BF),
         ],
-        in_specs=[full] * (4 + len(others)),
-        out_specs=[full] * 6,
+        in_specs=[pl.BlockSpec(memory_space=pl.ANY) if i in (5, 7) else full for i in range(4 + len(others))],
+        out_specs=[full] * 7,
         scratch_shapes=[
             pltpu.VMEM(mlp.shape, BF),
             pltpu.VMEM(((tp_count - 1) * run_rows, width), BF),
@@ -493,6 +506,7 @@
         + [pltpu.VMEM((rows, width // 2), BF)] * 2
         + [pltpu.VMEM((2 * rows, wide), BF)]
         + [pltpu.VMEM((width // 2, wide), BF)] * 2
+        + [pltpu.VMEM((rows, width), BF), pltpu.VMEM((rows, width), F32), pltpu.SemaphoreType.DMA((2,))]
         + [pltpu.SemaphoreType.DMA((copies,))] * 2
         + [pltpu.SemaphoreType.DMA((passes,))] * 2,
         compiler_params=pltpu.CompilerParams(
@@ -728,9 +742,10 @@
                 at = slice(k * room - rows.start, (k + 1) * room - rows.start)
                 turned = slice((i ^ k) * run, ((i ^ k) + 1) * run)
                 mlp_ref[k * room : (k + 1) * room, turned] = out[at]
-        if stage < 2:
-            for r in range(len(groups["mlp"]) // 2):
-                runs["mlp"].start(2 * r + stage)
+        for k in ks:
+            if k < 2:
+                for r in range(len(groups["mlp"]) // 2):
+                    runs["mlp"].start(2 * r + k)
     for name in groups:
         if isinstance(name, tuple) and name[0] != "load":
             runs[name].finish()
@@ -895,9 +910,13 @@
     wide = heads * HD
     group = width // part
     given, refs = refs[: len(names_in)], refs[len(names_in) :]
-    gains_ref, hidden_ref, qkv_ref, kv_ref, mixed_ref, branch_ref, dy_out, rides_ref = refs[:8]
+    gains_ref, hidden_out, qkv_out, kv_out, mixed_ref, branch_ref, dy_out, rides_ref = refs[:8]
     refs = refs[8:]
-    made, (full, slots_ref, picked, picked_ride, slot_info, send, recv, *bounces) = refs[: len(names_out)], refs[len(names_out) :]
+    made, refs = refs[: len(names_out)], refs[len(names_out) :]
+    hidden_ref, qkv_ref, kv_ref, early, full, slots_ref, picked, picked_ride, slot_info, send, recv, *bounces = refs
+    leaving = []
+    for i, pair in enumerate(((hidden_ref, hidden_out), (qkv_ref, qkv_out), (kv_ref, kv_out))):
+        leaving.append(pltpu.make_async_copy(*pair, early.at[i]))
     arrays = dict(
         gain_own=gain_ref,
         gains=gains_ref,
@@ -934,6 +953,7 @@
     normed = x * lax.rsqrt(jnp.mean(x * x, axis=-1, keepdims=True) + EPSILON)
     run.settle(gains_done)
     hidden_ref[...] = (normed * gain_of(gains_ref, 0, part)).astype(BF)
+    leaving[0].start()
     run.settle(first_done, gains_done)
     run.kick(dy_done, spread_done)
     dy_out[:, run_cols(run_of)] = slots_ref[...]
@@ -955,11 +975,12 @@
     kv_ref[:rows] = qkv_ref[:, experts * wide :]
     run.begin()
     run.settle(second_done, first_done)
+    run.start(len(moves) - 2)
     for plane in range(experts):
         project(plane)
+    leaving[1].start()
     run.settle(keys_done, rest_done)
-    run.settle(rest_done, second_done)
-    run.start(len(moves) - 1)
+    leaving[2].start()
 
     def step(i, carry):
         h, e = i // experts, i % experts
@@ -978,11 +999,18 @@
         mixed_ref[:, cols] = dot(place, mixed, 0, 0).astype(BF)
         return carry
 
-    lax.fori_loop(0, heads * experts, step, 0)
+    for part_of in range(2):
+        half = heads * experts // 2
+        lax.fori_loop(part_of * half, (part_of + 1) * half, step, 0, unroll=2)
+        if part_of == 0:
+            run.settle(rest_done, second_done)
+            run.start(len(moves) - 1)
     for j in range(group):
         rows_at = slice(j * part, (j + 1) * part)
         branch_ref[:, rows_at] = dot(mixed_ref[...], full[rows_at, (experts + 2) * wide :], 1, 1).astype(BF)
     run.finish()
+    for copy in leaving:
+        copy.wait()
 
 
 def front(number, ctx_count, heads, part, moves, later, given, made, small):
@@ -1008,10 +1036,12 @@
     marks = [len(gains_moves)]
     for more in (first_moves, second_moves, rest_moves, kv_moves, dy_moves, dy_spread):
         marks.append(marks[-1] + len(more))
-    whole = (FULL, (0, width), None)
     gathered = first_moves + second_moves + rest_moves
-    landed = tuple(m[1] for m in gathered)
-    keep = [(whole, ("kept", (0, width), None), None, landed)]
+    edge = (experts + 2) * wide
+    keep = []
+    for cols, some in (((0, edge), first_moves + second_moves), ((edge, full_wide - edge), rest_moves)):
+        rows_at = ((0, width), cols)
+        keep.append(((FULL, *rows_at), ("kept", *rows_at), None, tuple(m[1] for m in some)))
     moves = gains_moves + gathered + kv_moves + dy_moves + dy_spread + later + keep
     slots_shape = (experts * place.shape[1], width // experts)
     rides_shape = (experts * place.shape[1], HD)
@@ -1041,8 +1071,11 @@
         out_shape=[jax.ShapeDtypeStruct(*x) for x in small_out]
         + [jax.ShapeDtypeStruct(shape, BF) for shape in shapes_out],
         in_specs=[full] * len(small) + [any_spec] * len(names_in),
-        out_specs=[full] * len(small_out) + [any_spec] * len(names_out),
+        out_specs=[any_spec if i in (1, 2, 3) else full for i in range(len(small_out))]
+        + [any_spec] * len(names_out),
         scratch_shapes=[
+            *[pltpu.VMEM(*small_out[i]) for i in (1, 2, 3)],
+            pltpu.SemaphoreType.DMA((3,)),
             pltpu.VMEM((width, full_wide), BF),
             *[pltpu.VMEM(slots_shape, BF)] * 2,
             pltpu.VMEM(rides_shape, BF),
@@ -1071,8 +1104,6 @@
     back_ref,
     dy_ref,
     gate_ref,
-    qkv_ref,
-    kv_ref,
     place_ref,
     about_ref,
     segk_ref,
@@ -1081,14 +1112,16 @@
     sin_ref,
     mlp_first_ref,
     weight_ref,
+    qkv_any,
+    kv_any,
     *refs,
 ):
     experts, _, rows = place_ref.shape
-    keys = kv_ref.shape[0]
+    keys = kv_any.shape[0]
     wide = heads * HD
     width = tokens_ref.shape[1]
     given, refs = refs[: len(names_in)], refs[len(names_in) :]
-    out_ref, resid_ref, grad_branch_ref, gain_out_ref, back_one_ref, mlp_out_ref = refs[:6]
+    out_ref, resid_out, grad_branch_out, gain_out_ref, back_one_ref, mlp_out_ref = refs[:6]
     made, refs = refs[6 : 6 + len(names_out)], refs[6 + len(names_out) :]
     (
         full,
@@ -1101,6 +1134,10 @@
         mlp_mine,
         mlp_got,
         slot_info,
+        qkv_ref,
+        kv_ref,
+        resid_ref,
+        grad_branch_ref,
         send,
         recv,
         pass_send,
@@ -1112,7 +1149,23 @@
     bits = range(bits_of(ctx_count))
     greet(ctx_count, sorted({*masks_of(moves), *[1 << b for b in bits]}))
     run = Moves(ctx_count, moves, arrays, send, recv)
-    run.begin()
+    slow = [i for i, m in enumerate(moves) if m[0][0] != "mlp"]
+    pace = 2
+    paced = [slow[i : i + pace] for i in range(0, len(slow), pace)]
+    for i in range(len(moves)):
+        if i not in slow:
+            run.start(i)
+
+    def send_some(count):
+        for _ in range(min(count, len(paced))):
+            for i in paced.pop(0):
+                run.start(i)
+
+    send_some(2)
+    late_loads = []
+    for i, (far_ref, near_ref) in enumerate(((qkv_any, qkv_ref), (kv_any, kv_ref))):
+        late_loads.append(pltpu.make_async_copy(far_ref, near_ref, load.at[2 + i]))
+        late_loads[-1].start()
     slot_table(place_ref, about_ref, slot_info)
     edge = (experts + 2) * wide
     loads = []
@@ -1130,6 +1183,10 @@
     resid = dy_ref[...].astype(F32) + inverse * (scaled - normed * inner)
     resid_ref[...] = resid
     grad_branch_ref[...] = resid.astype(BF)
+    leaving = []
+    for i, pair in enumerate(((resid_ref, resid_out), (grad_branch_ref, grad_branch_out))):
+        leaving.append(pltpu.make_async_copy(*pair, load.at[4 + i]))
+        leaving[-1].start()
     loads[0].wait()
     for e in range(experts):
         cols = slice(edge + e * wide, edge + (e + 1) * wide)
@@ -1162,6 +1219,8 @@
             at += wide
             out_ref[:, at + h * HD : at + (h + 1) * HD] = mine[:, HD:]
 
+    for late in late_loads:
+        late.wait()
     for h in range(heads):
         dk_acc[...] = jnp.zeros_like(dk_acc)
         dv_acc[...] = jnp.zeros_like(dv_acc)
@@ -1189,13 +1248,17 @@
             out_ref[:, cols] = turn(back_q, cos_ref[:rows], -sin_ref[:rows]).astype(BF)
             return carry
 
-        lax.fori_loop(0, experts, step, 0)
+        for low in range(0, experts, 2):
+            lax.fori_loop(low, low + 2, step, 0, unroll=2)
+            if h < heads // 2:
+                send_some(1)
         total[h, :, :HD] = turn(dk_acc[...], cos_ref[...], -sin_ref[...]).astype(BF)
         total[h, :, HD:] = dv_acc[...].astype(BF)
         head_copy(h, 0).start()
         if h:
             head_sum(h - 1, 0)
     head_sum(heads - 1, 0)
+    send_some(len(paced))
     loads[1].wait()
     queries = experts * wide
     for j in range(width // part):
@@ -1222,10 +1285,12 @@
         for bit in bits:
             head_copy(h, bit).wait_send()
     run.finish()
-
-
-def attend_back(number, ctx_count, tp_count, heads, part, moves, given, made, weight, *small):
-    tokens, qkv, kv = small[0], small[6], small[7]
+    for copy in leaving:
+        copy.wait()
+
+
+def attend_back(number, ctx_count, tp_count, heads, part, moves, given, made, weight, qkv, kv, *small):
+    tokens = small[0]
     rows, width = tokens.shape
     keys = kv.shape[0]
     any_spec = pl.BlockSpec(memory_space=pl.ANY)
@@ -1253,10 +1318,11 @@
         ),
         out_shape=[jax.ShapeDtypeStruct(*x) for x in small_out]
         + [jax.ShapeDtypeStruct(shape, BF) for shape in made.values()],
-        in_specs=[full] * len(small) + [any_spec] * (1 + len(given)),
-        out_specs=[full] * len(small_out) + [any_spec] * len(made),
+        in_specs=[full] * len(small) + [any_spec] * (3 + len(given)),
+        out_specs=[any_spec if i in (1, 2) else full for i in range(len(small_out))]
+        + [any_spec] * len(made),
         input_output_aliases={
-            len(small) + 1 + list(given).index(n): len(small_out) + i for i, n in enumerate(made)
+            len(small) + 3 + list(given).index(n): len(small_out) + i for i, n in enumerate(made)
         },
         scratch_shapes=[
             pltpu.VMEM(weight.shape, BF),
@@ -1266,15 +1332,16 @@
         + [pltpu.VMEM((keys, HD), F32)] * 2
         + [pltpu.VMEM((heads, keys, 2 * HD), BF)] * 2
         + [pltpu.VMEM((slots, run), BF), pltpu.VMEM(((tp_count - 1) * slots, run), BF)]
-        + [pltpu.VMEM((*small[8].shape[:2], HD), F32)]
+        + [pltpu.VMEM((*small[6].shape[:2], HD), F32), pltpu.VMEM(qkv.shape, BF), pltpu.VMEM(kv.shape, BF)]
+        + [pltpu.VMEM(*small_out[i]) for i in (1, 2)]
         + [pltpu.SemaphoreType.DMA((len(moves),))] * 2
         + [pltpu.SemaphoreType.DMA((passes,))] * 2
-        + [pltpu.SemaphoreType.DMA((2,))],
+        + [pltpu.SemaphoreType.DMA((6,))],
         compiler_params=pltpu.CompilerParams(
             collective_id=number, has_side_effects=True, vmem_limit_bytes=VMEM_LIMIT
         ),
         name="attend_back",
-    )(*small, weight, *given.values())
+    )(*small, weight, qkv, kv, *given.values())
     return out[: len(small_out)], dict(zip(made, out[len(small_out) :]))
 
 
@@ -1595,16 +1662,17 @@
         got_in.update({k: made[("in", k)] for k in ks})
         got_down.update({k: made[("down", k)] for k in ks})
 
+    cuts = min(8, part // 16)
     moves, made_shapes = grad_moves(near, 1)
-    early, early_shapes = grad_moves(far, 4)
-    moves += early[: len(early) // 4]
+    early, early_shapes = grad_moves(far, cuts)
+    moves += early[: len(early) // cuts]
     made_shapes.update(early_shapes)
     grads_in, grads_down, _ = lax.optimization_barrier((grads_in, grads_down, back_two_part))
     given = {"in": grads_in, "down": grads_down}
     made = move("grads_near", 5, ctx_count, moves, given, made_shapes)
     keep_grads(made, near)
 
-    moves, made_shapes = grad_moves(far, 4, part // 4)
+    moves, made_shapes = grad_moves(far, cuts, part // cuts)
     back_two, given, made = lax.optimization_barrier((back_two, given, made))
     given.update({name: made[name] for name in made_shapes})
     given["mlp"] = mlp_slots
@@ -1618,14 +1686,14 @@
         given,
         made_shapes,
         attn_full,
+        qkv,
+        kv,
         tokens_rel,
         branch_sum,
         gains,
         back_two,
         grad_out,
         gate_attn,
-        qkv,
-        kv,
         place_attn,
         about,
         *key_row,
@@ -1635,7 +1703,7 @@
     )
     keep_grads(made, far)
     upper = list(range(1, bits_of(group)))
-    grad_attnw, kept, given, grad_tokens, gain_grads, mlp_sum = attn_grads(
+    grad_attnw, kept, *given, grad_tokens, gain_grads, mlp_sum = attn_grads(
         7,
         ctx_count,
         tp_count,
@@ -1656,11 +1724,10 @@
     )
     planes = attn_experts * 2 + 2
     lanes, last_lanes = lanes_of(planes, attn_experts + 2, upper)
-    half = given.shape[1] // 2
     came = []
     for i in range(2):
         bit = dict(lanes)[last_lanes[3 * i]][-1]
-        came.append(exchange(given[:, i * half : (i + 1) * half], 1 << bit))
+        came.append(exchange(given[i], 1 << bit))
     output, grad_tokens = last(me, group, tokens_rel, branch_sum, mlp_sum, grad_tokens)
     grad_in_out, grad_down_out = spread_grads(
         [got_in[k] for k in range(experts)],

time: 542 us -> 538 us (level)
    pallas_call x2, Pallas kernels: 114 us -> 108 us  [move(): pl.pallas_call(functools.partial(move_kernel, ctx_count, moves, plain + [...]
  transfers between devices with their start and end apart: 8 -> 8, of which waited for: 4 -> 4; matrix products, arithmetic and copies ran while one was open for 8% -> 8% of each run, Pallas kernels for 25% -> 24%
where the time goes in v7:
time: 538 us; the launch traced here: 530 us
  Pallas kernels  449 us (83%)
  local copies, waits for them, and re-layouts  40 us (7%)
  between operations  15.1 us (3%)
  waiting for transfers between devices  9.24 us (2%)
  other arithmetic  8.57 us (2%)
  starting transfers between devices  7.46 us (1%)
    pallas_call x2, Pallas kernels, move(): pl.pallas_call(functools.partial(move_kernel, ctx_count, moves, plain + [...  108 us
    pallas_call x1, Pallas kernels, run_experts(): pl.pallas_call(functools.partial(experts_kernel, ctx_count, experts, shar...  86.5 us
    pallas_call x1, Pallas kernels, attn_grads(): pl.pallas_call(functools.partial(attn_grads_kernel, ctx_count, groups, bi...  86.2 us
    pallas_call x1, Pallas kernels, front(): pl.pallas_call(functools.partial(front_kernel, ctx_count, moves, marks, n...  79.6 us
    pallas_call x1, Pallas kernels, attend_back(): pl.pallas_call(functools.partial(attend_back_kernel, ctx_count, moves, li...  61.9 us
    slice x1, local copies, waits for them, and re-layouts, expert_rows(): return [in_rows[:, 0, 0], in_rows[:, 0, 1], down_rows[:, 0]]  11.7 us
    pallas_call x1, Pallas kernels, spread_grads(): pl.pallas_call(functools.partial(spread_kernel, experts), grid_spec=pltpu...  10.8 us
  transfers between devices with their start and end apart: 8, of which 4 were waited for; matrix products, arithmetic and copies ran while one was open for 8% of the time, Pallas kernels for 24%

profile of v7, /device:TPU:0, one launch (start us, length us, event | category | flops | bytes accessed | tf_op | source)
XLA Modules:
  0.0 530.3 jit_solution(18427705603747101070)
XLA Ops:
  7.2 1.2 copy.92
  8.4 0.8 constant_dynamic-update-slice_fusion.1
  9.6 1.0 constant_dynamic-update-slice_fusion.refs_1_
  10.6 2.9 collective-permute-start.1
  13.5 1.5 collective-permute-start.3
  15.1 1.2 copy.91
  16.3 0.5 collective-permute-start
  16.9 0.6 fusion.7
  17.9 7.4 %constant_dynamic-slice_fusion.4 = (bf16[256,1,1408]{2,1,0:T(2,128)(2,1)}, bf16[256,1,1408]{2,1,0:T(2,128)(2,1)}, bf16[256,1,1408]{2,1,0:T(2,128)(2,1)}, bf16[256,1,1408]{2,1,0:T(2,128)(2,1)}) fusion(bf16[256,4,1408]{2,1,0:T(4,128)(2,1)S(1)} %copy-done, s32[]{:T(128)S(6)} %select_n.92, s32[]{:T(128)S(6)} %select_n.91, s32[]{:T(128)S(6)} %select_n.90, ...), kind=kLoop, calls=%fused_computation.41 | loop fusion | bytes 5767184 | tf_op jit(solution)/shard_map/dynamic_slice | solution.py:1441
  25.3 0.8 fusion.1
  26.2 0.5 copy-done.12
  26.7 1.2 convert_reduce_fusion
  28.0 3.0 fusion.4
  31.0 1.0 pad_maximum_fusion.cos_ref
  32.0 0.6 copy-done.10
  33.0 0.6 pad.13.about_ref
  33.7 0.6 pad.14.ride_ref
  34.3 0.6 pad.12.gain_ref
  34.9 11.7 %constant_dynamic-slice_fusion.5 = (bf16[256,1,1,1408]{3,2,1,0:T(2,128)(2,1)S(1)}, bf16[256,1,1,1408]{3,2,1,0:T(2,128)(2,1)S(1)}, bf16[256,1,1,1408]{3,2,1,0:T(2...) fusion(bf16[256,4,2,1408]{3,2,1,0:T(2,128)(2,1)} %param.20, ...), kind=kLoop, calls=%fused_computation.42 | loop fusion | bytes 11534356 | tf_op jit(solution)/shard_map/slice | solution.py:1496
  46.7 1.3 copy_bitcast_fusion.1
  48.0 1.3 copy_bitcast_fusion.4
  49.3 1.3 copy_bitcast_fusion.7
  50.6 1.0 pad_maximum_fusion.1.sin_ref
  51.7 6.0 %in_order.1 = (bf16[256,2048]{1,0:T(8,128)(2,1)}, bf16[256,2048]{1,0:T(8,128)(2,1)}) custom-call(s32[1]{0:T(128)} %bitcast.me_ref, bf16[256,2048]{1,0:T(8,128)(2,1)} %bitcast.61, bf16[256,2048]{1,0:T(8,128)(2,1)} %bitcast.62), custom_call_target="tpu_custom_call" | custom-call | tf_op jit(solution)/shard_map/in_order/pallas_call | solution.py:535
  57.7 0.6 add_convert_fusion.1
  58.3 0.9 fusion.3
  59.3 1.3 copy_bitcast_fusion.10
  60.6 0.6 copy-done.3
  61.6 1.3 copy_bitcast_fusion
  62.9 0.6 copy-done.1
  63.9 1.3 copy_bitcast_fusion.6
  65.2 5.5 %collective-permute-done.refs_2_ = bf16[256,2048]{1,0:T(8,128)(2,1)} collective-permute-done((bf16[256,2048]{1,0:T(8,128)(2,1)}, bf16[256,2048]{1,0:T(8,128)(2,1)}, u32[]{:S(2)}, u32[]{:S(2)}) %collective-permute-start) | collective-permute-done | bytes 1048608 | tf_op jit(solution)/shard_map/ppermute | solution.py:42
  70.7 1.5 collective-permute-done.2.refs_4_
  72.2 79.6 %front.1 = (bf16[128,512]{1,0:T(8,128)(2,1)}, bf16[256,2048]{1,0:T(8,128)(2,1)}, bf16[256,3072]{1,0:T(8,128)(2,1)}, bf16[1024,1024]{1,0:T(8,128)(2,1)}, bf16[256...) custom-call(bf16[256,2048]{1,0:T(8,128)(2,1)} %get-tuple-element.91., ...), custom_call_target="tpu_custom_call" | custom-call | tf_op jit(solution)/shard_map/front/pallas_call | solution.py:1067
  152.2 52.7 %weights_two.1 = (bf16[2048,2816]{1,0:T(8,128)(2,1)}, bf16[2048,1408]{1,0:T(8,128)(2,1)}) custom-call(bf16[256,1408]{1,0:T(8,128)(2,1)} %get-tuple-element.114.refs_9_.refs_0_, bf16[256,1408]{1,0:T(8,128)(2,1)} %get-tuple-element.115.refs_10_.refs_1_, ...), custom_call_target="tpu_custom_call", output_to_operand_aliasing={{0}: (10, {}), {1}: (9, {})} | custom-call | tf_op jit(solution)/shard_map/weights_two/pallas_call | solution.py:206
  205.0 86.5 %experts.1 = (bf16[1024,2816]{1,0:T(8,128)(2,1)}, bf16[1024,1408]{1,0:T(8,128)(2,1)}, bf16[576,2048]{1,0:T(8,128)(2,1)}, bf16[256,2048]{1,0:T(8,128)(2,1)}, bf16[864,512]{1,0:T(8,128)(2,1)}) custom-call(bf16[256,2048]{1,0:T(8,128)(2,1)} %get-tuple-element.91.tokens_ref.tokens_any.refs_0_, bf16[256,2048]{1,0:T(8,128)(2,1)} %all-reduce.6.cloned.1.call-done.branch_ref.refs_1_, ...), custom_call_target="tpu_custom_call" | custom-call | tf_op jit(solution)/shard_map/experts/pallas_call | solution.py:830
  291.5 0.8 copy.74.gate_ref
  292.3 55.7 %grads_near.1 = (bf16[256,2816]{1,0:T(8,128)(2,1)}, bf16[256,2816]{1,0:T(8,128)(2,1)}, bf16[256,1408]{1,0:T(8,128)(2,1)}, bf16[256,1408]{1,0:T(8,128)(2,1)}, bf1...) custom-call(bf16[1024,2816]{1,0:T(8,128)(2,1)} %get-tuple-element.144.refs_0_.refs_1_, ...), custom_call_target="tpu_custom_call" | custom-call | tf_op jit(solution)/shard_map/grads_near/pallas_call | solution.py:206
  348.0 61.9 %attend_back.1 = (bf16[256,3072]{1,0:T(8,128)(2,1)}, f32[256,2048]{1,0:T(8,128)}, bf16[256,2048]{1,0:T(8,128)(2,1)}, f32[1,2048]{1,0:T(1,128)}, bf16[256,2048]{1...) custom-call(bf16[256,2048]{1,0:T(8,128)(2,1)} %get-tuple-element.91., ...), custom_call_target="tpu_custom_call", output_to_operand_aliasing={{6}: (18, {}), {7}: (19, {})} | custom-call | tf_op jit(solution)/shard_map/attend_back/pallas_call | solution.py:1315
  409.9 86.2 %attn_grads.1 = (f32[256,2048]{1,0:T(8,128)}, f32[256,3072]{1,0:T(8,128)}, bf16[256,1536]{1,0:T(8,128)(2,1)}, bf16[256,1536]{1,0:T(8,128)(2,1)}, bf16[256,2048]{...) custom-call(bf16[256,2048]{1,0:T(8,128)(2,1)} %get-tuple-element.105.hidden_ref, ...), custom_call_target="tpu_custom_call" | custom-call | tf_op jit(solution)/shard_map/attn_grads/pallas_call | solution.py:487
  496.2 0.8 collective-permute-start.4
  497.0 1.2 collective-permute-start.5
  498.2 10.8 %spread_grads.1 = (f32[256,4,2,1408]{3,2,1,0:T(2,128)}, f32[256,4,1408]{2,1,0:T(4,128)}) custom-call(s32[1]{0:T(128)} %bitcast.35.me_ref, bf16[1024,2816]{1,0:T(8,128)(2,1)} %get-tuple-element.144.refs_0_.refs_1_, bf16[256,2816]{1,0:T(8,128)(2,1)} %get-tuple-element.135.refs_1_, bf16[256,2816]{1,0:T(8,128)(2,1)} %get-tuple-element.136.refs_2_, ...), custom_call_target="tpu_custom_call" | custom-call | tf_op jit(solution)/shard_map/spread_grads/pallas_call | solution.py:1369
  509.0 4.0 last.1
  513.0 1.3 fusion.9
  514.3 1.7 collective-permute-done.4.one_ref
  516.0 0.5 collective-permute-done.5.two_ref
  517.4 5.6 %lay_out.1 = (f32[256,4,512]{2,1,0:T(4,128)}, f32[256,2,512]{2,1,0:T(2,128)}, f32[256,4,512]{2,1,0:T(4,128)}) custom-call(f32[256,2048]{1,0:T(8,128)} %get-tuple-element.160.grad_ref, f32[256,3072]{1,0:T(8,128)} %get-tuple-element.161.keep_ref, bf16[256,1536]{1,0:T(8,128)(2,1)} %copy-done.8, bf16[256,1536]{1,0:T(8,128)(2,1)} %copy-done.9), custom_call_target="tpu_custom_call" | custom-call | tf_op jit(solution)/shard_map/lay_out/pallas_call | solution.py:597
  (109 shorter events, 3.6 us)
Async XLA Ops:
  7.2 2.1 copy-start.6
  7.2 197.8 %all-reduce.6.cloned.1.call-start = ((), (), s32[]{:S(2)}) async-start(), calls=%async_computation | async-start | bytes 2097152 | tf_op jit(solution)/shard_map/psum | solution.py:1615
  9.5 5.5 %copy-start.7 = (bf16[256,4,512]{2,1,0:T(4,128)(2,1)S(1)}, bf16[256,4,512]{2,1,0:T(4,128)(2,1)}, u32[]{:S(2)}) copy-start(bf16[256,4,512]{2,1,0:T(4,128)(2,1)} %param.18) | copy-start | bytes 3145732
  9.5 8.3 %copy-start = (bf16[256,4,1408]{2,1,0:T(4,128)(2,1)S(1)}, bf16[256,4,1408]{2,1,0:T(4,128)(2,1)}, u32[]{:S(2)}) copy-start(bf16[256,4,1408]{2,1,0:T(4,128)(2,1)} %param.21) | copy-start | bytes 8650756
  10.6 6.9 %copy-start.22 = (s32[1,256,2]{1,2,0:T(2,128)S(1)}, s32[1,256,2]{1,2,0:T(2,128)}, u32[]{:S(2)}) copy-start(s32[1,256,2]{1,2,0:T(2,128)} %param.25) | copy-start | bytes 6148
  10.6 60.1 %collective-permute-start.1 = (bf16[256,3072]{1,0:T(8,128)(2,1)}, bf16[256,3072]{1,0:T(8,128)(2,1)}, u32[]{:S(2)}, u32[]{:S(2)}) collective-permute-start(bf16[256,3072]{1,0:T(8,128)(2,1)} %constant_dynamic-update-slice_fusion.refs_1_), channel_id=1, source_target_pairs={{0,16},{4,20},{8,24},{12,28},{16,0},{20,4},{24,8},{28,12},{1,17},{... | collective-permute-start | bytes 4718600 | tf_op jit(solution)/shard_map/ppermute | solution.py:42
  13.5 58.6 %collective-permute-start.3 = (bf16[256,3072]{1,0:T(8,128)(2,1)}, bf16[256,3072]{1,0:T(8,128)(2,1)}, u32[]{:S(2)}, u32[]{:S(2)}) collective-permute-start(bf16[256,3072]{1,0:T(8,128)(2,1)} %constant_dynamic-update-slice_fusion.refs_1_), channel_id=1, source_target_pairs={{0,8},{4,12},{8,0},{12,4},{16,24},{20,28},{24,16},{28,20},{1,9},{5... | collective-permute-start | bytes 4718600 | tf_op jit(solution)/shard_map/ppermute | solution.py:42
  16.3 54.4 %collective-permute-start = (bf16[256,2048]{1,0:T(8,128)(2,1)}, bf16[256,2048]{1,0:T(8,128)(2,1)}, u32[]{:S(2)}, u32[]{:S(2)}) collective-permute-start(bf16[256,2048]{1,0:T(8,128)(2,1)} %bitcast.37.refs_0_), channel_id=1, source_target_pairs={{0,16},{4,20},{8,24},{12,28},{16,0},{20,4},{24,8},{28,12},{1,17},{... | collective-permute-start | bytes 3145736 | tf_op jit(solution)/shard_map/ppermute | solution.py:42
  16.8 55.3 %collective-permute-start.2 = (bf16[256,2048]{1,0:T(8,128)(2,1)}, bf16[256,2048]{1,0:T(8,128)(2,1)}, u32[]{:S(2)}, u32[]{:S(2)}) collective-permute-start(bf16[256,2048]{1,0:T(8,128)(2,1)} %bitcast.37.refs_0_), channel_id=1, source_target_pairs={{0,8},{4,12},{8,0},{12,4},{16,24},{20,28},{24,16},{28,20},{1,9},{5... | collective-permute-start | bytes 3145736 | tf_op jit(solution)/shard_map/ppermute | solution.py:42
  16.9 9.3 %copy-start.25 = (s32[256]{0:T(256)}, s32[256]{0:T(256)S(1)}, u32[]{:S(2)}) copy-start(s32[256]{0:T(256)S(1)} %iota_add_fusion.4) | copy-start | bytes 3076
  16.9 9.3 %copy-start.27 = (s32[256]{0:T(256)}, s32[256]{0:T(256)S(1)}, u32[]{:S(2)}) copy-start(s32[256]{0:T(256)S(1)} %iota_add_fusion.1) | copy-start | bytes 3076
  16.9 9.3 %copy-start.29 = (s32[256]{0:T(256)}, s32[256]{0:T(256)S(1)}, u32[]{:S(2)}) copy-start(s32[256]{0:T(256)S(1)} %iota_add_fusion.2) | copy-start | bytes 3076
  16.9 9.3 %copy-start.31 = (s32[256]{0:T(256)}, s32[256]{0:T(256)S(1)}, u32[]{:S(2)}) copy-start(s32[256]{0:T(256)S(1)} %iota_add_fusion.3) | copy-start | bytes 3076
  17.8 7.4 %copy-start.20 = (s32[1,256,2]{1,2,0:T(2,128)S(1)}, s32[1,256,2]{1,2,0:T(2,128)}, u32[]{:S(2)}) copy-start(s32[1,256,2]{1,2,0:T(2,128)} %param.23) | copy-start | bytes 6148
  17.9 8.3 %copy-start.33 = (s32[1,1024]{1,0:T(1,128)S(1)}, s32[1,1024]{1,0:T(1,128)}, u32[]{:S(2)}) copy-start(s32[1,1024]{1,0:T(1,128)} %param.22) | copy-start | bytes 12292
  25.2 6.7 %copy-start.21 = (s32[1,256,2]{1,2,0:T(2,128)S(1)}, s32[1,256,2]{1,2,0:T(2,128)}, u32[]{:S(2)}) copy-start(s32[1,256,2]{1,2,0:T(2,128)} %param.23) | copy-start | bytes 6148
  25.3 6.7 %copy-start.36 = (f32[1,256,2]{1,2,0:T(2,128)S(1)}, f32[1,256,2]{1,2,0:T(2,128)}, u32[]{:S(2)}) copy-start(f32[1,256,2]{1,2,0:T(2,128)} %param.24) | copy-start | bytes 6148
  25.3 7.3 %copy-start.34 = (bf16[256,1]{0,1:T(2,128)(2,1)S(1)}, bf16[256,1]{0,1:T(2,128)(2,1)}, u32[]{:S(2)}) copy-start(bf16[256,1]{0,1:T(2,128)(2,1)} %get-tuple-element.207) | copy-start | bytes 1540
  25.3 7.3 %copy-start.35 = (bf16[256,1]{0,1:T(2,128)(2,1)S(1)}, bf16[256,1]{0,1:T(2,128)(2,1)}, u32[]{:S(2)}) copy-start(bf16[256,1]{0,1:T(2,128)(2,1)} %get-tuple-element.208) | copy-start | bytes 1540
  25.3 7.5 %copy-start.23 = (s32[1,256,2]{1,2,0:T(2,128)S(1)}, s32[1,256,2]{1,2,0:T(2,128)}, u32[]{:S(2)}) copy-start(s32[1,256,2]{1,2,0:T(2,128)} %param.25) | copy-start | bytes 6148
  25.3 7.5 %copy-start.37 = (f32[1,256,2]{1,2,0:T(2,128)S(1)}, f32[1,256,2]{1,2,0:T(2,128)}, u32[]{:S(2)}) copy-start(f32[1,256,2]{1,2,0:T(2,128)} %param.26) | copy-start | bytes 6148
  26.1 0.6 copy-start.12
  26.1 0.6 copy-start.14
  26.1 0.6 copy-start.16
  26.2 0.6 copy-start.18
  28.0 6.4 %copy-start.38 = (bf16[256]{0:T(256)(128)(2,1)S(1)}, bf16[256]{0:T(256)(128)(2,1)}, u32[]{:S(2)}) copy-start(bf16[256]{0:T(256)(128)(2,1)} %param.16) | copy-start | bytes 1540
  28.0 6.3 %copy-start.39 = (bf16[256]{0:T(256)(128)(2,1)S(1)}, bf16[256]{0:T(256)(128)(2,1)}, u32[]{:S(2)}) copy-start(bf16[256]{0:T(256)(128)(2,1)} %param.15) | copy-start | bytes 1540
  32.0 0.6 copy-start.10
  49.3 1.3 copy-start.5
  51.6 6.0 %copy-start.13 = (s32[1,256]{1,0:T(1,128)S(1)}, s32[1,256]{1,0:T(1,128)}, u32[]{:S(2)}) copy-start(s32[1,256]{1,0:T(1,128)} %copy-done.12) | copy-start | bytes 3076
  51.6 6.0 %copy-start.15 = (s32[1,256]{1,0:T(1,128)S(1)}, s32[1,256]{1,0:T(1,128)}, u32[]{:S(2)}) copy-start(s32[1,256]{1,0:T(1,128)} %copy-done.14) | copy-start | bytes 3076
  51.6 6.0 %copy-start.17 = (s32[1,256]{1,0:T(1,128)S(1)}, s32[1,256]{1,0:T(1,128)}, u32[]{:S(2)}) copy-start(s32[1,256]{1,0:T(1,128)} %copy-done.16) | copy-start | bytes 3076
  51.6 6.0 %copy-start.19 = (s32[1,256]{1,0:T(1,128)S(1)}, s32[1,256]{1,0:T(1,128)}, u32[]{:S(2)}) copy-start(s32[1,256]{1,0:T(1,128)} %copy-done.18) | copy-start | bytes 3076
  51.6 6.1 %copy-start.26 = (s32[256]{0:T(256)S(1)}, s32[256]{0:T(256)}, u32[]{:S(2)}) copy-start(s32[256]{0:T(256)} %copy-done.25) | copy-start | bytes 3076
  51.6 6.1 %copy-start.28 = (s32[256]{0:T(256)S(1)}, s32[256]{0:T(256)}, u32[]{:S(2)}) copy-start(s32[256]{0:T(256)} %copy-done.27) | copy-start | bytes 3076
  51.7 6.1 %copy-start.30 = (s32[256]{0:T(256)S(1)}, s32[256]{0:T(256)}, u32[]{:S(2)}) copy-start(s32[256]{0:T(256)} %copy-done.29) | copy-start | bytes 3076
  51.7 6.1 %copy-start.32 = (s32[256]{0:T(256)S(1)}, s32[256]{0:T(256)}, u32[]{:S(2)}) copy-start(s32[256]{0:T(256)} %copy-done.31) | copy-start | bytes 3076
  51.7 6.7 %copy-start.24 = (s32[4,256]{1,0:T(4,128)S(1)}, s32[4,256]{1,0:T(4,128)}, u32[]{:S(2)}) copy-start(s32[4,256]{1,0:T(4,128)} %fusion.1) | copy-start | bytes 12292
  59.3 1.9 copy-start.3
  59.3 2.3 copy-start.4
  61.6 1.9 copy-start.1
  61.6 2.3 copy-start.2
  151.8 196.3 %all-reduce.8.cloned.1.call-start = ((), (), s32[]{:S(2)}) async-start(), calls=%async_computation.1 | async-start | bytes 2097152 | tf_op jit(solution)/shard_map/psum | solution.py:1647
  205.0 86.5 %copy-start.11 = (f32[256,4]{0,1:T(4,128)S(1)}, f32[256,4]{0,1:T(4,128)}, u32[]{:S(2)}) copy-start(f32[256,4]{0,1:T(4,128)} %copy-done.10) | copy-start | bytes 12292
  496.2 19.8 %collective-permute-start.4 = (bf16[256,1536]{1,0:T(8,128)(2,1)}, bf16[256,1536]{1,0:T(8,128)(2,1)S(1)}, u32[]{:S(2)}, u32[]{:S(2)}) collective-permute-start(bf16[256,1536]{1,0:T(8,128)(2,1)} %get-tuple-element.162), channel_id=1, source_target_pairs={{0,8},{4,12},{8,0},{12,4},{16,24},{20,28},{24,16},{28,20},{1,9},{5... | collective-permute-start | bytes 2359304 | tf_op jit(solution)/shard_map/ppermute | solution.py:42
  497.0 19.5 %collective-permute-start.5 = (bf16[256,1536]{1,0:T(8,128)(2,1)}, bf16[256,1536]{1,0:T(8,128)(2,1)S(1)}, u32[]{:S(2)}, u32[]{:S(2)}) collective-permute-start(bf16[256,1536]{1,0:T(8,128)(2,1)} %get-tuple-element.163), channel_id=1, source_target_pairs={{0,16},{4,20},{8,24},{12,28},{16,0},{20,4},{24,8},{28,12},{1,17},{... | collective-permute-start | bytes 2359304 | tf_op jit(solution)/shard_map/ppermute | solution.py:42
  516.0 0.9 copy-start.8
  516.5 0.9 copy-start.9
Sparse Core Ops, SparseCore 0:
  151.9 52.0 all-reduce.5
  291.6 49.9 all-reduce.7

commit v8 on v7

--- a/solution.py
+++ b/solution.py
@@ -627,7 +627,7 @@
     *refs,
 ):
     far_refs, refs = refs[: len(far_names)], refs[len(far_names) :]
-    grads_in, grads_down, mlp_ref, two_part, mlp_first = refs[:5]
+    grads_in, grads_down, mlp_out, two_part, mlp_first = refs[:5]
     (
         win,
         wdown,
@@ -643,6 +643,8 @@
         dy_got,
         gu_got,
         active_got,
+        mlp_ref,
+        leave,
         send,
         recv,
     ) = refs[5:]
@@ -746,6 +748,8 @@
             if k < 2:
                 for r in range(len(groups["mlp"]) // 2):
                     runs["mlp"].start(2 * r + k)
+    leaving = pltpu.make_async_copy(mlp_ref, mlp_out, leave)
+    leaving.start()
     for name in groups:
         if isinstance(name, tuple) and name[0] != "load":
             runs[name].finish()
@@ -775,6 +779,7 @@
     runs["back"].finish()
     runs["out"].finish()
     runs["mlp"].finish()
+    leaving.wait()
     runs["slots"].finish()
 
 
@@ -837,7 +842,7 @@
             jax.ShapeDtypeStruct(((tp_count - 1) * 2 * room, run), BF),
         ],
         in_specs=[full] * 6 + [any_spec] * (2 + len(far)),
-        out_specs=[any_spec] * 2 + [full] * 3,
+        out_specs=[any_spec] * 3 + [full] * 2,
         scratch_shapes=[
             pltpu.VMEM((width, 2 * units), BF),
             pltpu.VMEM((width, units), BF),
@@ -847,6 +852,8 @@
             *[pltpu.VMEM((others, experts * part), BF)] * 4,
             pltpu.VMEM((others, 2 * units), BF),
             pltpu.VMEM((others, units), BF),
+            pltpu.VMEM((slots, width), BF),
+            pltpu.SemaphoreType.DMA,
         ]
         + [pltpu.SemaphoreType.DMA((total,))] * 2,
         compiler_params=pltpu.CompilerParams(

time: 538 us -> 537 us (level)
  no operation moved by 1% of the time
where the time goes in v8:
time: 537 us; the launch traced here: 530 us
  Pallas kernels  448 us (83%)
  local copies, waits for them, and re-layouts  40 us (7%)
  between operations  15.1 us (3%)
  waiting for transfers between devices  9.23 us (2%)
  other arithmetic  8.57 us (2%)
  starting transfers between devices  7.47 us (1%)
    pallas_call x2, Pallas kernels, move(): pl.pallas_call(functools.partial(move_kernel, ctx_count, moves, plain + [...  108 us
    pallas_call x1, Pallas kernels, attn_grads(): pl.pallas_call(functools.partial(attn_grads_kernel, ctx_count, groups, bi...  86.2 us
    pallas_call x1, Pallas kernels, run_experts(): pl.pallas_call(functools.partial(experts_kernel, ctx_count, experts, shar...  85.8 us
    pallas_call x1, Pallas kernels, front(): pl.pallas_call(functools.partial(front_kernel, ctx_count, moves, marks, n...  79.6 us
    pallas_call x1, Pallas kernels, attend_back(): pl.pallas_call(functools.partial(attend_back_kernel, ctx_count, moves, li...  61.9 us
    slice x1, local copies, waits for them, and re-layouts, expert_rows(): return [in_rows[:, 0, 0], in_rows[:, 0, 1], down_rows[:, 0]]  11.7 us
    pallas_call x1, Pallas kernels, spread_grads(): pl.pallas_call(functools.partial(spread_kernel, experts), grid_spec=pltpu...  10.8 us
  transfers between devices with their start and end apart: 8, of which 4 were waited for; matrix products, arithmetic and copies ran while one was open for 8% of the time, Pallas kernels for 24%

profile of v8, /device:TPU:0, one launch (start us, length us, event | category | flops | bytes accessed | tf_op | source)
XLA Modules:
  0.0 529.5 jit_solution(4931005634121120313)
XLA Ops:
  7.2 1.2 copy.92
  8.4 0.8 constant_dynamic-update-slice_fusion.1
  9.6 1.0 constant_dynamic-update-slice_fusion.refs_1_
  10.6 2.9 collective-permute-start.1
  13.5 1.5 collective-permute-start.3
  15.1 1.2 copy.91
  16.3 0.5 collective-permute-start
  16.9 0.6 fusion.7
  17.9 7.4 %constant_dynamic-slice_fusion.4 = (bf16[256,1,1408]{2,1,0:T(2,128)(2,1)}, bf16[256,1,1408]{2,1,0:T(2,128)(2,1)}, bf16[256,1,1408]{2,1,0:T(2,128)(2,1)}, bf16[256,1,1408]{2,1,0:T(2,128)(2,1)}) fusion(bf16[256,4,1408]{2,1,0:T(4,128)(2,1)S(1)} %copy-done, s32[]{:T(128)S(6)} %select_n.92, s32[]{:T(128)S(6)} %select_n.91, s32[]{:T(128)S(6)} %select_n.90, ...), kind=kLoop, calls=%fused_computation.41 | loop fusion | bytes 5767184 | tf_op jit(solution)/shard_map/dynamic_slice | solution.py:1448
  25.3 0.8 fusion.1
  26.2 0.5 copy-done.12
  26.7 1.2 convert_reduce_fusion
  28.0 3.0 fusion.4
  31.0 1.0 pad_maximum_fusion.cos_ref
  32.0 0.6 copy-done.10
  33.0 0.6 pad.13.about_ref
  33.7 0.6 pad.14.ride_ref
  34.3 0.6 pad.12.gain_ref
  34.9 11.7 %constant_dynamic-slice_fusion.5 = (bf16[256,1,1,1408]{3,2,1,0:T(2,128)(2,1)S(1)}, bf16[256,1,1,1408]{3,2,1,0:T(2,128)(2,1)S(1)}, bf16[256,1,1,1408]{3,2,1,0:T(2...) fusion(bf16[256,4,2,1408]{3,2,1,0:T(2,128)(2,1)} %param.20, ...), kind=kLoop, calls=%fused_computation.42 | loop fusion | bytes 11534356 | tf_op jit(solution)/shard_map/slice | solution.py:1503
  46.7 1.3 copy_bitcast_fusion.1
  48.0 1.3 copy_bitcast_fusion.4
  49.3 1.3 copy_bitcast_fusion.7
  50.6 1.0 pad_maximum_fusion.1.sin_ref
  51.7 6.0 %in_order.1 = (bf16[256,2048]{1,0:T(8,128)(2,1)}, bf16[256,2048]{1,0:T(8,128)(2,1)}) custom-call(s32[1]{0:T(128)} %bitcast.me_ref, bf16[256,2048]{1,0:T(8,128)(2,1)} %bitcast.61, bf16[256,2048]{1,0:T(8,128)(2,1)} %bitcast.62), custom_call_target="tpu_custom_call" | custom-call | tf_op jit(solution)/shard_map/in_order/pallas_call | solution.py:535
  57.7 0.6 add_convert_fusion.1
  58.3 0.9 fusion.3
  59.3 1.3 copy_bitcast_fusion.10
  60.6 0.6 copy-done.3
  61.6 1.3 copy_bitcast_fusion
  62.9 0.6 copy-done.1
  63.9 1.3 copy_bitcast_fusion.6
  65.2 5.5 %collective-permute-done.refs_2_ = bf16[256,2048]{1,0:T(8,128)(2,1)} collective-permute-done((bf16[256,2048]{1,0:T(8,128)(2,1)}, bf16[256,2048]{1,0:T(8,128)(2,1)}, u32[]{:S(2)}, u32[]{:S(2)}) %collective-permute-start) | collective-permute-done | bytes 1048608 | tf_op jit(solution)/shard_map/ppermute | solution.py:42
  70.7 1.5 collective-permute-done.2.refs_4_
  72.2 79.6 %front.1 = (bf16[128,512]{1,0:T(8,128)(2,1)}, bf16[256,2048]{1,0:T(8,128)(2,1)}, bf16[256,3072]{1,0:T(8,128)(2,1)}, bf16[1024,1024]{1,0:T(8,128)(2,1)}, bf16[256...) custom-call(bf16[256,2048]{1,0:T(8,128)(2,1)} %get-tuple-element.91., ...), custom_call_target="tpu_custom_call" | custom-call | tf_op jit(solution)/shard_map/front/pallas_call | solution.py:1074
  152.2 52.7 %weights_two.1 = (bf16[2048,2816]{1,0:T(8,128)(2,1)}, bf16[2048,1408]{1,0:T(8,128)(2,1)}) custom-call(bf16[256,1408]{1,0:T(8,128)(2,1)} %get-tuple-element.114.refs_9_.refs_0_, bf16[256,1408]{1,0:T(8,128)(2,1)} %get-tuple-element.115.refs_10_.refs_1_, ...), custom_call_target="tpu_custom_call", output_to_operand_aliasing={{0}: (10, {}), {1}: (9, {})} | custom-call | tf_op jit(solution)/shard_map/weights_two/pallas_call | solution.py:206
  205.0 85.8 %experts.1 = (bf16[1024,2816]{1,0:T(8,128)(2,1)}, bf16[1024,1408]{1,0:T(8,128)(2,1)}, bf16[576,2048]{1,0:T(8,128)(2,1)}, bf16[256,2048]{1,0:T(8,128)(2,1)}, bf16[864,512]{1,0:T(8,128)(2,1)}) custom-call(bf16[256,2048]{1,0:T(8,128)(2,1)} %get-tuple-element.91.tokens_ref.tokens_any.refs_0_, bf16[256,2048]{1,0:T(8,128)(2,1)} %all-reduce.6.cloned.1.call-done.branch_ref.refs_1_, ...), custom_call_target="tpu_custom_call" | custom-call | tf_op jit(solution)/shard_map/experts/pallas_call | solution.py:835
  290.8 0.8 copy.74.gate_ref
  291.6 55.7 %grads_near.1 = (bf16[256,2816]{1,0:T(8,128)(2,1)}, bf16[256,2816]{1,0:T(8,128)(2,1)}, bf16[256,1408]{1,0:T(8,128)(2,1)}, bf16[256,1408]{1,0:T(8,128)(2,1)}, bf1...) custom-call(bf16[1024,2816]{1,0:T(8,128)(2,1)} %get-tuple-element.144.refs_0_.refs_1_, ...), custom_call_target="tpu_custom_call" | custom-call | tf_op jit(solution)/shard_map/grads_near/pallas_call | solution.py:206
  347.3 61.9 %attend_back.1 = (bf16[256,3072]{1,0:T(8,128)(2,1)}, f32[256,2048]{1,0:T(8,128)}, bf16[256,2048]{1,0:T(8,128)(2,1)}, f32[1,2048]{1,0:T(1,128)}, bf16[256,2048]{1...) custom-call(bf16[256,2048]{1,0:T(8,128)(2,1)} %get-tuple-element.91., ...), custom_call_target="tpu_custom_call", output_to_operand_aliasing={{6}: (18, {}), {7}: (19, {})} | custom-call | tf_op jit(solution)/shard_map/attend_back/pallas_call | solution.py:1322
  409.2 86.2 %attn_grads.1 = (f32[256,2048]{1,0:T(8,128)}, f32[256,3072]{1,0:T(8,128)}, bf16[256,1536]{1,0:T(8,128)(2,1)}, bf16[256,1536]{1,0:T(8,128)(2,1)}, bf16[256,2048]{...) custom-call(bf16[256,2048]{1,0:T(8,128)(2,1)} %get-tuple-element.105.hidden_ref, ...), custom_call_target="tpu_custom_call" | custom-call | tf_op jit(solution)/shard_map/attn_grads/pallas_call | solution.py:487
  495.5 0.8 collective-permute-start.4
  496.3 1.2 collective-permute-start.5
  497.5 10.8 %spread_grads.1 = (f32[256,4,2,1408]{3,2,1,0:T(2,128)}, f32[256,4,1408]{2,1,0:T(4,128)}) custom-call(s32[1]{0:T(128)} %bitcast.35.me_ref, bf16[1024,2816]{1,0:T(8,128)(2,1)} %get-tuple-element.144.refs_0_.refs_1_, bf16[256,2816]{1,0:T(8,128)(2,1)} %get-tuple-element.135.refs_1_, bf16[256,2816]{1,0:T(8,128)(2,1)} %get-tuple-element.136.refs_2_, ...), custom_call_target="tpu_custom_call" | custom-call | tf_op jit(solution)/shard_map/spread_grads/pallas_call | solution.py:1376
  508.3 4.0 last.1
  512.3 1.3 fusion.9
  513.6 1.7 collective-permute-done.4.one_ref
  515.3 0.5 collective-permute-done.5.two_ref
  516.7 5.6 %lay_out.1 = (f32[256,4,512]{2,1,0:T(4,128)}, f32[256,2,512]{2,1,0:T(2,128)}, f32[256,4,512]{2,1,0:T(4,128)}) custom-call(f32[256,2048]{1,0:T(8,128)} %get-tuple-element.160.grad_ref, f32[256,3072]{1,0:T(8,128)} %get-tuple-element.161.keep_ref, bf16[256,1536]{1,0:T(8,128)(2,1)} %copy-done.8, bf16[256,1536]{1,0:T(8,128)(2,1)} %copy-done.9), custom_call_target="tpu_custom_call" | custom-call | tf_op jit(solution)/shard_map/lay_out/pallas_call | solution.py:597
  (109 shorter events, 3.6 us)
Async XLA Ops:
  7.2 2.1 copy-start.6
  7.2 197.8 %all-reduce.6.cloned.1.call-start = ((), (), s32[]{:S(2)}) async-start(), calls=%async_computation | async-start | bytes 2097152 | tf_op jit(solution)/shard_map/psum | solution.py:1622
  9.5 5.5 %copy-start.7 = (bf16[256,4,512]{2,1,0:T(4,128)(2,1)S(1)}, bf16[256,4,512]{2,1,0:T(4,128)(2,1)}, u32[]{:S(2)}) copy-start(bf16[256,4,512]{2,1,0:T(4,128)(2,1)} %param.18) | copy-start | bytes 3145732
  9.5 8.3 %copy-start = (bf16[256,4,1408]{2,1,0:T(4,128)(2,1)S(1)}, bf16[256,4,1408]{2,1,0:T(4,128)(2,1)}, u32[]{:S(2)}) copy-start(bf16[256,4,1408]{2,1,0:T(4,128)(2,1)} %param.21) | copy-start | bytes 8650756
  10.6 6.9 %copy-start.22 = (s32[1,256,2]{1,2,0:T(2,128)S(1)}, s32[1,256,2]{1,2,0:T(2,128)}, u32[]{:S(2)}) copy-start(s32[1,256,2]{1,2,0:T(2,128)} %param.25) | copy-start | bytes 6148
  10.6 60.1 %collective-permute-start.1 = (bf16[256,3072]{1,0:T(8,128)(2,1)}, bf16[256,3072]{1,0:T(8,128)(2,1)}, u32[]{:S(2)}, u32[]{:S(2)}) collective-permute-start(bf16[256,3072]{1,0:T(8,128)(2,1)} %constant_dynamic-update-slice_fusion.refs_1_), channel_id=1, source_target_pairs={{0,16},{4,20},{8,24},{12,28},{16,0},{20,4},{24,8},{28,12},{1,17},{... | collective-permute-start | bytes 4718600 | tf_op jit(solution)/shard_map/ppermute | solution.py:42
  13.5 58.6 %collective-permute-start.3 = (bf16[256,3072]{1,0:T(8,128)(2,1)}, bf16[256,3072]{1,0:T(8,128)(2,1)}, u32[]{:S(2)}, u32[]{:S(2)}) collective-permute-start(bf16[256,3072]{1,0:T(8,128)(2,1)} %constant_dynamic-update-slice_fusion.refs_1_), channel_id=1, source_target_pairs={{0,8},{4,12},{8,0},{12,4},{16,24},{20,28},{24,16},{28,20},{1,9},{5... | collective-permute-start | bytes 4718600 | tf_op jit(solution)/shard_map/ppermute | solution.py:42
  16.3 54.4 %collective-permute-start = (bf16[256,2048]{1,0:T(8,128)(2,1)}, bf16[256,2048]{1,0:T(8,128)(2,1)}, u32[]{:S(2)}, u32[]{:S(2)}) collective-permute-start(bf16[256,2048]{1,0:T(8,128)(2,1)} %bitcast.37.refs_0_), channel_id=1, source_target_pairs={{0,16},{4,20},{8,24},{12,28},{16,0},{20,4},{24,8},{28,12},{1,17},{... | collective-permute-start | bytes 3145736 | tf_op jit(solution)/shard_map/ppermute | solution.py:42
  16.8 55.3 %collective-permute-start.2 = (bf16[256,2048]{1,0:T(8,128)(2,1)}, bf16[256,2048]{1,0:T(8,128)(2,1)}, u32[]{:S(2)}, u32[]{:S(2)}) collective-permute-start(bf16[256,2048]{1,0:T(8,128)(2,1)} %bitcast.37.refs_0_), channel_id=1, source_target_pairs={{0,8},{4,12},{8,0},{12,4},{16,24},{20,28},{24,16},{28,20},{1,9},{5... | collective-permute-start | bytes 3145736 | tf_op jit(solution)/shard_map/ppermute | solution.py:42
  16.9 9.3 %copy-start.25 = (s32[256]{0:T(256)}, s32[256]{0:T(256)S(1)}, u32[]{:S(2)}) copy-start(s32[256]{0:T(256)S(1)} %iota_add_fusion.4) | copy-start | bytes 3076
  16.9 9.3 %copy-start.27 = (s32[256]{0:T(256)}, s32[256]{0:T(256)S(1)}, u32[]{:S(2)}) copy-start(s32[256]{0:T(256)S(1)} %iota_add_fusion.1) | copy-start | bytes 3076
  16.9 9.3 %copy-start.29 = (s32[256]{0:T(256)}, s32[256]{0:T(256)S(1)}, u32[]{:S(2)}) copy-start(s32[256]{0:T(256)S(1)} %iota_add_fusion.2) | copy-start | bytes 3076
  16.9 9.3 %copy-start.31 = (s32[256]{0:T(256)}, s32[256]{0:T(256)S(1)}, u32[]{:S(2)}) copy-start(s32[256]{0:T(256)S(1)} %iota_add_fusion.3) | copy-start | bytes 3076
  17.8 7.4 %copy-start.20 = (s32[1,256,2]{1,2,0:T(2,128)S(1)}, s32[1,256,2]{1,2,0:T(2,128)}, u32[]{:S(2)}) copy-start(s32[1,256,2]{1,2,0:T(2,128)} %param.23) | copy-start | bytes 6148
  17.9 8.3 %copy-start.33 = (s32[1,1024]{1,0:T(1,128)S(1)}, s32[1,1024]{1,0:T(1,128)}, u32[]{:S(2)}) copy-start(s32[1,1024]{1,0:T(1,128)} %param.22) | copy-start | bytes 12292
  25.2 6.7 %copy-start.21 = (s32[1,256,2]{1,2,0:T(2,128)S(1)}, s32[1,256,2]{1,2,0:T(2,128)}, u32[]{:S(2)}) copy-start(s32[1,256,2]{1,2,0:T(2,128)} %param.23) | copy-start | bytes 6148
  25.3 6.7 %copy-start.36 = (f32[1,256,2]{1,2,0:T(2,128)S(1)}, f32[1,256,2]{1,2,0:T(2,128)}, u32[]{:S(2)}) copy-start(f32[1,256,2]{1,2,0:T(2,128)} %param.24) | copy-start | bytes 6148
  25.3 7.3 %copy-start.34 = (bf16[256,1]{0,1:T(2,128)(2,1)S(1)}, bf16[256,1]{0,1:T(2,128)(2,1)}, u32[]{:S(2)}) copy-start(bf16[256,1]{0,1:T(2,128)(2,1)} %get-tuple-element.207) | copy-start | bytes 1540
  25.3 7.3 %copy-start.35 = (bf16[256,1]{0,1:T(2,128)(2,1)S(1)}, bf16[256,1]{0,1:T(2,128)(2,1)}, u32[]{:S(2)}) copy-start(bf16[256,1]{0,1:T(2,128)(2,1)} %get-tuple-element.208) | copy-start | bytes 1540
  25.3 7.5 %copy-start.23 = (s32[1,256,2]{1,2,0:T(2,128)S(1)}, s32[1,256,2]{1,2,0:T(2,128)}, u32[]{:S(2)}) copy-start(s32[1,256,2]{1,2,0:T(2,128)} %param.25) | copy-start | bytes 6148
  25.3 7.5 %copy-start.37 = (f32[1,256,2]{1,2,0:T(2,128)S(1)}, f32[1,256,2]{1,2,0:T(2,128)}, u32[]{:S(2)}) copy-start(f32[1,256,2]{1,2,0:T(2,128)} %param.26) | copy-start | bytes 6148
  26.1 0.6 copy-start.12
  26.1 0.6 copy-start.14
  26.1 0.6 copy-start.16
  26.2 0.6 copy-start.18
  28.0 6.4 %copy-start.38 = (bf16[256]{0:T(256)(128)(2,1)S(1)}, bf16[256]{0:T(256)(128)(2,1)}, u32[]{:S(2)}) copy-start(bf16[256]{0:T(256)(128)(2,1)} %param.16) | copy-start | bytes 1540
  28.0 6.3 %copy-start.39 = (bf16[256]{0:T(256)(128)(2,1)S(1)}, bf16[256]{0:T(256)(128)(2,1)}, u32[]{:S(2)}) copy-start(bf16[256]{0:T(256)(128)(2,1)} %param.15) | copy-start | bytes 1540
  32.0 0.6 copy-start.10
  49.3 1.3 copy-start.5
  51.6 6.0 %copy-start.13 = (s32[1,256]{1,0:T(1,128)S(1)}, s32[1,256]{1,0:T(1,128)}, u32[]{:S(2)}) copy-start(s32[1,256]{1,0:T(1,128)} %copy-done.12) | copy-start | bytes 3076
  51.6 6.0 %copy-start.15 = (s32[1,256]{1,0:T(1,128)S(1)}, s32[1,256]{1,0:T(1,128)}, u32[]{:S(2)}) copy-start(s32[1,256]{1,0:T(1,128)} %copy-done.14) | copy-start | bytes 3076
  51.6 6.0 %copy-start.17 = (s32[1,256]{1,0:T(1,128)S(1)}, s32[1,256]{1,0:T(1,128)}, u32[]{:S(2)}) copy-start(s32[1,256]{1,0:T(1,128)} %copy-done.16) | copy-start | bytes 3076
  51.6 6.0 %copy-start.19 = (s32[1,256]{1,0:T(1,128)S(1)}, s32[1,256]{1,0:T(1,128)}, u32[]{:S(2)}) copy-start(s32[1,256]{1,0:T(1,128)} %copy-done.18) | copy-start | bytes 3076
  51.6 6.1 %copy-start.26 = (s32[256]{0:T(256)S(1)}, s32[256]{0:T(256)}, u32[]{:S(2)}) copy-start(s32[256]{0:T(256)} %copy-done.25) | copy-start | bytes 3076
  51.6 6.1 %copy-start.28 = (s32[256]{0:T(256)S(1)}, s32[256]{0:T(256)}, u32[]{:S(2)}) copy-start(s32[256]{0:T(256)} %copy-done.27) | copy-start | bytes 3076
  51.7 6.1 %copy-start.30 = (s32[256]{0:T(256)S(1)}, s32[256]{0:T(256)}, u32[]{:S(2)}) copy-start(s32[256]{0:T(256)} %copy-done.29) | copy-start | bytes 3076
  51.7 6.1 %copy-start.32 = (s32[256]{0:T(256)S(1)}, s32[256]{0:T(256)}, u32[]{:S(2)}) copy-start(s32[256]{0:T(256)} %copy-done.31) | copy-start | bytes 3076
  51.7 6.7 %copy-start.24 = (s32[4,256]{1,0:T(4,128)S(1)}, s32[4,256]{1,0:T(4,128)}, u32[]{:S(2)}) copy-start(s32[4,256]{1,0:T(4,128)} %fusion.1) | copy-start | bytes 12292
  59.3 1.9 copy-start.3
  59.3 2.3 copy-start.4
  61.6 1.9 copy-start.1
  61.6 2.3 copy-start.2
  151.8 195.5 %all-reduce.8.cloned.1.call-start = ((), (), s32[]{:S(2)}) async-start(), calls=%async_computation.1 | async-start | bytes 2097152 | tf_op jit(solution)/shard_map/psum | solution.py:1654
  205.0 85.8 %copy-start.11 = (f32[256,4]{0,1:T(4,128)S(1)}, f32[256,4]{0,1:T(4,128)}, u32[]{:S(2)}) copy-start(f32[256,4]{0,1:T(4,128)} %copy-done.10) | copy-start | bytes 12292
  495.5 19.8 %collective-permute-start.4 = (bf16[256,1536]{1,0:T(8,128)(2,1)}, bf16[256,1536]{1,0:T(8,128)(2,1)S(1)}, u32[]{:S(2)}, u32[]{:S(2)}) collective-permute-start(bf16[256,1536]{1,0:T(8,128)(2,1)} %get-tuple-element.162), channel_id=1, source_target_pairs={{0,8},{4,12},{8,0},{12,4},{16,24},{20,28},{24,16},{28,20},{1,9},{5... | collective-permute-start | bytes 2359304 | tf_op jit(solution)/shard_map/ppermute | solution.py:42
  496.3 19.5 %collective-permute-start.5 = (bf16[256,1536]{1,0:T(8,128)(2,1)}, bf16[256,1536]{1,0:T(8,128)(2,1)S(1)}, u32[]{:S(2)}, u32[]{:S(2)}) collective-permute-start(bf16[256,1536]{1,0:T(8,128)(2,1)} %get-tuple-element.163), channel_id=1, source_target_pairs={{0,16},{4,20},{8,24},{12,28},{16,0},{20,4},{24,8},{28,12},{1,17},{... | collective-permute-start | bytes 2359304 | tf_op jit(solution)/shard_map/ppermute | solution.py:42
  515.3 0.9 copy-start.8
  515.8 0.9 copy-start.9
Sparse Core Ops, SparseCore 0:
  151.9 52.0 all-reduce.5
  290.9 49.9 all-reduce.7
